TPU v7x, 512 devices: a whole 4x8x8 slice. The times are simulated.
512 devices in a mesh: cuts: 16 (over x_hi, y), space: 32 (over z, x_lo, core).
Axes of the slice: x: 4 (x_hi: 2, x_lo: 2; x = x_hi * 2 + x_lo), y: 8, z: 8, core: 2. Of those that a mesh axis runs over, the one named last changes fastest.
Arguments:
- starts: float32 [16, 128, 64, 512], P('cuts', 'space'), may hold values from -6 to 6
- velocity: float32 [3, 128, 64, 512], P(None, 'space'), may hold values from -1 to 1
- diffusivity: float32 [128, 64, 512], P('space'), may hold values from 0.02 to 0.1
Outputs:
- new_ends: float32 [16, 128, 64, 512], P('cuts', 'space')
All inputs are finite; a program needn't handle non-finite values.
Results may differ from a plain program's by a relative error of at most 0.00002.
Values sent between devices are 32-bit elements; how exact they have to be, the bound alone decides.
No kernel may reach another device: no remote copies, remote signals or barrier semaphores. Data moves between devices by JAX's collectives and lax.ppermute only.
A program may use at most 64 MiB of HBM per device.

v0:
```python
import jax
import jax.numpy as jnp
from jax import lax
from jax.sharding import PartitionSpec as P

RATIO = 4
FINE_STEPS = 16
COARSE_STEPS = 4


time_step = 0.2


def padded(cells, sides, width):
    for axis, dim in sides:
        count = lax.axis_size(axis)
        head = lax.slice_in_dim(cells, 0, width, axis=dim)
        tail = lax.slice_in_dim(cells, cells.shape[dim] - width, cells.shape[dim], axis=dim)
        cells = jnp.concatenate(
            [
                lax.ppermute(tail, axis, [(i, (i + 1) % count) for i in range(count)]),
                cells,
                lax.ppermute(head, axis, [((i + 1) % count, i) for i in range(count)]),
            ],
            axis=dim,
        )
    return cells


def from_behind(block, axis, distance):
    devices = range(lax.axis_size(axis))
    route = [(i - distance, i) for i in devices if i - distance in devices]
    return lax.ppermute(block, axis, route)


def advance(extended, velocity, diffusion, step_size, spacing):
    centre = extended[1:-1]
    forward_x = extended[2:]
    backward_x = extended[:-2]
    forward_y = jnp.roll(centre, -1, 1)
    backward_y = jnp.roll(centre, 1, 1)
    forward_z = jnp.roll(centre, -1, 2)
    backward_z = jnp.roll(centre, 1, 2)
    transport = jnp.maximum(velocity[0], 0.0) * (centre - backward_x) + jnp.minimum(
        velocity[0], 0.0
    ) * (forward_x - centre)
    transport = (
        transport
        + jnp.maximum(velocity[1], 0.0) * (centre - backward_y)
        + jnp.minimum(velocity[1], 0.0) * (forward_y - centre)
    )
    transport = (
        transport
        + jnp.maximum(velocity[2], 0.0) * (centre - backward_z)
        + jnp.minimum(velocity[2], 0.0) * (forward_z - centre)
    )
    laplace = (
        forward_x + backward_x + forward_y + backward_y + forward_z + backward_z - 6.0 * centre
    )
    return centre + step_size * (diffusion * laplace / (spacing * spacing) - transport / spacing)


def restrict(current):
    extent_x, extent_y, extent_z = current.shape
    blocks = current.reshape(
        extent_x // RATIO, RATIO, extent_y // RATIO, RATIO, extent_z // RATIO, RATIO
    )
    return jnp.mean(blocks, axis=(1, 3, 5))


def prolong(current):
    extent_x, extent_y, extent_z = current.shape
    spread = jnp.broadcast_to(
        current[:, None, :, None, :, None], (extent_x, RATIO, extent_y, RATIO, extent_z, RATIO)
    )
    return spread.reshape(extent_x * RATIO, extent_y * RATIO, extent_z * RATIO)


def coarse_run(current, velocity, diffusion):
    for substep in range(COARSE_STEPS):
        extended = padded(current, (("space", 0),), 1)
        current = advance(extended, velocity, diffusion, time_step * RATIO, 1.0 * RATIO)
    return current


def shards(starts, velocity, diffusivity):
    current = starts[0]
    stacked = jnp.concatenate([velocity, diffusivity[None]], axis=0)
    halo_width = 1

    def sweep_block(round_index, state_now):
        extended = padded(state_now, (("space", 0),), halo_width)
        extended = advance(extended, stacked[:3], stacked[3], time_step, 1.0)
        return extended

    fine_end = lax.fori_loop(0, FINE_STEPS // halo_width, sweep_block, current)
    coarse_velocity = jnp.stack([restrict(velocity[component]) for component in range(3)])
    coarse_diffusion = restrict(diffusivity)
    coarse_old = restrict(current)
    image_old = coarse_run(coarse_old, coarse_velocity, coarse_diffusion)
    jump_term = restrict(fine_end) - image_old
    position = lax.axis_index("cuts")
    slice_count = lax.axis_size("cuts")

    def relay_link(link_index, carried):
        arrived = from_behind(
            coarse_run(carried, coarse_velocity, coarse_diffusion) + jump_term, "cuts", 1
        )
        return jnp.where(position == 0, coarse_old, arrived)

    coarse_new = lax.fori_loop(0, slice_count - 1, relay_link, coarse_old)
    image_new = coarse_run(coarse_new, coarse_velocity, coarse_diffusion)
    result = prolong(image_new) + fine_end - prolong(image_old)
    return result[None]


def solution(mesh):
    placed = (P("cuts", "space", None, None), P(None, "space", None, None), P("space", None, None))
    return jax.shard_map(
        shards,
        mesh=mesh,
        in_specs=placed,
        out_specs=P("cuts", "space", None, None),
        check_vma=False,
    )
```

profile of v0, /device:TPU:4, one launch (start us, length us, event | category | flops | bytes accessed | tf_op | source)
XLA Modules:
  0.0 1080.5 jit_solution(8159671552711735953)
XLA Ops:
  3.0 5.7 reduce_sum.70
  11.2 11.0 %collective-permute-start.11 = (f32[1,16,128]{2,1,0:T(8,128)S(1)}, f32[1,16,128]{2,1,0:T(8,128)S(1)}, u32[]{:S(2)}, u32[]{:S(2)}) collective-permute-start(f32[1,16,128]{2,1,0:T(8,128)S(1)} %multiply_bitcast_fusion.4), channel_id=1, source_target_pairs={{1,0},{2,1},{3,2},{4,3},{5,4},{6,5},{7,6},{8,7},{9,8},{10,9},{11,1... | collective-permute-start | bytes 24584 | tf_op jit(solution)/shard_map/ppermute | solution.py:23
  25.0 5.7 reduce_sum.109
  33.3 5.7 reduce_sum.82
  41.5 5.7 reduce_sum.85
  50.8 5.7 reduce_sum.76
  59.1 245.4 %while.22 = (s32[]{:T(128)}, f32[4,64,512]{2,1,0:T(8,128)}, f32[4,64,512]{2,1,0:T(8,128)}, f32[3,4,64,512]{3,2,1,0:T(8,128)S(1)}, s32[]{:T(128)}) while((s32[]{:T(128)}, f32[4,64,512]{2,1,0:T(8,128)}, f32[4,64,512]{2,1,0:T(8,128)}, f32[3,4,64,512]{3,2,1,0:T(8,128)S(1)}, s32[]{:T(128)}) %tuple.144), condition=%wide.region_11.12_spmd, body=%wide.region_10.11_spmd.sunk | while | flops 5242882 | bytes 12320909 | solution.py:96
  62.8 5.8 collective-permute-start.1
  78.0 5.9 collective-permute-start.1
  93.3 5.9 collective-permute-start.1
  108.7 5.9 collective-permute-start.1
  124.0 5.9 collective-permute-start.1
  139.4 5.9 collective-permute-start.1
  154.7 5.9 collective-permute-start.1
  170.0 5.9 collective-permute-start.1
  185.4 5.9 collective-permute-start.1
  200.7 5.9 collective-permute-start.1
  216.1 5.9 collective-permute-start.1
  231.4 5.9 collective-permute-start.1
  246.8 5.9 collective-permute-start.1
  262.1 5.9 collective-permute-start.1
  277.4 5.9 collective-permute-start.1
  292.8 5.9 collective-permute-start.1
  305.6 5.7 reduce_sum.112
  314.8 5.9 collective-permute-start.13
  322.6 5.1 collective-permute-done.14
  346.0 682.4 %while.23 = (s32[]{:T(128)}, f32[1,16,128]{2,1,0:T(8,128)S(1)}, pred[]{:T(512)}, f32[1,16,128]{2,1,0:T(8,128)S(1)}, f32[1,16,128]{2,1,0:T(8,128)S(1)}, /*index=5...) while((s32[]{:T(128)}, f32[1,16,128]{2,1,0:T(8,128)S(1)}, ...), condition=%wide.region_15.16_spmd, body=%wide.region_14.15_spmd.sunk | while | flops 331778 | bytes 983502 | solution.py:111
  350.5 4.5 collective-permute-done.3
  359.6 4.5 collective-permute-done.5
  368.7 4.5 collective-permute-done.7
  377.7 4.5 collective-permute-done.9
  385.8 5.7 collective-permute-done.10
  396.0 4.5 collective-permute-done.3
  429.7 7.2 collective-permute-done.10
  441.5 4.5 collective-permute-done.3
  475.2 7.2 collective-permute-done.10
  487.0 4.5 collective-permute-done.3
  520.7 7.3 collective-permute-done.10
  566.3 7.2 collective-permute-done.10
  611.8 7.2 collective-permute-done.10
  657.3 7.2 collective-permute-done.10
  702.7 7.2 collective-permute-done.10
  748.2 7.2 collective-permute-done.10
  778.1 4.5 collective-permute-done.7
  793.7 7.2 collective-permute-done.10
  823.6 4.5 collective-permute-done.7
  839.2 7.2 collective-permute-done.10
  869.1 4.5 collective-permute-done.7
  884.7 7.2 collective-permute-done.10
  905.5 4.5 collective-permute-done.5
  914.6 4.5 collective-permute-done.7
  923.7 4.5 collective-permute-done.9
  930.2 7.2 collective-permute-done.10
  951.0 4.5 collective-permute-done.5
  960.1 4.5 collective-permute-done.7
  969.2 4.5 collective-permute-done.9
  975.7 7.2 collective-permute-done.10
  996.5 4.5 collective-permute-done.5
  1014.7 4.5 collective-permute-done.9
  1021.2 7.2 collective-permute-done.10
  1035.4 4.9 broadcast_in_dim.33
  1040.5 5.3 collective-permute-start.21
  1047.9 5.0 collective-permute-done.22
  1073.6 4.9 broadcast_in_dim.29
  (803 shorter events, 719.5 us)
Async XLA Ops:
  11.2 302.6 %collective-permute-start.11 = (f32[1,16,128]{2,1,0:T(8,128)S(1)}, f32[1,16,128]{2,1,0:T(8,128)S(1)}, u32[]{:S(2)}, u32[]{:S(2)}) collective-permute-start(f32[1,16,128]{2,1,0:T(8,128)S(1)} %multiply_bitcast_fusion.4), channel_id=1, source_target_pairs={{1,0},{2,1},{3,2},{4,3},{5,4},{6,5},{7,6},{8,7},{9,8},{10,9},{11,1... | collective-permute-start | bytes 24584 | tf_op jit(solution)/shard_map/ppermute | solution.py:23
  22.2 291.6 %collective-permute-start.12 = (f32[1,16,128]{2,1,0:T(8,128)S(1)}, f32[1,16,128]{2,1,0:T(8,128)}, u32[]{:S(2)}, u32[]{:S(2)}) collective-permute-start(f32[1,16,128]{2,1,0:T(8,128)S(1)} %multiply_bitcast_fusion.4), channel_id=1, source_target_pairs={{0,1},{1,2},{2,3},{3,4},{4,5},{5,6},{6,7},{7,8},{8,9},{9,10},{10,1... | collective-permute-start | bytes 24584 | tf_op jit(solution)/shard_map/ppermute | solution.py:21
  60.9 9.1 collective-permute-start
  62.8 8.6 collective-permute-start.1
  76.1 9.2 collective-permute-start
  78.0 8.7 collective-permute-start.1
  91.4 9.2 collective-permute-start
  93.3 8.7 collective-permute-start.1
  106.8 9.2 collective-permute-start
  108.7 8.7 collective-permute-start.1
  122.1 9.2 collective-permute-start
  124.0 8.7 collective-permute-start.1
  137.4 9.2 collective-permute-start
  139.4 8.7 collective-permute-start.1
  152.8 9.2 collective-permute-start
  154.7 8.7 collective-permute-start.1
  168.1 9.2 collective-permute-start
  170.0 8.7 collective-permute-start.1
  183.5 9.2 collective-permute-start
  185.4 8.7 collective-permute-start.1
  198.8 9.2 collective-permute-start
  200.7 8.7 collective-permute-start.1
  214.2 9.2 collective-permute-start
  216.1 8.7 collective-permute-start.1
  229.5 9.2 collective-permute-start
  231.4 8.7 collective-permute-start.1
  244.8 9.2 collective-permute-start
  246.8 8.7 collective-permute-start.1
  260.2 9.2 collective-permute-start
  262.1 8.7 collective-permute-start.1
  275.5 9.2 collective-permute-start
  277.4 8.7 collective-permute-start.1
  290.9 9.2 collective-permute-start
  292.8 8.7 collective-permute-start.1
  314.8 7.8 collective-permute-start.13
  320.7 7.1 collective-permute-start.14
  329.8 7.1 collective-permute-start.16
  347.9 7.1 collective-permute-start.3
  357.0 7.1 collective-permute-start.5
  366.1 7.1 collective-permute-start.7
  375.2 7.1 collective-permute-start.9
  382.3 9.1 collective-permute-start.10
  393.4 7.1 collective-permute-start.3
  402.5 7.1 collective-permute-start.5
  411.6 7.1 collective-permute-start.7
  420.7 7.1 collective-permute-start.9
  427.8 9.1 collective-permute-start.10
  438.9 7.1 collective-permute-start.3
  473.3 9.1 collective-permute-start.10
  518.8 9.2 collective-permute-start.10
  564.4 9.1 collective-permute-start.10
  609.8 9.1 collective-permute-start.10
  655.3 9.1 collective-permute-start.10
  700.8 9.1 collective-permute-start.10
  746.3 9.1 collective-permute-start.10
  791.8 9.1 collective-permute-start.10
  837.3 9.1 collective-permute-start.10
  882.8 9.1 collective-permute-start.10
  928.3 9.1 collective-permute-start.10
  973.8 9.1 collective-permute-start.10
  1019.2 9.1 collective-permute-start.10
  1028.4 12.0 %collective-permute-start.19 = (f32[1,16,128]{2,1,0:T(8,128)S(1)}, f32[1,16,128]{2,1,0:T(8,128)S(1)}, u32[]{:S(2)}, u32[]{:S(2)}) collective-permute-start(f32[1,16,128]{2,1,0:T(8,128)S(1)} %get-tuple-element.133), channel_id=1, source_target_pairs={{1,0},{2,1},{3,2},{4,3},{5,4},{6,5},{7,6},{8,7},{9,8},{10,9},{11,1... | collective-permute-start | bytes 24584 | tf_op jit(solution)/shard_map/ppermute | solution.py:23
  1030.3 10.1 collective-permute-start.20
  1040.5 7.4 collective-permute-start.21
  (122 other events, 715.3 us)
where the time goes:
time: 1090 us; the launch traced here: 1080 us
  starting transfers between devices  463 us (42%)
  waiting for transfers between devices  427 us (39%)
  local copies, waits for them, and re-layouts  113 us (10%)
  other arithmetic  74.5 us (7%)
    ppermute x84, waiting for transfers between devices, padded(): lax.ppermute(tail, axis, [(i, (i + 1) % count) for i in range(count)])  298 us
    ppermute x84, starting transfers between devices, padded(): lax.ppermute(head, axis, [((i + 1) % count, i) for i in range(count)])  240 us
    ppermute x84, starting transfers between devices, padded(): lax.ppermute(tail, axis, [(i, (i + 1) % count) for i in range(count)])  193 us
    ppermute x15, waiting for transfers between devices, from_behind(): return lax.ppermute(block, axis, route)  107 us
    add x67, other arithmetic, advance(): centre + step_size * (diffusion * laplace / (spacing * spacing) - transpo...  52.4 us
    reduce_sum x6, local copies, waits for them, and re-layouts, restrict(): return jnp.mean(blocks, axis=(1, 3, 5))  34.2 us
    ppermute x15, starting transfers between devices, from_behind(): return lax.ppermute(block, axis, route)  30.2 us
    ppermute x84, waiting for transfers between devices, padded(): lax.ppermute(head, axis, [((i + 1) % count, i) for i in range(count)])  22.4 us
  transfers between devices with their start and end apart: 183, of which 97 were waited for; matrix products, arithmetic and copies ran while one was open for 15% of the time, Pallas kernels for 0%

commit v1 on v0

v1 whole, which is shorter than its diff:
```python
import functools

import jax
import jax.numpy as jnp
from jax import lax
from jax.experimental import pallas as pl
from jax.experimental.pallas import tpu as pltpu
from jax.sharding import PartitionSpec as P

RATIO = 4
LAYERS = 4
REACH = 3
TILE = (8, 4, 8, 128)
COARSE = (2, 8, 128)
ROUNDS = (1, 4, 4, 4, 3)
STEP = 0.2
VMEM = pl.BlockSpec(memory_space=pltpu.VMEM)
F32 = jnp.float32
MIB = 1024 * 1024


def call(body, outs, scratch=(), smem=0, ins=0, limit=32):
    specs = [pl.BlockSpec(memory_space=pltpu.SMEM)] * smem + [VMEM] * ins
    return pl.pallas_call(
        body,
        out_shape=[jax.ShapeDtypeStruct(s, F32) for s in outs],
        in_specs=specs,
        out_specs=[VMEM] * len(outs),
        scratch_shapes=list(scratch),
        compiler_params=pltpu.CompilerParams(vmem_limit_bytes=limit * MIB),
    )


def comb(transposed):
    a = lax.broadcasted_iota(jnp.int32, (512, 512), 0)
    b = lax.broadcasted_iota(jnp.int32, (512, 512), 1)
    natural, apart = (b, a) if transposed else (a, b)
    hit = natural == 4 * (apart & 127) + (apart >> 7)
    return jnp.where(hit, 1.0, 0.0).astype(jnp.bfloat16)


def exact_dot(rows, matrix):
    high = rows.astype(jnp.bfloat16)
    rest = rows - high.astype(F32)
    middle = rest.astype(jnp.bfloat16)
    low = (rest - middle.astype(F32)).astype(jnp.bfloat16)
    dot = functools.partial(jnp.dot, preferred_element_type=F32)
    return (dot(high, matrix) + dot(middle, matrix)) + dot(low, matrix)


def split_layer(rows, matrix, buffer):
    apart = exact_dot(rows, matrix)
    for q in range(4):
        buffer[q] = apart[:, q * 128 : (q + 1) * 128]
    return [[buffer[q, pl.ds(j, 8, stride=8), :] for q in range(4)] for j in range(8)]


def half_sum(tiles, h):
    total = None
    for j in range(4 * h, 4 * h + 4):
        for q in range(4):
            total = tiles[j][q] if total is None else total + tiles[j][q]
    return total


def state_kernel(starts, state, first, last, coarse, buffer):
    matrix = comb(False)
    sums = [None, None]
    for x in range(LAYERS):
        tiles = split_layer(starts[0, x], matrix, buffer.at[x])
        for j in range(8):
            for q in range(4):
                state[x, j, q] = tiles[j][q]
                if x == 0:
                    first[0, j, q] = tiles[j][q]
                if x == LAYERS - 1:
                    last[0, j, q] = tiles[j][q]
        for h in range(2):
            part = half_sum(tiles, h)
            sums[h] = part if sums[h] is None else sums[h] + part
    for h in range(2):
        coarse[h] = sums[h] * (1.0 / 64)


def weigh(velocity, diffusion, step, spacing):
    spread = diffusion * (step / (spacing * spacing))
    weights = [None]
    for component in velocity:
        moved = component * (step / spacing)
        weights.append(spread + jnp.maximum(moved, 0.0))
        weights.append(spread - jnp.minimum(moved, 0.0))
    total = weights[1]
    for weight in weights[2:]:
        total = total + weight
    weights[0] = 1.0 - total
    return weights


def field_kernel(velocity, diffusivity, own, head, tail, coarse, buffer):
    matrix = comb(False)
    for f in range(4):
        for h in range(2):
            coarse[f, h] = jnp.zeros((8, 128), F32)

    def layer(x, carry):
        for f in range(4):
            rows = velocity[f, x] if f < 3 else diffusivity[x]
            tiles = split_layer(rows, matrix, buffer.at[f])
            for h in range(2):
                coarse[f, h] += half_sum(tiles, h) * (1.0 / 64)
            for j in range(8):
                for q in range(4):
                    own[x, f, j, q] = tiles[j][q]
        return carry

    lax.fori_loop(0, LAYERS, layer, 0)
    head[...] = own[:REACH]
    tail[...] = own[LAYERS - REACH :]


def weight_kernel(count, fields, weights):
    def layer(x, carry):
        for j in range(8):
            for q in range(4):
                parts = [fields[x, f, j, q] for f in range(4)]
                for i, weight in enumerate(weigh(parts[:3], parts[3], STEP, 1.0)):
                    weights[x, i, j, q] = weight
        return carry

    lax.fori_loop(0, count, layer, 0)


def fine_layer(source, weights, target, x, wx, tx):
    tiles = [[source[x, j, q] for q in range(4)] for j in range(8)]
    for j in range(8):
        for q in range(4):
            behind_y = tiles[j - 1][q] if j > 0 else pltpu.roll(tiles[7][q], 1, 0)
            ahead_y = tiles[j + 1][q] if j < 7 else pltpu.roll(tiles[0][q], 7, 0)
            behind_z = tiles[j][q - 1] if q > 0 else pltpu.roll(tiles[j][3], 1, 1)
            ahead_z = tiles[j][q + 1] if q < 3 else pltpu.roll(tiles[j][0], 127, 1)
            target[tx, j, q] = (
                (weights[wx, 0, j, q] * tiles[j][q] + weights[wx, 1, j, q] * source[x - 1, j, q])
                + (weights[wx, 2, j, q] * source[x + 1, j, q] + weights[wx, 3, j, q] * behind_y)
                + (weights[wx, 4, j, q] * ahead_y + weights[wx, 5, j, q] * behind_z)
                + weights[wx, 6, j, q] * ahead_z
            )


def round_kernel(width, final, *refs):
    if width > 1:
        state, left, right, own, own_left, own_right, *refs = refs
    else:
        state, left, right, own, *refs = refs
        own_left = own_right = None
    if final:
        later, out, residual, one, two = refs
    else:
        out, one, two = refs
    for x in range(width):
        one[LAYERS - width + x] = left[x]
        one[2 * LAYERS + x] = right[x]
    for x in range(LAYERS):
        one[LAYERS + x] = state[x]
    source, target = one, two
    for step in range(1, width + 1):
        ends = step == width
        goal = out if ends else target
        shift = LAYERS if ends else 0

        def sweep(begin, end, weights, offset, source=source, goal=goal, shift=shift):
            if end <= begin:
                return

            def body(x, carry):
                fine_layer(source, weights, goal, x, x - offset, x - shift)
                return carry

            lax.fori_loop(begin, end, body, 0)

        sweep(LAYERS - width + step, LAYERS, own_left, LAYERS - REACH)
        sweep(LAYERS, 2 * LAYERS, own, LAYERS)
        sweep(2 * LAYERS, 2 * LAYERS + width - step, own_right, 2 * LAYERS)
        source, target = target, source
    if final:
        for h in range(2):
            total = None
            for x in range(LAYERS):
                part = half_sum([[out[x, j, q] for q in range(4)] for j in range(8)], h)
                total = part if total is None else total + part
            residual[h] = total * (1.0 / 64) - later[h]


def coarse_step(read, weights, write, count):
    first = read(0)
    behind, now = read(count - 1), first
    for x in range(count):
        ahead = read(x + 1) if x + 1 < count else first
        for h in range(2):
            behind_y = now[0] if h else pltpu.roll(now[1], 1, 0)
            ahead_y = pltpu.roll(now[0], 7, 0) if h else now[1]
            behind_z = pltpu.roll(now[h], 1, 1)
            ahead_z = pltpu.roll(now[h], 127, 1)
            write(
                x,
                h,
                (weights[x, 0, h] * now[h] + weights[x, 1, h] * behind[h])
                + (weights[x, 2, h] * ahead[h] + weights[x, 3, h] * behind_y)
                + (weights[x, 4, h] * ahead_y + weights[x, 5, h] * behind_z)
                + weights[x, 6, h] * ahead_z,
            )
        behind, now = now, ahead


def chain_kernel(place, residuals, fields, state, out, weights, one, two, buffer):
    count = fields.shape[0]
    slice_index = place[0]
    layer_index = place[1]

    def prepare(x, carry):
        for h in range(2):
            parts = [fields[x, f, h] for f in range(4)]
            for i, weight in enumerate(weigh(parts[:3], parts[3], STEP * RATIO, 1.0 * RATIO)):
                weights[x, i, h] = weight
            one[x, h] = jnp.zeros((8, 128), F32)
        return carry

    lax.fori_loop(0, count, prepare, 0)

    def reader(ref):
        return lambda x: [ref[x, h] for h in range(2)]

    def writer(ref):
        def write(x, h, value):
            ref[x, h] = value

        return write

    def link(m, carry):
        def entering(x):
            return [one[x, h] + residuals[x, m, h] for h in range(2)]

        coarse_step(entering, weights, writer(two), count)
        coarse_step(reader(two), weights, writer(one), count)
        coarse_step(reader(one), weights, writer(two), count)
        coarse_step(reader(two), weights, writer(one), count)
        return carry

    lax.fori_loop(0, slice_index, link, 0)
    change = [one[layer_index, h] for h in range(2)]
    matrix = comb(True)
    for x in range(LAYERS):
        for j in range(8):
            for q in range(4):
                buffer[x, q, pl.ds(j, 8, stride=8), :] = state[x, j, q] + change[j // 4]
        rows = jnp.concatenate([buffer[x, q] for q in range(4)], axis=1)
        out[0, x] = exact_dot(rows, matrix)


def shift(block, axis, distance):
    count = lax.axis_size(axis)
    return lax.ppermute(block, axis, [(i, (i + distance) % count) for i in range(count)])


def shards(starts, velocity, diffusivity):
    count = lax.axis_size("space")
    block = (LAYERS, *TILE)
    state, first, last, coarse_old = call(
        state_kernel,
        [block, (1, *TILE), (1, *TILE), COARSE],
        [pltpu.VMEM((LAYERS, 4, 64, 128), F32)],
        ins=1,
    )(starts)
    left, right = shift(last, "space", 1), shift(first, "space", -1)
    own, head, tail, coarse_fields = call(
        field_kernel,
        [(LAYERS, 4, *TILE), (REACH, 4, *TILE), (REACH, 4, *TILE), (4, *COARSE)],
        [pltpu.VMEM((4, 4, 64, 128), F32)],
        ins=2,
    )(velocity, diffusivity)
    fields_left, fields_right = shift(tail, "space", 1), shift(head, "space", -1)
    coarse_later = shift(coarse_old, "cuts", -1)
    all_fields = lax.all_gather(coarse_fields, "space")

    def weights_of(fields):
        layers = fields.shape[0]
        return call(functools.partial(weight_kernel, layers), [(layers, 7, *TILE)], ins=1)(fields)[0]

    own_weights = weights_of(own)
    scratch = [pltpu.VMEM((3 * LAYERS, *TILE), F32)] * 2
    sides = None
    for index, width in enumerate(ROUNDS):
        final = index == len(ROUNDS) - 1
        if index > 0:
            left = shift(state[LAYERS - width :], "space", 1)
            right = shift(state[:width], "space", -1)
        operands = [state, left, right, own_weights]
        if width > 1:
            if sides is None:
                sides = [weights_of(fields_left), weights_of(fields_right)]
            operands += sides
        if final:
            operands.append(coarse_later)
        outs = call(
            functools.partial(round_kernel, width, final),
            [block, COARSE] if final else [block],
            scratch,
            ins=len(operands),
        )(*operands)
        state = outs[0]
    residuals = lax.all_gather(lax.all_gather(outs[1], "cuts"), "space")
    place = jnp.stack([lax.axis_index("cuts"), lax.axis_index("space")]).astype(jnp.int32)
    return call(
        chain_kernel,
        [(1, LAYERS, 64, 512)],
        [
            pltpu.VMEM((count, 7, *COARSE), F32),
            pltpu.VMEM((count, *COARSE), F32),
            pltpu.VMEM((count, *COARSE), F32),
            pltpu.VMEM((LAYERS, 4, 64, 128), F32),
        ],
        smem=1,
        ins=3,
    )(place, residuals, all_fields, state)[0]


def solution(mesh):
    placed = (P("cuts", "space", None, None), P(None, "space", None, None), P("space", None, None))
    return jax.shard_map(
        shards,
        mesh=mesh,
        in_specs=placed,
        out_specs=P("cuts", "space", None, None),
        check_vma=False,
    )
```

time: 1090 us -> 277 us (0.25)
  the two profiles are of different devices: /device:TPU:4 before, /device:TPU:61 now
where the time goes in v1:
time: 277 us; the launch traced here: 276 us
  waiting for transfers between devices  143 us (52%)
  starting transfers between devices  43.6 us (16%)
  Pallas kernels  38.4 us (14%)
  blocking collectives  31.2 us (11%)
  between operations  13.6 us (5%)
  local copies, waits for them, and re-layouts  5.96 us (2%)
    all_gather x1, waiting for transfers between devices, shards(): residuals = lax.all_gather(lax.all_gather(outs[1], 'cuts'), 'space')  79.2 us
    ppermute x13, waiting for transfers between devices, shift(): lax.ppermute(block, axis, [(i, (i + distance) % count) for i in range(cou...  64.2 us
    ppermute x13, starting transfers between devices, shift(): lax.ppermute(block, axis, [(i, (i + distance) % count) for i in range(cou...  43.5 us
    all_gather x1, blocking collectives, shards(): residuals = lax.all_gather(lax.all_gather(outs[1], 'cuts'), 'space')  31.2 us
    pallas_call x5, Pallas kernels, shards(): call(functools.partial(round_kernel, width, final), [block, COARSE] if fi...  14.6 us
    pallas_call x1, Pallas kernels, shards(): call(chain_kernel, [(1, LAYERS, 64, 512)], [pltpu.VMEM((count, 7, *COARSE...  13 us
    pallas_call x1, Pallas kernels, shards(): call(field_kernel, [(LAYERS, 4, *TILE), (REACH, 4, *TILE), (REACH, 4, *TI...  7.07 us
    unnamed x14, local copies, waits for them, and re-layouts  5.87 us
  transfers between devices with their start and end apart: 15, of which 8 were waited for; matrix products, arithmetic and copies ran while one was open for 0% of the time, Pallas kernels for 7%

profile of v1, /device:TPU:61, one launch (start us, length us, event | category | flops | bytes accessed | tf_op | source)
XLA Modules:
  0.0 276.4 jit_solution(12909954515182012979)
XLA Ops:
  6.5 0.0 all-gather.8.cloned.1.call-start
  6.5 0.0 copy-start.3
  6.5 1.4 copy-done.3
  7.9 0.0 copy-start.6
  7.9 1.0 copy-done.6
  9.0 0.0 copy-start.5
  9.0 7.1 %shard_map.38 = (f32[4,4,8,4,8,128]{5,4,3,2,1,0:T(8,128)S(1)}, f32[3,4,8,4,8,128]{5,4,3,2,1,0:T(8,128)}, f32[3,4,8,4,8,128]{5,4,3,2,1,0:T(8,128)}, f32[4,2,8,128]{3,2,1,0:T(8,128)}) custom-call(f32[3,4,64,512]{3,2,1,0:T(8,128)S(1)} %copy-done.3, f32[4,64,512]{2,1,0:T(8,128)S(1)} %copy-done.6), custom_call_target="tpu_custom_call" | custom-call | tf_op jit(solution)/shard_map/pallas_call | solution.py:274
  16.1 3.4 %collective-permute-start.4 = (f32[3,4,8,4,8,128]{5,4,3,2,1,0:T(8,128)}, f32[3,4,8,4,8,128]{5,4,3,2,1,0:T(8,128)}, u32[]{:S(2)}, u32[]{:S(2)}) collective-permute-start(f32[3,4,8,4,8,128]{5,4,3,2,1,0:T(8,128)} %get-tuple-element.19), channel_id=1, source_target_pairs={{0,1},{1,2},{2,3},{3,4},{4,5},{5,6},{6,7},{7,8},{8,9},{9,10},{10,1... | collective-permute-start | bytes 4718600 | tf_op jit(solution)/shard_map/ppermute | solution.py:261
  19.4 1.9 collective-permute-start.5
  21.4 0.0 copy-done.5
  21.4 1.3 shard_map.37
  22.7 3.6 %collective-permute-start = (f32[1,8,4,8,128]{4,3,2,1,0:T(8,128)S(1)}, f32[1,8,4,8,128]{4,3,2,1,0:T(8,128)S(1)}, u32[]{:S(2)}, u32[]{:S(2)}) collective-permute-start(f32[1,8,4,8,128]{4,3,2,1,0:T(8,128)S(1)} %get-tuple-element.16), channel_id=1, source_target_pairs={{0,1},{1,2},{2,3},{3,4},{4,5},{5,6},{6,7},{7,8},{8,9},{9,10},{10,1... | collective-permute-start | bytes 393224 | tf_op jit(solution)/shard_map/ppermute | solution.py:261
  26.3 8.5 %collective-permute-start.1 = (f32[1,8,4,8,128]{4,3,2,1,0:T(8,128)S(1)}, f32[1,8,4,8,128]{4,3,2,1,0:T(8,128)S(1)}, u32[]{:S(2)}, u32[]{:S(2)}) collective-permute-start(f32[1,8,4,8,128]{4,3,2,1,0:T(8,128)S(1)} %get-tuple-element.17), channel_id=1, source_target_pairs={{0,31},{1,0},{2,1},{3,2},{4,3},{5,4},{6,5},{7,6},{8,7},{9,8},{10,9... | collective-permute-start | bytes 393224 | tf_op jit(solution)/shard_map/ppermute | solution.py:261
  34.8 0.4 shard_map.39.refs_3_
  35.3 0.0 copy-start
  35.3 21.4 %collective-permute-done.refs_1_ = f32[1,8,4,8,128]{4,3,2,1,0:T(8,128)S(1)} collective-permute-done((f32[1,8,4,8,128]{4,3,2,1,0:T(8,128)S(1)}, f32[1,8,4,8,128]{4,3,2,1,0:T(8,128)S(1)}, u32[]{:S(2)}, u32[]{:S(2)}) %collective-permute-start) | collective-permute-done | bytes 131104 | tf_op jit(solution)/shard_map/ppermute | solution.py:261
  56.7 10.0 %collective-permute-done.1.refs_2_ = f32[1,8,4,8,128]{4,3,2,1,0:T(8,128)S(1)} collective-permute-done((f32[1,8,4,8,128]{4,3,2,1,0:T(8,128)S(1)}, f32[1,8,4,8,128]{4,3,2,1,0:T(8,128)S(1)}, u32[]{:S(2)}, u32[]{:S(2)}) %collective-permute-start.1) | collective-permute-done | bytes 131104 | tf_op jit(solution)/shard_map/ppermute | solution.py:261
  66.7 0.6 shard_map.40.refs_0_
  67.3 0.0 copy-done
  67.3 1.9 collective-permute-start.2
  69.2 2.4 collective-permute-start.3
  71.6 0.0 all-gather.8.cloned.1.call-update
  71.6 0.0 all-gather.6.cloned.1.call-start
  71.7 0.0 collective-permute-done.4.fields
  71.7 1.7 shard_map.41.refs_4_
  73.4 0.0 copy-start.1
  73.4 0.0 collective-permute-done.5.fields
  73.4 0.3 shard_map.42.refs_5_
  73.8 7.2 %collective-permute-done.2.refs_1_ = f32[4,8,4,8,128]{4,3,2,1,0:T(8,128)S(1)} collective-permute-done((f32[4,8,4,8,128]{4,3,2,1,0:T(8,128)S(1)}, f32[4,8,4,8,128]{4,3,2,1,0:T(8,128)S(1)}, u32[]{:S(2)}, u32[]{:S(2)}) %collective-permute-start.2) | collective-permute-done | bytes 524320 | tf_op jit(solution)/shard_map/ppermute | solution.py:261
  80.9 0.0 collective-permute-done.3.refs_2_
  80.9 0.0 copy-done.1
  80.9 3.8 %shard_map.43.refs_0_ = f32[4,8,4,8,128]{4,3,2,1,0:T(8,128)S(1)} custom-call(f32[4,8,4,8,128]{4,3,2,1,0:T(8,128)S(1)} %shard_map.40.refs_0_, f32[4,8,4,8,128]{4,3,2,1,0:T(8,128)S(1)} %collective-permute-done.2.refs_1_, f32[4,8,4,8,128]{4,3,2,1,0:T(8,128)S(1)} %collective-permute-done.3.refs_2_, f32[4,7,8,4,8,128]{5,4,3,2,1,0:T(8,128)S(1)} %copy-done.1, ...), custom_call_target="tpu_custom_call" | custom-call | tf_op jit(solution)/shard_map/pallas_call | solution.py:303
  84.8 4.4 %collective-permute-start.6 = (f32[4,8,4,8,128]{4,3,2,1,0:T(8,128)S(1)}, f32[4,8,4,8,128]{4,3,2,1,0:T(8,128)S(1)}, u32[]{:S(2)}, u32[]{:S(2)}) collective-permute-start(f32[4,8,4,8,128]{4,3,2,1,0:T(8,128)S(1)} %shard_map.43.refs_0_), channel_id=1, source_target_pairs={{0,1},{1,2},{2,3},{3,4},{4,5},{5,6},{6,7},{7,8},{8,9},{9,10},{10,1... | collective-permute-start | bytes 1572872 | tf_op jit(solution)/shard_map/ppermute | solution.py:261
  89.2 1.9 collective-permute-start.7
  91.1 10.4 %collective-permute-done.6.refs_1_ = f32[4,8,4,8,128]{4,3,2,1,0:T(8,128)S(1)} collective-permute-done((f32[4,8,4,8,128]{4,3,2,1,0:T(8,128)S(1)}, f32[4,8,4,8,128]{4,3,2,1,0:T(8,128)S(1)}, u32[]{:S(2)}, u32[]{:S(2)}) %collective-permute-start.6) | collective-permute-done | bytes 524320 | tf_op jit(solution)/shard_map/ppermute | solution.py:261
  101.5 0.2 collective-permute-done.7.refs_2_
  101.7 3.8 %shard_map.44.refs_0_ = f32[4,8,4,8,128]{4,3,2,1,0:T(8,128)S(1)} custom-call(f32[4,8,4,8,128]{4,3,2,1,0:T(8,128)S(1)} %shard_map.43.refs_0_, f32[4,8,4,8,128]{4,3,2,1,0:T(8,128)S(1)} %collective-permute-done.6.refs_1_, f32[4,8,4,8,128]{4,3,2,1,0:T(8,128)S(1)} %collective-permute-done.7.refs_2_, f32[4,7,8,4,8,128]{5,4,3,2,1,0:T(8,128)S(1)} %copy-done.1, ...), custom_call_target="tpu_custom_call" | custom-call | tf_op jit(solution)/shard_map/pallas_call | solution.py:303
  105.5 4.2 %collective-permute-start.8 = (f32[4,8,4,8,128]{4,3,2,1,0:T(8,128)S(1)}, f32[4,8,4,8,128]{4,3,2,1,0:T(8,128)S(1)}, u32[]{:S(2)}, u32[]{:S(2)}) collective-permute-start(f32[4,8,4,8,128]{4,3,2,1,0:T(8,128)S(1)} %shard_map.44.refs_0_), channel_id=1, source_target_pairs={{0,1},{1,2},{2,3},{3,4},{4,5},{5,6},{6,7},{7,8},{8,9},{9,10},{10,1... | collective-permute-start | bytes 1572872 | tf_op jit(solution)/shard_map/ppermute | solution.py:261
  109.8 1.9 collective-permute-start.9
  111.7 10.0 %collective-permute-done.8.refs_1_ = f32[4,8,4,8,128]{4,3,2,1,0:T(8,128)S(1)} collective-permute-done((f32[4,8,4,8,128]{4,3,2,1,0:T(8,128)S(1)}, f32[4,8,4,8,128]{4,3,2,1,0:T(8,128)S(1)}, u32[]{:S(2)}, u32[]{:S(2)}) %collective-permute-start.8) | collective-permute-done | bytes 524320 | tf_op jit(solution)/shard_map/ppermute | solution.py:261
  121.7 0.0 collective-permute-done.9.refs_2_
  121.7 3.8 %shard_map.45.refs_0_ = f32[4,8,4,8,128]{4,3,2,1,0:T(8,128)S(1)} custom-call(f32[4,8,4,8,128]{4,3,2,1,0:T(8,128)S(1)} %shard_map.44.refs_0_, f32[4,8,4,8,128]{4,3,2,1,0:T(8,128)S(1)} %collective-permute-done.8.refs_1_, f32[4,8,4,8,128]{4,3,2,1,0:T(8,128)S(1)} %collective-permute-done.9.refs_2_, f32[4,7,8,4,8,128]{5,4,3,2,1,0:T(8,128)S(1)} %copy-done.1, ...), custom_call_target="tpu_custom_call" | custom-call | tf_op jit(solution)/shard_map/pallas_call | solution.py:303
  125.5 0.1 fusion
  125.6 4.5 %collective-permute-start.10 = (f32[3,8,4,8,128]{4,3,2,1,0:T(8,128)S(1)}, f32[3,8,4,8,128]{4,3,2,1,0:T(8,128)S(1)}, u32[]{:S(2)}, u32[]{:S(2)}) collective-permute-start(f32[3,8,4,8,128]{4,3,2,1,0:T(8,128)S(1)} %get-tuple-element.26), channel_id=1, source_target_pairs={{0,1},{1,2},{2,3},{3,4},{4,5},{5,6},{6,7},{7,8},{8,9},{9,10},{10,1... | collective-permute-start | bytes 1179656 | tf_op jit(solution)/shard_map/ppermute | solution.py:261
  130.1 1.9 collective-permute-start.11
  132.0 2.9 %collective-permute-start.12 = (f32[2,8,128]{2,1,0:T(8,128)S(1)}, f32[2,8,128]{2,1,0:T(8,128)S(1)}, u32[]{:S(2)}, u32[]{:S(2)}) collective-permute-start(f32[2,8,128]{2,1,0:T(8,128)S(1)} %get-tuple-element.21), channel_id=1, source_target_pairs={{0,480},{32,0},{64,32},{96,64},{128,96},{160,128},{192,160},{224,1... | collective-permute-start | bytes 24584 | tf_op jit(solution)/shard_map/ppermute | solution.py:261
  135.0 5.1 %collective-permute-done.12.refs_6_ = f32[2,8,128]{2,1,0:T(8,128)S(1)} collective-permute-done((f32[2,8,128]{2,1,0:T(8,128)S(1)}, f32[2,8,128]{2,1,0:T(8,128)S(1)}, u32[]{:S(2)}, u32[]{:S(2)}) %collective-permute-start.12) | collective-permute-done | bytes 8224 | tf_op jit(solution)/shard_map/ppermute | solution.py:261
  140.0 0.0 collective-permute-done.10.refs_1_
  140.0 0.0 collective-permute-done.11.refs_2_
  140.0 2.5 shard_map.46
  142.6 31.2 %all-gather = f32[32,8,128]{2,1,0:T(8,128)} all-gather(f32[2,8,128]{2,1,0:T(8,128)S(1)} %get-tuple-element.22), channel_id=2, replica_groups=mesh['cuts'=16,'space'=32] {'cuts'}, dimensions={0}, use_global_device_ids=true | all-gather | bytes 139264 | tf_op jit(solution)/shard_map/all_gather | solution.py:310
  173.8 0.0 all-gather.6.cloned.1.call-update
  173.8 0.1 pad_add_fusion.place
  173.9 0.0 all-gather.8.cloned.1.call-done
  173.9 79.2 %all-gather.6.cloned.1.call-done = f32[512,2,8,128]{3,2,1,0:T(8,128)} async-done(((f32[16,2,8,128]{3,2,1,0:T(8,128)}), f32[512,2,8,128]{3,2,1,0:T(8,128)}) %all-gather.6.cloned.1.call-update) | async-done | bytes 4194320 | tf_op jit(solution)/shard_map/all_gather | solution.py:310
  253.1 0.0 copy-start.2
  253.1 2.2 copy-done.2
  255.3 0.0 copy-start.4
  255.3 1.2 copy-done.4
  256.5 13.0 %shard_map.47 = f32[1,4,64,512]{3,2,1,0:T(8,128)} custom-call(s32[2]{0:T(128)S(1)} %pad_add_fusion.place, f32[32,16,2,8,128]{4,3,2,1,0:T(8,128)S(1)} %bitcast.5, f32[32,4,2,8,128]{4,3,2,1,0:T(8,128)S(1)} %bitcast.6, f32[4,8,4,8,128]{4,3,2,1,0:T(8,128)S(1)} %get-tuple-element.24.state), custom_call_target="tpu_custom_call" | custom-call | tf_op jit(solution)/shard_map/pallas_call | solution.py:312
Async XLA Ops:
  6.5 167.4 %all-gather.8.cloned.1.call-start = ((), (), s32[]{:S(2)}) async-start(), calls=%async_computation.1 | async-start | bytes 1081344 | tf_op jit(solution)/shard_map/all_gather | solution.py:282
  6.5 1.4 copy-start.3
  7.9 1.0 copy-start.6
  9.0 12.4 %copy-start.5 = (f32[1,4,64,512]{3,2,1,0:T(8,128)S(1)}, f32[1,4,64,512]{3,2,1,0:T(8,128)}, u32[]{:S(2)}) copy-start(f32[1,4,64,512]{3,2,1,0:T(8,128)} %starts.1) | copy-start | bytes 1572868
  16.1 55.6 %collective-permute-start.4 = (f32[3,4,8,4,8,128]{5,4,3,2,1,0:T(8,128)}, f32[3,4,8,4,8,128]{5,4,3,2,1,0:T(8,128)}, u32[]{:S(2)}, u32[]{:S(2)}) collective-permute-start(f32[3,4,8,4,8,128]{5,4,3,2,1,0:T(8,128)} %get-tuple-element.19), channel_id=1, source_target_pairs={{0,1},{1,2},{2,3},{3,4},{4,5},{5,6},{6,7},{7,8},{8,9},{9,10},{10,1... | collective-permute-start | bytes 4718600 | tf_op jit(solution)/shard_map/ppermute | solution.py:261
  19.4 54.0 %collective-permute-start.5 = (f32[3,4,8,4,8,128]{5,4,3,2,1,0:T(8,128)}, f32[3,4,8,4,8,128]{5,4,3,2,1,0:T(8,128)S(1)}, u32[]{:S(2)}, u32[]{:S(2)}) collective-permute-start(f32[3,4,8,4,8,128]{5,4,3,2,1,0:T(8,128)} %get-tuple-element.20), channel_id=1, source_target_pairs={{0,31},{1,0},{2,1},{3,2},{4,3},{5,4},{6,5},{7,6},{8,7},{9,8},{10,9... | collective-permute-start | bytes 4718600 | tf_op jit(solution)/shard_map/ppermute | solution.py:261
  22.7 34.0 %collective-permute-start = (f32[1,8,4,8,128]{4,3,2,1,0:T(8,128)S(1)}, f32[1,8,4,8,128]{4,3,2,1,0:T(8,128)S(1)}, u32[]{:S(2)}, u32[]{:S(2)}) collective-permute-start(f32[1,8,4,8,128]{4,3,2,1,0:T(8,128)S(1)} %get-tuple-element.16), channel_id=1, source_target_pairs={{0,1},{1,2},{2,3},{3,4},{4,5},{5,6},{6,7},{7,8},{8,9},{9,10},{10,1... | collective-permute-start | bytes 393224 | tf_op jit(solution)/shard_map/ppermute | solution.py:261
  26.3 40.3 %collective-permute-start.1 = (f32[1,8,4,8,128]{4,3,2,1,0:T(8,128)S(1)}, f32[1,8,4,8,128]{4,3,2,1,0:T(8,128)S(1)}, u32[]{:S(2)}, u32[]{:S(2)}) collective-permute-start(f32[1,8,4,8,128]{4,3,2,1,0:T(8,128)S(1)} %get-tuple-element.17), channel_id=1, source_target_pairs={{0,31},{1,0},{2,1},{3,2},{4,3},{5,4},{6,5},{7,6},{8,7},{9,8},{10,9... | collective-permute-start | bytes 393224 | tf_op jit(solution)/shard_map/ppermute | solution.py:261
  35.3 32.0 %copy-start = (f32[4,7,8,4,8,128]{5,4,3,2,1,0:T(8,128)}, f32[4,7,8,4,8,128]{5,4,3,2,1,0:T(8,128)S(1)}, u32[]{:S(2)}) copy-start(f32[4,7,8,4,8,128]{5,4,3,2,1,0:T(8,128)S(1)} %shard_map.39.refs_3_) | copy-start | bytes 11010052
  67.3 13.7 %collective-permute-start.2 = (f32[4,8,4,8,128]{4,3,2,1,0:T(8,128)S(1)}, f32[4,8,4,8,128]{4,3,2,1,0:T(8,128)S(1)}, u32[]{:S(2)}, u32[]{:S(2)}) collective-permute-start(f32[4,8,4,8,128]{4,3,2,1,0:T(8,128)S(1)} %shard_map.40.refs_0_), channel_id=1, source_target_pairs={{0,1},{1,2},{2,3},{3,4},{4,5},{5,6},{6,7},{7,8},{8,9},{9,10},{10,1... | collective-permute-start | bytes 1572872 | tf_op jit(solution)/shard_map/ppermute | solution.py:261
  69.2 11.7 %collective-permute-start.3 = (f32[4,8,4,8,128]{4,3,2,1,0:T(8,128)S(1)}, f32[4,8,4,8,128]{4,3,2,1,0:T(8,128)S(1)}, u32[]{:S(2)}, u32[]{:S(2)}) collective-permute-start(f32[4,8,4,8,128]{4,3,2,1,0:T(8,128)S(1)} %shard_map.40.refs_0_), channel_id=1, source_target_pairs={{0,31},{1,0},{2,1},{3,2},{4,3},{5,4},{6,5},{7,6},{8,7},{9,8},{10,9... | collective-permute-start | bytes 1572872 | tf_op jit(solution)/shard_map/ppermute | solution.py:261
  71.6 181.5 %all-gather.6.cloned.1.call-start = ((), (), s32[]{:S(2)}) async-start(), calls=%async_computation | async-start | bytes 4325376 | tf_op jit(solution)/shard_map/all_gather | solution.py:310
  73.4 7.5 %copy-start.1 = (f32[4,7,8,4,8,128]{5,4,3,2,1,0:T(8,128)S(1)}, f32[4,7,8,4,8,128]{5,4,3,2,1,0:T(8,128)}, u32[]{:S(2)}) copy-start(f32[4,7,8,4,8,128]{5,4,3,2,1,0:T(8,128)} %copy-done) | copy-start | bytes 11010052
  84.8 16.8 %collective-permute-start.6 = (f32[4,8,4,8,128]{4,3,2,1,0:T(8,128)S(1)}, f32[4,8,4,8,128]{4,3,2,1,0:T(8,128)S(1)}, u32[]{:S(2)}, u32[]{:S(2)}) collective-permute-start(f32[4,8,4,8,128]{4,3,2,1,0:T(8,128)S(1)} %shard_map.43.refs_0_), channel_id=1, source_target_pairs={{0,1},{1,2},{2,3},{3,4},{4,5},{5,6},{6,7},{7,8},{8,9},{9,10},{10,1... | collective-permute-start | bytes 1572872 | tf_op jit(solution)/shard_map/ppermute | solution.py:261
  89.2 12.5 %collective-permute-start.7 = (f32[4,8,4,8,128]{4,3,2,1,0:T(8,128)S(1)}, f32[4,8,4,8,128]{4,3,2,1,0:T(8,128)S(1)}, u32[]{:S(2)}, u32[]{:S(2)}) collective-permute-start(f32[4,8,4,8,128]{4,3,2,1,0:T(8,128)S(1)} %shard_map.43.refs_0_), channel_id=1, source_target_pairs={{0,31},{1,0},{2,1},{3,2},{4,3},{5,4},{6,5},{7,6},{8,7},{9,8},{10,9... | collective-permute-start | bytes 1572872 | tf_op jit(solution)/shard_map/ppermute | solution.py:261
  105.5 16.2 %collective-permute-start.8 = (f32[4,8,4,8,128]{4,3,2,1,0:T(8,128)S(1)}, f32[4,8,4,8,128]{4,3,2,1,0:T(8,128)S(1)}, u32[]{:S(2)}, u32[]{:S(2)}) collective-permute-start(f32[4,8,4,8,128]{4,3,2,1,0:T(8,128)S(1)} %shard_map.44.refs_0_), channel_id=1, source_target_pairs={{0,1},{1,2},{2,3},{3,4},{4,5},{5,6},{6,7},{7,8},{8,9},{9,10},{10,1... | collective-permute-start | bytes 1572872 | tf_op jit(solution)/shard_map/ppermute | solution.py:261
  109.8 11.9 %collective-permute-start.9 = (f32[4,8,4,8,128]{4,3,2,1,0:T(8,128)S(1)}, f32[4,8,4,8,128]{4,3,2,1,0:T(8,128)S(1)}, u32[]{:S(2)}, u32[]{:S(2)}) collective-permute-start(f32[4,8,4,8,128]{4,3,2,1,0:T(8,128)S(1)} %shard_map.44.refs_0_), channel_id=1, source_target_pairs={{0,31},{1,0},{2,1},{3,2},{4,3},{5,4},{6,5},{7,6},{8,7},{9,8},{10,9... | collective-permute-start | bytes 1572872 | tf_op jit(solution)/shard_map/ppermute | solution.py:261
  125.6 14.4 %collective-permute-start.10 = (f32[3,8,4,8,128]{4,3,2,1,0:T(8,128)S(1)}, f32[3,8,4,8,128]{4,3,2,1,0:T(8,128)S(1)}, u32[]{:S(2)}, u32[]{:S(2)}) collective-permute-start(f32[3,8,4,8,128]{4,3,2,1,0:T(8,128)S(1)} %get-tuple-element.26), channel_id=1, source_target_pairs={{0,1},{1,2},{2,3},{3,4},{4,5},{5,6},{6,7},{7,8},{8,9},{9,10},{10,1... | collective-permute-start | bytes 1179656 | tf_op jit(solution)/shard_map/ppermute | solution.py:261
  130.1 9.9 %collective-permute-start.11 = (f32[3,8,4,8,128]{4,3,2,1,0:T(8,128)S(1)}, f32[3,8,4,8,128]{4,3,2,1,0:T(8,128)S(1)}, u32[]{:S(2)}, u32[]{:S(2)}) collective-permute-start(f32[3,8,4,8,128]{4,3,2,1,0:T(8,128)S(1)} %get-tuple-element.25), channel_id=1, source_target_pairs={{0,31},{1,0},{2,1},{3,2},{4,3},{5,4},{6,5},{7,6},{8,7},{9,8},{10,9... | collective-permute-start | bytes 1179656 | tf_op jit(solution)/shard_map/ppermute | solution.py:261
  132.0 8.0 %collective-permute-start.12 = (f32[2,8,128]{2,1,0:T(8,128)S(1)}, f32[2,8,128]{2,1,0:T(8,128)S(1)}, u32[]{:S(2)}, u32[]{:S(2)}) collective-permute-start(f32[2,8,128]{2,1,0:T(8,128)S(1)} %get-tuple-element.21), channel_id=1, source_target_pairs={{0,480},{32,0},{64,32},{96,64},{128,96},{160,128},{192,160},{224,1... | collective-permute-start | bytes 24584 | tf_op jit(solution)/shard_map/ppermute | solution.py:261
  253.1 2.2 copy-start.2
  255.3 1.2 copy-start.4
Sparse Core Ops, SparseCore 0:
  71.8 69.3 all-gather.7
  173.9 79.1 all-gather.5

commit v2 on v1

--- a/solution.py
+++ b/solution.py
@@ -12,15 +12,16 @@
 REACH = 3
 TILE = (8, 4, 8, 128)
 COARSE = (2, 8, 128)
-ROUNDS = (1, 4, 4, 4, 3)
+ROUNDS = (1, 2, 2, 4, 4, 3)
 STEP = 0.2
 VMEM = pl.BlockSpec(memory_space=pltpu.VMEM)
 F32 = jnp.float32
 MIB = 1024 * 1024
 
 
-def call(body, outs, scratch=(), smem=0, ins=0, limit=32):
+def call(body, outs, scratch=(), smem=0, ins=0, limit=32, after=0):
     specs = [pl.BlockSpec(memory_space=pltpu.SMEM)] * smem + [VMEM] * ins
+    specs += [pl.BlockSpec(memory_space=pl.ANY)] * after
     return pl.pallas_call(
         body,
         out_shape=[jax.ShapeDtypeStruct(s, F32) for s in outs],
@@ -96,7 +97,7 @@
     return weights
 
 
-def field_kernel(velocity, diffusivity, own, head, tail, coarse, buffer):
+def field_kernel(velocity, diffusivity, earlier, own, first, head, last, tail, coarse, buffer):
     matrix = comb(False)
     for f in range(4):
         for h in range(2):
@@ -114,8 +115,10 @@
         return carry
 
     lax.fori_loop(0, LAYERS, layer, 0)
-    head[...] = own[:REACH]
-    tail[...] = own[LAYERS - REACH :]
+    first[...] = own[:1]
+    head[...] = own[1:REACH]
+    last[...] = own[LAYERS - 1 :]
+    tail[...] = own[LAYERS - REACH : LAYERS - 1]
 
 
 def weight_kernel(count, fields, weights):
@@ -147,11 +150,14 @@
 
 
 def round_kernel(width, final, *refs):
+    state, left, right, own, *refs = refs
+    parts = [(LAYERS, 2 * LAYERS, own)]
     if width > 1:
-        state, left, right, own, own_left, own_right, *refs = refs
-    else:
-        state, left, right, own, *refs = refs
-        own_left = own_right = None
+        near_left, near_right, *refs = refs
+        parts += [(LAYERS - 1, LAYERS, near_left), (2 * LAYERS, 2 * LAYERS + 1, near_right)]
+    if width > 2:
+        far_left, far_right, *refs = refs
+        parts += [(1, LAYERS - 1, far_left), (2 * LAYERS + 1, 3 * LAYERS - 1, far_right)]
     if final:
         later, out, residual, one, two = refs
     else:
@@ -166,20 +172,15 @@
         ends = step == width
         goal = out if ends else target
         shift = LAYERS if ends else 0
-
-        def sweep(begin, end, weights, offset, source=source, goal=goal, shift=shift):
-            if end <= begin:
-                return
-
-            def body(x, carry):
-                fine_layer(source, weights, goal, x, x - offset, x - shift)
-                return carry
-
-            lax.fori_loop(begin, end, body, 0)
-
-        sweep(LAYERS - width + step, LAYERS, own_left, LAYERS - REACH)
-        sweep(LAYERS, 2 * LAYERS, own, LAYERS)
-        sweep(2 * LAYERS, 2 * LAYERS + width - step, own_right, 2 * LAYERS)
+        low, high = LAYERS - width + step, 2 * LAYERS + width - step
+        for begin, end, weights in parts:
+            if max(begin, low) < min(end, high):
+
+                def body(x, carry, begin=begin, weights=weights, source=source, goal=goal, shift=shift):
+                    fine_layer(source, weights, goal, x, x - begin, x - shift)
+                    return carry
+
+                lax.fori_loop(max(begin, low), min(end, high), body, 0)
         source, target = target, source
     if final:
         for h in range(2):
@@ -187,7 +188,9 @@
             for x in range(LAYERS):
                 part = half_sum([[out[x, j, q] for q in range(4)] for j in range(8)], h)
                 total = part if total is None else total + part
-            residual[h] = total * (1.0 / 64) - later[h]
+            total = total * (1.0 / 64) - later[h]
+            for copy in range(residual.shape[0]):
+                residual[copy, h] = total
 
 
 def coarse_step(read, weights, write, count):
@@ -211,17 +214,19 @@
         behind, now = now, ahead
 
 
-def chain_kernel(place, residuals, fields, state, out, weights, one, two, buffer):
+def chain_kernel(place, residuals, fields, shares, weights, one, two):
     count = fields.shape[0]
+    slices = shares.shape[0]
     slice_index = place[0]
     layer_index = place[1]
+    shares[...] = jnp.zeros(shares.shape, F32)
 
     def prepare(x, carry):
         for h in range(2):
             parts = [fields[x, f, h] for f in range(4)]
             for i, weight in enumerate(weigh(parts[:3], parts[3], STEP * RATIO, 1.0 * RATIO)):
                 weights[x, i, h] = weight
-            one[x, h] = jnp.zeros((8, 128), F32)
+            one[x, h] = residuals[x, h]
         return carry
 
     lax.fori_loop(0, count, prepare, 0)
@@ -235,18 +240,23 @@
 
         return write
 
-    def link(m, carry):
-        def entering(x):
-            return [one[x, h] + residuals[x, m, h] for h in range(2)]
-
-        coarse_step(entering, weights, writer(two), count)
-        coarse_step(reader(two), weights, writer(one), count)
-        coarse_step(reader(one), weights, writer(two), count)
-        coarse_step(reader(two), weights, writer(one), count)
+    def link(n, carry):
+        for source, target in ((one, two), (two, one)) * 2:
+            coarse_step(reader(source), weights, writer(target), count)
+        for h in range(2):
+            shares[n, h] = one[layer_index, h]
         return carry
 
-    lax.fori_loop(0, slice_index, link, 0)
-    change = [one[layer_index, h] for h in range(2)]
+    lax.fori_loop(slice_index + 1, slices, link, 0)
+
+
+def finish_kernel(shares, state, out, buffer):
+    change = []
+    for h in range(2):
+        total = shares[0, h]
+        for n in range(1, shares.shape[0]):
+            total = total + shares[n, h]
+        change.append(total)
     matrix = comb(True)
     for x in range(LAYERS):
         for j in range(8):
@@ -261,8 +271,20 @@
     return lax.ppermute(block, axis, [(i, (i + distance) % count) for i in range(count)])
 
 
+def shift_fields(block, distance):
+    slices, count = lax.axis_size("cuts"), lax.axis_size("space")
+    route = []
+    for n in range(slices):
+        for p in range(count):
+            source = (p - distance) % count
+            there = n if p // 2 == source // 2 else (n + slices // 2) % slices
+            route.append((there * count + source, n * count + p))
+    return lax.ppermute(block, ("cuts", "space"), route)
+
+
 def shards(starts, velocity, diffusivity):
     count = lax.axis_size("space")
+    slices = lax.axis_size("cuts")
     block = (LAYERS, *TILE)
     state, first, last, coarse_old = call(
         state_kernel,
@@ -271,23 +293,26 @@
         ins=1,
     )(starts)
     left, right = shift(last, "space", 1), shift(first, "space", -1)
-    own, head, tail, coarse_fields = call(
+    edges = [(1, 4, *TILE), (REACH - 1, 4, *TILE)]
+    own, near_head, far_head, near_tail, far_tail, coarse_fields = call(
         field_kernel,
-        [(LAYERS, 4, *TILE), (REACH, 4, *TILE), (REACH, 4, *TILE), (4, *COARSE)],
+        [(LAYERS, 4, *TILE), *edges, *edges, (4, *COARSE)],
         [pltpu.VMEM((4, 4, 64, 128), F32)],
         ins=2,
-    )(velocity, diffusivity)
-    fields_left, fields_right = shift(tail, "space", 1), shift(head, "space", -1)
+        after=1,
+    )(velocity, diffusivity, coarse_old)
+    near = [shift_fields(near_tail, 1), shift_fields(near_head, -1)]
+    far = [shift_fields(far_tail, 1), shift_fields(far_head, -1)]
+    all_fields = lax.all_gather(coarse_fields, "space")
     coarse_later = shift(coarse_old, "cuts", -1)
-    all_fields = lax.all_gather(coarse_fields, "space")
 
     def weights_of(fields):
         layers = fields.shape[0]
         return call(functools.partial(weight_kernel, layers), [(layers, 7, *TILE)], ins=1)(fields)[0]
 
     own_weights = weights_of(own)
-    scratch = [pltpu.VMEM((3 * LAYERS, *TILE), F32)] * 2
-    sides = None
+    near = [weights_of(fields) for fields in near]
+    far = [weights_of(fields) for fields in far]
     for index, width in enumerate(ROUNDS):
         final = index == len(ROUNDS) - 1
         if index > 0:
@@ -295,32 +320,38 @@
             right = shift(state[:width], "space", -1)
         operands = [state, left, right, own_weights]
         if width > 1:
-            if sides is None:
-                sides = [weights_of(fields_left), weights_of(fields_right)]
-            operands += sides
+            operands += near
+        if width > 2:
+            operands += far
         if final:
             operands.append(coarse_later)
         outs = call(
             functools.partial(round_kernel, width, final),
-            [block, COARSE] if final else [block],
-            scratch,
+            [block, (count, *COARSE)] if final else [block],
+            [pltpu.VMEM((3 * LAYERS, *TILE), F32)] * 2,
             ins=len(operands),
         )(*operands)
         state = outs[0]
-    residuals = lax.all_gather(lax.all_gather(outs[1], "cuts"), "space")
+    residuals = lax.all_to_all(outs[1], "space", 0, 0)
     place = jnp.stack([lax.axis_index("cuts"), lax.axis_index("space")]).astype(jnp.int32)
-    return call(
+    shares = call(
         chain_kernel,
-        [(1, LAYERS, 64, 512)],
+        [(slices, *COARSE)],
         [
             pltpu.VMEM((count, 7, *COARSE), F32),
             pltpu.VMEM((count, *COARSE), F32),
             pltpu.VMEM((count, *COARSE), F32),
-            pltpu.VMEM((LAYERS, 4, 64, 128), F32),
         ],
         smem=1,
-        ins=3,
-    )(place, residuals, all_fields, state)[0]
+        ins=2,
+    )(place, residuals, all_fields)[0]
+    shares = lax.all_to_all(shares, "cuts", 0, 0)
+    return call(
+        finish_kernel,
+        [(1, LAYERS, 64, 512)],
+        [pltpu.VMEM((LAYERS, 4, 64, 128), F32)],
+        ins=2,
+    )(shares, state)[0]
 
 
 def solution(mesh):

time: 277 us -> 188 us (0.68)
  the two profiles are of different devices: /device:TPU:61 before, /device:TPU:8 now
where the time goes in v2:
time: 188 us; the launch traced here: 187 us
  starting transfers between devices  80.6 us (43%)
  Pallas kernels  38.4 us (20%)
  waiting for transfers between devices  33.8 us (18%)
  blocking collectives  15.3 us (8%)
  between operations  13.7 us (7%)
  local copies, waits for them, and re-layouts  4.84 us (3%)
    ppermute x13, starting transfers between devices, shift(): lax.ppermute(block, axis, [(i, (i + distance) % count) for i in range(cou...  54.9 us
    ppermute x13, waiting for transfers between devices, shift(): lax.ppermute(block, axis, [(i, (i + distance) % count) for i in range(cou...  20.5 us
    ppermute x4, starting transfers between devices, shift_fields(): return lax.ppermute(block, ('cuts', 'space'), route)  17.8 us
    pallas_call x6, Pallas kernels, shards(): call(functools.partial(round_kernel, width, final), [block, (count, *COAR...  15.7 us
    all_to_all x1, blocking collectives, shards(): shares = lax.all_to_all(shares, 'cuts', 0, 0)  15.3 us
    all_gather x1, waiting for transfers between devices, shards(): all_fields = lax.all_gather(coarse_fields, 'space')  13.3 us
    pallas_call x1, Pallas kernels, shards(): call(chain_kernel, [(slices, *COARSE)], [pltpu.VMEM((count, 7, *COARSE),...  10.3 us
    all_to_all x1, starting transfers between devices, shards(): residuals = lax.all_to_all(outs[1], 'space', 0, 0)  7.89 us
  transfers between devices with their start and end apart: 19, of which 8 were waited for; matrix products, arithmetic and copies ran while one was open for 0% of the time, Pallas kernels for 13%

profile of v2, /device:TPU:8, one launch (start us, length us, event | category | flops | bytes accessed | tf_op | source)
XLA Modules:
  0.0 186.7 jit_solution(10374414346930468901)
XLA Ops:
  6.5 0.0 all-gather.3.cloned.1.call-start
  6.5 1.0 copy-done.4
  7.6 1.3 shard_map.37
  8.9 1.9 %collective-permute-start = (f32[1,8,4,8,128]{4,3,2,1,0:T(8,128)S(1)}, f32[1,8,4,8,128]{4,3,2,1,0:T(8,128)S(1)}, u32[]{:S(2)}, u32[]{:S(2)}) collective-permute-start(f32[1,8,4,8,128]{4,3,2,1,0:T(8,128)S(1)} %get-tuple-element.18), channel_id=1, source_target_pairs={{0,1},{1,2},{2,3},{3,4},{4,5},{5,6},{6,7},{7,8},{8,9},{9,10},{10,1... | collective-permute-start | bytes 393224 | tf_op jit(solution)/shard_map/ppermute | solution.py:271
  10.8 11.3 %collective-permute-start.1 = (f32[1,8,4,8,128]{4,3,2,1,0:T(8,128)S(1)}, f32[1,8,4,8,128]{4,3,2,1,0:T(8,128)S(1)}, u32[]{:S(2)}, u32[]{:S(2)}) collective-permute-start(f32[1,8,4,8,128]{4,3,2,1,0:T(8,128)S(1)} %get-tuple-element.19), channel_id=1, source_target_pairs={{0,31},{1,0},{2,1},{3,2},{4,3},{5,4},{6,5},{7,6},{8,7},{9,8},{10,9... | collective-permute-start | bytes 393224 | tf_op jit(solution)/shard_map/ppermute | solution.py:271
  22.1 0.0 copy-start.2
  22.1 1.4 copy-done.2
  23.5 1.0 copy-done.5
  24.6 6.7 %shard_map.38 = (f32[4,4,8,4,8,128]{5,4,3,2,1,0:T(8,128)S(1)}, f32[1,4,8,4,8,128]{5,4,3,2,1,0:T(8,128)S(1)}, f32[2,4,8,4,8,128]{5,4,3,2,1,0:T(8,128)}, f32[1,4,8...) custom-call(f32[3,4,64,512]{3,2,1,0:T(8,128)S(1)} %copy-done.2, ...), custom_call_target="tpu_custom_call" | custom-call | tf_op jit(solution)/shard_map/pallas_call | solution.py:297
  31.3 1.9 %collective-permute-start.4 = (f32[1,4,8,4,8,128]{5,4,3,2,1,0:T(8,128)S(1)}, f32[1,4,8,4,8,128]{5,4,3,2,1,0:T(8,128)S(1)}, u32[]{:S(2)}, u32[]{:S(2)}) collective-permute-start(f32[1,4,8,4,8,128]{5,4,3,2,1,0:T(8,128)S(1)} %get-tuple-element.22), channel_id=1, source_target_pairs={{287,0},{0,1},{257,2},{2,3},{259,4},{4,5},{261,6},{6,7},{263,8},{8... | collective-permute-start | bytes 1572872 | tf_op jit(solution)/shard_map/ppermute | solution.py:282
  33.2 7.0 %collective-permute-start.5 = (f32[1,4,8,4,8,128]{5,4,3,2,1,0:T(8,128)S(1)}, f32[1,4,8,4,8,128]{5,4,3,2,1,0:T(8,128)S(1)}, u32[]{:S(2)}, u32[]{:S(2)}) collective-permute-start(f32[1,4,8,4,8,128]{5,4,3,2,1,0:T(8,128)S(1)} %get-tuple-element.23), channel_id=1, source_target_pairs={{1,0},{258,1},{3,2},{260,3},{5,4},{262,5},{7,6},{264,7},{9,8},{266... | collective-permute-start | bytes 1572872 | tf_op jit(solution)/shard_map/ppermute | solution.py:282
  40.2 0.4 shard_map.39.refs_3_
  40.6 0.0 copy-start
  40.6 0.0 collective-permute-done.refs_1_
  40.6 0.0 collective-permute-done.1.refs_2_
  40.6 0.6 shard_map.40.refs_0_
  41.3 1.9 %collective-permute-start.2 = (f32[2,8,4,8,128]{4,3,2,1,0:T(8,128)S(1)}, f32[2,8,4,8,128]{4,3,2,1,0:T(8,128)S(1)}, u32[]{:S(2)}, u32[]{:S(2)}) collective-permute-start(f32[2,8,4,8,128]{4,3,2,1,0:T(8,128)S(1)} %get-tuple-element.34), channel_id=1, source_target_pairs={{0,1},{1,2},{2,3},{3,4},{4,5},{5,6},{6,7},{7,8},{8,9},{9,10},{10,1... | collective-permute-start | bytes 786440 | tf_op jit(solution)/shard_map/ppermute | solution.py:271
  43.2 5.8 %collective-permute-start.3 = (f32[2,8,4,8,128]{4,3,2,1,0:T(8,128)S(1)}, f32[2,8,4,8,128]{4,3,2,1,0:T(8,128)S(1)}, u32[]{:S(2)}, u32[]{:S(2)}) collective-permute-start(f32[2,8,4,8,128]{4,3,2,1,0:T(8,128)S(1)} %get-tuple-element.33), channel_id=1, source_target_pairs={{0,31},{1,0},{2,1},{3,2},{4,3},{5,4},{6,5},{7,6},{8,7},{9,8},{10,9... | collective-permute-start | bytes 786440 | tf_op jit(solution)/shard_map/ppermute | solution.py:271
  48.9 1.9 %collective-permute-start.10 = (f32[2,4,8,4,8,128]{5,4,3,2,1,0:T(8,128)}, f32[2,4,8,4,8,128]{5,4,3,2,1,0:T(8,128)S(1)}, u32[]{:S(2)}, u32[]{:S(2)}) collective-permute-start(f32[2,4,8,4,8,128]{5,4,3,2,1,0:T(8,128)} %get-tuple-element.24), channel_id=1, source_target_pairs={{287,0},{0,1},{257,2},{2,3},{259,4},{4,5},{261,6},{6,7},{263,8},{8... | collective-permute-start | bytes 3145736 | tf_op jit(solution)/shard_map/ppermute | solution.py:282
  50.9 0.0 collective-permute-done.4.fields
  50.9 7.0 %collective-permute-start.11 = (f32[2,4,8,4,8,128]{5,4,3,2,1,0:T(8,128)}, f32[2,4,8,4,8,128]{5,4,3,2,1,0:T(8,128)}, u32[]{:S(2)}, u32[]{:S(2)}) collective-permute-start(f32[2,4,8,4,8,128]{5,4,3,2,1,0:T(8,128)} %get-tuple-element.25), channel_id=1, source_target_pairs={{1,0},{258,1},{3,2},{260,3},{5,4},{262,5},{7,6},{264,7},{9,8},{266... | collective-permute-start | bytes 3145736 | tf_op jit(solution)/shard_map/ppermute | solution.py:282
  57.9 0.1 shard_map.41.refs_4_
  58.0 0.0 collective-permute-done.5.fields
  58.0 0.1 shard_map.42.refs_5_
  58.1 0.0 collective-permute-done.2.refs_1_
  58.1 0.0 collective-permute-done.3.refs_2_
  58.1 1.4 shard_map.43.refs_0_
  59.6 1.9 %collective-permute-start.6 = (f32[2,8,4,8,128]{4,3,2,1,0:T(8,128)S(1)}, f32[2,8,4,8,128]{4,3,2,1,0:T(8,128)S(1)}, u32[]{:S(2)}, u32[]{:S(2)}) collective-permute-start(f32[2,8,4,8,128]{4,3,2,1,0:T(8,128)S(1)} %get-tuple-element.32), channel_id=1, source_target_pairs={{0,1},{1,2},{2,3},{3,4},{4,5},{5,6},{6,7},{7,8},{8,9},{9,10},{10,1... | collective-permute-start | bytes 786440 | tf_op jit(solution)/shard_map/ppermute | solution.py:271
  61.5 5.8 %collective-permute-start.7 = (f32[2,8,4,8,128]{4,3,2,1,0:T(8,128)S(1)}, f32[2,8,4,8,128]{4,3,2,1,0:T(8,128)S(1)}, u32[]{:S(2)}, u32[]{:S(2)}) collective-permute-start(f32[2,8,4,8,128]{4,3,2,1,0:T(8,128)S(1)} %get-tuple-element.31), channel_id=1, source_target_pairs={{0,31},{1,0},{2,1},{3,2},{4,3},{5,4},{6,5},{7,6},{8,7},{9,8},{10,9... | collective-permute-start | bytes 786440 | tf_op jit(solution)/shard_map/ppermute | solution.py:271
  67.3 2.4 %collective-permute-done.6.refs_1_ = f32[2,8,4,8,128]{4,3,2,1,0:T(8,128)S(1)} collective-permute-done((f32[2,8,4,8,128]{4,3,2,1,0:T(8,128)S(1)}, f32[2,8,4,8,128]{4,3,2,1,0:T(8,128)S(1)}, u32[]{:S(2)}, u32[]{:S(2)}) %collective-permute-start.6) | collective-permute-done | bytes 262176 | tf_op jit(solution)/shard_map/ppermute | solution.py:271
  69.7 3.5 %collective-permute-done.7.refs_2_ = f32[2,8,4,8,128]{4,3,2,1,0:T(8,128)S(1)} collective-permute-done((f32[2,8,4,8,128]{4,3,2,1,0:T(8,128)S(1)}, f32[2,8,4,8,128]{4,3,2,1,0:T(8,128)S(1)}, u32[]{:S(2)}, u32[]{:S(2)}) %collective-permute-start.7) | collective-permute-done | bytes 262176 | tf_op jit(solution)/shard_map/ppermute | solution.py:271
  73.2 1.4 shard_map.44.refs_0_
  74.7 1.9 %collective-permute-start.8 = (f32[4,8,4,8,128]{4,3,2,1,0:T(8,128)S(1)}, f32[4,8,4,8,128]{4,3,2,1,0:T(8,128)}, u32[]{:S(2)}, u32[]{:S(2)}) collective-permute-start(f32[4,8,4,8,128]{4,3,2,1,0:T(8,128)S(1)} %shard_map.44.refs_0_), channel_id=1, source_target_pairs={{0,1},{1,2},{2,3},{3,4},{4,5},{5,6},{6,7},{7,8},{8,9},{9,10},{10,1... | collective-permute-start | bytes 1572872 | tf_op jit(solution)/shard_map/ppermute | solution.py:271
  76.6 6.0 %collective-permute-start.9 = (f32[4,8,4,8,128]{4,3,2,1,0:T(8,128)S(1)}, f32[4,8,4,8,128]{4,3,2,1,0:T(8,128)}, u32[]{:S(2)}, u32[]{:S(2)}) collective-permute-start(f32[4,8,4,8,128]{4,3,2,1,0:T(8,128)S(1)} %shard_map.44.refs_0_), channel_id=1, source_target_pairs={{0,31},{1,0},{2,1},{3,2},{4,3},{5,4},{6,5},{7,6},{8,7},{9,8},{10,9... | collective-permute-start | bytes 1572872 | tf_op jit(solution)/shard_map/ppermute | solution.py:271
  82.6 0.0 all-gather.3.cloned.1.call-update
  82.6 0.0 collective-permute-done.10.fields
  82.7 0.0 copy-start.1
  82.7 0.2 shard_map.45.refs_6_
  82.9 0.0 collective-permute-done.11.fields
  82.9 1.6 shard_map.46.refs_7_
  84.5 3.2 %collective-permute-done.8.refs_1_ = f32[4,8,4,8,128]{4,3,2,1,0:T(8,128)} collective-permute-done((f32[4,8,4,8,128]{4,3,2,1,0:T(8,128)S(1)}, f32[4,8,4,8,128]{4,3,2,1,0:T(8,128)}, u32[]{:S(2)}, u32[]{:S(2)}) %collective-permute-start.8) | collective-permute-done | bytes 524320 | tf_op jit(solution)/shard_map/ppermute | solution.py:271
  87.6 1.7 collective-permute-done.9.refs_2_
  89.3 5.1 %shard_map.47.refs_0_ = f32[4,8,4,8,128]{4,3,2,1,0:T(8,128)S(1)} custom-call(f32[4,8,4,8,128]{4,3,2,1,0:T(8,128)S(1)} %shard_map.44.refs_0_, f32[4,8,4,8,128]{4,3,2,1,0:T(8,128)} %collective-permute-done.8.refs_1_, f32[4,8,4,8,128]{4,3,2,1,0:T(8,128)} %collective-permute-done.9.refs_2_, f32[4,7,8,4,8,128]{5,4,3,2,1,0:T(8,128)S(1)} %copy-done.1, ...), custom_call_target="tpu_custom_call" | custom-call | tf_op jit(solution)/shard_map/pallas_call | solution.py:328
  94.4 1.9 %collective-permute-start.12 = (f32[4,8,4,8,128]{4,3,2,1,0:T(8,128)S(1)}, f32[4,8,4,8,128]{4,3,2,1,0:T(8,128)S(1)}, u32[]{:S(2)}, u32[]{:S(2)}) collective-permute-start(f32[4,8,4,8,128]{4,3,2,1,0:T(8,128)S(1)} %shard_map.47.refs_0_), channel_id=1, source_target_pairs={{0,1},{1,2},{2,3},{3,4},{4,5},{5,6},{6,7},{7,8},{8,9},{9,10},{10,1... | collective-permute-start | bytes 1572872 | tf_op jit(solution)/shard_map/ppermute | solution.py:271
  96.3 6.0 %collective-permute-start.13 = (f32[4,8,4,8,128]{4,3,2,1,0:T(8,128)S(1)}, f32[4,8,4,8,128]{4,3,2,1,0:T(8,128)S(1)}, u32[]{:S(2)}, u32[]{:S(2)}) collective-permute-start(f32[4,8,4,8,128]{4,3,2,1,0:T(8,128)S(1)} %shard_map.47.refs_0_), channel_id=1, source_target_pairs={{0,31},{1,0},{2,1},{3,2},{4,3},{5,4},{6,5},{7,6},{8,7},{9,8},{10,9... | collective-permute-start | bytes 1572872 | tf_op jit(solution)/shard_map/ppermute | solution.py:271
  102.3 5.0 %collective-permute-done.12.refs_1_ = f32[4,8,4,8,128]{4,3,2,1,0:T(8,128)S(1)} collective-permute-done((f32[4,8,4,8,128]{4,3,2,1,0:T(8,128)S(1)}, f32[4,8,4,8,128]{4,3,2,1,0:T(8,128)S(1)}, u32[]{:S(2)}, u32[]{:S(2)}) %collective-permute-start.12) | collective-permute-done | bytes 524320 | tf_op jit(solution)/shard_map/ppermute | solution.py:271
  107.4 1.7 collective-permute-done.13.refs_2_
  109.1 3.9 %shard_map.48.refs_0_ = f32[4,8,4,8,128]{4,3,2,1,0:T(8,128)S(1)} custom-call(f32[4,8,4,8,128]{4,3,2,1,0:T(8,128)S(1)} %shard_map.47.refs_0_, f32[4,8,4,8,128]{4,3,2,1,0:T(8,128)S(1)} %collective-permute-done.12.refs_1_, f32[4,8,4,8,128]{4,3,2,1,0:T(8,128)S(1)} %collective-permute-done.13.refs_2_, f32[4,7,8,4,8,128]{5,4,3,2,1,0:T(8,128)S(1)} %copy-done.1, ...), custom_call_target="tpu_custom_call" | custom-call | tf_op jit(solution)/shard_map/pallas_call | solution.py:328
  112.9 0.1 fusion
  113.0 1.9 %collective-permute-start.14 = (f32[3,8,4,8,128]{4,3,2,1,0:T(8,128)S(1)}, f32[3,8,4,8,128]{4,3,2,1,0:T(8,128)S(1)}, u32[]{:S(2)}, u32[]{:S(2)}) collective-permute-start(f32[3,8,4,8,128]{4,3,2,1,0:T(8,128)S(1)} %get-tuple-element.30), channel_id=1, source_target_pairs={{0,1},{1,2},{2,3},{3,4},{4,5},{5,6},{6,7},{7,8},{8,9},{9,10},{10,1... | collective-permute-start | bytes 1179656 | tf_op jit(solution)/shard_map/ppermute | solution.py:271
  114.9 6.0 %collective-permute-start.15 = (f32[3,8,4,8,128]{4,3,2,1,0:T(8,128)S(1)}, f32[3,8,4,8,128]{4,3,2,1,0:T(8,128)S(1)}, u32[]{:S(2)}, u32[]{:S(2)}) collective-permute-start(f32[3,8,4,8,128]{4,3,2,1,0:T(8,128)S(1)} %get-tuple-element.29), channel_id=1, source_target_pairs={{0,31},{1,0},{2,1},{3,2},{4,3},{5,4},{6,5},{7,6},{8,7},{9,8},{10,9... | collective-permute-start | bytes 1179656 | tf_op jit(solution)/shard_map/ppermute | solution.py:271
  120.9 2.5 %collective-permute-start.16 = (f32[2,8,128]{2,1,0:T(8,128)S(1)}, f32[2,8,128]{2,1,0:T(8,128)S(1)}, u32[]{:S(2)}, u32[]{:S(2)}) collective-permute-start(f32[2,8,128]{2,1,0:T(8,128)S(1)} %get-tuple-element.20.earlier), channel_id=1, source_target_pairs={{0,480},{32,0},{64,32},{96,64},{128,96},{160,128},{192,160},{224,1... | collective-permute-start | bytes 24584 | tf_op jit(solution)/shard_map/ppermute | solution.py:271
  123.5 3.0 %collective-permute-done.16.refs_8_ = f32[2,8,128]{2,1,0:T(8,128)S(1)} collective-permute-done((f32[2,8,128]{2,1,0:T(8,128)S(1)}, f32[2,8,128]{2,1,0:T(8,128)S(1)}, u32[]{:S(2)}, u32[]{:S(2)}) %collective-permute-start.16) | collective-permute-done | bytes 8224 | tf_op jit(solution)/shard_map/ppermute | solution.py:271
  126.5 0.0 collective-permute-done.14.refs_1_
  126.5 0.0 collective-permute-done.15.refs_2_
  126.5 3.2 %shard_map.49 = (f32[4,8,4,8,128]{4,3,2,1,0:T(8,128)S(1)}, f32[32,2,8,128]{3,2,1,0:T(8,128)}) custom-call(f32[4,8,4,8,128]{4,3,2,1,0:T(8,128)S(1)} %shard_map.48.refs_0_, f32[3,8,4,8,128]{4,3,2,1,0:T(8,128)S(1)} %collective-permute-done.14.refs_1_, f32[3,8,4,8,128]{4,3,2,1,0:T(8,128)S(1)} %collective-permute-done.15.refs_2_, ...), custom_call_target="tpu_custom_call" | custom-call | tf_op jit(solution)/shard_map/pallas_call | solution.py:328
  129.7 7.9 %all-to-all-start = ((f32[32,2,8,128]{3,2,1,0:T(8,128)}), f32[32,2,8,128]{3,2,1,0:T(8,128)S(1)}, u32[]{:S(2)}, u32[]{:S(2)}) async-start(f32[32,2,8,128]{3,2,1,0:T(8,128)} %get-tuple-element.26), calls=%async_computation | async-start | bytes 524288 | tf_op jit(solution)/shard_map/all_to_all | solution.py:335
  137.6 0.1 pad_add_fusion.place
  137.7 13.3 %all-gather.3.cloned.1.call-done = f32[128,2,8,128]{3,2,1,0:T(8,128)} async-done(((f32[4,2,8,128]{3,2,1,0:T(8,128)}), f32[128,2,8,128]{3,2,1,0:T(8,128)}) %all-gather.3.cloned.1.call-update) | async-done | bytes 1048592 | tf_op jit(solution)/shard_map/all_gather | solution.py:306
  151.0 0.0 all-to-all-done.residuals
  151.0 1.2 copy-done.3
  152.2 10.3 %shard_map.50 = f32[16,2,8,128]{3,2,1,0:T(8,128)S(1)} custom-call(s32[2]{0:T(128)S(1)} %pad_add_fusion.place, f32[32,2,8,128]{3,2,1,0:T(8,128)S(1)} %all-to-all-done.residuals, f32[32,4,2,8,128]{4,3,2,1,0:T(8,128)S(1)} %bitcast.3), custom_call_target="tpu_custom_call" | custom-call | tf_op jit(solution)/shard_map/pallas_call | solution.py:337
  162.5 15.3 %all_to_all.10.shares = f32[16,2,8,128]{3,2,1,0:T(8,128)S(1)} all-to-all(f32[16,2,8,128]{3,2,1,0:T(8,128)S(1)} %shard_map.50), channel_id=1, replica_groups=mesh['cuts'=16,'space'=32] {'cuts'}, dimensions={0} | all-to-all | bytes 262144 | tf_op jit(solution)/shard_map/all_to_all | solution.py:348
  177.8 2.1 %shard_map.51 = f32[1,4,64,512]{3,2,1,0:T(8,128)} custom-call(f32[16,2,8,128]{3,2,1,0:T(8,128)S(1)} %all_to_all.10.shares, f32[4,8,4,8,128]{4,3,2,1,0:T(8,128)S(1)} %get-tuple-element.28.state), custom_call_target="tpu_custom_call" | custom-call | tf_op jit(solution)/shard_map/pallas_call | solution.py:349
  (7 shorter events, 0.1 us)
Async XLA Ops:
  6.5 144.4 %all-gather.3.cloned.1.call-start = ((), (), s32[]{:S(2)}) async-start(), calls=%async_computation.2 | async-start | bytes 1081344 | tf_op jit(solution)/shard_map/all_gather | solution.py:306
  6.5 1.0 copy-start.4
  8.9 31.7 %collective-permute-start = (f32[1,8,4,8,128]{4,3,2,1,0:T(8,128)S(1)}, f32[1,8,4,8,128]{4,3,2,1,0:T(8,128)S(1)}, u32[]{:S(2)}, u32[]{:S(2)}) collective-permute-start(f32[1,8,4,8,128]{4,3,2,1,0:T(8,128)S(1)} %get-tuple-element.18), channel_id=1, source_target_pairs={{0,1},{1,2},{2,3},{3,4},{4,5},{5,6},{6,7},{7,8},{8,9},{9,10},{10,1... | collective-permute-start | bytes 393224 | tf_op jit(solution)/shard_map/ppermute | solution.py:271
  10.8 29.8 %collective-permute-start.1 = (f32[1,8,4,8,128]{4,3,2,1,0:T(8,128)S(1)}, f32[1,8,4,8,128]{4,3,2,1,0:T(8,128)S(1)}, u32[]{:S(2)}, u32[]{:S(2)}) collective-permute-start(f32[1,8,4,8,128]{4,3,2,1,0:T(8,128)S(1)} %get-tuple-element.19), channel_id=1, source_target_pairs={{0,31},{1,0},{2,1},{3,2},{4,3},{5,4},{6,5},{7,6},{8,7},{9,8},{10,9... | collective-permute-start | bytes 393224 | tf_op jit(solution)/shard_map/ppermute | solution.py:271
  22.1 1.4 copy-start.2
  23.5 1.0 copy-start.5
  31.3 19.6 %collective-permute-start.4 = (f32[1,4,8,4,8,128]{5,4,3,2,1,0:T(8,128)S(1)}, f32[1,4,8,4,8,128]{5,4,3,2,1,0:T(8,128)S(1)}, u32[]{:S(2)}, u32[]{:S(2)}) collective-permute-start(f32[1,4,8,4,8,128]{5,4,3,2,1,0:T(8,128)S(1)} %get-tuple-element.22), channel_id=1, source_target_pairs={{287,0},{0,1},{257,2},{2,3},{259,4},{4,5},{261,6},{6,7},{263,8},{8... | collective-permute-start | bytes 1572872 | tf_op jit(solution)/shard_map/ppermute | solution.py:282
  33.2 24.8 %collective-permute-start.5 = (f32[1,4,8,4,8,128]{5,4,3,2,1,0:T(8,128)S(1)}, f32[1,4,8,4,8,128]{5,4,3,2,1,0:T(8,128)S(1)}, u32[]{:S(2)}, u32[]{:S(2)}) collective-permute-start(f32[1,4,8,4,8,128]{5,4,3,2,1,0:T(8,128)S(1)} %get-tuple-element.23), channel_id=1, source_target_pairs={{1,0},{258,1},{3,2},{260,3},{5,4},{262,5},{7,6},{264,7},{9,8},{266... | collective-permute-start | bytes 1572872 | tf_op jit(solution)/shard_map/ppermute | solution.py:282
  40.6 32.6 %copy-start = (f32[4,7,8,4,8,128]{5,4,3,2,1,0:T(8,128)}, f32[4,7,8,4,8,128]{5,4,3,2,1,0:T(8,128)S(1)}, u32[]{:S(2)}) copy-start(f32[4,7,8,4,8,128]{5,4,3,2,1,0:T(8,128)S(1)} %shard_map.39.refs_3_) | copy-start | bytes 11010052
  41.3 16.8 %collective-permute-start.2 = (f32[2,8,4,8,128]{4,3,2,1,0:T(8,128)S(1)}, f32[2,8,4,8,128]{4,3,2,1,0:T(8,128)S(1)}, u32[]{:S(2)}, u32[]{:S(2)}) collective-permute-start(f32[2,8,4,8,128]{4,3,2,1,0:T(8,128)S(1)} %get-tuple-element.34), channel_id=1, source_target_pairs={{0,1},{1,2},{2,3},{3,4},{4,5},{5,6},{6,7},{7,8},{8,9},{9,10},{10,1... | collective-permute-start | bytes 786440 | tf_op jit(solution)/shard_map/ppermute | solution.py:271
  43.2 14.9 %collective-permute-start.3 = (f32[2,8,4,8,128]{4,3,2,1,0:T(8,128)S(1)}, f32[2,8,4,8,128]{4,3,2,1,0:T(8,128)S(1)}, u32[]{:S(2)}, u32[]{:S(2)}) collective-permute-start(f32[2,8,4,8,128]{4,3,2,1,0:T(8,128)S(1)} %get-tuple-element.33), channel_id=1, source_target_pairs={{0,31},{1,0},{2,1},{3,2},{4,3},{5,4},{6,5},{7,6},{8,7},{9,8},{10,9... | collective-permute-start | bytes 786440 | tf_op jit(solution)/shard_map/ppermute | solution.py:271
  48.9 33.7 %collective-permute-start.10 = (f32[2,4,8,4,8,128]{5,4,3,2,1,0:T(8,128)}, f32[2,4,8,4,8,128]{5,4,3,2,1,0:T(8,128)S(1)}, u32[]{:S(2)}, u32[]{:S(2)}) collective-permute-start(f32[2,4,8,4,8,128]{5,4,3,2,1,0:T(8,128)} %get-tuple-element.24), channel_id=1, source_target_pairs={{287,0},{0,1},{257,2},{2,3},{259,4},{4,5},{261,6},{6,7},{263,8},{8... | collective-permute-start | bytes 3145736 | tf_op jit(solution)/shard_map/ppermute | solution.py:282
  50.9 32.0 %collective-permute-start.11 = (f32[2,4,8,4,8,128]{5,4,3,2,1,0:T(8,128)}, f32[2,4,8,4,8,128]{5,4,3,2,1,0:T(8,128)}, u32[]{:S(2)}, u32[]{:S(2)}) collective-permute-start(f32[2,4,8,4,8,128]{5,4,3,2,1,0:T(8,128)} %get-tuple-element.25), channel_id=1, source_target_pairs={{1,0},{258,1},{3,2},{260,3},{5,4},{262,5},{7,6},{264,7},{9,8},{266... | collective-permute-start | bytes 3145736 | tf_op jit(solution)/shard_map/ppermute | solution.py:282
  59.6 10.1 %collective-permute-start.6 = (f32[2,8,4,8,128]{4,3,2,1,0:T(8,128)S(1)}, f32[2,8,4,8,128]{4,3,2,1,0:T(8,128)S(1)}, u32[]{:S(2)}, u32[]{:S(2)}) collective-permute-start(f32[2,8,4,8,128]{4,3,2,1,0:T(8,128)S(1)} %get-tuple-element.32), channel_id=1, source_target_pairs={{0,1},{1,2},{2,3},{3,4},{4,5},{5,6},{6,7},{7,8},{8,9},{9,10},{10,1... | collective-permute-start | bytes 786440 | tf_op jit(solution)/shard_map/ppermute | solution.py:271
  61.5 11.7 %collective-permute-start.7 = (f32[2,8,4,8,128]{4,3,2,1,0:T(8,128)S(1)}, f32[2,8,4,8,128]{4,3,2,1,0:T(8,128)S(1)}, u32[]{:S(2)}, u32[]{:S(2)}) collective-permute-start(f32[2,8,4,8,128]{4,3,2,1,0:T(8,128)S(1)} %get-tuple-element.31), channel_id=1, source_target_pairs={{0,31},{1,0},{2,1},{3,2},{4,3},{5,4},{6,5},{7,6},{8,7},{9,8},{10,9... | collective-permute-start | bytes 786440 | tf_op jit(solution)/shard_map/ppermute | solution.py:271
  74.7 13.0 %collective-permute-start.8 = (f32[4,8,4,8,128]{4,3,2,1,0:T(8,128)S(1)}, f32[4,8,4,8,128]{4,3,2,1,0:T(8,128)}, u32[]{:S(2)}, u32[]{:S(2)}) collective-permute-start(f32[4,8,4,8,128]{4,3,2,1,0:T(8,128)S(1)} %shard_map.44.refs_0_), channel_id=1, source_target_pairs={{0,1},{1,2},{2,3},{3,4},{4,5},{5,6},{6,7},{7,8},{8,9},{9,10},{10,1... | collective-permute-start | bytes 1572872 | tf_op jit(solution)/shard_map/ppermute | solution.py:271
  76.6 12.7 %collective-permute-start.9 = (f32[4,8,4,8,128]{4,3,2,1,0:T(8,128)S(1)}, f32[4,8,4,8,128]{4,3,2,1,0:T(8,128)}, u32[]{:S(2)}, u32[]{:S(2)}) collective-permute-start(f32[4,8,4,8,128]{4,3,2,1,0:T(8,128)S(1)} %shard_map.44.refs_0_), channel_id=1, source_target_pairs={{0,31},{1,0},{2,1},{3,2},{4,3},{5,4},{6,5},{7,6},{8,7},{9,8},{10,9... | collective-permute-start | bytes 1572872 | tf_op jit(solution)/shard_map/ppermute | solution.py:271
  82.7 6.6 %copy-start.1 = (f32[4,7,8,4,8,128]{5,4,3,2,1,0:T(8,128)S(1)}, f32[4,7,8,4,8,128]{5,4,3,2,1,0:T(8,128)}, u32[]{:S(2)}) copy-start(f32[4,7,8,4,8,128]{5,4,3,2,1,0:T(8,128)} %copy-done) | copy-start | bytes 11010052
  94.4 13.0 %collective-permute-start.12 = (f32[4,8,4,8,128]{4,3,2,1,0:T(8,128)S(1)}, f32[4,8,4,8,128]{4,3,2,1,0:T(8,128)S(1)}, u32[]{:S(2)}, u32[]{:S(2)}) collective-permute-start(f32[4,8,4,8,128]{4,3,2,1,0:T(8,128)S(1)} %shard_map.47.refs_0_), channel_id=1, source_target_pairs={{0,1},{1,2},{2,3},{3,4},{4,5},{5,6},{6,7},{7,8},{8,9},{9,10},{10,1... | collective-permute-start | bytes 1572872 | tf_op jit(solution)/shard_map/ppermute | solution.py:271
  96.3 12.8 %collective-permute-start.13 = (f32[4,8,4,8,128]{4,3,2,1,0:T(8,128)S(1)}, f32[4,8,4,8,128]{4,3,2,1,0:T(8,128)S(1)}, u32[]{:S(2)}, u32[]{:S(2)}) collective-permute-start(f32[4,8,4,8,128]{4,3,2,1,0:T(8,128)S(1)} %shard_map.47.refs_0_), channel_id=1, source_target_pairs={{0,31},{1,0},{2,1},{3,2},{4,3},{5,4},{6,5},{7,6},{8,7},{9,8},{10,9... | collective-permute-start | bytes 1572872 | tf_op jit(solution)/shard_map/ppermute | solution.py:271
  113.0 13.5 %collective-permute-start.14 = (f32[3,8,4,8,128]{4,3,2,1,0:T(8,128)S(1)}, f32[3,8,4,8,128]{4,3,2,1,0:T(8,128)S(1)}, u32[]{:S(2)}, u32[]{:S(2)}) collective-permute-start(f32[3,8,4,8,128]{4,3,2,1,0:T(8,128)S(1)} %get-tuple-element.30), channel_id=1, source_target_pairs={{0,1},{1,2},{2,3},{3,4},{4,5},{5,6},{6,7},{7,8},{8,9},{9,10},{10,1... | collective-permute-start | bytes 1179656 | tf_op jit(solution)/shard_map/ppermute | solution.py:271
  114.9 11.5 %collective-permute-start.15 = (f32[3,8,4,8,128]{4,3,2,1,0:T(8,128)S(1)}, f32[3,8,4,8,128]{4,3,2,1,0:T(8,128)S(1)}, u32[]{:S(2)}, u32[]{:S(2)}) collective-permute-start(f32[3,8,4,8,128]{4,3,2,1,0:T(8,128)S(1)} %get-tuple-element.29), channel_id=1, source_target_pairs={{0,31},{1,0},{2,1},{3,2},{4,3},{5,4},{6,5},{7,6},{8,7},{9,8},{10,9... | collective-permute-start | bytes 1179656 | tf_op jit(solution)/shard_map/ppermute | solution.py:271
  120.9 5.5 %collective-permute-start.16 = (f32[2,8,128]{2,1,0:T(8,128)S(1)}, f32[2,8,128]{2,1,0:T(8,128)S(1)}, u32[]{:S(2)}, u32[]{:S(2)}) collective-permute-start(f32[2,8,128]{2,1,0:T(8,128)S(1)} %get-tuple-element.20.earlier), channel_id=1, source_target_pairs={{0,480},{32,0},{64,32},{96,64},{128,96},{160,128},{192,160},{224,1... | collective-permute-start | bytes 24584 | tf_op jit(solution)/shard_map/ppermute | solution.py:271
  129.7 21.3 %all-to-all-start = ((f32[32,2,8,128]{3,2,1,0:T(8,128)}), f32[32,2,8,128]{3,2,1,0:T(8,128)S(1)}, u32[]{:S(2)}, u32[]{:S(2)}) async-start(f32[32,2,8,128]{3,2,1,0:T(8,128)} %get-tuple-element.26), calls=%async_computation | async-start | bytes 524288 | tf_op jit(solution)/shard_map/all_to_all | solution.py:335
  151.0 1.2 copy-start.3
Sparse Core Ops, SparseCore 0:
  82.8 68.1 all-gather.2

commit v3 on v2

v3 whole, which is shorter than its diff:
```python
import functools

import jax
import jax.numpy as jnp
from jax import lax
from jax.experimental import pallas as pl
from jax.experimental.pallas import tpu as pltpu
from jax.sharding import PartitionSpec as P

RATIO = 4
LAYERS = 4
REACH = 2
TILE = (8, 4, 8, 128)
COARSE = (2, 8, 128)
ROUNDS = (1, 3, 3, 3, 3, 3)
STEP = 0.2
VMEM = pl.BlockSpec(memory_space=pltpu.VMEM)
SMEM = pl.BlockSpec(memory_space=pltpu.SMEM)
ANY = pl.BlockSpec(memory_space=pl.ANY)
F32 = jnp.float32
MIB = 1024 * 1024


def call(body, outs, ins, scratch=(), limit=32):
    return pl.pallas_call(
        body,
        out_shape=[jax.ShapeDtypeStruct(s, F32) for s in outs],
        in_specs=ins,
        out_specs=[VMEM] * len(outs),
        scratch_shapes=list(scratch),
        compiler_params=pltpu.CompilerParams(vmem_limit_bytes=limit * MIB),
    )


def comb(transposed):
    a = lax.broadcasted_iota(jnp.int32, (512, 512), 0)
    b = lax.broadcasted_iota(jnp.int32, (512, 512), 1)
    natural, apart = (b, a) if transposed else (a, b)
    hit = natural == 4 * (apart & 127) + (apart >> 7)
    return jnp.where(hit, 1.0, 0.0).astype(jnp.bfloat16)


def exact_dot(rows, matrix):
    count = rows.shape[0]
    high = rows.astype(jnp.bfloat16)
    rest = rows - high.astype(F32)
    middle = rest.astype(jnp.bfloat16)
    low = (rest - middle.astype(F32)).astype(jnp.bfloat16)
    parts = jnp.concatenate([high, middle, low], axis=0)
    moved = jnp.dot(parts, matrix, preferred_element_type=F32)
    return (moved[:count] + moved[count : 2 * count]) + moved[2 * count :]


def split_rows(rows, matrix, buffer):
    apart = exact_dot(rows, matrix)
    for q in range(4):
        buffer[q] = apart[:, q * 128 : (q + 1) * 128]


def split_tile(buffer, block, j, q):
    return buffer[q, pl.ds(64 * block + j, 8, stride=8), :]


def half_sum(tiles, h):
    total = None
    for j in range(4 * h, 4 * h + 4):
        for q in range(4):
            total = tiles[j][q] if total is None else total + tiles[j][q]
    return total


def copy_edges(state, outer, inner, core, width):
    spare = LAYERS - width
    for x in range(width):
        outer[x] = state[core * spare + x]
        inner[x] = state[(1 - core) * spare + x]


def state_kernel(place, starts, earlier, state, outer, inner, coarse, raw, buffer, ready):
    for x in range(LAYERS):
        pltpu.make_async_copy(starts.at[0, x], raw.at[x], ready.at[x]).start()
    matrix = comb(False)
    for x in range(LAYERS):
        pltpu.make_async_copy(starts.at[0, x], raw.at[x], ready.at[x]).wait()
    split_rows(raw[...].reshape(LAYERS * 64, 512), matrix, buffer)
    sums = [None, None]
    for x in range(LAYERS):
        tiles = [[split_tile(buffer, x, j, q) for q in range(4)] for j in range(8)]
        for j in range(8):
            for q in range(4):
                state[x, j, q] = tiles[j][q]
        for h in range(2):
            part = half_sum(tiles, h)
            sums[h] = part if sums[h] is None else sums[h] + part
    for h in range(2):
        coarse[h] = sums[h] * (1.0 / 64)
    copy_edges(state, outer, inner, place[2], ROUNDS[0])


def weigh(velocity, diffusion, step, spacing):
    spread = diffusion * (step / (spacing * spacing))
    weights = [None]
    for component in velocity:
        moved = component * (step / spacing)
        weights.append(spread + jnp.maximum(moved, 0.0))
        weights.append(spread - jnp.minimum(moved, 0.0))
    total = weights[1]
    for weight in weights[2:]:
        total = total + weight
    weights[0] = 1.0 - total
    return weights


def field_kernel(place, velocity, diffusivity, own, outer, inner, coarse, raw, buffer, ready):
    def copies(x):
        return (
            pltpu.make_async_copy(velocity.at[:, x], raw.at[x, pl.ds(0, 3)], ready.at[x, 0]),
            pltpu.make_async_copy(diffusivity.at[x], raw.at[x, 3], ready.at[x, 1]),
        )

    for x in range(LAYERS):
        for copy in copies(x):
            copy.start()
    matrix = comb(False)
    for f in range(4):
        for h in range(2):
            coarse[f, h] = jnp.zeros((8, 128), F32)

    def layer(x, carry):
        for copy in copies(x):
            copy.wait()
        split_rows(raw[x].reshape(4 * 64, 512), matrix, buffer)
        for f in range(4):
            tiles = [[split_tile(buffer, f, j, q) for q in range(4)] for j in range(8)]
            for h in range(2):
                coarse[f, h] += half_sum(tiles, h) * (1.0 / 64)
            for j in range(8):
                for q in range(4):
                    own[x, f, j, q] = tiles[j][q]
        return carry

    lax.fori_loop(0, LAYERS, layer, 0)
    core = place[2]
    spare = LAYERS - REACH

    def edge(x, carry):
        outer[x] = own[core * spare + x]
        inner[x] = own[(1 - core) * spare + x]
        return carry

    lax.fori_loop(0, REACH, edge, 0)


def weight_kernel(count, fields, weights):
    def layer(x, carry):
        for j in range(8):
            for q in range(4):
                parts = [fields[x, f, j, q] for f in range(4)]
                for i, weight in enumerate(weigh(parts[:3], parts[3], STEP, 1.0)):
                    weights[x, i, j, q] = weight
        return carry

    lax.fori_loop(0, count, layer, 0)


def fine_layer(source, weights, target, x, wx, tx):
    tiles = [[source[x, j, q] for q in range(4)] for j in range(8)]
    for j in range(8):
        for q in range(4):
            behind_y = tiles[j - 1][q] if j > 0 else pltpu.roll(tiles[7][q], 1, 0)
            ahead_y = tiles[j + 1][q] if j < 7 else pltpu.roll(tiles[0][q], 7, 0)
            behind_z = tiles[j][q - 1] if q > 0 else pltpu.roll(tiles[j][3], 1, 1)
            ahead_z = tiles[j][q + 1] if q < 3 else pltpu.roll(tiles[j][0], 127, 1)
            target[tx, j, q] = (
                (weights[wx, 0, j, q] * tiles[j][q] + weights[wx, 1, j, q] * source[x - 1, j, q])
                + (weights[wx, 2, j, q] * source[x + 1, j, q] + weights[wx, 3, j, q] * behind_y)
                + (weights[wx, 4, j, q] * ahead_y + weights[wx, 5, j, q] * behind_z)
                + weights[wx, 6, j, q] * ahead_z
            )


def round_kernel(width, after, final, place, *refs):
    state, outer, inner, own, *refs = refs
    if width > 1:
        own_outer, own_inner, *refs = refs
    if final:
        later, fields, out, residual, one, two = refs
    else:
        refs = refs[len(refs) - 3 - 2 * (after < LAYERS) :]
        out, *edges, one, two = refs
    core = place[2]
    low, high = LAYERS - width, 2 * LAYERS
    outer_begin = low + core * (high - low)
    inner_begin = high - core * (high - low)
    for x in range(width):
        one[outer_begin + x] = outer[x]
        one[inner_begin + x] = inner[x]
    for x in range(LAYERS):
        one[LAYERS + x] = state[x]
    source, target = one, two
    for step in range(1, width + 1):
        ends = step == width
        goal = out if ends else target
        shift = LAYERS if ends else 0
        depth = width - step

        def sweep(begin, count, weights, first, source=source, goal=goal, shift=shift):
            def body(i, carry):
                fine_layer(source, weights, goal, begin + i, first + i, begin + i - shift)
                return carry

            lax.fori_loop(0, count, body, 0)

        sweep(LAYERS, LAYERS, own, 0)
        if depth > 0:
            below, above = LAYERS - depth, 2 * LAYERS
            skip = REACH - depth
            sweep(below + core * (above - below), depth, own_outer, (1 - core) * skip)
            sweep(above - core * (above - below), depth, own_inner, core * skip)
        source, target = target, source
    if final:
        for h in range(2):
            total = None
            for x in range(LAYERS):
                part = half_sum([[out[x, j, q] for q in range(4)] for j in range(8)], h)
                total = part if total is None else total + part
            total = total * (1.0 / 64) - later[h]
            for copy in range(residual.shape[0]):
                residual[copy, h] = total
    elif after < LAYERS:
        copy_edges(out, *edges, core, after)


def coarse_step(read, weights, write, count):
    stride = 4

    def group(g, carry):
        behind, now = carry
        for i in range(stride):
            x = g * stride + i
            ahead = read(x + 1)
            for h in range(2):
                behind_y = now[0] if h else pltpu.roll(now[1], 1, 0)
                ahead_y = pltpu.roll(now[0], 7, 0) if h else now[1]
                behind_z = pltpu.roll(now[h], 1, 1)
                ahead_z = pltpu.roll(now[h], 127, 1)
                write(
                    x,
                    h,
                    (weights[x, 0, h] * now[h] + weights[x, 1, h] * behind[h])
                    + (weights[x, 2, h] * ahead[h] + weights[x, 3, h] * behind_y)
                    + (weights[x, 4, h] * ahead_y + weights[x, 5, h] * behind_z)
                    + weights[x, 6, h] * ahead_z,
                )
            behind, now = now, ahead
        return behind, now

    lax.fori_loop(0, count // stride, group, (read(count - 1), read(0)))


def chain_kernel(place, residuals, fields, shares, weights, one, two):
    count = weights.shape[0]
    slices = shares.shape[0]
    slice_index = place[0]
    layer_index = place[1]
    shares[...] = jnp.zeros(shares.shape, F32)

    def prepare(x, carry):
        for h in range(2):
            parts = [fields[x, f, h] for f in range(4)]
            for i, weight in enumerate(weigh(parts[:3], parts[3], STEP * RATIO, 1.0 * RATIO)):
                weights[x, i, h] = weight
            one[x, h] = residuals[x, h]
        return carry

    lax.fori_loop(0, count, prepare, 0)
    one[count] = one[0]

    def reader(ref):
        return lambda x: [ref[x, h] for h in range(2)]

    def writer(ref):
        def write(x, h, value):
            ref[x, h] = value

        return write

    def link(n, carry):
        for source, target in ((one, two), (two, one)) * 2:
            coarse_step(reader(source), weights, writer(target), count)
            target[count] = target[0]
        for h in range(2):
            shares[n, h] = one[layer_index, h]
        return carry

    lax.fori_loop(slice_index + 1, slices, link, 0)


def finish_kernel(shares, state, out, buffer):
    change = []
    for h in range(2):
        total = shares[0, h]
        for n in range(1, shares.shape[0]):
            total = total + shares[n, h]
        change.append(total)
    matrix = comb(True)
    for x in range(LAYERS):
        for j in range(8):
            for q in range(4):
                buffer[q, pl.ds(64 * x + j, 8, stride=8), :] = state[x, j, q] + change[j // 4]
    rows = jnp.concatenate([buffer[q] for q in range(4)], axis=1)
    out[0] = exact_dot(rows, matrix).reshape(LAYERS, 64, 512)


def swap_inner(block):
    count = lax.axis_size("space")
    return lax.ppermute(block, "space", [(p, p ^ 1) for p in range(count)])


def outer_partner(p, count):
    return (p + 1) % count if p % 2 else (p - 1) % count


def swap_outer(block):
    count = lax.axis_size("space")
    return lax.ppermute(block, "space", [(p, outer_partner(p, count)) for p in range(count)])


def swap_outer_fields(block):
    slices, count = lax.axis_size("cuts"), lax.axis_size("space")
    route = []
    for n in range(slices):
        there = (n + slices // 2) % slices
        route += [(n * count + p, there * count + outer_partner(p, count)) for p in range(count)]
    return lax.ppermute(block, ("cuts", "space"), route)


def shards(starts, velocity, diffusivity):
    count = lax.axis_size("space")
    slices = lax.axis_size("cuts")
    block = (LAYERS, *TILE)
    row = lax.axis_index("space")
    place = jnp.stack([lax.axis_index("cuts"), row, row % 2]).astype(jnp.int32)
    split_scratch = pltpu.VMEM((4, 256, 128), F32)
    own, field_outer, field_inner, coarse_fields = call(
        field_kernel,
        [(LAYERS, 4, *TILE), (REACH, 4, *TILE), (REACH, 4, *TILE), (4, *COARSE)],
        [SMEM, ANY, ANY],
        [pltpu.VMEM((LAYERS, 4, 64, 512), F32), split_scratch, pltpu.SemaphoreType.DMA((LAYERS, 2))],
        limit=60,
    )(place, velocity, diffusivity)
    field_outer = swap_outer_fields(field_outer)
    field_inner = swap_inner(field_inner)
    group = 4
    some_fields = lax.all_gather(
        coarse_fields,
        "space",
        axis_index_groups=[[g * group + i for i in range(group)] for g in range(count // group)],
    )
    all_fields = lax.all_gather(
        some_fields,
        "space",
        axis_index_groups=[[g * group + i for g in range(count // group)] for i in range(group)],
    ).reshape(count, 4, *COARSE)
    edge = (ROUNDS[0], *TILE)
    state, outer, inner, coarse_old = call(
        state_kernel,
        [block, edge, edge, COARSE],
        [SMEM, ANY, ANY],
        [pltpu.VMEM((LAYERS, 64, 512), F32), split_scratch, pltpu.SemaphoreType.DMA((LAYERS,))],
    )(place, starts, coarse_fields)
    coarse_later = lax.ppermute(coarse_old, "cuts", [((n + 1) % slices, n) for n in range(slices)])

    def weights_of(fields):
        layers = fields.shape[0]
        return call(functools.partial(weight_kernel, layers), [(layers, 7, *TILE)], [VMEM])(fields)[0]

    own_weights = weights_of(own)
    sides = [weights_of(field_outer), weights_of(field_inner)]
    for index, width in enumerate(ROUNDS):
        final = index == len(ROUNDS) - 1
        after = LAYERS if final else ROUNDS[index + 1]
        operands = [place, state, swap_outer(outer), swap_inner(inner), own_weights]
        specs = [SMEM] + [VMEM] * 4
        if width > 1:
            operands += sides
            specs += [VMEM] * 2
        outs = [block]
        if final:
            operands += [coarse_later, all_fields]
            specs += [VMEM, ANY]
            outs.append((count, *COARSE))
        elif index == 2:
            operands.append(some_fields)
            specs.append(ANY)
        if after < LAYERS:
            outs += [(after, *TILE)] * 2
        outs = call(
            functools.partial(round_kernel, width, after, final),
            outs,
            specs,
            [pltpu.VMEM((3 * LAYERS, *TILE), F32)] * 2,
        )(*operands)
        state = outs[0]
        outer, inner = outs[1:] if after < LAYERS else (state, state)
    residuals = lax.all_to_all(outs[1], "space", 0, 0)
    shares = call(
        chain_kernel,
        [(slices, *COARSE)],
        [SMEM, VMEM, VMEM],
        [
            pltpu.VMEM((count, 7, *COARSE), F32),
            pltpu.VMEM((count + 1, *COARSE), F32),
            pltpu.VMEM((count + 1, *COARSE), F32),
        ],
    )(place, residuals, all_fields)[0]
    shares = lax.all_to_all(shares, "cuts", 0, 0)
    return call(finish_kernel, [(1, LAYERS, 64, 512)], [VMEM, VMEM], [split_scratch])(shares, state)[0]


def solution(mesh):
    placed = (P("cuts", "space", None, None), P(None, "space", None, None), P("space", None, None))
    return jax.shard_map(
        shards,
        mesh=mesh,
        in_specs=placed,
        out_specs=P("cuts", "space", None, None),
        check_vma=False,
    )
```

time: 188 us -> 219 us (1.16)
  the two profiles are of different devices: /device:TPU:8 before, /device:TPU:2 now
where the time goes in v3:
time: 219 us; the launch traced here: 218 us
  Pallas kernels  73.9 us (34%)
  starting transfers between devices  48.5 us (22%)
  blocking collectives  42.2 us (19%)
  waiting for transfers between devices  27.4 us (13%)
  between operations  13.7 us (6%)
  local copies, waits for them, and re-layouts  11.5 us (5%)
    pallas_call x1, Pallas kernels, shards(): call(chain_kernel, [(slices, *COARSE)], [SMEM, VMEM, VMEM], [pltpu.VMEM((...  43.8 us
    ppermute x6, waiting for transfers between devices, swap_outer(): lax.ppermute(block, 'space', [(p, outer_partner(p, count)) for p in range...  26 us
    ppermute x6, starting transfers between devices, swap_outer(): lax.ppermute(block, 'space', [(p, outer_partner(p, count)) for p in range...  22.4 us
    pallas_call x6, Pallas kernels, shards(): call(functools.partial(round_kernel, width, after, final), outs, specs, [...  19.1 us
    all_to_all x1, blocking collectives, shards(): residuals = lax.all_to_all(outs[1], 'space', 0, 0)  18.5 us
    ppermute x7, starting transfers between devices, swap_inner(): return lax.ppermute(block, 'space', [(p, p ^ 1) for p in range(count)])  15.9 us
    all_to_all x1, blocking collectives, shards(): shares = lax.all_to_all(shares, 'cuts', 0, 0)  12.7 us
    unnamed x26, local copies, waits for them, and re-layouts  11.5 us
  transfers between devices with their start and end apart: 16, of which 4 were waited for; matrix products, arithmetic and copies ran while one was open for 0% of the time, Pallas kernels for 9%

profile of v3, /device:TPU:2, one launch (start us, length us, event | category | flops | bytes accessed | tf_op | source)
XLA Modules:
  0.0 217.9 jit_solution(1499139299225067091)
XLA Ops:
  6.5 0.0 all-gather.4.cloned.1.call-start
  6.5 0.7 pad_add_fusion.place
  7.2 6.7 %shard_map.37 = (f32[4,4,8,4,8,128]{5,4,3,2,1,0:T(8,128)}, f32[2,4,8,4,8,128]{5,4,3,2,1,0:T(8,128)}, f32[2,4,8,4,8,128]{5,4,3,2,1,0:T(8,128)}, f32[4,2,8,128]{3,2,1,0:T(8,128)}) custom-call(s32[3]{0:T(128)} %pad_add_fusion.place, f32[3,4,64,512]{3,2,1,0:T(8,128)} %velocity.1, f32[4,64,512]{2,1,0:T(8,128)} %diffusivity.1), custom_call_target="tpu_custom_call" | custom-call | tf_op jit(solution)/shard_map/pallas_call | solution.py:345
  13.9 2.8 %collective-permute-start.4 = (f32[2,4,8,4,8,128]{5,4,3,2,1,0:T(8,128)}, f32[2,4,8,4,8,128]{5,4,3,2,1,0:T(8,128)S(1)}, u32[]{:S(2)}, u32[]{:S(2)}) collective-permute-start(f32[2,4,8,4,8,128]{5,4,3,2,1,0:T(8,128)} %get-tuple-element.38), channel_id=1, source_target_pairs={{0,287},{1,258},{2,257},{3,260},{4,259},{5,262},{6,261},{7,264},{8... | collective-permute-start | bytes 3145736 | tf_op jit(solution)/shard_map/ppermute | solution.py:335
  16.8 4.4 %collective-permute-start.5 = (f32[2,4,8,4,8,128]{5,4,3,2,1,0:T(8,128)}, f32[2,4,8,4,8,128]{5,4,3,2,1,0:T(8,128)S(1)}, u32[]{:S(2)}, u32[]{:S(2)}) collective-permute-start(f32[2,4,8,4,8,128]{5,4,3,2,1,0:T(8,128)} %get-tuple-element.39), channel_id=1, source_target_pairs={{0,1},{1,0},{2,3},{3,2},{4,5},{5,4},{6,7},{7,6},{8,9},{9,8},{10,11... | collective-permute-start | bytes 3145736 | tf_op jit(solution)/shard_map/ppermute | solution.py:317
  21.2 0.0 copy-done.10
  21.2 0.0 copy-done.12
  21.2 0.0 copy-start.11
  21.2 0.7 copy-done.11
  22.0 2.1 shard_map.38
  24.0 9.8 %collective-permute-start = (f32[1,8,4,8,128]{4,3,2,1,0:T(8,128)S(1)}, f32[1,8,4,8,128]{4,3,2,1,0:T(8,128)S(1)}, u32[]{:S(2)}, u32[]{:S(2)}) collective-permute-start(f32[1,8,4,8,128]{4,3,2,1,0:T(8,128)S(1)} %get-tuple-element.32), channel_id=1, source_target_pairs={{0,31},{1,2},{2,1},{3,4},{4,3},{5,6},{6,5},{7,8},{8,7},{9,10},{10,... | collective-permute-start | bytes 393224 | tf_op jit(solution)/shard_map/ppermute | solution.py:326
  33.9 1.9 collective-permute-start.1
  35.8 0.0 copy-start.6
  35.8 1.6 copy-done.6
  37.4 0.4 shard_map.39.refs_3_
  37.8 0.0 copy-start
  37.8 0.0 collective-permute-done.refs_1_
  37.8 0.0 collective-permute-done.1.refs_2_
  37.8 2.1 shard_map.40
  39.9 0.0 copy-done
  39.9 2.6 %collective-permute-start.2 = (f32[3,8,4,8,128]{4,3,2,1,0:T(8,128)}, f32[3,8,4,8,128]{4,3,2,1,0:T(8,128)}, u32[]{:S(2)}, u32[]{:S(2)}) collective-permute-start(f32[3,8,4,8,128]{4,3,2,1,0:T(8,128)} %get-tuple-element.36), channel_id=1, source_target_pairs={{0,31},{1,2},{2,1},{3,4},{4,3},{5,6},{6,5},{7,8},{8,7},{9,10},{10,... | collective-permute-start | bytes 1179656 | tf_op jit(solution)/shard_map/ppermute | solution.py:326
  42.5 1.9 collective-permute-start.3
  44.5 11.0 %all-gather = f32[16,2,8,128]{3,2,1,0:T(8,128)} all-gather(f32[4,2,8,128]{3,2,1,0:T(8,128)S(1)} %copy-done.11), channel_id=2, replica_groups={{0,1,2,3},{4,5,6,7},{8,9,10,11},{12,13,14,15},{16,17,18,19},{20,21,22,2..., dimensions={0}, use_global_device_ids=true | all-gather | bytes 163840 | tf_op jit(solution)/shard_map/all_gather | solution.py:355
  55.4 0.0 all-gather.4.cloned.1.call-update
  55.5 0.0 collective-permute-done.4.fields
  55.5 0.0 copy-start.8
  55.5 1.0 copy-done.8
  56.4 1.2 copy-done.9
  57.7 0.2 shard_map.41.refs_4_
  57.9 0.0 collective-permute-done.5.fields
  57.9 0.2 shard_map.42.refs_5_
  58.1 0.0 collective-permute-done.2.refs_1_
  58.1 0.0 collective-permute-done.3.refs_2_
  58.1 2.2 %copy-done.1 = f32[4,7,8,4,8,128]{5,4,3,2,1,0:T(8,128)S(1)} copy-done((f32[4,7,8,4,8,128]{5,4,3,2,1,0:T(8,128)S(1)}, f32[4,7,8,4,8,128]{5,4,3,2,1,0:T(8,128)}, u32[]{:S(2)}) %copy-start.1) | copy-done | bytes 3670040
  60.4 3.7 %shard_map.43 = (f32[4,8,4,8,128]{4,3,2,1,0:T(8,128)S(1)}, f32[3,8,4,8,128]{4,3,2,1,0:T(8,128)S(1)}, f32[3,8,4,8,128]{4,3,2,1,0:T(8,128)S(1)}) custom-call(s32[3]{0:T(128)S(1)} %copy-done.12, f32[4,8,4,8,128]{4,3,2,1,0:T(8,128)S(1)} %get-tuple-element.35.refs_0_, f32[3,8,4,8,128]{4,3,2,1,0:T(8,128)} %collective-permute-done.2.refs_1_, ...), custom_call_target="tpu_custom_call" | custom-call | tf_op jit(solution)/shard_map/pallas_call | solution.py:398
  64.1 3.3 %collective-permute-start.6 = (f32[3,8,4,8,128]{4,3,2,1,0:T(8,128)S(1)}, f32[3,8,4,8,128]{4,3,2,1,0:T(8,128)S(1)}, u32[]{:S(2)}, u32[]{:S(2)}) collective-permute-start(f32[3,8,4,8,128]{4,3,2,1,0:T(8,128)S(1)} %get-tuple-element.41), channel_id=1, source_target_pairs={{0,31},{1,2},{2,1},{3,4},{4,3},{5,6},{6,5},{7,8},{8,7},{9,10},{10,... | collective-permute-start | bytes 1179656 | tf_op jit(solution)/shard_map/ppermute | solution.py:326
  67.4 1.9 collective-permute-start.7
  69.3 8.1 %collective-permute-done.6.refs_1_ = f32[3,8,4,8,128]{4,3,2,1,0:T(8,128)S(1)} collective-permute-done((f32[3,8,4,8,128]{4,3,2,1,0:T(8,128)S(1)}, f32[3,8,4,8,128]{4,3,2,1,0:T(8,128)S(1)}, u32[]{:S(2)}, u32[]{:S(2)}) %collective-permute-start.6) | collective-permute-done | bytes 393248 | tf_op jit(solution)/shard_map/ppermute | solution.py:326
  77.4 0.0 collective-permute-done.7.refs_2_
  77.4 3.1 %shard_map.44 = (f32[4,8,4,8,128]{4,3,2,1,0:T(8,128)S(1)}, f32[3,8,4,8,128]{4,3,2,1,0:T(8,128)S(1)}, f32[3,8,4,8,128]{4,3,2,1,0:T(8,128)S(1)}) custom-call(s32[3]{0:T(128)S(1)} %copy-done.12, f32[4,8,4,8,128]{4,3,2,1,0:T(8,128)S(1)} %get-tuple-element.40.refs_0_, f32[3,8,4,8,128]{4,3,2,1,0:T(8,128)S(1)} %collective-permute-done.6.refs_1_, ...), custom_call_target="tpu_custom_call" | custom-call | tf_op jit(solution)/shard_map/pallas_call | solution.py:398
  80.5 2.9 %collective-permute-start.8 = (f32[3,8,4,8,128]{4,3,2,1,0:T(8,128)S(1)}, f32[3,8,4,8,128]{4,3,2,1,0:T(8,128)S(1)}, u32[]{:S(2)}, u32[]{:S(2)}) collective-permute-start(f32[3,8,4,8,128]{4,3,2,1,0:T(8,128)S(1)} %get-tuple-element.44), channel_id=1, source_target_pairs={{0,31},{1,2},{2,1},{3,4},{4,3},{5,6},{6,5},{7,8},{8,7},{9,10},{10,... | collective-permute-start | bytes 1179656 | tf_op jit(solution)/shard_map/ppermute | solution.py:326
  83.5 1.9 collective-permute-start.9
  85.4 8.4 %collective-permute-done.8.refs_1_ = f32[3,8,4,8,128]{4,3,2,1,0:T(8,128)S(1)} collective-permute-done((f32[3,8,4,8,128]{4,3,2,1,0:T(8,128)S(1)}, f32[3,8,4,8,128]{4,3,2,1,0:T(8,128)S(1)}, u32[]{:S(2)}, u32[]{:S(2)}) %collective-permute-start.8) | collective-permute-done | bytes 393248 | tf_op jit(solution)/shard_map/ppermute | solution.py:326
  93.8 0.0 collective-permute-done.9.refs_2_
  93.8 3.1 %shard_map.45 = (f32[4,8,4,8,128]{4,3,2,1,0:T(8,128)S(1)}, f32[3,8,4,8,128]{4,3,2,1,0:T(8,128)S(1)}, f32[3,8,4,8,128]{4,3,2,1,0:T(8,128)S(1)}) custom-call(s32[3]{0:T(128)S(1)} %copy-done.12, f32[4,8,4,8,128]{4,3,2,1,0:T(8,128)S(1)} %get-tuple-element.43.refs_0_, f32[3,8,4,8,128]{4,3,2,1,0:T(8,128)S(1)} %collective-permute-done.8.refs_1_, ...), custom_call_target="tpu_custom_call" | custom-call | tf_op jit(solution)/shard_map/pallas_call | solution.py:398
  97.0 1.9 collective-permute-start.10
  98.9 1.9 collective-permute-start.11
  100.8 9.5 %collective-permute-done.10.refs_1_ = f32[3,8,4,8,128]{4,3,2,1,0:T(8,128)S(1)} collective-permute-done((f32[3,8,4,8,128]{4,3,2,1,0:T(8,128)S(1)}, f32[3,8,4,8,128]{4,3,2,1,0:T(8,128)S(1)}, u32[]{:S(2)}, u32[]{:S(2)}) %collective-permute-start.10) | collective-permute-done | bytes 393248 | tf_op jit(solution)/shard_map/ppermute | solution.py:326
  110.3 0.0 collective-permute-done.11.refs_2_
  110.3 4.0 %shard_map.46 = (f32[4,8,4,8,128]{4,3,2,1,0:T(8,128)S(1)}, f32[3,8,4,8,128]{4,3,2,1,0:T(8,128)}, f32[3,8,4,8,128]{4,3,2,1,0:T(8,128)}) custom-call(s32[3]{0:T(128)S(1)} %copy-done.12, f32[4,8,4,8,128]{4,3,2,1,0:T(8,128)S(1)} %get-tuple-element.46.refs_0_, f32[3,8,4,8,128]{4,3,2,1,0:T(8,128)S(1)} %collective-permute-done.10.refs_1_, ...), custom_call_target="tpu_custom_call" | custom-call | tf_op jit(solution)/shard_map/pallas_call | solution.py:398
  114.3 1.9 collective-permute-start.12
  116.2 1.9 collective-permute-start.13
  118.1 7.3 %collective-permute-start.14 = (f32[2,8,128]{2,1,0:T(8,128)S(1)}, f32[2,8,128]{2,1,0:T(8,128)S(1)}, u32[]{:S(2)}, u32[]{:S(2)}) collective-permute-start(f32[2,8,128]{2,1,0:T(8,128)S(1)} %get-tuple-element.52), channel_id=1, source_target_pairs={{32,0},{64,32},{96,64},{128,96},{160,128},{192,160},{224,192},{256... | collective-permute-start | bytes 24584 | tf_op jit(solution)/shard_map/ppermute | solution.py:372
  125.4 1.3 collective-permute-done.14.refs_6_
  126.7 0.0 collective-permute-done.12.refs_1_
  126.7 0.0 collective-permute-done.13.refs_2_
  126.7 2.0 copy-done.2
  128.8 1.5 copy-done.4
  130.3 1.2 copy-done.5
  131.5 3.1 %shard_map.47 = (f32[4,8,4,8,128]{4,3,2,1,0:T(8,128)S(1)}, f32[32,2,8,128]{3,2,1,0:T(8,128)S(1)}) custom-call(s32[3]{0:T(128)S(1)} %copy-done.12, f32[4,8,4,8,128]{4,3,2,1,0:T(8,128)S(1)} %get-tuple-element.49.refs_0_, f32[3,8,4,8,128]{4,3,2,1,0:T(8,128)S(1)} %collective-permute-done.12.refs_1_, f32[3,8,4,8,128]{4,3,2,1,0:T(8,128)S(1)} %collective-permute-done.13.refs_2_, ...), custom_call_target="tpu_custom_call" | custom-call | tf_op jit(solution)/shard_map/pallas_call | solution.py:398
  134.6 18.5 %all_to_all.10.residuals = f32[32,2,8,128]{3,2,1,0:T(8,128)S(1)} all-to-all(f32[32,2,8,128]{3,2,1,0:T(8,128)S(1)} %get-tuple-element.53), channel_id=1, replica_groups=mesh['cuts'=16,'space'=32] {'space'}, dimensions={0} | all-to-all | bytes 524288 | tf_op jit(solution)/shard_map/all_to_all | solution.py:406
  153.1 43.8 %shard_map.48 = f32[16,2,8,128]{3,2,1,0:T(8,128)S(1)} custom-call(s32[3]{0:T(128)S(1)} %copy-done.12, f32[32,2,8,128]{3,2,1,0:T(8,128)S(1)} %all_to_all.10.residuals, f32[32,4,2,8,128]{4,3,2,1,0:T(8,128)S(1)} %copy-done.5), custom_call_target="tpu_custom_call" | custom-call | tf_op jit(solution)/shard_map/pallas_call | solution.py:407
  196.8 12.7 %all_to_all.11.shares = f32[16,2,8,128]{3,2,1,0:T(8,128)S(1)} all-to-all(f32[16,2,8,128]{3,2,1,0:T(8,128)S(1)} %shard_map.48), channel_id=1, replica_groups=mesh['cuts'=16,'space'=32] {'cuts'}, dimensions={0} | all-to-all | bytes 262144 | tf_op jit(solution)/shard_map/all_to_all | solution.py:417
  209.6 1.4 shard_map.49
  (12 shorter events, 0.0 us)
Async XLA Ops:
  6.5 14.7 %copy-start.10 = (f32[1,4,64,512]{3,2,1,0:T(8,128)S(1)}, f32[1,4,64,512]{3,2,1,0:T(8,128)}, u32[]{:S(2)}) copy-start(f32[1,4,64,512]{3,2,1,0:T(8,128)} %starts.1) | copy-start | bytes 1572868
  6.5 120.2 %all-gather.4.cloned.1.call-start = ((), (), s32[]{:S(2)}) async-start(), calls=%async_computation.2 | async-start | bytes 1179648 | tf_op jit(solution)/shard_map/all_gather | solution.py:360
  7.2 14.0 %copy-start.12 = (s32[3]{0:T(128)S(1)}, s32[3]{0:T(128)}, u32[]{:S(2)}) copy-start(s32[3]{0:T(128)} %pad_add_fusion.place) | copy-start | bytes 40
  13.9 41.5 %collective-permute-start.4 = (f32[2,4,8,4,8,128]{5,4,3,2,1,0:T(8,128)}, f32[2,4,8,4,8,128]{5,4,3,2,1,0:T(8,128)S(1)}, u32[]{:S(2)}, u32[]{:S(2)}) collective-permute-start(f32[2,4,8,4,8,128]{5,4,3,2,1,0:T(8,128)} %get-tuple-element.38), channel_id=1, source_target_pairs={{0,287},{1,258},{2,257},{3,260},{4,259},{5,262},{6,261},{7,264},{8... | collective-permute-start | bytes 3145736 | tf_op jit(solution)/shard_map/ppermute | solution.py:335
  16.8 41.1 %collective-permute-start.5 = (f32[2,4,8,4,8,128]{5,4,3,2,1,0:T(8,128)}, f32[2,4,8,4,8,128]{5,4,3,2,1,0:T(8,128)S(1)}, u32[]{:S(2)}, u32[]{:S(2)}) collective-permute-start(f32[2,4,8,4,8,128]{5,4,3,2,1,0:T(8,128)} %get-tuple-element.39), channel_id=1, source_target_pairs={{0,1},{1,0},{2,3},{3,2},{4,5},{5,4},{6,7},{7,6},{8,9},{9,8},{10,11... | collective-permute-start | bytes 3145736 | tf_op jit(solution)/shard_map/ppermute | solution.py:317
  21.2 0.8 copy-start.11
  24.0 13.8 %collective-permute-start = (f32[1,8,4,8,128]{4,3,2,1,0:T(8,128)S(1)}, f32[1,8,4,8,128]{4,3,2,1,0:T(8,128)S(1)}, u32[]{:S(2)}, u32[]{:S(2)}) collective-permute-start(f32[1,8,4,8,128]{4,3,2,1,0:T(8,128)S(1)} %get-tuple-element.32), channel_id=1, source_target_pairs={{0,31},{1,2},{2,1},{3,4},{4,3},{5,6},{6,5},{7,8},{8,7},{9,10},{10,... | collective-permute-start | bytes 393224 | tf_op jit(solution)/shard_map/ppermute | solution.py:326
  33.9 4.0 %collective-permute-start.1 = (f32[1,8,4,8,128]{4,3,2,1,0:T(8,128)S(1)}, f32[1,8,4,8,128]{4,3,2,1,0:T(8,128)S(1)}, u32[]{:S(2)}, u32[]{:S(2)}) collective-permute-start(f32[1,8,4,8,128]{4,3,2,1,0:T(8,128)S(1)} %get-tuple-element.33), channel_id=1, source_target_pairs={{0,1},{1,0},{2,3},{3,2},{4,5},{5,4},{6,7},{7,6},{8,9},{9,8},{10,11... | collective-permute-start | bytes 393224 | tf_op jit(solution)/shard_map/ppermute | solution.py:317
  35.8 1.6 copy-start.6
  37.8 2.1 copy-start
  39.9 18.2 %collective-permute-start.2 = (f32[3,8,4,8,128]{4,3,2,1,0:T(8,128)}, f32[3,8,4,8,128]{4,3,2,1,0:T(8,128)}, u32[]{:S(2)}, u32[]{:S(2)}) collective-permute-start(f32[3,8,4,8,128]{4,3,2,1,0:T(8,128)} %get-tuple-element.36), channel_id=1, source_target_pairs={{0,31},{1,2},{2,1},{3,4},{4,3},{5,6},{6,5},{7,8},{8,7},{9,10},{10,... | collective-permute-start | bytes 1179656 | tf_op jit(solution)/shard_map/ppermute | solution.py:326
  42.5 15.6 %collective-permute-start.3 = (f32[3,8,4,8,128]{4,3,2,1,0:T(8,128)}, f32[3,8,4,8,128]{4,3,2,1,0:T(8,128)}, u32[]{:S(2)}, u32[]{:S(2)}) collective-permute-start(f32[3,8,4,8,128]{4,3,2,1,0:T(8,128)} %get-tuple-element.37), channel_id=1, source_target_pairs={{0,1},{1,0},{2,3},{3,2},{4,5},{5,4},{6,7},{7,6},{8,9},{9,8},{10,11... | collective-permute-start | bytes 1179656 | tf_op jit(solution)/shard_map/ppermute | solution.py:317
  55.5 1.0 copy-start.8
  56.4 1.2 copy-start.9
  57.7 2.7 %copy-start.1 = (f32[4,7,8,4,8,128]{5,4,3,2,1,0:T(8,128)S(1)}, f32[4,7,8,4,8,128]{5,4,3,2,1,0:T(8,128)}, u32[]{:S(2)}) copy-start(f32[4,7,8,4,8,128]{5,4,3,2,1,0:T(8,128)} %copy-done) | copy-start | bytes 11010052
  58.1 52.2 %copy-start.3 = (f32[2,7,8,4,8,128]{5,4,3,2,1,0:T(8,128)}, f32[2,7,8,4,8,128]{5,4,3,2,1,0:T(8,128)S(1)}, u32[]{:S(2)}) copy-start(f32[2,7,8,4,8,128]{5,4,3,2,1,0:T(8,128)S(1)} %shard_map.42.refs_5_) | copy-start | bytes 5505028
  60.4 17.1 %copy-start.7 = (f32[16,2,8,128]{3,2,1,0:T(8,128)S(1)}, f32[16,2,8,128]{3,2,1,0:T(8,128)}, u32[]{:S(2)}) copy-start(f32[16,2,8,128]{3,2,1,0:T(8,128)} %all-gather) | copy-start | bytes 393220
  64.1 13.3 %collective-permute-start.6 = (f32[3,8,4,8,128]{4,3,2,1,0:T(8,128)S(1)}, f32[3,8,4,8,128]{4,3,2,1,0:T(8,128)S(1)}, u32[]{:S(2)}, u32[]{:S(2)}) collective-permute-start(f32[3,8,4,8,128]{4,3,2,1,0:T(8,128)S(1)} %get-tuple-element.41), channel_id=1, source_target_pairs={{0,31},{1,2},{2,1},{3,4},{4,3},{5,6},{6,5},{7,8},{8,7},{9,10},{10,... | collective-permute-start | bytes 1179656 | tf_op jit(solution)/shard_map/ppermute | solution.py:326
  67.4 10.0 %collective-permute-start.7 = (f32[3,8,4,8,128]{4,3,2,1,0:T(8,128)S(1)}, f32[3,8,4,8,128]{4,3,2,1,0:T(8,128)S(1)}, u32[]{:S(2)}, u32[]{:S(2)}) collective-permute-start(f32[3,8,4,8,128]{4,3,2,1,0:T(8,128)S(1)} %get-tuple-element.42), channel_id=1, source_target_pairs={{0,1},{1,0},{2,3},{3,2},{4,5},{5,4},{6,7},{7,6},{8,9},{9,8},{10,11... | collective-permute-start | bytes 1179656 | tf_op jit(solution)/shard_map/ppermute | solution.py:317
  80.5 13.3 %collective-permute-start.8 = (f32[3,8,4,8,128]{4,3,2,1,0:T(8,128)S(1)}, f32[3,8,4,8,128]{4,3,2,1,0:T(8,128)S(1)}, u32[]{:S(2)}, u32[]{:S(2)}) collective-permute-start(f32[3,8,4,8,128]{4,3,2,1,0:T(8,128)S(1)} %get-tuple-element.44), channel_id=1, source_target_pairs={{0,31},{1,2},{2,1},{3,4},{4,3},{5,6},{6,5},{7,8},{8,7},{9,10},{10,... | collective-permute-start | bytes 1179656 | tf_op jit(solution)/shard_map/ppermute | solution.py:326
  83.5 10.4 %collective-permute-start.9 = (f32[3,8,4,8,128]{4,3,2,1,0:T(8,128)S(1)}, f32[3,8,4,8,128]{4,3,2,1,0:T(8,128)S(1)}, u32[]{:S(2)}, u32[]{:S(2)}) collective-permute-start(f32[3,8,4,8,128]{4,3,2,1,0:T(8,128)S(1)} %get-tuple-element.45), channel_id=1, source_target_pairs={{0,1},{1,0},{2,3},{3,2},{4,5},{5,4},{6,7},{7,6},{8,9},{9,8},{10,11... | collective-permute-start | bytes 1179656 | tf_op jit(solution)/shard_map/ppermute | solution.py:317
  97.0 13.3 %collective-permute-start.10 = (f32[3,8,4,8,128]{4,3,2,1,0:T(8,128)S(1)}, f32[3,8,4,8,128]{4,3,2,1,0:T(8,128)S(1)}, u32[]{:S(2)}, u32[]{:S(2)}) collective-permute-start(f32[3,8,4,8,128]{4,3,2,1,0:T(8,128)S(1)} %get-tuple-element.47), channel_id=1, source_target_pairs={{0,31},{1,2},{2,1},{3,4},{4,3},{5,6},{6,5},{7,8},{8,7},{9,10},{10,... | collective-permute-start | bytes 1179656 | tf_op jit(solution)/shard_map/ppermute | solution.py:326
  98.9 11.4 %collective-permute-start.11 = (f32[3,8,4,8,128]{4,3,2,1,0:T(8,128)S(1)}, f32[3,8,4,8,128]{4,3,2,1,0:T(8,128)S(1)}, u32[]{:S(2)}, u32[]{:S(2)}) collective-permute-start(f32[3,8,4,8,128]{4,3,2,1,0:T(8,128)S(1)} %get-tuple-element.48), channel_id=1, source_target_pairs={{0,1},{1,0},{2,3},{3,2},{4,5},{5,4},{6,7},{7,6},{8,9},{9,8},{10,11... | collective-permute-start | bytes 1179656 | tf_op jit(solution)/shard_map/ppermute | solution.py:317
  114.3 12.5 %collective-permute-start.12 = (f32[3,8,4,8,128]{4,3,2,1,0:T(8,128)}, f32[3,8,4,8,128]{4,3,2,1,0:T(8,128)S(1)}, u32[]{:S(2)}, u32[]{:S(2)}) collective-permute-start(f32[3,8,4,8,128]{4,3,2,1,0:T(8,128)} %get-tuple-element.50), channel_id=1, source_target_pairs={{0,31},{1,2},{2,1},{3,4},{4,3},{5,6},{6,5},{7,8},{8,7},{9,10},{10,... | collective-permute-start | bytes 1179656 | tf_op jit(solution)/shard_map/ppermute | solution.py:326
  116.2 10.6 %collective-permute-start.13 = (f32[3,8,4,8,128]{4,3,2,1,0:T(8,128)}, f32[3,8,4,8,128]{4,3,2,1,0:T(8,128)S(1)}, u32[]{:S(2)}, u32[]{:S(2)}) collective-permute-start(f32[3,8,4,8,128]{4,3,2,1,0:T(8,128)} %get-tuple-element.51), channel_id=1, source_target_pairs={{0,1},{1,0},{2,3},{3,2},{4,5},{5,4},{6,7},{7,6},{8,9},{9,8},{10,11... | collective-permute-start | bytes 1179656 | tf_op jit(solution)/shard_map/ppermute | solution.py:317
  118.1 8.6 %collective-permute-start.14 = (f32[2,8,128]{2,1,0:T(8,128)S(1)}, f32[2,8,128]{2,1,0:T(8,128)S(1)}, u32[]{:S(2)}, u32[]{:S(2)}) collective-permute-start(f32[2,8,128]{2,1,0:T(8,128)S(1)} %get-tuple-element.52), channel_id=1, source_target_pairs={{32,0},{64,32},{96,64},{128,96},{160,128},{192,160},{224,192},{256... | collective-permute-start | bytes 24584 | tf_op jit(solution)/shard_map/ppermute | solution.py:372
  126.7 2.0 copy-start.2
  128.8 1.5 copy-start.4
  130.3 1.2 copy-start.5
Sparse Core Ops, SparseCore 0:
  55.6 40.4 all-gather.3

commit v4 on v3

v4 whole, which is shorter than its diff:
```python
import functools

import jax
import jax.numpy as jnp
from jax import lax
from jax.experimental import pallas as pl
from jax.experimental.pallas import tpu as pltpu
from jax.sharding import PartitionSpec as P

RATIO = 4
LAYERS = 4
REACH = 3
ROUNDS = 4
TILE = (8, 8, 512)
COARSE = (2, 8, 128)
STEP = 0.2
VMEM = pl.BlockSpec(memory_space=pltpu.VMEM)
SMEM = pl.BlockSpec(memory_space=pltpu.SMEM)
ANY = pl.BlockSpec(memory_space=pl.ANY)
F32 = jnp.float32
MIB = 1024 * 1024


def call(body, outs, ins, scratch=(), limit=24):
    return pl.pallas_call(
        body,
        out_shape=[jax.ShapeDtypeStruct(s, F32) for s in outs],
        in_specs=ins,
        out_specs=[VMEM] * len(outs),
        scratch_shapes=list(scratch),
        compiler_params=pltpu.CompilerParams(vmem_limit_bytes=limit * MIB),
    )


def fours(shape, fine):
    z = lax.broadcasted_iota(jnp.int32, shape, fine)
    block = lax.broadcasted_iota(jnp.int32, shape, 1 - fine)
    return jnp.where((z >> 2) == block, 1.0, 0.0).astype(jnp.bfloat16)


def exact_dot(rows, matrix):
    count = rows.shape[0]
    high = rows.astype(jnp.bfloat16)
    rest = rows - high.astype(F32)
    middle = rest.astype(jnp.bfloat16)
    low = (rest - middle.astype(F32)).astype(jnp.bfloat16)
    parts = jnp.concatenate([high, middle, low], axis=0)
    moved = jnp.dot(parts, matrix, preferred_element_type=F32)
    return (moved[:count] + moved[count : 2 * count]) + moved[2 * count :]


def spread(rows, buffer):
    for c in range(4):
        buffer[c] = rows[:, 128 * c : 128 * c + 128]


def spread_tile(buffer, j):
    return jnp.concatenate([buffer[c, pl.ds(j, 8, stride=8), :] for c in range(4)], axis=1)


def half_sums(read):
    sums = []
    for h in range(2):
        total = read(4 * h)
        for j in range(4 * h + 1, 4 * h + 4):
            total = total + read(j)
        sums.append(total)
    return sums


def weigh(velocity, diffusion, step, spacing):
    spread = diffusion * (step / (spacing * spacing))
    weights = [None]
    for component in velocity:
        moved = component * (step / spacing)
        weights.append(spread + jnp.maximum(moved, 0.0))
        weights.append(spread - jnp.minimum(moved, 0.0))
    total = weights[1]
    for weight in weights[2:]:
        total = total + weight
    weights[0] = 1.0 - total
    return weights


def own_kernel(velocity, diffusivity, starts, weights, coarse_fields, coarse_old, buffer):
    def layer(x, carry):
        for f in range(3):
            spread(velocity[f, x], buffer.at[f])
        spread(diffusivity[x], buffer.at[3])
        for j in range(8):
            parts = [spread_tile(buffer.at[f], j) for f in range(4)]
            for i, weight in enumerate(weigh(parts[:3], parts[3], STEP, 1.0)):
                weights[x, i, j] = weight
        return carry

    lax.fori_loop(0, LAYERS, layer, 0)
    sums = []
    for f in range(5):
        layers = [velocity[f, x] if f < 3 else (diffusivity[x], starts[x])[f - 3] for x in range(LAYERS)]
        spread((layers[0] + layers[1]) + (layers[2] + layers[3]), buffer.at[f])
        sums += half_sums(lambda j, f=f: spread_tile(buffer.at[f], j))
    means = exact_dot(jnp.concatenate(sums, axis=0), fours((512, 128), 0)) * (1.0 / 64)
    for f in range(5):
        for h in range(2):
            mean = means[16 * f + 8 * h : 16 * f + 8 * h + 8]
            if f < 4:
                coarse_fields[f, h] = mean
            else:
                coarse_old[h] = mean


def side_kernel(velocity, mixed, weights, buffer):
    def layer(x, carry):
        for f in range(3):
            spread(velocity[f, x], buffer.at[f])
        spread(mixed[LAYERS + x], buffer.at[3])
        for j in range(8):
            parts = [spread_tile(buffer.at[f], j) for f in range(4)]
            for i, weight in enumerate(weigh(parts[:3], parts[3], STEP, 1.0)):
                weights[x, i, j] = weight
        return carry

    lax.fori_loop(0, REACH, layer, 0)


def fine_layer(source, weights, target, x, wx, tx):
    tiles = [source[x, j] for j in range(8)]
    for j in range(8):
        behind_y = tiles[j - 1] if j > 0 else pltpu.roll(tiles[7], 1, 0)
        ahead_y = tiles[j + 1] if j < 7 else pltpu.roll(tiles[0], 7, 0)
        behind_z = pltpu.roll(tiles[j], 1, 1)
        ahead_z = pltpu.roll(tiles[j], 511, 1)
        target[tx, j] = (
            (weights[wx, 0, j] * tiles[j] + weights[wx, 1, j] * source[x - 1, j])
            + (weights[wx, 2, j] * source[x + 1, j] + weights[wx, 3, j] * behind_y)
            + (weights[wx, 4, j] * ahead_y + weights[wx, 5, j] * behind_z)
            + weights[wx, 6, j] * ahead_z
        )


def round_kernel(raw, final, place, state, inner, outer, own, own_inner, own_outer, *refs):
    if final:
        later, fields, out, residual, one, two, buffer = refs
    else:
        out, one, two, buffer = refs[-4:]
    core = place[2]

    def enter(x, carry):
        blocks = ((state, LAYERS), (outer, 2 * LAYERS * core), (inner, 2 * LAYERS * (1 - core)))
        for i, (ref, begin) in enumerate(blocks):
            if raw:
                spread(ref[x], buffer.at[i])
            for j in range(8):
                one[begin + x, j] = spread_tile(buffer.at[i], j) if raw else ref[x, j]
        return carry

    lax.fori_loop(0, LAYERS, enter, 0)
    source, target = one, two
    for step in range(1, LAYERS + 1):
        ends = step == LAYERS
        goal = out if ends else target
        shift = LAYERS if ends else 0
        depth = LAYERS - step

        def sweep(begin, count, weights, first, source=source, goal=goal, shift=shift):
            def body(i, carry):
                fine_layer(source, weights, goal, begin + i, first + i, begin + i - shift)
                return carry

            lax.fori_loop(0, count, body, 0)

        sweep(LAYERS, LAYERS, own, 0)
        if depth > 0:
            below, above = LAYERS - depth, 2 * LAYERS
            skip = REACH - depth
            sweep(below + core * (above - below), depth, own_outer, (1 - core) * skip)
            sweep(above - core * (above - below), depth, own_inner, core * skip)
        source, target = target, source
    if final:
        sums = half_sums(lambda j: (out[0, j] + out[1, j]) + (out[2, j] + out[3, j]))
        means = exact_dot(jnp.concatenate(sums, axis=0), fours((512, 128), 0)) * (1.0 / 64)
        for h in range(2):
            left = means[8 * h : 8 * h + 8] - later[h]
            for copy in range(residual.shape[0]):
                residual[copy, h] = left


def coarse_step(read, weights, write, count):
    first = read(0)
    behind, now = read(count - 1), first
    for x in range(count):
        ahead = read(x + 1) if x + 1 < count else first
        for h in range(2):
            behind_y = now[0] if h else pltpu.roll(now[1], 1, 0)
            ahead_y = pltpu.roll(now[0], 7, 0) if h else now[1]
            behind_z = pltpu.roll(now[h], 1, 1)
            ahead_z = pltpu.roll(now[h], 127, 1)
            write(
                x,
                h,
                (weights[x, 0, h] * now[h] + weights[x, 1, h] * behind[h])
                + (weights[x, 2, h] * ahead[h] + weights[x, 3, h] * behind_y)
                + (weights[x, 4, h] * ahead_y + weights[x, 5, h] * behind_z)
                + weights[x, 6, h] * ahead_z,
            )
        behind, now = now, ahead


def chain_kernel(place, residuals, fields, shares, weights, one, two):
    count = weights.shape[0]
    slices = shares.shape[0]
    slice_index = place[0]
    layer_index = place[1]
    shares[...] = jnp.zeros(shares.shape, F32)

    def prepare(x, carry):
        for h in range(2):
            parts = [fields[x, f, h] for f in range(4)]
            for i, weight in enumerate(weigh(parts[:3], parts[3], STEP * RATIO, 1.0 * RATIO)):
                weights[x, i, h] = weight
            one[x, h] = residuals[x, h]
        return carry

    lax.fori_loop(0, count, prepare, 0)

    def reader(ref):
        return lambda x: [ref[x, h] for h in range(2)]

    def writer(ref):
        def write(x, h, value):
            ref[x, h] = value

        return write

    def link(n, carry):
        for source, target in ((one, two), (two, one)) * 2:
            coarse_step(reader(source), weights, writer(target), count)
        for h in range(2):
            shares[n, h] = one[layer_index, h]
        return carry

    lax.fori_loop(slice_index + 1, slices, link, 0)


def finish_kernel(shares, state, out, buffer):
    change = []
    for h in range(2):
        total = shares[0, h]
        for n in range(1, shares.shape[0]):
            total = total + shares[n, h]
        change.append(total)
    wide = exact_dot(jnp.concatenate(change, axis=0), fours((128, 512), 1))
    for x in range(LAYERS):
        for j in range(8):
            h = j // 4
            tile = state[x, j] + wide[8 * h : 8 * h + 8]
            for c in range(4):
                buffer[x, c, pl.ds(j, 8, stride=8), :] = tile[:, 128 * c : 128 * c + 128]
        for c in range(4):
            out[0, x, :, 128 * c : 128 * c + 128] = buffer[x, c]


def swap_inner(block):
    count = lax.axis_size("space")
    return lax.ppermute(block, "space", [(p, p ^ 1) for p in range(count)])


def outer_partner(p, count):
    return (p + 1) % count if p % 2 else (p - 1) % count


def swap_outer(block):
    count = lax.axis_size("space")
    return lax.ppermute(block, "space", [(p, outer_partner(p, count)) for p in range(count)])


def swap_outer_fields(block):
    slices, count = lax.axis_size("cuts"), lax.axis_size("space")
    route = []
    for n in range(slices):
        there = (n + slices // 2) % slices
        route += [(n * count + p, there * count + outer_partner(p, count)) for p in range(count)]
    return lax.ppermute(block, ("cuts", "space"), route)


def shards(starts, velocity, diffusivity):
    count = lax.axis_size("space")
    slices = lax.axis_size("cuts")
    block = (LAYERS, *TILE)
    row = lax.axis_index("space")
    core = row & 1
    columns = pltpu.VMEM((5, 4, 64, 128), F32)
    place = jnp.stack([lax.axis_index("cuts"), row, core]).astype(jnp.int32)

    def halo(begin):
        cut = functools.partial(lax.dynamic_slice_in_dim, start_index=begin, slice_size=REACH)
        mixed = jnp.concatenate([starts[0], cut(diffusivity, axis=0)], axis=0)
        return cut(velocity, axis=1), mixed

    velocity_outer, mixed_outer = halo(core)
    velocity_inner, mixed_inner = halo(1 - core)
    velocity_inner = swap_inner(velocity_inner)
    mixed_inner = swap_inner(mixed_inner)
    velocity_outer = swap_outer_fields(velocity_outer)
    mixed_outer = swap_outer(mixed_outer)
    own_weights, coarse_fields, coarse_old = call(
        own_kernel,
        [(LAYERS, 7, *TILE), (4, *COARSE), COARSE],
        [VMEM] * 3,
        [columns],
    )(velocity, diffusivity, starts[0])
    group = 4
    some_fields = lax.all_gather(
        coarse_fields,
        "space",
        axis_index_groups=[[g * group + i for i in range(group)] for g in range(count // group)],
    )
    all_fields = lax.all_gather(
        some_fields,
        "space",
        axis_index_groups=[[g * group + i for g in range(count // group)] for i in range(group)],
    ).reshape(count, 4, *COARSE)
    coarse_later = lax.ppermute(coarse_old, "cuts", [((n + 1) % slices, n) for n in range(slices)])
    sides = [
        call(side_kernel, [(REACH, 7, *TILE)], [VMEM] * 2, [columns])(*halos)[0]
        for halos in ((velocity_inner, mixed_inner), (velocity_outer, mixed_outer))
    ]
    state, outer, inner = starts[0], mixed_outer, mixed_inner
    for index in range(ROUNDS):
        final = index == ROUNDS - 1
        if index > 0:
            inner, outer = swap_inner(state), swap_outer(state)
        operands = [place, state, inner, outer, own_weights, *sides]
        specs = [SMEM] + [VMEM] * 6
        outs = [block]
        if final:
            operands += [coarse_later, all_fields]
            specs += [VMEM, ANY]
            outs.append((count, *COARSE))
        elif index == 0:
            operands.append(some_fields)
            specs.append(ANY)
        outs = call(
            functools.partial(round_kernel, index == 0, final),
            outs,
            specs,
            [pltpu.VMEM((3 * LAYERS, *TILE), F32)] * 2 + [columns],
        )(*operands)
        state = outs[0]
    residuals = lax.all_to_all(outs[1], "space", 0, 0)
    shares = call(
        chain_kernel,
        [(slices, *COARSE)],
        [SMEM, VMEM, VMEM],
        [
            pltpu.VMEM((count, 7, *COARSE), F32),
            pltpu.VMEM((count, *COARSE), F32),
            pltpu.VMEM((count, *COARSE), F32),
        ],
    )(place, residuals, all_fields)[0]
    shares = lax.all_to_all(shares, "cuts", 0, 0)
    return call(finish_kernel, [(1, LAYERS, 64, 512)], [VMEM, VMEM], [columns])(shares, state)[0]


def solution(mesh):
    placed = (P("cuts", "space", None, None), P(None, "space", None, None), P("space", None, None))
    return jax.shard_map(
        shards,
        mesh=mesh,
        in_specs=placed,
        out_specs=P("cuts", "space", None, None),
        check_vma=False,
    )
```

time: 219 us -> 187 us (0.85)
  Pallas kernels: 73.9 us -> 37.9 us
  blocking collectives: 42.2 us -> 49.7 us
  starting transfers between devices: 48.5 us -> 44 us
  local copies, waits for them, and re-layouts: 11.5 us -> 15.4 us
  waiting for transfers between devices: 27.4 us -> 24.4 us
    pallas_call x1, Pallas kernels: 43.8 us -> 11 us  [shards(): call(chain_kernel, [(slices, *COARSE)], [SMEM, VMEM, VMEM], [pltpu.VMEM((...]
    all_gather x1, blocking collectives: 11 us -> 18.5 us  [shards(): lax.all_gather(coarse_fields, 'space', axis_index_groups=[[g * group + i...]
    ppermute x7 -> x5, starting transfers between devices: 15.9 us -> 12.1 us  [swap_inner(): return lax.ppermute(block, 'space', [(p, p ^ 1) for p in range(count)])]
    dynamic_slice x0 -> x2, local copies, waits for them, and re-layouts: none -> 3.46 us  [the longest x1 3.39 us: halo(): return (cut(velocity, axis=1), mixed)]
    pallas_call x12 -> x8, Pallas kernels: 30.2 us -> 26.9 us  [the longest x4 21.7 us: shards(): call(functools.partial(round_kernel, index == 0, final), outs, specs, [pl...]
    ppermute x6 -> x4, waiting for transfers between devices: 26 us -> 23 us  [swap_outer(): lax.ppermute(block, 'space', [(p, outer_partner(p, count)) for p in range...]
    ppermute x6 -> x4, starting transfers between devices: 22.4 us -> 23.5 us  [swap_outer(): lax.ppermute(block, 'space', [(p, outer_partner(p, count)) for p in range...]
    unnamed x26 -> x30, local copies, waits for them, and re-layouts: 11.5 us -> 11.9 us
  transfers between devices with their start and end apart: 16 -> 12, of which waited for: 4 -> 4; matrix products, arithmetic and copies ran while one was open for 0% -> 1% of each run, Pallas kernels for 9% -> 11%
where the time goes in v4:
time: 187 us; the launch traced here: 186 us
  blocking collectives  49.7 us (27%)
  starting transfers between devices  44 us (24%)
  Pallas kernels  37.9 us (20%)
  waiting for transfers between devices  24.4 us (13%)
  local copies, waits for them, and re-layouts  15.4 us (8%)
  between operations  13.7 us (7%)
    ppermute x4, starting transfers between devices, swap_outer(): lax.ppermute(block, 'space', [(p, outer_partner(p, count)) for p in range...  23.5 us
    ppermute x4, waiting for transfers between devices, swap_outer(): lax.ppermute(block, 'space', [(p, outer_partner(p, count)) for p in range...  23 us
    pallas_call x4, Pallas kernels, shards(): call(functools.partial(round_kernel, index == 0, final), outs, specs, [pl...  21.7 us
    all_gather x1, blocking collectives, shards(): lax.all_gather(coarse_fields, 'space', axis_index_groups=[[g * group + i...  18.5 us
    all_to_all x1, blocking collectives, shards(): residuals = lax.all_to_all(outs[1], 'space', 0, 0)  16.5 us
    all_to_all x1, blocking collectives, shards(): shares = lax.all_to_all(shares, 'cuts', 0, 0)  14.6 us
    ppermute x5, starting transfers between devices, swap_inner(): return lax.ppermute(block, 'space', [(p, p ^ 1) for p in range(count)])  12.1 us
    unnamed x30, local copies, waits for them, and re-layouts  11.9 us
  transfers between devices with their start and end apart: 12, of which 4 were waited for; matrix products, arithmetic and copies ran while one was open for 1% of the time, Pallas kernels for 11%

profile of v4, /device:TPU:2, one launch (start us, length us, event | category | flops | bytes accessed | tf_op | source)
XLA Modules:
  0.0 186.5 jit_solution(11781691517143148603)
XLA Ops:
  6.5 0.0 all-gather.4.cloned.1.call-start
  6.5 0.0 copy-start.11
  6.5 3.4 %constant_dynamic-slice_fusion = (f32[3,3,64,512]{3,2,1,0:T(8,128)}, f32[3,3,64,512]{3,2,1,0:T(8,128)}) fusion(f32[3,4,64,512]{3,2,1,0:T(8,128)} %velocity.1, s32[]{:T(128)S(6)} %select_n.9, s32[]{:T(128)S(6)} %select_n.8), kind=kLoop, calls=%fused_computation.2 | loop fusion | bytes 4718600 | tf_op jit(solution)/shard_map/dynamic_slice | solution.py:298
  9.9 0.0 copy-start.6
  9.9 3.0 %collective-permute-start.3 = (f32[3,3,64,512]{3,2,1,0:T(8,128)}, f32[3,3,64,512]{3,2,1,0:T(8,128)}, u32[]{:S(2)}, u32[]{:S(2)}) collective-permute-start(f32[3,3,64,512]{3,2,1,0:T(8,128)} %get-tuple-element.15), channel_id=1, source_target_pairs={{0,287},{1,258},{2,257},{3,260},{4,259},{5,262},{6,261},{7,264},{8... | collective-permute-start | bytes 3538952 | tf_op jit(solution)/shard_map/ppermute | solution.py:283
  12.9 4.4 %collective-permute-start.2 = (f32[3,3,64,512]{3,2,1,0:T(8,128)}, f32[3,3,64,512]{3,2,1,0:T(8,128)S(1)}, u32[]{:S(2)}, u32[]{:S(2)}) collective-permute-start(f32[3,3,64,512]{3,2,1,0:T(8,128)} %get-tuple-element.16), channel_id=1, source_target_pairs={{0,1},{1,0},{2,3},{3,2},{4,5},{5,4},{6,7},{7,6},{8,9},{9,8},{10,11... | collective-permute-start | bytes 3538952 | tf_op jit(solution)/shard_map/ppermute | solution.py:265
  17.3 0.0 copy-done.11
  17.3 0.1 constant_dynamic-slice_fusion.2
  17.4 0.0 copy-done.6
  17.4 0.0 copy-start.5
  17.4 1.5 pad_maximum_fusion
  18.9 1.9 %collective-permute-start = (f32[7,64,512]{2,1,0:T(8,128)}, f32[7,64,512]{2,1,0:T(8,128)S(1)}, u32[]{:S(2)}, u32[]{:S(2)}) collective-permute-start(f32[7,64,512]{2,1,0:T(8,128)} %get-tuple-element.18), channel_id=1, source_target_pairs={{0,1},{1,0},{2,3},{3,2},{4,5},{5,4},{6,7},{7,6},{8,9},{9,8},{10,11... | collective-permute-start | bytes 2752520 | tf_op jit(solution)/shard_map/ppermute | solution.py:265
  20.8 9.8 %collective-permute-start.1 = (f32[7,64,512]{2,1,0:T(8,128)}, f32[7,64,512]{2,1,0:T(8,128)}, u32[]{:S(2)}, u32[]{:S(2)}) collective-permute-start(f32[7,64,512]{2,1,0:T(8,128)} %get-tuple-element.17), channel_id=1, source_target_pairs={{0,31},{1,2},{2,1},{3,4},{4,3},{5,6},{6,5},{7,8},{8,7},{9,10},{10,... | collective-permute-start | bytes 2752520 | tf_op jit(solution)/shard_map/ppermute | solution.py:274
  30.6 0.0 copy-done.5
  30.7 1.3 shard_map.37
  32.0 0.0 copy-start.2
  32.0 1.8 copy-done.2
  33.7 18.5 %all-gather = f32[16,2,8,128]{3,2,1,0:T(8,128)} all-gather(f32[4,2,8,128]{3,2,1,0:T(8,128)S(1)} %get-tuple-element.11), channel_id=2, replica_groups={{0,1,2,3},{4,5,6,7},{8,9,10,11},{12,13,14,15},{16,17,18,19},{20,21,22,2..., dimensions={0}, use_global_device_ids=true | all-gather | bytes 163840 | tf_op jit(solution)/shard_map/all_gather | solution.py:313
  52.3 0.0 all-gather.4.cloned.1.call-update
  52.3 0.1 pad_add_fusion.place
  52.4 0.0 collective-permute-done.mixed.inner
  52.4 0.0 copy-start.8
  52.4 0.9 copy-done.8
  53.3 0.0 collective-permute-done.2.velocity
  53.3 1.0 copy-done.13
  54.4 1.2 copy-done.9
  55.5 1.3 copy-done.14
  56.8 0.6 shard_map.38.own_inner
  57.4 0.0 copy-start.10
  57.4 0.0 copy-start.12
  57.4 0.0 collective-permute-done.1.mixed.outer
  57.4 0.0 collective-permute-done.3.velocity
  57.4 0.0 copy-start.3
  57.4 2.2 %shard_map.39.own_outer = f32[3,7,8,8,512]{4,3,2,1,0:T(8,128)S(1)} custom-call(f32[3,3,64,512]{3,2,1,0:T(8,128)} %collective-permute-done.3.velocity, f32[7,64,512]{2,1,0:T(8,128)} %collective-permute-done.1.mixed.outer), custom_call_target="tpu_custom_call" | custom-call | tf_op jit(solution)/shard_map/pallas_call | solution.py:325
  59.7 0.0 copy-start
  59.7 0.0 copy-done.10
  59.7 0.0 copy-done.12
  59.7 0.7 copy-done.3
  60.4 6.2 %shard_map.40.state = f32[4,8,8,512]{3,2,1,0:T(8,128)S(1)} custom-call(s32[3]{0:T(128)S(1)} %pad_add_fusion.place, f32[4,64,512]{2,1,0:T(8,128)S(1)} %bitcast.7, f32[7,64,512]{2,1,0:T(8,128)S(1)} %copy-done.10, f32[7,64,512]{2,1,0:T(8,128)} %collective-permute-done.1.mixed.outer, f32[4,7,8,8,512]{4,3,2,1,0:T(8,128)S(1)} %copy-done.3, ...), custom_call_target="tpu_custom_call" | custom-call | tf_op jit(solution)/shard_map/pallas_call | solution.py:343
  66.6 5.7 %collective-permute-start.5 = (f32[4,8,8,512]{3,2,1,0:T(8,128)S(1)}, f32[4,8,8,512]{3,2,1,0:T(8,128)S(1)}, u32[]{:S(2)}, u32[]{:S(2)}) collective-permute-start(f32[4,8,8,512]{3,2,1,0:T(8,128)S(1)} %shard_map.40.state), channel_id=1, source_target_pairs={{0,31},{1,2},{2,1},{3,4},{4,3},{5,6},{6,5},{7,8},{8,7},{9,10},{10,... | collective-permute-start | bytes 1572872 | tf_op jit(solution)/shard_map/ppermute | solution.py:274
  72.3 1.9 %collective-permute-start.4 = (f32[4,8,8,512]{3,2,1,0:T(8,128)S(1)}, f32[4,8,8,512]{3,2,1,0:T(8,128)S(1)}, u32[]{:S(2)}, u32[]{:S(2)}) collective-permute-start(f32[4,8,8,512]{3,2,1,0:T(8,128)S(1)} %shard_map.40.state), channel_id=1, source_target_pairs={{0,1},{1,0},{2,3},{3,2},{4,5},{5,4},{6,7},{7,6},{8,9},{9,8},{10,11... | collective-permute-start | bytes 1572872 | tf_op jit(solution)/shard_map/ppermute | solution.py:265
  74.2 9.9 %collective-permute-done.5.outer = f32[4,8,8,512]{3,2,1,0:T(8,128)S(1)} collective-permute-done((f32[4,8,8,512]{3,2,1,0:T(8,128)S(1)}, f32[4,8,8,512]{3,2,1,0:T(8,128)S(1)}, u32[]{:S(2)}, u32[]{:S(2)}) %collective-permute-start.5) | collective-permute-done | bytes 524320 | tf_op jit(solution)/shard_map/ppermute | solution.py:274
  84.1 0.0 collective-permute-done.4.inner
  84.1 5.0 %shard_map.41.state = f32[4,8,8,512]{3,2,1,0:T(8,128)S(1)} custom-call(s32[3]{0:T(128)S(1)} %pad_add_fusion.place, f32[4,8,8,512]{3,2,1,0:T(8,128)S(1)} %shard_map.40.state, f32[4,8,8,512]{3,2,1,0:T(8,128)S(1)} %collective-permute-done.4.inner, f32[4,8,8,512]{3,2,1,0:T(8,128)S(1)} %collective-permute-done.5.outer, f32[4,7,8,8,512]{4,3,2,1,0:T(8,128)S(1)} %copy-done.3, ...), custom_call_target="tpu_custom_call" | custom-call | tf_op jit(solution)/shard_map/pallas_call | solution.py:343
  89.2 4.2 %collective-permute-start.7 = (f32[4,8,8,512]{3,2,1,0:T(8,128)S(1)}, f32[4,8,8,512]{3,2,1,0:T(8,128)S(1)}, u32[]{:S(2)}, u32[]{:S(2)}) collective-permute-start(f32[4,8,8,512]{3,2,1,0:T(8,128)S(1)} %shard_map.41.state), channel_id=1, source_target_pairs={{0,31},{1,2},{2,1},{3,4},{4,3},{5,6},{6,5},{7,8},{8,7},{9,10},{10,... | collective-permute-start | bytes 1572872 | tf_op jit(solution)/shard_map/ppermute | solution.py:274
  93.4 1.9 %collective-permute-start.6 = (f32[4,8,8,512]{3,2,1,0:T(8,128)S(1)}, f32[4,8,8,512]{3,2,1,0:T(8,128)S(1)}, u32[]{:S(2)}, u32[]{:S(2)}) collective-permute-start(f32[4,8,8,512]{3,2,1,0:T(8,128)S(1)} %shard_map.41.state), channel_id=1, source_target_pairs={{0,1},{1,0},{2,3},{3,2},{4,5},{5,4},{6,7},{7,6},{8,9},{9,8},{10,11... | collective-permute-start | bytes 1572872 | tf_op jit(solution)/shard_map/ppermute | solution.py:265
  95.3 10.4 %collective-permute-done.7.outer = f32[4,8,8,512]{3,2,1,0:T(8,128)S(1)} collective-permute-done((f32[4,8,8,512]{3,2,1,0:T(8,128)S(1)}, f32[4,8,8,512]{3,2,1,0:T(8,128)S(1)}, u32[]{:S(2)}, u32[]{:S(2)}) %collective-permute-start.7) | collective-permute-done | bytes 524320 | tf_op jit(solution)/shard_map/ppermute | solution.py:274
  105.7 0.0 collective-permute-done.6.inner
  105.7 0.0 copy-done
  105.7 5.0 %shard_map.42.state = f32[4,8,8,512]{3,2,1,0:T(8,128)S(1)} custom-call(s32[3]{0:T(128)S(1)} %pad_add_fusion.place, f32[4,8,8,512]{3,2,1,0:T(8,128)S(1)} %shard_map.41.state, f32[4,8,8,512]{3,2,1,0:T(8,128)S(1)} %collective-permute-done.6.inner, f32[4,8,8,512]{3,2,1,0:T(8,128)S(1)} %collective-permute-done.7.outer, f32[4,7,8,8,512]{4,3,2,1,0:T(8,128)S(1)} %copy-done.3, ...), custom_call_target="tpu_custom_call" | custom-call | tf_op jit(solution)/shard_map/pallas_call | solution.py:343
  110.7 3.8 %collective-permute-start.9 = (f32[4,8,8,512]{3,2,1,0:T(8,128)S(1)}, f32[4,8,8,512]{3,2,1,0:T(8,128)}, u32[]{:S(2)}, u32[]{:S(2)}) collective-permute-start(f32[4,8,8,512]{3,2,1,0:T(8,128)S(1)} %shard_map.42.state), channel_id=1, source_target_pairs={{0,31},{1,2},{2,1},{3,4},{4,3},{5,6},{6,5},{7,8},{8,7},{9,10},{10,... | collective-permute-start | bytes 1572872 | tf_op jit(solution)/shard_map/ppermute | solution.py:274
  114.5 1.9 %collective-permute-start.8 = (f32[4,8,8,512]{3,2,1,0:T(8,128)S(1)}, f32[4,8,8,512]{3,2,1,0:T(8,128)}, u32[]{:S(2)}, u32[]{:S(2)}) collective-permute-start(f32[4,8,8,512]{3,2,1,0:T(8,128)S(1)} %shard_map.42.state), channel_id=1, source_target_pairs={{0,1},{1,0},{2,3},{3,2},{4,5},{5,4},{6,7},{7,6},{8,9},{9,8},{10,11... | collective-permute-start | bytes 1572872 | tf_op jit(solution)/shard_map/ppermute | solution.py:265
  116.4 5.4 %collective-permute-start.10 = (f32[2,8,128]{2,1,0:T(8,128)S(1)}, f32[2,8,128]{2,1,0:T(8,128)S(1)}, u32[]{:S(2)}, u32[]{:S(2)}) collective-permute-start(f32[2,8,128]{2,1,0:T(8,128)S(1)} %get-tuple-element.12), channel_id=1, source_target_pairs={{32,0},{64,32},{96,64},{128,96},{160,128},{192,160},{224,192},{256... | collective-permute-start | bytes 24584 | tf_op jit(solution)/shard_map/ppermute | solution.py:323
  121.9 1.3 collective-permute-done.10.refs_0_
  123.2 2.7 %collective-permute-done.9.outer = f32[4,8,8,512]{3,2,1,0:T(8,128)} collective-permute-done((f32[4,8,8,512]{3,2,1,0:T(8,128)S(1)}, f32[4,8,8,512]{3,2,1,0:T(8,128)}, u32[]{:S(2)}, u32[]{:S(2)}) %collective-permute-start.9) | collective-permute-done | bytes 524320 | tf_op jit(solution)/shard_map/ppermute | solution.py:274
  126.0 0.0 collective-permute-done.8.inner
  126.0 1.8 copy-done.1
  127.8 2.0 %copy-done.4 = f32[4,7,8,8,512]{4,3,2,1,0:T(8,128)S(1)} copy-done((f32[4,7,8,8,512]{4,3,2,1,0:T(8,128)S(1)}, f32[4,7,8,8,512]{4,3,2,1,0:T(8,128)}, u32[]{:S(2)}) %copy-start.4) | copy-done | bytes 3670040
  129.8 1.2 copy-done.7
  131.0 5.4 %shard_map.43 = (f32[4,8,8,512]{3,2,1,0:T(8,128)S(1)}, f32[32,2,8,128]{3,2,1,0:T(8,128)S(1)}) custom-call(s32[3]{0:T(128)S(1)} %pad_add_fusion.place, f32[4,8,8,512]{3,2,1,0:T(8,128)S(1)} %shard_map.42.state, f32[4,8,8,512]{3,2,1,0:T(8,128)} %collective-permute-done.8.inner, f32[4,8,8,512]{3,2,1,0:T(8,128)} %collective-permute-done.9.outer, ...), custom_call_target="tpu_custom_call" | custom-call | tf_op jit(solution)/shard_map/pallas_call | solution.py:343
  136.5 16.5 %all_to_all.10.residuals = f32[32,2,8,128]{3,2,1,0:T(8,128)S(1)} all-to-all(f32[32,2,8,128]{3,2,1,0:T(8,128)S(1)} %get-tuple-element.13), channel_id=1, replica_groups=mesh['cuts'=16,'space'=32] {'space'}, dimensions={0} | all-to-all | bytes 524288 | tf_op jit(solution)/shard_map/all_to_all | solution.py:350
  153.0 11.0 %shard_map.44 = f32[16,2,8,128]{3,2,1,0:T(8,128)S(1)} custom-call(s32[3]{0:T(128)S(1)} %pad_add_fusion.place, f32[32,2,8,128]{3,2,1,0:T(8,128)S(1)} %all_to_all.10.residuals, f32[32,4,2,8,128]{4,3,2,1,0:T(8,128)S(1)} %copy-done.7), custom_call_target="tpu_custom_call" | custom-call | tf_op jit(solution)/shard_map/pallas_call | solution.py:351
  163.9 14.6 %all_to_all.11.shares = f32[16,2,8,128]{3,2,1,0:T(8,128)S(1)} all-to-all(f32[16,2,8,128]{3,2,1,0:T(8,128)S(1)} %shard_map.44), channel_id=1, replica_groups=mesh['cuts'=16,'space'=32] {'cuts'}, dimensions={0} | all-to-all | bytes 262144 | tf_op jit(solution)/shard_map/all_to_all | solution.py:361
  178.5 1.1 shard_map.45
  (7 shorter events, 0.0 us)
Async XLA Ops:
  6.5 116.7 %all-gather.4.cloned.1.call-start = ((), (), s32[]{:S(2)}) async-start(), calls=%async_computation.2 | async-start | bytes 1179648 | tf_op jit(solution)/shard_map/all_gather | solution.py:318
  6.5 10.8 %copy-start.11 = (f32[4,64,512]{2,1,0:T(8,128)S(1)}, f32[4,64,512]{2,1,0:T(8,128)}, u32[]{:S(2)}) copy-start(f32[4,64,512]{2,1,0:T(8,128)} %diffusivity.1) | copy-start | bytes 1572868
  9.9 7.5 %copy-start.6 = (f32[1,4,64,512]{3,2,1,0:T(8,128)S(1)}, f32[1,4,64,512]{3,2,1,0:T(8,128)}, u32[]{:S(2)}) copy-start(f32[1,4,64,512]{3,2,1,0:T(8,128)} %param.3) | copy-start | bytes 1572868
  9.9 47.5 %collective-permute-start.3 = (f32[3,3,64,512]{3,2,1,0:T(8,128)}, f32[3,3,64,512]{3,2,1,0:T(8,128)}, u32[]{:S(2)}, u32[]{:S(2)}) collective-permute-start(f32[3,3,64,512]{3,2,1,0:T(8,128)} %get-tuple-element.15), channel_id=1, source_target_pairs={{0,287},{1,258},{2,257},{3,260},{4,259},{5,262},{6,261},{7,264},{8... | collective-permute-start | bytes 3538952 | tf_op jit(solution)/shard_map/ppermute | solution.py:283
  12.9 40.4 %collective-permute-start.2 = (f32[3,3,64,512]{3,2,1,0:T(8,128)}, f32[3,3,64,512]{3,2,1,0:T(8,128)S(1)}, u32[]{:S(2)}, u32[]{:S(2)}) collective-permute-start(f32[3,3,64,512]{3,2,1,0:T(8,128)} %get-tuple-element.16), channel_id=1, source_target_pairs={{0,1},{1,0},{2,3},{3,2},{4,5},{5,4},{6,7},{7,6},{8,9},{9,8},{10,11... | collective-permute-start | bytes 3538952 | tf_op jit(solution)/shard_map/ppermute | solution.py:265
  17.4 13.2 %copy-start.5 = (f32[3,4,64,512]{3,2,1,0:T(8,128)S(1)}, f32[3,4,64,512]{3,2,1,0:T(8,128)}, u32[]{:S(2)}) copy-start(f32[3,4,64,512]{3,2,1,0:T(8,128)} %velocity.1) | copy-start | bytes 4718596
  18.9 33.5 %collective-permute-start = (f32[7,64,512]{2,1,0:T(8,128)}, f32[7,64,512]{2,1,0:T(8,128)S(1)}, u32[]{:S(2)}, u32[]{:S(2)}) collective-permute-start(f32[7,64,512]{2,1,0:T(8,128)} %get-tuple-element.18), channel_id=1, source_target_pairs={{0,1},{1,0},{2,3},{3,2},{4,5},{5,4},{6,7},{7,6},{8,9},{9,8},{10,11... | collective-permute-start | bytes 2752520 | tf_op jit(solution)/shard_map/ppermute | solution.py:265
  20.8 36.6 %collective-permute-start.1 = (f32[7,64,512]{2,1,0:T(8,128)}, f32[7,64,512]{2,1,0:T(8,128)}, u32[]{:S(2)}, u32[]{:S(2)}) collective-permute-start(f32[7,64,512]{2,1,0:T(8,128)} %get-tuple-element.17), channel_id=1, source_target_pairs={{0,31},{1,2},{2,1},{3,4},{4,3},{5,6},{6,5},{7,8},{8,7},{9,10},{10,... | collective-permute-start | bytes 2752520 | tf_op jit(solution)/shard_map/ppermute | solution.py:274
  32.0 1.8 copy-start.2
  52.4 0.9 copy-start.8
  53.3 1.0 copy-start.13
  54.4 1.2 copy-start.9
  55.5 1.3 copy-start.14
  57.4 2.3 %copy-start.10 = (f32[7,64,512]{2,1,0:T(8,128)S(1)}, f32[7,64,512]{2,1,0:T(8,128)}, u32[]{:S(2)}) copy-start(f32[7,64,512]{2,1,0:T(8,128)} %copy-done.8) | copy-start | bytes 2752516
  57.4 2.3 %copy-start.12 = (f32[16,2,8,128]{3,2,1,0:T(8,128)S(1)}, f32[16,2,8,128]{3,2,1,0:T(8,128)}, u32[]{:S(2)}) copy-start(f32[16,2,8,128]{3,2,1,0:T(8,128)} %all-gather) | copy-start | bytes 393220
  57.4 3.0 %copy-start.3 = (f32[4,7,8,8,512]{4,3,2,1,0:T(8,128)S(1)}, f32[4,7,8,8,512]{4,3,2,1,0:T(8,128)}, u32[]{:S(2)}) copy-start(f32[4,7,8,8,512]{4,3,2,1,0:T(8,128)} %copy-done.2) | copy-start | bytes 11010052
  59.7 46.0 %copy-start = (f32[3,7,8,8,512]{4,3,2,1,0:T(8,128)}, f32[3,7,8,8,512]{4,3,2,1,0:T(8,128)S(1)}, u32[]{:S(2)}) copy-start(f32[3,7,8,8,512]{4,3,2,1,0:T(8,128)S(1)} %shard_map.39.own_outer) | copy-start | bytes 8257540
  66.6 17.5 %collective-permute-start.5 = (f32[4,8,8,512]{3,2,1,0:T(8,128)S(1)}, f32[4,8,8,512]{3,2,1,0:T(8,128)S(1)}, u32[]{:S(2)}, u32[]{:S(2)}) collective-permute-start(f32[4,8,8,512]{3,2,1,0:T(8,128)S(1)} %shard_map.40.state), channel_id=1, source_target_pairs={{0,31},{1,2},{2,1},{3,4},{4,3},{5,6},{6,5},{7,8},{8,7},{9,10},{10,... | collective-permute-start | bytes 1572872 | tf_op jit(solution)/shard_map/ppermute | solution.py:274
  72.3 11.8 %collective-permute-start.4 = (f32[4,8,8,512]{3,2,1,0:T(8,128)S(1)}, f32[4,8,8,512]{3,2,1,0:T(8,128)S(1)}, u32[]{:S(2)}, u32[]{:S(2)}) collective-permute-start(f32[4,8,8,512]{3,2,1,0:T(8,128)S(1)} %shard_map.40.state), channel_id=1, source_target_pairs={{0,1},{1,0},{2,3},{3,2},{4,5},{5,4},{6,7},{7,6},{8,9},{9,8},{10,11... | collective-permute-start | bytes 1572872 | tf_op jit(solution)/shard_map/ppermute | solution.py:265
  89.2 16.5 %collective-permute-start.7 = (f32[4,8,8,512]{3,2,1,0:T(8,128)S(1)}, f32[4,8,8,512]{3,2,1,0:T(8,128)S(1)}, u32[]{:S(2)}, u32[]{:S(2)}) collective-permute-start(f32[4,8,8,512]{3,2,1,0:T(8,128)S(1)} %shard_map.41.state), channel_id=1, source_target_pairs={{0,31},{1,2},{2,1},{3,4},{4,3},{5,6},{6,5},{7,8},{8,7},{9,10},{10,... | collective-permute-start | bytes 1572872 | tf_op jit(solution)/shard_map/ppermute | solution.py:274
  93.4 12.3 %collective-permute-start.6 = (f32[4,8,8,512]{3,2,1,0:T(8,128)S(1)}, f32[4,8,8,512]{3,2,1,0:T(8,128)S(1)}, u32[]{:S(2)}, u32[]{:S(2)}) collective-permute-start(f32[4,8,8,512]{3,2,1,0:T(8,128)S(1)} %shard_map.41.state), channel_id=1, source_target_pairs={{0,1},{1,0},{2,3},{3,2},{4,5},{5,4},{6,7},{7,6},{8,9},{9,8},{10,11... | collective-permute-start | bytes 1572872 | tf_op jit(solution)/shard_map/ppermute | solution.py:265
  110.7 15.3 %collective-permute-start.9 = (f32[4,8,8,512]{3,2,1,0:T(8,128)S(1)}, f32[4,8,8,512]{3,2,1,0:T(8,128)}, u32[]{:S(2)}, u32[]{:S(2)}) collective-permute-start(f32[4,8,8,512]{3,2,1,0:T(8,128)S(1)} %shard_map.42.state), channel_id=1, source_target_pairs={{0,31},{1,2},{2,1},{3,4},{4,3},{5,6},{6,5},{7,8},{8,7},{9,10},{10,... | collective-permute-start | bytes 1572872 | tf_op jit(solution)/shard_map/ppermute | solution.py:274
  114.5 11.5 %collective-permute-start.8 = (f32[4,8,8,512]{3,2,1,0:T(8,128)S(1)}, f32[4,8,8,512]{3,2,1,0:T(8,128)}, u32[]{:S(2)}, u32[]{:S(2)}) collective-permute-start(f32[4,8,8,512]{3,2,1,0:T(8,128)S(1)} %shard_map.42.state), channel_id=1, source_target_pairs={{0,1},{1,0},{2,3},{3,2},{4,5},{5,4},{6,7},{7,6},{8,9},{9,8},{10,11... | collective-permute-start | bytes 1572872 | tf_op jit(solution)/shard_map/ppermute | solution.py:265
  116.4 6.8 %collective-permute-start.10 = (f32[2,8,128]{2,1,0:T(8,128)S(1)}, f32[2,8,128]{2,1,0:T(8,128)S(1)}, u32[]{:S(2)}, u32[]{:S(2)}) collective-permute-start(f32[2,8,128]{2,1,0:T(8,128)S(1)} %get-tuple-element.12), channel_id=1, source_target_pairs={{32,0},{64,32},{96,64},{128,96},{160,128},{192,160},{224,192},{256... | collective-permute-start | bytes 24584 | tf_op jit(solution)/shard_map/ppermute | solution.py:323
  126.0 1.8 copy-start.1
  127.8 2.0 %copy-start.4 = (f32[4,7,8,8,512]{4,3,2,1,0:T(8,128)S(1)}, f32[4,7,8,8,512]{4,3,2,1,0:T(8,128)}, u32[]{:S(2)}) copy-start(f32[4,7,8,8,512]{4,3,2,1,0:T(8,128)} %copy-done.2) | copy-start | bytes 11010052
  129.8 1.2 copy-start.7
Sparse Core Ops, SparseCore 0:
  52.4 40.4 all-gather.3

commit v5 on v4

--- a/solution.py
+++ b/solution.py
@@ -21,12 +21,12 @@
 MIB = 1024 * 1024
 
 
-def call(body, outs, ins, scratch=(), limit=24):
+def call(body, outs, ins, scratch=(), limit=24, out=VMEM):
     return pl.pallas_call(
         body,
         out_shape=[jax.ShapeDtypeStruct(s, F32) for s in outs],
         in_specs=ins,
-        out_specs=[VMEM] * len(outs),
+        out_specs=[out] * len(outs),
         scratch_shapes=list(scratch),
         compiler_params=pltpu.CompilerParams(vmem_limit_bytes=limit * MIB),
     )
@@ -80,6 +80,19 @@
         total = total + weight
     weights[0] = 1.0 - total
     return weights
+
+
+def cut_kernel(place, velocity, diffusivity, starts, fields, mixed, ready, *, outer):
+    begin = place[2] if outer else 1 - place[2]
+    copies = [
+        pltpu.make_async_copy(velocity.at[:, pl.ds(begin, REACH)], fields, ready.at[0]),
+        pltpu.make_async_copy(diffusivity.at[pl.ds(begin, REACH)], mixed.at[pl.ds(LAYERS, REACH)], ready.at[1]),
+        pltpu.make_async_copy(starts.at[0], mixed.at[pl.ds(0, LAYERS)], ready.at[2]),
+    ]
+    for copy in copies:
+        copy.start()
+    for copy in copies:
+        copy.wait()
 
 
 def own_kernel(velocity, diffusivity, starts, weights, coarse_fields, coarse_old, buffer):
@@ -124,29 +137,21 @@
 
 
 def fine_layer(source, weights, target, x, wx, tx):
-    tiles = [source[x, j] for j in range(8)]
+    first, last = source[x, 0], source[x, 7]
+    behind, now = pltpu.roll(last, 1, 0), first
     for j in range(8):
-        behind_y = tiles[j - 1] if j > 0 else pltpu.roll(tiles[7], 1, 0)
-        ahead_y = tiles[j + 1] if j < 7 else pltpu.roll(tiles[0], 7, 0)
-        behind_z = pltpu.roll(tiles[j], 1, 1)
-        ahead_z = pltpu.roll(tiles[j], 511, 1)
+        ahead = pltpu.roll(first, 7, 0) if j == 7 else last if j == 6 else source[x, j + 1]
         target[tx, j] = (
-            (weights[wx, 0, j] * tiles[j] + weights[wx, 1, j] * source[x - 1, j])
-            + (weights[wx, 2, j] * source[x + 1, j] + weights[wx, 3, j] * behind_y)
-            + (weights[wx, 4, j] * ahead_y + weights[wx, 5, j] * behind_z)
-            + weights[wx, 6, j] * ahead_z
+            (weights[wx, 0, j] * now + weights[wx, 1, j] * source[x - 1, j])
+            + (weights[wx, 2, j] * source[x + 1, j] + weights[wx, 3, j] * behind)
+            + (weights[wx, 4, j] * ahead + weights[wx, 5, j] * pltpu.roll(now, 1, 1))
+            + weights[wx, 6, j] * pltpu.roll(now, 511, 1)
         )
-
-
-def round_kernel(raw, final, place, state, inner, outer, own, own_inner, own_outer, *refs):
-    if final:
-        later, fields, out, residual, one, two, buffer = refs
-    else:
-        out, one, two, buffer = refs[-4:]
-    core = place[2]
-
-    def enter(x, carry):
-        blocks = ((state, LAYERS), (outer, 2 * LAYERS * core), (inner, 2 * LAYERS * (1 - core)))
+        behind, now = now, ahead
+
+
+def enter(one, blocks, raw, buffer):
+    def layer(x, carry):
         for i, (ref, begin) in enumerate(blocks):
             if raw:
                 spread(ref[x], buffer.at[i])
@@ -154,27 +159,53 @@
                 one[begin + x, j] = spread_tile(buffer.at[i], j) if raw else ref[x, j]
         return carry
 
-    lax.fori_loop(0, LAYERS, enter, 0)
+    lax.fori_loop(0, LAYERS, layer, 0)
+
+
+def sweep(source, goal, begin, count, weights, first, shift=0):
+    def body(i, carry):
+        fine_layer(source, weights, goal, begin + i, first + i, begin + i - shift)
+        return carry
+
+    lax.fori_loop(0, count, body, 0)
+
+
+def inner_kernel(raw, place, state, inner, own, own_inner, passed, one, two, buffer):
+    core = place[2]
+    enter(one, ((state, LAYERS), (inner, 2 * LAYERS * (1 - core))), raw, buffer)
+    source, target = one, two
+    for step in range(1, LAYERS):
+        count = LAYERS - step
+        sweep(source, target, LAYERS + (1 - core) * step, count, own, (1 - core) * step)
+        above, below = 2 * LAYERS, step
+        sweep(source, target, above - core * (above - below), count, own_inner, core * (step - 1))
+        for i in range(2):
+            on_first, on_second = LAYERS + step + i, 2 * LAYERS - 1 - step - i
+            passed[step - 1, i] = target[on_first - core * (on_first - on_second)]
+        source, target = target, source
+
+
+def outer_kernel(raw, final, place, state, outer, own, own_outer, passed, *refs):
+    if final:
+        later, *refs, out, residual, one, two, buffer = refs
+    else:
+        out, one, two, buffer = refs[-4:]
+    core = place[2]
+    enter(one, ((state, LAYERS), (outer, 2 * LAYERS * core)), raw, buffer)
     source, target = one, two
     for step in range(1, LAYERS + 1):
         ends = step == LAYERS
         goal = out if ends else target
         shift = LAYERS if ends else 0
-        depth = LAYERS - step
-
-        def sweep(begin, count, weights, first, source=source, goal=goal, shift=shift):
-            def body(i, carry):
-                fine_layer(source, weights, goal, begin + i, first + i, begin + i - shift)
-                return carry
-
-            lax.fori_loop(0, count, body, 0)
-
-        sweep(LAYERS, LAYERS, own, 0)
-        if depth > 0:
-            below, above = LAYERS - depth, 2 * LAYERS
-            skip = REACH - depth
-            sweep(below + core * (above - below), depth, own_outer, (1 - core) * skip)
-            sweep(above - core * (above - below), depth, own_inner, core * skip)
+        count = LAYERS - step
+        if count:
+            below, above = step, 2 * LAYERS
+            sweep(source, goal, below + core * (above - below), count, own_outer, (1 - core) * (step - 1))
+        sweep(source, goal, LAYERS + core * count, step, own, core * count, shift)
+        if not ends:
+            for i in range(2):
+                on_first, on_second = LAYERS + step + i, 2 * LAYERS - 1 - step - i
+                target[on_first - core * (on_first - on_second)] = passed[step - 1, i]
         source, target = target, source
     if final:
         sums = half_sums(lambda j: (out[0, j] + out[1, j]) + (out[2, j] + out[3, j]))
@@ -213,15 +244,14 @@
     layer_index = place[1]
     shares[...] = jnp.zeros(shares.shape, F32)
 
-    def prepare(x, carry):
+    bits = count.bit_length() - 1
+    for i in range(count):
+        x = layer_index ^ sum(((i >> b) & 1) << (bits - 1 - b) for b in range(bits))
         for h in range(2):
-            parts = [fields[x, f, h] for f in range(4)]
-            for i, weight in enumerate(weigh(parts[:3], parts[3], STEP * RATIO, 1.0 * RATIO)):
-                weights[x, i, h] = weight
-            one[x, h] = residuals[x, h]
-        return carry
-
-    lax.fori_loop(0, count, prepare, 0)
+            parts = [fields[i, f, h] for f in range(4)]
+            for k, weight in enumerate(weigh(parts[:3], parts[3], STEP * RATIO, 1.0 * RATIO)):
+                weights[x, k, h] = weight
+            one[i, h] = residuals[i, h]
 
     def reader(ref):
         return lambda x: [ref[x, h] for h in range(2)]
@@ -283,69 +313,79 @@
     return lax.ppermute(block, ("cuts", "space"), route)
 
 
+def double(block, bit):
+    slices, count = lax.axis_size("cuts"), lax.axis_size("space")
+    if bit == 2:
+        axes = ("cuts", "space")
+        route = [
+            (n * count + p, (n + slices // 2) % slices * count + (p ^ bit)) for n in range(slices) for p in range(count)
+        ]
+    else:
+        axes = "space"
+        route = [(p, p ^ bit) for p in range(count)]
+    return jnp.concatenate([block, lax.ppermute(block, axes, route)], axis=0)
+
+
 def shards(starts, velocity, diffusivity):
     count = lax.axis_size("space")
     slices = lax.axis_size("cuts")
     block = (LAYERS, *TILE)
     row = lax.axis_index("space")
-    core = row & 1
+    place = jnp.stack([lax.axis_index("cuts"), row, row & 1]).astype(jnp.int32)
     columns = pltpu.VMEM((5, 4, 64, 128), F32)
-    place = jnp.stack([lax.axis_index("cuts"), row, core]).astype(jnp.int32)
-
-    def halo(begin):
-        cut = functools.partial(lax.dynamic_slice_in_dim, start_index=begin, slice_size=REACH)
-        mixed = jnp.concatenate([starts[0], cut(diffusivity, axis=0)], axis=0)
-        return cut(velocity, axis=1), mixed
-
-    velocity_outer, mixed_outer = halo(core)
-    velocity_inner, mixed_inner = halo(1 - core)
-    velocity_inner = swap_inner(velocity_inner)
+
+    def cut(outer):
+        return call(
+            functools.partial(cut_kernel, outer=outer),
+            [(3, REACH, 64, 512), (LAYERS + REACH, 64, 512)],
+            [SMEM, ANY, ANY, ANY],
+            [pltpu.SemaphoreType.DMA((3,))],
+            limit=60,
+            out=ANY,
+        )(place, velocity, diffusivity, starts)
+
+    fields_outer, mixed_outer = cut(True)
+    fields_inner, mixed_inner = cut(False)
     mixed_inner = swap_inner(mixed_inner)
-    velocity_outer = swap_outer_fields(velocity_outer)
     mixed_outer = swap_outer(mixed_outer)
+    fields_inner = swap_inner(fields_inner)
+    fields_outer = swap_outer_fields(fields_outer)
     own_weights, coarse_fields, coarse_old = call(
         own_kernel,
         [(LAYERS, 7, *TILE), (4, *COARSE), COARSE],
         [VMEM] * 3,
         [columns],
     )(velocity, diffusivity, starts[0])
-    group = 4
-    some_fields = lax.all_gather(
-        coarse_fields,
-        "space",
-        axis_index_groups=[[g * group + i for i in range(group)] for g in range(count // group)],
-    )
-    all_fields = lax.all_gather(
-        some_fields,
-        "space",
-        axis_index_groups=[[g * group + i for g in range(count // group)] for i in range(group)],
-    ).reshape(count, 4, *COARSE)
     coarse_later = lax.ppermute(coarse_old, "cuts", [((n + 1) % slices, n) for n in range(slices)])
-    sides = [
+    gathered = [coarse_fields[None]]
+    for bit in (16, 8, 4, 2, 1):
+        gathered.append(double(gathered[-1], bit))
+    inner_weights, outer_weights = [
         call(side_kernel, [(REACH, 7, *TILE)], [VMEM] * 2, [columns])(*halos)[0]
-        for halos in ((velocity_inner, mixed_inner), (velocity_outer, mixed_outer))
+        for halos in ((fields_inner, mixed_inner), (fields_outer, mixed_outer))
     ]
-    state, outer, inner = starts[0], mixed_outer, mixed_inner
+    state, inner, outer = starts[0], mixed_inner, mixed_outer
+    scratch = [pltpu.VMEM((3 * LAYERS, *TILE), F32)] * 2 + [columns]
     for index in range(ROUNDS):
-        final = index == ROUNDS - 1
+        raw, final = index == 0, index == ROUNDS - 1
         if index > 0:
             inner, outer = swap_inner(state), swap_outer(state)
-        operands = [place, state, inner, outer, own_weights, *sides]
-        specs = [SMEM] + [VMEM] * 6
+        passed = call(
+            functools.partial(inner_kernel, raw),
+            [(LAYERS - 1, 2, *TILE)],
+            [SMEM] + [VMEM] * 4,
+            scratch,
+        )(place, state, inner, own_weights, inner_weights)[0]
+        operands = [place, state, outer, own_weights, outer_weights, passed]
+        specs = [SMEM] + [VMEM] * 5
         outs = [block]
         if final:
-            operands += [coarse_later, all_fields]
-            specs += [VMEM, ANY]
+            operands.append(coarse_later)
+            specs.append(VMEM)
             outs.append((count, *COARSE))
-        elif index == 0:
-            operands.append(some_fields)
-            specs.append(ANY)
-        outs = call(
-            functools.partial(round_kernel, index == 0, final),
-            outs,
-            specs,
-            [pltpu.VMEM((3 * LAYERS, *TILE), F32)] * 2 + [columns],
-        )(*operands)
+        operands.append(gathered[index + 2])
+        specs.append(ANY)
+        outs = call(functools.partial(outer_kernel, raw, final), outs, specs, scratch)(*operands)
         state = outs[0]
     residuals = lax.all_to_all(outs[1], "space", 0, 0)
     shares = call(
@@ -357,7 +397,7 @@
             pltpu.VMEM((count, *COARSE), F32),
             pltpu.VMEM((count, *COARSE), F32),
         ],
-    )(place, residuals, all_fields)[0]
+    )(place, residuals, gathered[-1])[0]
     shares = lax.all_to_all(shares, "cuts", 0, 0)
     return call(finish_kernel, [(1, LAYERS, 64, 512)], [VMEM, VMEM], [columns])(shares, state)[0]
 

time: 187 us -> 299 us (1.60)
  Pallas kernels: 37.9 us -> 169 us
  starting transfers between devices: 44 us -> 66.6 us
  blocking collectives: 49.7 us -> 33.3 us
  local copies, waits for them, and re-layouts: 15.4 us -> 0.16 us
  between operations: 13.7 us -> 0.44 us
  waiting for transfers between devices: 24.4 us -> 28.1 us
    pallas_call x4 -> x10, Pallas kernels: 21.7 us -> 154 us  [the longest x2 131 us: cut(): call(functools.partial(cut_kernel, outer=outer), [(3, REACH, 64, 512), (L...]
    all_gather x1 -> x0, blocking collectives: 18.5 us -> none  [shards(): lax.all_gather(coarse_fields, 'space', axis_index_groups=[[g * group + i...]
    ppermute x0 -> x5, starting transfers between devices: none -> 17.7 us  [double(): return jnp.concatenate([block, lax.ppermute(block, axes, route)], axis=0)]
    ppermute x0 -> x5, waiting for transfers between devices: none -> 17.6 us  [double(): return jnp.concatenate([block, lax.ppermute(block, axes, route)], axis=0)]
    ppermute x4, waiting for transfers between devices: 23 us -> 10.5 us  [swap_outer(): lax.ppermute(block, 'space', [(p, outer_partner(p, count)) for p in range...]
    unnamed x30 -> x13, local copies, waits for them, and re-layouts: 11.9 us -> 0.12 us
    ppermute x5, starting transfers between devices: 12.1 us -> 19.9 us  [swap_inner(): return lax.ppermute(block, 'space', [(p, p ^ 1) for p in range(count)])]
    ppermute x4, starting transfers between devices: 23.5 us -> 18.8 us  [swap_outer(): lax.ppermute(block, 'space', [(p, outer_partner(p, count)) for p in range...]
  transfers between devices with their start and end apart: 12 -> 16, of which waited for: 4 -> 5; matrix products, arithmetic and copies ran while one was open for 1% -> 0% of each run, Pallas kernels for 11% -> 28%
where the time goes in v5:
time: 299 us; the launch traced here: 298 us
  Pallas kernels  169 us (57%)
  starting transfers between devices  66.6 us (22%)
  blocking collectives  33.3 us (11%)
  waiting for transfers between devices  28.1 us (9%)
    pallas_call x2, Pallas kernels, cut(): call(functools.partial(cut_kernel, outer=outer), [(3, REACH, 64, 512), (L...  131 us
    ppermute x5, starting transfers between devices, swap_inner(): return lax.ppermute(block, 'space', [(p, p ^ 1) for p in range(count)])  19.9 us
    all_to_all x1, blocking collectives, shards(): residuals = lax.all_to_all(outs[1], 'space', 0, 0)  18.9 us
    ppermute x4, starting transfers between devices, swap_outer(): lax.ppermute(block, 'space', [(p, outer_partner(p, count)) for p in range...  18.8 us
    ppermute x5, starting transfers between devices, double(): return jnp.concatenate([block, lax.ppermute(block, axes, route)], axis=0)  17.7 us
    ppermute x5, waiting for transfers between devices, double(): return jnp.concatenate([block, lax.ppermute(block, axes, route)], axis=0)  17.6 us
    all_to_all x1, blocking collectives, shards(): shares = lax.all_to_all(shares, 'cuts', 0, 0)  14.4 us
    pallas_call x4, Pallas kernels, shards(): call(functools.partial(outer_kernel, raw, final), outs, specs, scratch)  13.4 us
  transfers between devices with their start and end apart: 16, of which 5 were waited for; matrix products, arithmetic and copies ran while one was open for 0% of the time, Pallas kernels for 28%

profile of v5, /device:TPU:2, one launch (start us, length us, event | category | flops | bytes accessed | tf_op | source)
XLA Modules:
  0.0 298.1 jit_solution(12744210540689025303)
XLA Ops:
  0.0 0.6 pad_add_fusion.place
  0.6 65.3 %shard_map.40 = (f32[3,3,64,512]{3,2,1,0:T(8,128)}, f32[7,64,512]{2,1,0:T(8,128)}) custom-call(s32[3]{0:T(128)} %pad_add_fusion.place, f32[3,4,64,512]{3,2,1,0:T(8,128)} %velocity.5, f32[4,64,512]{2,1,0:T(8,128)} %diffusivity.5, f32[1,4,64,512]{3,2,1,0:T(8,128)} %starts.3), custom_call_target="tpu_custom_call" | custom-call | tf_op jit(solution)/shard_map/pallas_call | solution.py:338
  65.9 0.0 copy-start
  65.9 0.0 copy-start.1
  66.0 0.0 copy-start.2
  66.0 2.1 collective-permute-start.3
  68.0 65.3 %shard_map.37 = (f32[3,3,64,512]{3,2,1,0:T(8,128)}, f32[7,64,512]{2,1,0:T(8,128)}) custom-call(s32[3]{0:T(128)} %pad_add_fusion.place, f32[3,4,64,512]{3,2,1,0:T(8,128)} %velocity.5, f32[4,64,512]{2,1,0:T(8,128)} %diffusivity.5, f32[1,4,64,512]{3,2,1,0:T(8,128)} %starts.3), custom_call_target="tpu_custom_call" | custom-call | tf_op jit(solution)/shard_map/pallas_call | solution.py:338
  133.4 3.5 %collective-permute-start.1 = (f32[3,3,64,512]{3,2,1,0:T(8,128)}, f32[3,3,64,512]{3,2,1,0:T(8,128)S(1)}, u32[]{:S(2)}, u32[]{:S(2)}) collective-permute-start(f32[3,3,64,512]{3,2,1,0:T(8,128)} %get-tuple-element.16), channel_id=1, source_target_pairs={{0,287},{1,258},{2,257},{3,260},{4,259},{5,262},{6,261},{7,264},{8... | collective-permute-start | bytes 3538952 | tf_op jit(solution)/shard_map/ppermute | solution.py:313
  136.9 3.7 %collective-permute-start.2 = (f32[7,64,512]{2,1,0:T(8,128)}, f32[7,64,512]{2,1,0:T(8,128)S(1)}, u32[]{:S(2)}, u32[]{:S(2)}) collective-permute-start(f32[7,64,512]{2,1,0:T(8,128)} %get-tuple-element.17), channel_id=1, source_target_pairs={{0,1},{1,0},{2,3},{3,2},{4,5},{5,4},{6,7},{7,6},{8,9},{9,8},{10,11... | collective-permute-start | bytes 2752520 | tf_op jit(solution)/shard_map/ppermute | solution.py:295
  140.6 10.5 %collective-permute-start = (f32[7,64,512]{2,1,0:T(8,128)}, f32[7,64,512]{2,1,0:T(8,128)S(1)}, u32[]{:S(2)}, u32[]{:S(2)}) collective-permute-start(f32[7,64,512]{2,1,0:T(8,128)} %get-tuple-element.14), channel_id=1, source_target_pairs={{0,31},{1,2},{2,1},{3,4},{4,3},{5,6},{6,5},{7,8},{8,7},{9,10},{10,... | collective-permute-start | bytes 2752520 | tf_op jit(solution)/shard_map/ppermute | solution.py:304
  151.1 0.0 copy-done
  151.1 0.0 copy-done.1
  151.1 0.0 copy-done.2
  151.1 1.3 shard_map.38
  152.4 2.0 collective-permute-start.4
  154.4 8.5 %collective-permute-done.4 = f32[1,4,2,8,128]{4,3,2,1,0:T(8,128)S(1)} collective-permute-done((f32[1,4,2,8,128]{4,3,2,1,0:T(8,128)S(1)}, f32[1,4,2,8,128]{4,3,2,1,0:T(8,128)S(1)}, u32[]{:S(2)}, u32[]{:S(2)}) %collective-permute-start.4) | collective-permute-done | bytes 32800 | tf_op jit(solution)/shard_map/ppermute | solution.py:326
  162.9 1.9 collective-permute-start.5
  164.8 5.1 %collective-permute-done.5 = f32[2,4,2,8,128]{4,3,2,1,0:T(8,128)S(1)} collective-permute-done((f32[2,4,2,8,128]{4,3,2,1,0:T(8,128)S(1)}, f32[2,4,2,8,128]{4,3,2,1,0:T(8,128)S(1)}, u32[]{:S(2)}, u32[]{:S(2)}) %collective-permute-start.5) | collective-permute-done | bytes 65568 | tf_op jit(solution)/shard_map/ppermute | solution.py:326
  170.0 0.0 copy-start.3
  170.0 0.0 collective-permute-done.2.mixed.inner
  170.0 0.0 collective-permute-done.3.velocity
  170.0 0.6 shard_map.41.own_inner
  170.6 0.0 copy-done.3
  170.6 2.8 shard_map.42.passed
  173.4 0.0 collective-permute-done.mixed.outer
  173.4 0.0 collective-permute-done.1.velocity
  173.4 0.6 shard_map.39.own_outer
  174.0 3.5 %shard_map.43.state = f32[4,8,8,512]{3,2,1,0:T(8,128)S(1)} custom-call(s32[3]{0:T(128)S(1)} %copy-done.3, f32[4,64,512]{2,1,0:T(8,128)S(1)} %bitcast.9, f32[7,64,512]{2,1,0:T(8,128)S(1)} %collective-permute-done.mixed.outer, f32[4,7,8,8,512]{4,3,2,1,0:T(8,128)S(1)} %get-tuple-element.15.own, f32[3,7,8,8,512]{4,3,2,1,0:T(8,128)S(1)} %shard_map.39.own_outer, ...), custom_call_target="tpu_custom_call" | custom-call | tf_op jit(solution)/shard_map/pallas_call | solution.py:388
  177.4 10.3 %collective-permute-start.7 = (f32[4,8,8,512]{3,2,1,0:T(8,128)S(1)}, f32[4,8,8,512]{3,2,1,0:T(8,128)S(1)}, u32[]{:S(2)}, u32[]{:S(2)}) collective-permute-start(f32[4,8,8,512]{3,2,1,0:T(8,128)S(1)} %shard_map.43.state), channel_id=1, source_target_pairs={{0,1},{1,0},{2,3},{3,2},{4,5},{5,4},{6,7},{7,6},{8,9},{9,8},{10,11... | collective-permute-start | bytes 1572872 | tf_op jit(solution)/shard_map/ppermute | solution.py:295
  187.7 1.9 collective-permute-start.6
  189.7 5.9 %collective-permute-start.8 = (f32[4,4,2,8,128]{4,3,2,1,0:T(8,128)S(1)}, f32[4,4,2,8,128]{4,3,2,1,0:T(8,128)S(1)}, u32[]{:S(2)}, u32[]{:S(2)}) collective-permute-start(f32[4,4,2,8,128]{4,3,2,1,0:T(8,128)S(1)} %pad_maximum_fusion.1.refs_0_), channel_id=1, source_target_pairs={{0,4},{1,5},{2,6},{3,7},{4,0},{5,1},{6,2},{7,3},{8,12},{9,13},{10,... | collective-permute-start | bytes 393224 | tf_op jit(solution)/shard_map/ppermute | solution.py:326
  195.6 3.9 %collective-permute-done.8 = f32[4,4,2,8,128]{4,3,2,1,0:T(8,128)S(1)} collective-permute-done((f32[4,4,2,8,128]{4,3,2,1,0:T(8,128)S(1)}, f32[4,4,2,8,128]{4,3,2,1,0:T(8,128)S(1)}, u32[]{:S(2)}, u32[]{:S(2)}) %collective-permute-start.8) | collective-permute-done | bytes 131104 | tf_op jit(solution)/shard_map/ppermute | solution.py:326
  199.5 4.8 %collective-permute-start.11 = (f32[8,4,2,8,128]{4,3,2,1,0:T(8,128)S(1)}, f32[8,4,2,8,128]{4,3,2,1,0:T(8,128)S(1)}, u32[]{:S(2)}, u32[]{:S(2)}) collective-permute-start(f32[8,4,2,8,128]{4,3,2,1,0:T(8,128)S(1)} %pad_maximum_fusion.refs_0_), channel_id=1, source_target_pairs={{0,258},{1,259},{2,256},{3,257},{4,262},{5,263},{6,260},{7,261},{8... | collective-permute-start | bytes 786440 | tf_op jit(solution)/shard_map/ppermute | solution.py:326
  204.3 0.0 collective-permute-done.7.inner
  204.3 2.5 shard_map.44.passed
  206.8 0.0 collective-permute-done.6.outer
  206.9 3.3 %shard_map.45.state = f32[4,8,8,512]{3,2,1,0:T(8,128)S(1)} custom-call(s32[3]{0:T(128)S(1)} %copy-done.3, f32[4,8,8,512]{3,2,1,0:T(8,128)S(1)} %shard_map.43.state, f32[4,8,8,512]{3,2,1,0:T(8,128)S(1)} %collective-permute-done.6.outer, f32[4,7,8,8,512]{4,3,2,1,0:T(8,128)S(1)} %get-tuple-element.15.own, f32[3,7,8,8,512]{4,3,2,1,0:T(8,128)S(1)} %shard_map.39.own_outer, ...), custom_call_target="tpu_custom_call" | custom-call | tf_op jit(solution)/shard_map/pallas_call | solution.py:388
  210.1 1.9 collective-permute-start.10
  212.0 3.2 %collective-permute-start.9 = (f32[4,8,8,512]{3,2,1,0:T(8,128)S(1)}, f32[4,8,8,512]{3,2,1,0:T(8,128)S(1)}, u32[]{:S(2)}, u32[]{:S(2)}) collective-permute-start(f32[4,8,8,512]{3,2,1,0:T(8,128)S(1)} %shard_map.45.state), channel_id=1, source_target_pairs={{0,31},{1,2},{2,1},{3,4},{4,3},{5,6},{6,5},{7,8},{8,7},{9,10},{10,... | collective-permute-start | bytes 1572872 | tf_op jit(solution)/shard_map/ppermute | solution.py:304
  215.3 0.0 collective-permute-done.11
  215.4 3.2 %collective-permute-start.15 = (f32[16,4,2,8,128]{4,3,2,1,0:T(8,128)S(1)}, f32[16,4,2,8,128]{4,3,2,1,0:T(8,128)S(1)}, u32[]{:S(2)}, u32[]{:S(2)}) collective-permute-start(f32[16,4,2,8,128]{4,3,2,1,0:T(8,128)S(1)} %get-tuple-element.24.refs_0_), channel_id=1, source_target_pairs={{0,1},{1,0},{2,3},{3,2},{4,5},{5,4},{6,7},{7,6},{8,9},{9,8},{10,11... | collective-permute-start | bytes 1572872 | tf_op jit(solution)/shard_map/ppermute | solution.py:326
  218.5 0.0 collective-permute-done.10.inner
  218.6 2.5 shard_map.46.passed
  221.1 7.0 %collective-permute-done.9.outer = f32[4,8,8,512]{3,2,1,0:T(8,128)S(1)} collective-permute-done((f32[4,8,8,512]{3,2,1,0:T(8,128)S(1)}, f32[4,8,8,512]{3,2,1,0:T(8,128)S(1)}, u32[]{:S(2)}, u32[]{:S(2)}) %collective-permute-start.9) | collective-permute-done | bytes 524320 | tf_op jit(solution)/shard_map/ppermute | solution.py:304
  228.2 3.3 %shard_map.47.state = f32[4,8,8,512]{3,2,1,0:T(8,128)S(1)} custom-call(s32[3]{0:T(128)S(1)} %copy-done.3, f32[4,8,8,512]{3,2,1,0:T(8,128)S(1)} %shard_map.45.state, f32[4,8,8,512]{3,2,1,0:T(8,128)S(1)} %collective-permute-done.9.outer, f32[4,7,8,8,512]{4,3,2,1,0:T(8,128)S(1)} %get-tuple-element.15.own, f32[3,7,8,8,512]{4,3,2,1,0:T(8,128)S(1)} %shard_map.39.own_outer, ...), custom_call_target="tpu_custom_call" | custom-call | tf_op jit(solution)/shard_map/pallas_call | solution.py:388
  231.4 1.9 collective-permute-start.13
  233.4 3.2 %collective-permute-start.12 = (f32[4,8,8,512]{3,2,1,0:T(8,128)S(1)}, f32[4,8,8,512]{3,2,1,0:T(8,128)S(1)}, u32[]{:S(2)}, u32[]{:S(2)}) collective-permute-start(f32[4,8,8,512]{3,2,1,0:T(8,128)S(1)} %shard_map.47.state), channel_id=1, source_target_pairs={{0,31},{1,2},{2,1},{3,4},{4,3},{5,6},{6,5},{7,8},{8,7},{9,10},{10,... | collective-permute-start | bytes 1572872 | tf_op jit(solution)/shard_map/ppermute | solution.py:304
  236.6 6.8 %collective-permute-start.14 = (f32[2,8,128]{2,1,0:T(8,128)S(1)}, f32[2,8,128]{2,1,0:T(8,128)S(1)}, u32[]{:S(2)}, u32[]{:S(2)}) collective-permute-start(f32[2,8,128]{2,1,0:T(8,128)S(1)} %get-tuple-element.20), channel_id=1, source_target_pairs={{32,0},{64,32},{96,64},{128,96},{160,128},{192,160},{224,192},{256... | collective-permute-start | bytes 24584 | tf_op jit(solution)/shard_map/ppermute | solution.py:359
  243.4 0.0 collective-permute-done.15
  243.4 0.0 collective-permute-done.13.inner
  243.4 2.5 shard_map.48.passed
  246.0 0.0 collective-permute-done.14.refs_0_
  246.0 3.5 %collective-permute-done.12.outer = f32[4,8,8,512]{3,2,1,0:T(8,128)S(1)} collective-permute-done((f32[4,8,8,512]{3,2,1,0:T(8,128)S(1)}, f32[4,8,8,512]{3,2,1,0:T(8,128)S(1)}, u32[]{:S(2)}, u32[]{:S(2)}) %collective-permute-start.12) | collective-permute-done | bytes 524320 | tf_op jit(solution)/shard_map/ppermute | solution.py:304
  249.5 3.4 %shard_map.49 = (f32[4,8,8,512]{3,2,1,0:T(8,128)S(1)}, f32[32,2,8,128]{3,2,1,0:T(8,128)S(1)}) custom-call(s32[3]{0:T(128)S(1)} %copy-done.3, f32[4,8,8,512]{3,2,1,0:T(8,128)S(1)} %shard_map.47.state, f32[4,8,8,512]{3,2,1,0:T(8,128)S(1)} %collective-permute-done.12.outer, f32[4,7,8,8,512]{4,3,2,1,0:T(8,128)S(1)} %get-tuple-element.15.own, ...), custom_call_target="tpu_custom_call" | custom-call | tf_op jit(solution)/shard_map/pallas_call | solution.py:388
  252.9 18.9 %all_to_all.10.residuals = f32[32,2,8,128]{3,2,1,0:T(8,128)S(1)} all-to-all(f32[32,2,8,128]{3,2,1,0:T(8,128)S(1)} %get-tuple-element.21), channel_id=1, replica_groups=mesh['cuts'=16,'space'=32] {'space'}, dimensions={0} | all-to-all | bytes 524288 | tf_op jit(solution)/shard_map/all_to_all | solution.py:390
  271.9 10.7 %shard_map.50 = f32[16,2,8,128]{3,2,1,0:T(8,128)S(1)} custom-call(s32[3]{0:T(128)S(1)} %copy-done.3, f32[32,2,8,128]{3,2,1,0:T(8,128)S(1)} %all_to_all.10.residuals, f32[32,4,2,8,128]{4,3,2,1,0:T(8,128)S(1)} %constant_dynamic-update-slice_fusion.5.refs_1_.fields), custom_call_target="tpu_custom_call" | custom-call | tf_op jit(solution)/shard_map/pallas_call | solution.py:391
  282.6 14.4 %all_to_all.11.shares = f32[16,2,8,128]{3,2,1,0:T(8,128)S(1)} all-to-all(f32[16,2,8,128]{3,2,1,0:T(8,128)S(1)} %shard_map.50), channel_id=1, replica_groups=mesh['cuts'=16,'space'=32] {'cuts'}, dimensions={0} | all-to-all | bytes 262144 | tf_op jit(solution)/shard_map/all_to_all | solution.py:401
  297.0 1.1 shard_map.51
  (9 shorter events, 0.2 us)
Async XLA Ops:
  65.9 85.2 %copy-start = (f32[3,4,64,512]{3,2,1,0:T(8,128)S(1)}, f32[3,4,64,512]{3,2,1,0:T(8,128)}, u32[]{:S(2)}) copy-start(f32[3,4,64,512]{3,2,1,0:T(8,128)} %velocity.5) | copy-start | bytes 4718596
  65.9 85.2 %copy-start.1 = (f32[1,4,64,512]{3,2,1,0:T(8,128)S(1)}, f32[1,4,64,512]{3,2,1,0:T(8,128)}, u32[]{:S(2)}) copy-start(f32[1,4,64,512]{3,2,1,0:T(8,128)} %starts.3) | copy-start | bytes 1572868
  66.0 85.2 %copy-start.2 = (f32[4,64,512]{2,1,0:T(8,128)S(1)}, f32[4,64,512]{2,1,0:T(8,128)}, u32[]{:S(2)}) copy-start(f32[4,64,512]{2,1,0:T(8,128)} %diffusivity.5) | copy-start | bytes 1572868
  66.0 104.0 %collective-permute-start.3 = (f32[3,3,64,512]{3,2,1,0:T(8,128)}, f32[3,3,64,512]{3,2,1,0:T(8,128)S(1)}, u32[]{:S(2)}, u32[]{:S(2)}) collective-permute-start(f32[3,3,64,512]{3,2,1,0:T(8,128)} %get-tuple-element.18), channel_id=1, source_target_pairs={{0,1},{1,0},{2,3},{3,2},{4,5},{5,4},{6,7},{7,6},{8,9},{9,8},{10,11... | collective-permute-start | bytes 3538952 | tf_op jit(solution)/shard_map/ppermute | solution.py:295
  133.4 40.0 %collective-permute-start.1 = (f32[3,3,64,512]{3,2,1,0:T(8,128)}, f32[3,3,64,512]{3,2,1,0:T(8,128)S(1)}, u32[]{:S(2)}, u32[]{:S(2)}) collective-permute-start(f32[3,3,64,512]{3,2,1,0:T(8,128)} %get-tuple-element.16), channel_id=1, source_target_pairs={{0,287},{1,258},{2,257},{3,260},{4,259},{5,262},{6,261},{7,264},{8... | collective-permute-start | bytes 3538952 | tf_op jit(solution)/shard_map/ppermute | solution.py:313
  136.9 33.1 %collective-permute-start.2 = (f32[7,64,512]{2,1,0:T(8,128)}, f32[7,64,512]{2,1,0:T(8,128)S(1)}, u32[]{:S(2)}, u32[]{:S(2)}) collective-permute-start(f32[7,64,512]{2,1,0:T(8,128)} %get-tuple-element.17), channel_id=1, source_target_pairs={{0,1},{1,0},{2,3},{3,2},{4,5},{5,4},{6,7},{7,6},{8,9},{9,8},{10,11... | collective-permute-start | bytes 2752520 | tf_op jit(solution)/shard_map/ppermute | solution.py:295
  140.6 32.8 %collective-permute-start = (f32[7,64,512]{2,1,0:T(8,128)}, f32[7,64,512]{2,1,0:T(8,128)S(1)}, u32[]{:S(2)}, u32[]{:S(2)}) collective-permute-start(f32[7,64,512]{2,1,0:T(8,128)} %get-tuple-element.14), channel_id=1, source_target_pairs={{0,31},{1,2},{2,1},{3,4},{4,3},{5,6},{6,5},{7,8},{8,7},{9,10},{10,... | collective-permute-start | bytes 2752520 | tf_op jit(solution)/shard_map/ppermute | solution.py:304
  152.4 10.5 %collective-permute-start.4 = (f32[1,4,2,8,128]{4,3,2,1,0:T(8,128)S(1)}, f32[1,4,2,8,128]{4,3,2,1,0:T(8,128)S(1)}, u32[]{:S(2)}, u32[]{:S(2)}) collective-permute-start(f32[1,4,2,8,128]{4,3,2,1,0:T(8,128)S(1)} %bitcast.10), channel_id=1, source_target_pairs={{0,16},{1,17},{2,18},{3,19},{4,20},{5,21},{6,22},{7,23},{8,24},{9,... | collective-permute-start | bytes 98312 | tf_op jit(solution)/shard_map/ppermute | solution.py:326
  162.9 7.0 %collective-permute-start.5 = (f32[2,4,2,8,128]{4,3,2,1,0:T(8,128)S(1)}, f32[2,4,2,8,128]{4,3,2,1,0:T(8,128)S(1)}, u32[]{:S(2)}, u32[]{:S(2)}) collective-permute-start(f32[2,4,2,8,128]{4,3,2,1,0:T(8,128)S(1)} %pad_maximum_fusion.2), channel_id=1, source_target_pairs={{0,8},{1,9},{2,10},{3,11},{4,12},{5,13},{6,14},{7,15},{8,0},{9,1},... | collective-permute-start | bytes 196616 | tf_op jit(solution)/shard_map/ppermute | solution.py:326
  170.0 0.6 copy-start.3
  177.4 26.8 %collective-permute-start.7 = (f32[4,8,8,512]{3,2,1,0:T(8,128)S(1)}, f32[4,8,8,512]{3,2,1,0:T(8,128)S(1)}, u32[]{:S(2)}, u32[]{:S(2)}) collective-permute-start(f32[4,8,8,512]{3,2,1,0:T(8,128)S(1)} %shard_map.43.state), channel_id=1, source_target_pairs={{0,1},{1,0},{2,3},{3,2},{4,5},{5,4},{6,7},{7,6},{8,9},{9,8},{10,11... | collective-permute-start | bytes 1572872 | tf_op jit(solution)/shard_map/ppermute | solution.py:295
  187.7 19.1 %collective-permute-start.6 = (f32[4,8,8,512]{3,2,1,0:T(8,128)S(1)}, f32[4,8,8,512]{3,2,1,0:T(8,128)S(1)}, u32[]{:S(2)}, u32[]{:S(2)}) collective-permute-start(f32[4,8,8,512]{3,2,1,0:T(8,128)S(1)} %shard_map.43.state), channel_id=1, source_target_pairs={{0,31},{1,2},{2,1},{3,4},{4,3},{5,6},{6,5},{7,8},{8,7},{9,10},{10,... | collective-permute-start | bytes 1572872 | tf_op jit(solution)/shard_map/ppermute | solution.py:304
  189.7 9.8 %collective-permute-start.8 = (f32[4,4,2,8,128]{4,3,2,1,0:T(8,128)S(1)}, f32[4,4,2,8,128]{4,3,2,1,0:T(8,128)S(1)}, u32[]{:S(2)}, u32[]{:S(2)}) collective-permute-start(f32[4,4,2,8,128]{4,3,2,1,0:T(8,128)S(1)} %pad_maximum_fusion.1.refs_0_), channel_id=1, source_target_pairs={{0,4},{1,5},{2,6},{3,7},{4,0},{5,1},{6,2},{7,3},{8,12},{9,13},{10,... | collective-permute-start | bytes 393224 | tf_op jit(solution)/shard_map/ppermute | solution.py:326
  199.5 15.8 %collective-permute-start.11 = (f32[8,4,2,8,128]{4,3,2,1,0:T(8,128)S(1)}, f32[8,4,2,8,128]{4,3,2,1,0:T(8,128)S(1)}, u32[]{:S(2)}, u32[]{:S(2)}) collective-permute-start(f32[8,4,2,8,128]{4,3,2,1,0:T(8,128)S(1)} %pad_maximum_fusion.refs_0_), channel_id=1, source_target_pairs={{0,258},{1,259},{2,256},{3,257},{4,262},{5,263},{6,260},{7,261},{8... | collective-permute-start | bytes 786440 | tf_op jit(solution)/shard_map/ppermute | solution.py:326
  210.1 8.4 %collective-permute-start.10 = (f32[4,8,8,512]{3,2,1,0:T(8,128)S(1)}, f32[4,8,8,512]{3,2,1,0:T(8,128)S(1)}, u32[]{:S(2)}, u32[]{:S(2)}) collective-permute-start(f32[4,8,8,512]{3,2,1,0:T(8,128)S(1)} %shard_map.45.state), channel_id=1, source_target_pairs={{0,1},{1,0},{2,3},{3,2},{4,5},{5,4},{6,7},{7,6},{8,9},{9,8},{10,11... | collective-permute-start | bytes 1572872 | tf_op jit(solution)/shard_map/ppermute | solution.py:295
  212.0 16.1 %collective-permute-start.9 = (f32[4,8,8,512]{3,2,1,0:T(8,128)S(1)}, f32[4,8,8,512]{3,2,1,0:T(8,128)S(1)}, u32[]{:S(2)}, u32[]{:S(2)}) collective-permute-start(f32[4,8,8,512]{3,2,1,0:T(8,128)S(1)} %shard_map.45.state), channel_id=1, source_target_pairs={{0,31},{1,2},{2,1},{3,4},{4,3},{5,6},{6,5},{7,8},{8,7},{9,10},{10,... | collective-permute-start | bytes 1572872 | tf_op jit(solution)/shard_map/ppermute | solution.py:304
  215.4 28.0 %collective-permute-start.15 = (f32[16,4,2,8,128]{4,3,2,1,0:T(8,128)S(1)}, f32[16,4,2,8,128]{4,3,2,1,0:T(8,128)S(1)}, u32[]{:S(2)}, u32[]{:S(2)}) collective-permute-start(f32[16,4,2,8,128]{4,3,2,1,0:T(8,128)S(1)} %get-tuple-element.24.refs_0_), channel_id=1, source_target_pairs={{0,1},{1,0},{2,3},{3,2},{4,5},{5,4},{6,7},{7,6},{8,9},{9,8},{10,11... | collective-permute-start | bytes 1572872 | tf_op jit(solution)/shard_map/ppermute | solution.py:326
  231.4 12.0 %collective-permute-start.13 = (f32[4,8,8,512]{3,2,1,0:T(8,128)S(1)}, f32[4,8,8,512]{3,2,1,0:T(8,128)S(1)}, u32[]{:S(2)}, u32[]{:S(2)}) collective-permute-start(f32[4,8,8,512]{3,2,1,0:T(8,128)S(1)} %shard_map.47.state), channel_id=1, source_target_pairs={{0,1},{1,0},{2,3},{3,2},{4,5},{5,4},{6,7},{7,6},{8,9},{9,8},{10,11... | collective-permute-start | bytes 1572872 | tf_op jit(solution)/shard_map/ppermute | solution.py:295
  233.4 16.1 %collective-permute-start.12 = (f32[4,8,8,512]{3,2,1,0:T(8,128)S(1)}, f32[4,8,8,512]{3,2,1,0:T(8,128)S(1)}, u32[]{:S(2)}, u32[]{:S(2)}) collective-permute-start(f32[4,8,8,512]{3,2,1,0:T(8,128)S(1)} %shard_map.47.state), channel_id=1, source_target_pairs={{0,31},{1,2},{2,1},{3,4},{4,3},{5,6},{6,5},{7,8},{8,7},{9,10},{10,... | collective-permute-start | bytes 1572872 | tf_op jit(solution)/shard_map/ppermute | solution.py:304
  236.6 9.4 %collective-permute-start.14 = (f32[2,8,128]{2,1,0:T(8,128)S(1)}, f32[2,8,128]{2,1,0:T(8,128)S(1)}, u32[]{:S(2)}, u32[]{:S(2)}) collective-permute-start(f32[2,8,128]{2,1,0:T(8,128)S(1)} %get-tuple-element.20), channel_id=1, source_target_pairs={{32,0},{64,32},{96,64},{128,96},{160,128},{192,160},{224,192},{256... | collective-permute-start | bytes 24584 | tf_op jit(solution)/shard_map/ppermute | solution.py:359

commit v6 on v5

--- a/solution.py
+++ b/solution.py
@@ -122,7 +122,7 @@
                 coarse_old[h] = mean
 
 
-def side_kernel(velocity, mixed, weights, buffer):
+def side_kernel(velocity, mixed, earlier, weights, buffer):
     def layer(x, carry):
         for f in range(3):
             spread(velocity[f, x], buffer.at[f])
@@ -185,11 +185,15 @@
         source, target = target, source
 
 
-def outer_kernel(raw, final, place, state, outer, own, own_outer, passed, *refs):
+def outer_kernel(raw, final, place, state, passed, outer, own, own_outer, *refs):
     if final:
-        later, *refs, out, residual, one, two, buffer = refs
+        later, after, out, residual, one, two, buffer = refs
     else:
-        out, one, two, buffer = refs[-4:]
+        *parts, early, out, joined, one, two, buffer = refs
+        begin = 0
+        for part in parts:
+            joined[begin : begin + part.shape[0]] = part[...]
+            begin += part.shape[0]
     core = place[2]
     enter(one, ((state, LAYERS), (outer, 2 * LAYERS * core)), raw, buffer)
     source, target = one, two
@@ -237,21 +241,28 @@
         behind, now = now, ahead
 
 
-def chain_kernel(place, residuals, fields, shares, weights, one, two):
+def mask_of(i):
+    return 8 * (i & 3) | (i & 4) | ((i >> 2) & 2) | (i >> 4)
+
+
+def coarse_weight_kernel(place, some, others, weights):
+    row = place[1]
+    half = some.shape[0]
+    for i in range(2 * half):
+        x = row ^ mask_of(i)
+        for h in range(2):
+            parts = [(some if i < half else others)[i % half, f, h] for f in range(4)]
+            for k, weight in enumerate(weigh(parts[:3], parts[3], STEP * RATIO, 1.0 * RATIO)):
+                weights[x, k, h] = weight
+
+
+def chain_kernel(place, residuals, weights, shares, one, two):
     count = weights.shape[0]
     slices = shares.shape[0]
     slice_index = place[0]
     layer_index = place[1]
     shares[...] = jnp.zeros(shares.shape, F32)
-
-    bits = count.bit_length() - 1
-    for i in range(count):
-        x = layer_index ^ sum(((i >> b) & 1) << (bits - 1 - b) for b in range(bits))
-        for h in range(2):
-            parts = [fields[i, f, h] for f in range(4)]
-            for k, weight in enumerate(weigh(parts[:3], parts[3], STEP * RATIO, 1.0 * RATIO)):
-                weights[x, k, h] = weight
-            one[i, h] = residuals[i, h]
+    one[...] = residuals[...]
 
     def reader(ref):
         return lambda x: [ref[x, h] for h in range(2)]
@@ -313,17 +324,14 @@
     return lax.ppermute(block, ("cuts", "space"), route)
 
 
-def double(block, bit):
+def across(block, bits):
     slices, count = lax.axis_size("cuts"), lax.axis_size("space")
-    if bit == 2:
-        axes = ("cuts", "space")
+    if bits == 2:
         route = [
-            (n * count + p, (n + slices // 2) % slices * count + (p ^ bit)) for n in range(slices) for p in range(count)
+            (n * count + p, (n + slices // 2) % slices * count + (p ^ bits)) for n in range(slices) for p in range(count)
         ]
-    else:
-        axes = "space"
-        route = [(p, p ^ bit) for p in range(count)]
-    return jnp.concatenate([block, lax.ppermute(block, axes, route)], axis=0)
+        return lax.ppermute(block, ("cuts", "space"), route)
+    return lax.ppermute(block, "space", [(p, p ^ bits) for p in range(count)])
 
 
 def shards(starts, velocity, diffusivity):
@@ -341,7 +349,6 @@
             [SMEM, ANY, ANY, ANY],
             [pltpu.SemaphoreType.DMA((3,))],
             limit=60,
-            out=ANY,
         )(place, velocity, diffusivity, starts)
 
     fields_outer, mixed_outer = cut(True)
@@ -357,13 +364,9 @@
         [columns],
     )(velocity, diffusivity, starts[0])
     coarse_later = lax.ppermute(coarse_old, "cuts", [((n + 1) % slices, n) for n in range(slices)])
-    gathered = [coarse_fields[None]]
-    for bit in (16, 8, 4, 2, 1):
-        gathered.append(double(gathered[-1], bit))
-    inner_weights, outer_weights = [
-        call(side_kernel, [(REACH, 7, *TILE)], [VMEM] * 2, [columns])(*halos)[0]
-        for halos in ((fields_inner, mixed_inner), (fields_outer, mixed_outer))
-    ]
+    gathered = coarse_fields[None]
+    weigh_side = call(side_kernel, [(REACH, 7, *TILE)], [VMEM, VMEM, ANY], [columns])
+    inner_weights = weigh_side(fields_inner, mixed_inner, coarse_old)[0]
     state, inner, outer = starts[0], mixed_inner, mixed_outer
     scratch = [pltpu.VMEM((3 * LAYERS, *TILE), F32)] * 2 + [columns]
     for index in range(ROUNDS):
@@ -376,28 +379,32 @@
             [SMEM] + [VMEM] * 4,
             scratch,
         )(place, state, inner, own_weights, inner_weights)[0]
-        operands = [place, state, outer, own_weights, outer_weights, passed]
-        specs = [SMEM] + [VMEM] * 5
-        outs = [block]
+        if raw:
+            outer_weights = weigh_side(fields_outer, mixed_outer, passed)[0]
+        operands = [place, state, passed, outer, own_weights, outer_weights]
         if final:
-            operands.append(coarse_later)
-            specs.append(VMEM)
-            outs.append((count, *COARSE))
-        operands.append(gathered[index + 2])
-        specs.append(ANY)
-        outs = call(functools.partial(outer_kernel, raw, final), outs, specs, scratch)(*operands)
-        state = outs[0]
-    residuals = lax.all_to_all(outs[1], "space", 0, 0)
+            weights = call(
+                coarse_weight_kernel,
+                [(count, 7, *COARSE)],
+                [SMEM, VMEM, VMEM],
+            )(place, gathered, across(gathered, 1))[0]
+            operands += [coarse_later, weights]
+            specs = [SMEM] + [VMEM] * 6 + [ANY]
+            outs = [block, (count, *COARSE)]
+        else:
+            bits = ((8, 16, 24), (4,), (2,))[index]
+            parts = [gathered] + [across(gathered, b) for b in bits]
+            operands += parts + [coarse_later if index == 1 else coarse_old]
+            specs = [SMEM] + [VMEM] * (5 + len(parts)) + [ANY]
+            outs = [block, (len(parts) * gathered.shape[0], 4, *COARSE)]
+        state, gathered = call(functools.partial(outer_kernel, raw, final), outs, specs, scratch)(*operands)
+    residuals = lax.all_to_all(gathered, "space", 0, 0)
     shares = call(
         chain_kernel,
         [(slices, *COARSE)],
         [SMEM, VMEM, VMEM],
-        [
-            pltpu.VMEM((count, 7, *COARSE), F32),
-            pltpu.VMEM((count, *COARSE), F32),
-            pltpu.VMEM((count, *COARSE), F32),
-        ],
-    )(place, residuals, gathered[-1])[0]
+        [pltpu.VMEM((count, *COARSE), F32)] * 2,
+    )(place, residuals, weights)[0]
     shares = lax.all_to_all(shares, "cuts", 0, 0)
     return call(finish_kernel, [(1, LAYERS, 64, 512)], [VMEM, VMEM], [columns])(shares, state)[0]
 

time: 299 us -> 167 us (0.56)
  Pallas kernels: 169 us -> 48.5 us
  waiting for transfers between devices: 28.1 us -> 19.8 us
    pallas_call x2, Pallas kernels: 131 us -> 7.05 us  [cut(): call(functools.partial(cut_kernel, outer=outer), [(3, REACH, 64, 512), (L...]
    ppermute x5 -> x6, waiting for transfers between devices: 17.6 us -> 3.46 us  [the longest x1 3.44 us: across(): return lax.ppermute(block, ('cuts', 'space'), route)]
    ppermute x5, starting transfers between devices: 19.9 us -> 11.5 us  [swap_inner(): return lax.ppermute(block, 'space', [(p, p ^ 1) for p in range(count)])]
    ppermute x4, waiting for transfers between devices: 10.5 us -> 16.4 us  [swap_outer(): lax.ppermute(block, 'space', [(p, outer_partner(p, count)) for p in range...]
    ppermute x5 -> x6, starting transfers between devices: 17.7 us -> 22.8 us  [the longest x5 17.6 us: across(): return lax.ppermute(block, 'space', [(p, p ^ bits) for p in range(count)])]
  transfers between devices with their start and end apart: 16 -> 17, of which waited for: 5 -> 5; matrix products, arithmetic and copies ran while one was open for 0% -> 0% of each run, Pallas kernels for 28% -> 10%
where the time goes in v6:
time: 167 us; the launch traced here: 166 us
  starting transfers between devices  64.2 us (38%)
  Pallas kernels  48.5 us (29%)
  blocking collectives  32.6 us (20%)
  waiting for transfers between devices  19.8 us (12%)
    ppermute x4, starting transfers between devices, swap_outer(): lax.ppermute(block, 'space', [(p, outer_partner(p, count)) for p in range...  21.4 us
    all_to_all x1, blocking collectives, shards(): residuals = lax.all_to_all(gathered, 'space', 0, 0)  19 us
    ppermute x5, starting transfers between devices, across(): return lax.ppermute(block, 'space', [(p, p ^ bits) for p in range(count)])  17.6 us
    ppermute x4, waiting for transfers between devices, swap_outer(): lax.ppermute(block, 'space', [(p, outer_partner(p, count)) for p in range...  16.4 us
    all_to_all x1, blocking collectives, shards(): shares = lax.all_to_all(shares, 'cuts', 0, 0)  13.7 us
    pallas_call x4, Pallas kernels, shards(): call(functools.partial(outer_kernel, raw, final), outs, specs, scratch)  13.5 us
    pallas_call x1, Pallas kernels, shards(): call(chain_kernel, [(slices, *COARSE)], [SMEM, VMEM, VMEM], [pltpu.VMEM((...  13.3 us
    ppermute x5, starting transfers between devices, swap_inner(): return lax.ppermute(block, 'space', [(p, p ^ 1) for p in range(count)])  11.5 us
  transfers between devices with their start and end apart: 17, of which 5 were waited for; matrix products, arithmetic and copies ran while one was open for 0% of the time, Pallas kernels for 10%

profile of v6, /device:TPU:2, one launch (start us, length us, event | category | flops | bytes accessed | tf_op | source)
XLA Modules:
  0.0 166.3 jit_solution(5872927367566423825)
XLA Ops:
  0.0 0.7 pad_add_fusion.place
  0.7 3.5 %shard_map.37 = (f32[3,3,64,512]{3,2,1,0:T(8,128)}, f32[7,64,512]{2,1,0:T(8,128)}) custom-call(s32[3]{0:T(128)} %pad_add_fusion.place, f32[3,4,64,512]{3,2,1,0:T(8,128)} %velocity.5, f32[4,64,512]{2,1,0:T(8,128)} %diffusivity.5, f32[1,4,64,512]{3,2,1,0:T(8,128)} %starts.3), custom_call_target="tpu_custom_call" | custom-call | tf_op jit(solution)/shard_map/pallas_call | solution.py:346
  4.2 0.0 copy-start
  4.2 0.0 copy-start.1
  4.2 0.0 copy-start.2
  4.2 2.1 %collective-permute-start.1 = (f32[3,3,64,512]{3,2,1,0:T(8,128)}, f32[3,3,64,512]{3,2,1,0:T(8,128)S(1)}, u32[]{:S(2)}, u32[]{:S(2)}) collective-permute-start(f32[3,3,64,512]{3,2,1,0:T(8,128)} %get-tuple-element.22), channel_id=1, source_target_pairs={{0,1},{1,0},{2,3},{3,2},{4,5},{5,4},{6,7},{7,6},{8,9},{9,8},{10,11... | collective-permute-start | bytes 3538952 | tf_op jit(solution)/shard_map/ppermute | solution.py:306
  6.3 3.5 %shard_map.41 = (f32[3,3,64,512]{3,2,1,0:T(8,128)}, f32[7,64,512]{2,1,0:T(8,128)}) custom-call(s32[3]{0:T(128)} %pad_add_fusion.place, f32[3,4,64,512]{3,2,1,0:T(8,128)} %velocity.5, f32[4,64,512]{2,1,0:T(8,128)} %diffusivity.5, f32[1,4,64,512]{3,2,1,0:T(8,128)} %starts.3), custom_call_target="tpu_custom_call" | custom-call | tf_op jit(solution)/shard_map/pallas_call | solution.py:346
  9.8 3.5 %collective-permute-start.3 = (f32[3,3,64,512]{3,2,1,0:T(8,128)}, f32[3,3,64,512]{3,2,1,0:T(8,128)S(1)}, u32[]{:S(2)}, u32[]{:S(2)}) collective-permute-start(f32[3,3,64,512]{3,2,1,0:T(8,128)} %get-tuple-element.25), channel_id=1, source_target_pairs={{0,287},{1,258},{2,257},{3,260},{4,259},{5,262},{6,261},{7,264},{8... | collective-permute-start | bytes 3538952 | tf_op jit(solution)/shard_map/ppermute | solution.py:324
  13.3 3.7 %collective-permute-start = (f32[7,64,512]{2,1,0:T(8,128)}, f32[7,64,512]{2,1,0:T(8,128)S(1)}, u32[]{:S(2)}, u32[]{:S(2)}) collective-permute-start(f32[7,64,512]{2,1,0:T(8,128)} %get-tuple-element.20), channel_id=1, source_target_pairs={{0,1},{1,0},{2,3},{3,2},{4,5},{5,4},{6,7},{7,6},{8,9},{9,8},{10,11... | collective-permute-start | bytes 2752520 | tf_op jit(solution)/shard_map/ppermute | solution.py:306
  17.1 10.5 %collective-permute-start.2 = (f32[7,64,512]{2,1,0:T(8,128)}, f32[7,64,512]{2,1,0:T(8,128)S(1)}, u32[]{:S(2)}, u32[]{:S(2)}) collective-permute-start(f32[7,64,512]{2,1,0:T(8,128)} %get-tuple-element.24), channel_id=1, source_target_pairs={{0,31},{1,2},{2,1},{3,4},{4,3},{5,6},{6,5},{7,8},{8,7},{9,10},{10,... | collective-permute-start | bytes 2752520 | tf_op jit(solution)/shard_map/ppermute | solution.py:315
  27.5 0.0 copy-done
  27.6 0.0 copy-done.1
  27.6 0.0 copy-done.2
  27.6 1.3 shard_map.38
  28.9 2.5 %collective-permute-start.6 = (f32[1,4,2,8,128]{4,3,2,1,0:T(8,128)S(1)}, f32[1,4,2,8,128]{4,3,2,1,0:T(8,128)S(1)}, u32[]{:S(2)}, u32[]{:S(2)}) collective-permute-start(f32[1,4,2,8,128]{4,3,2,1,0:T(8,128)S(1)} %bitcast.8), channel_id=1, source_target_pairs={{0,24},{1,25},{2,26},{3,27},{4,28},{5,29},{6,30},{7,31},{8,16},{9,... | collective-permute-start | bytes 98312 | tf_op jit(solution)/shard_map/ppermute | solution.py:334
  31.3 0.0 collective-permute-done.mixed.inner
  31.3 1.9 %collective-permute-start.5 = (f32[1,4,2,8,128]{4,3,2,1,0:T(8,128)S(1)}, f32[1,4,2,8,128]{4,3,2,1,0:T(8,128)S(1)}, u32[]{:S(2)}, u32[]{:S(2)}) collective-permute-start(f32[1,4,2,8,128]{4,3,2,1,0:T(8,128)S(1)} %bitcast.9), channel_id=1, source_target_pairs={{0,16},{1,17},{2,18},{3,19},{4,20},{5,21},{6,22},{7,23},{8,24},{9,... | collective-permute-start | bytes 98312 | tf_op jit(solution)/shard_map/ppermute | solution.py:334
  33.3 0.0 collective-permute-done.1.velocity
  33.3 7.9 %collective-permute-start.4 = (f32[1,4,2,8,128]{4,3,2,1,0:T(8,128)S(1)}, f32[1,4,2,8,128]{4,3,2,1,0:T(8,128)S(1)}, u32[]{:S(2)}, u32[]{:S(2)}) collective-permute-start(f32[1,4,2,8,128]{4,3,2,1,0:T(8,128)S(1)} %bitcast.10), channel_id=1, source_target_pairs={{0,8},{1,9},{2,10},{3,11},{4,12},{5,13},{6,14},{7,15},{8,0},{9,1},... | collective-permute-start | bytes 98312 | tf_op jit(solution)/shard_map/ppermute | solution.py:334
  41.1 0.0 copy-start.3
  41.2 0.6 shard_map.39.own_inner
  41.7 0.1 copy-done.3
  41.8 2.8 %shard_map.40.earlier.passed = f32[3,2,8,8,512]{4,3,2,1,0:T(8,128)S(1)} custom-call(s32[3]{0:T(128)S(1)} %copy-done.3, f32[4,64,512]{2,1,0:T(8,128)S(1)} %bitcast.6, f32[7,64,512]{2,1,0:T(8,128)S(1)} %collective-permute-done.mixed.inner, f32[4,7,8,8,512]{4,3,2,1,0:T(8,128)S(1)} %get-tuple-element.21.own, f32[3,7,8,8,512]{4,3,2,1,0:T(8,128)S(1)} %shard_map.39.own_inner), custom_call_target="tpu_custom_call" | custom-call | tf_op jit(solution)/shard_map/pallas_call | solution.py:376
  44.6 4.1 %collective-permute-done.2.mixed.outer = f32[7,64,512]{2,1,0:T(8,128)S(1)} collective-permute-done((f32[7,64,512]{2,1,0:T(8,128)}, f32[7,64,512]{2,1,0:T(8,128)S(1)}, u32[]{:S(2)}, u32[]{:S(2)}) %collective-permute-start.2) | collective-permute-done | bytes 917536 | tf_op jit(solution)/shard_map/ppermute | solution.py:315
  48.7 0.0 collective-permute-done.3.velocity
  48.7 0.6 shard_map.42.own_outer
  49.2 0.0 collective-permute-done.6.refs_3_
  49.2 0.0 collective-permute-done.5.refs_2_
  49.2 0.0 collective-permute-done.4.refs_1_
  49.3 3.5 %shard_map.43 = (f32[4,8,8,512]{3,2,1,0:T(8,128)S(1)}, f32[4,4,2,8,128]{4,3,2,1,0:T(8,128)S(1)}) custom-call(s32[3]{0:T(128)S(1)} %copy-done.3, f32[4,64,512]{2,1,0:T(8,128)S(1)} %bitcast.7, f32[3,2,8,8,512]{4,3,2,1,0:T(8,128)S(1)} %shard_map.40.earlier.passed, f32[7,64,512]{2,1,0:T(8,128)S(1)} %collective-permute-done.2.mixed.outer, ...), custom_call_target="tpu_custom_call" | custom-call | tf_op jit(solution)/shard_map/pallas_call | solution.py:400
  52.7 1.9 %collective-permute-start.7 = (f32[4,8,8,512]{3,2,1,0:T(8,128)S(1)}, f32[4,8,8,512]{3,2,1,0:T(8,128)S(1)}, u32[]{:S(2)}, u32[]{:S(2)}) collective-permute-start(f32[4,8,8,512]{3,2,1,0:T(8,128)S(1)} %get-tuple-element.27.state), channel_id=1, source_target_pairs={{0,1},{1,0},{2,3},{3,2},{4,5},{5,4},{6,7},{7,6},{8,9},{9,8},{10,11... | collective-permute-start | bytes 1572872 | tf_op jit(solution)/shard_map/ppermute | solution.py:306
  54.7 3.6 %collective-permute-start.8 = (f32[4,8,8,512]{3,2,1,0:T(8,128)S(1)}, f32[4,8,8,512]{3,2,1,0:T(8,128)S(1)}, u32[]{:S(2)}, u32[]{:S(2)}) collective-permute-start(f32[4,8,8,512]{3,2,1,0:T(8,128)S(1)} %get-tuple-element.27.state), channel_id=1, source_target_pairs={{0,31},{1,2},{2,1},{3,4},{4,3},{5,6},{6,5},{7,8},{8,7},{9,10},{10,... | collective-permute-start | bytes 1572872 | tf_op jit(solution)/shard_map/ppermute | solution.py:315
  58.3 3.0 %collective-permute-start.9 = (f32[4,4,2,8,128]{4,3,2,1,0:T(8,128)S(1)}, f32[4,4,2,8,128]{4,3,2,1,0:T(8,128)S(1)}, u32[]{:S(2)}, u32[]{:S(2)}) collective-permute-start(f32[4,4,2,8,128]{4,3,2,1,0:T(8,128)S(1)} %get-tuple-element.28.refs_0_), channel_id=1, source_target_pairs={{0,4},{1,5},{2,6},{3,7},{4,0},{5,1},{6,2},{7,3},{8,12},{9,13},{10,... | collective-permute-start | bytes 393224 | tf_op jit(solution)/shard_map/ppermute | solution.py:334
  61.3 5.0 %collective-permute-start.10 = (f32[2,8,128]{2,1,0:T(8,128)S(1)}, f32[2,8,128]{2,1,0:T(8,128)S(1)}, u32[]{:S(2)}, u32[]{:S(2)}) collective-permute-start(f32[2,8,128]{2,1,0:T(8,128)S(1)} %get-tuple-element.23.earlier.refs_4_.refs_2_), channel_id=1, source_target_pairs={{32,0},{64,32},{96,64},{128,96},{160,128},{192,160},{224,192},{256... | collective-permute-start | bytes 24584 | tf_op jit(solution)/shard_map/ppermute | solution.py:366
  66.4 0.0 collective-permute-done.7.inner
  66.4 2.5 %shard_map.44.passed = f32[3,2,8,8,512]{4,3,2,1,0:T(8,128)S(1)} custom-call(s32[3]{0:T(128)S(1)} %copy-done.3, f32[4,8,8,512]{3,2,1,0:T(8,128)S(1)} %get-tuple-element.27.state, f32[4,8,8,512]{3,2,1,0:T(8,128)S(1)} %collective-permute-done.7.inner, f32[4,7,8,8,512]{4,3,2,1,0:T(8,128)S(1)} %get-tuple-element.21.own, f32[3,7,8,8,512]{4,3,2,1,0:T(8,128)S(1)} %shard_map.39.own_inner), custom_call_target="tpu_custom_call" | custom-call | tf_op jit(solution)/shard_map/pallas_call | solution.py:376
  68.9 0.0 collective-permute-done.10.refs_2_.refs_0_
  68.9 0.0 collective-permute-done.9.refs_1_
  68.9 1.8 %collective-permute-done.8.outer = f32[4,8,8,512]{3,2,1,0:T(8,128)S(1)} collective-permute-done((f32[4,8,8,512]{3,2,1,0:T(8,128)S(1)}, f32[4,8,8,512]{3,2,1,0:T(8,128)S(1)}, u32[]{:S(2)}, u32[]{:S(2)}) %collective-permute-start.8) | collective-permute-done | bytes 524320 | tf_op jit(solution)/shard_map/ppermute | solution.py:315
  70.8 3.3 %shard_map.45 = (f32[4,8,8,512]{3,2,1,0:T(8,128)S(1)}, f32[8,4,2,8,128]{4,3,2,1,0:T(8,128)S(1)}) custom-call(s32[3]{0:T(128)S(1)} %copy-done.3, f32[4,8,8,512]{3,2,1,0:T(8,128)S(1)} %get-tuple-element.27.state, f32[3,2,8,8,512]{4,3,2,1,0:T(8,128)S(1)} %shard_map.44.passed, f32[4,8,8,512]{3,2,1,0:T(8,128)S(1)} %collective-permute-done.8.outer, ...), custom_call_target="tpu_custom_call" | custom-call | tf_op jit(solution)/shard_map/pallas_call | solution.py:400
  74.1 1.9 %collective-permute-start.11 = (f32[4,8,8,512]{3,2,1,0:T(8,128)S(1)}, f32[4,8,8,512]{3,2,1,0:T(8,128)S(1)}, u32[]{:S(2)}, u32[]{:S(2)}) collective-permute-start(f32[4,8,8,512]{3,2,1,0:T(8,128)S(1)} %get-tuple-element.29.state), channel_id=1, source_target_pairs={{0,1},{1,0},{2,3},{3,2},{4,5},{5,4},{6,7},{7,6},{8,9},{9,8},{10,11... | collective-permute-start | bytes 1572872 | tf_op jit(solution)/shard_map/ppermute | solution.py:306
  76.0 3.6 %collective-permute-start.12 = (f32[4,8,8,512]{3,2,1,0:T(8,128)S(1)}, f32[4,8,8,512]{3,2,1,0:T(8,128)S(1)}, u32[]{:S(2)}, u32[]{:S(2)}) collective-permute-start(f32[4,8,8,512]{3,2,1,0:T(8,128)S(1)} %get-tuple-element.29.state), channel_id=1, source_target_pairs={{0,31},{1,2},{2,1},{3,4},{4,3},{5,6},{6,5},{7,8},{8,7},{9,10},{10,... | collective-permute-start | bytes 1572872 | tf_op jit(solution)/shard_map/ppermute | solution.py:315
  79.6 5.1 %collective-permute-start.13 = (f32[8,4,2,8,128]{4,3,2,1,0:T(8,128)S(1)}, f32[8,4,2,8,128]{4,3,2,1,0:T(8,128)S(1)}, u32[]{:S(2)}, u32[]{:S(2)}) collective-permute-start(f32[8,4,2,8,128]{4,3,2,1,0:T(8,128)S(1)} %get-tuple-element.30.refs_0_), channel_id=1, source_target_pairs={{0,258},{1,259},{2,256},{3,257},{4,262},{5,263},{6,260},{7,261},{8... | collective-permute-start | bytes 786440 | tf_op jit(solution)/shard_map/ppermute | solution.py:333
  84.8 0.0 collective-permute-done.11.inner
  84.8 2.5 %shard_map.46.passed = f32[3,2,8,8,512]{4,3,2,1,0:T(8,128)S(1)} custom-call(s32[3]{0:T(128)S(1)} %copy-done.3, f32[4,8,8,512]{3,2,1,0:T(8,128)S(1)} %get-tuple-element.29.state, f32[4,8,8,512]{3,2,1,0:T(8,128)S(1)} %collective-permute-done.11.inner, f32[4,7,8,8,512]{4,3,2,1,0:T(8,128)S(1)} %get-tuple-element.21.own, f32[3,7,8,8,512]{4,3,2,1,0:T(8,128)S(1)} %shard_map.39.own_inner), custom_call_target="tpu_custom_call" | custom-call | tf_op jit(solution)/shard_map/pallas_call | solution.py:376
  87.4 3.4 %collective-permute-done.13.refs_1_ = f32[8,4,2,8,128]{4,3,2,1,0:T(8,128)S(1)} collective-permute-done((f32[8,4,2,8,128]{4,3,2,1,0:T(8,128)S(1)}, f32[8,4,2,8,128]{4,3,2,1,0:T(8,128)S(1)}, u32[]{:S(2)}, u32[]{:S(2)}) %collective-permute-start.13) | collective-permute-done | bytes 262176 | tf_op jit(solution)/shard_map/ppermute | solution.py:333
  90.8 1.3 collective-permute-done.12.outer
  92.1 3.3 %shard_map.47 = (f32[4,8,8,512]{3,2,1,0:T(8,128)S(1)}, f32[16,4,2,8,128]{4,3,2,1,0:T(8,128)S(1)}) custom-call(s32[3]{0:T(128)S(1)} %copy-done.3, f32[4,8,8,512]{3,2,1,0:T(8,128)S(1)} %get-tuple-element.29.state, f32[3,2,8,8,512]{4,3,2,1,0:T(8,128)S(1)} %shard_map.46.passed, f32[4,8,8,512]{3,2,1,0:T(8,128)S(1)} %collective-permute-done.12.outer, ...), custom_call_target="tpu_custom_call" | custom-call | tf_op jit(solution)/shard_map/pallas_call | solution.py:400
  95.4 1.9 %collective-permute-start.14 = (f32[4,8,8,512]{3,2,1,0:T(8,128)S(1)}, f32[4,8,8,512]{3,2,1,0:T(8,128)S(1)}, u32[]{:S(2)}, u32[]{:S(2)}) collective-permute-start(f32[4,8,8,512]{3,2,1,0:T(8,128)S(1)} %get-tuple-element.31.state), channel_id=1, source_target_pairs={{0,1},{1,0},{2,3},{3,2},{4,5},{5,4},{6,7},{7,6},{8,9},{9,8},{10,11... | collective-permute-start | bytes 1572872 | tf_op jit(solution)/shard_map/ppermute | solution.py:306
  97.3 2.4 %collective-permute-start.16 = (f32[16,4,2,8,128]{4,3,2,1,0:T(8,128)S(1)}, f32[16,4,2,8,128]{4,3,2,1,0:T(8,128)S(1)}, u32[]{:S(2)}, u32[]{:S(2)}) collective-permute-start(f32[16,4,2,8,128]{4,3,2,1,0:T(8,128)S(1)} %get-tuple-element.32.some), channel_id=1, source_target_pairs={{0,1},{1,0},{2,3},{3,2},{4,5},{5,4},{6,7},{7,6},{8,9},{9,8},{10,11... | collective-permute-start | bytes 1572872 | tf_op jit(solution)/shard_map/ppermute | solution.py:334
  99.7 3.6 %collective-permute-start.15 = (f32[4,8,8,512]{3,2,1,0:T(8,128)S(1)}, f32[4,8,8,512]{3,2,1,0:T(8,128)S(1)}, u32[]{:S(2)}, u32[]{:S(2)}) collective-permute-start(f32[4,8,8,512]{3,2,1,0:T(8,128)S(1)} %get-tuple-element.31.state), channel_id=1, source_target_pairs={{0,31},{1,2},{2,1},{3,4},{4,3},{5,6},{6,5},{7,8},{8,7},{9,10},{10,... | collective-permute-start | bytes 1572872 | tf_op jit(solution)/shard_map/ppermute | solution.py:315
  103.4 0.0 collective-permute-done.14.inner
  103.4 2.5 %shard_map.48.passed = f32[3,2,8,8,512]{4,3,2,1,0:T(8,128)S(1)} custom-call(s32[3]{0:T(128)S(1)} %copy-done.3, f32[4,8,8,512]{3,2,1,0:T(8,128)S(1)} %get-tuple-element.31.state, f32[4,8,8,512]{3,2,1,0:T(8,128)S(1)} %collective-permute-done.14.inner, f32[4,7,8,8,512]{4,3,2,1,0:T(8,128)S(1)} %get-tuple-element.21.own, f32[3,7,8,8,512]{4,3,2,1,0:T(8,128)S(1)} %shard_map.39.own_inner), custom_call_target="tpu_custom_call" | custom-call | tf_op jit(solution)/shard_map/pallas_call | solution.py:376
  106.0 0.0 collective-permute-done.16.others
  106.0 0.7 shard_map.49.refs_1_.weights
  106.7 9.1 %collective-permute-done.15.outer = f32[4,8,8,512]{3,2,1,0:T(8,128)S(1)} collective-permute-done((f32[4,8,8,512]{3,2,1,0:T(8,128)S(1)}, f32[4,8,8,512]{3,2,1,0:T(8,128)S(1)}, u32[]{:S(2)}, u32[]{:S(2)}) %collective-permute-start.15) | collective-permute-done | bytes 524320 | tf_op jit(solution)/shard_map/ppermute | solution.py:315
  115.9 3.4 %shard_map.50 = (f32[4,8,8,512]{3,2,1,0:T(8,128)S(1)}, f32[32,2,8,128]{3,2,1,0:T(8,128)S(1)}) custom-call(s32[3]{0:T(128)S(1)} %copy-done.3, f32[4,8,8,512]{3,2,1,0:T(8,128)S(1)} %get-tuple-element.31.state, f32[3,2,8,8,512]{4,3,2,1,0:T(8,128)S(1)} %shard_map.48.passed, f32[4,8,8,512]{3,2,1,0:T(8,128)S(1)} %collective-permute-done.15.outer, ...), custom_call_target="tpu_custom_call" | custom-call | tf_op jit(solution)/shard_map/pallas_call | solution.py:400
  119.3 19.0 %all_to_all.10.residuals = f32[32,2,8,128]{3,2,1,0:T(8,128)S(1)} all-to-all(f32[32,2,8,128]{3,2,1,0:T(8,128)S(1)} %get-tuple-element.33), channel_id=1, replica_groups=mesh['cuts'=16,'space'=32] {'space'}, dimensions={0} | all-to-all | bytes 524288 | tf_op jit(solution)/shard_map/all_to_all | solution.py:401
  138.3 13.3 %shard_map.51 = f32[16,2,8,128]{3,2,1,0:T(8,128)S(1)} custom-call(s32[3]{0:T(128)S(1)} %copy-done.3, f32[32,2,8,128]{3,2,1,0:T(8,128)S(1)} %all_to_all.10.residuals, f32[32,7,2,8,128]{4,3,2,1,0:T(8,128)S(1)} %shard_map.49.refs_1_.weights), custom_call_target="tpu_custom_call" | custom-call | tf_op jit(solution)/shard_map/pallas_call | solution.py:402
  151.6 13.7 %all_to_all.11.shares = f32[16,2,8,128]{3,2,1,0:T(8,128)S(1)} all-to-all(f32[16,2,8,128]{3,2,1,0:T(8,128)S(1)} %shard_map.51), channel_id=1, replica_groups=mesh['cuts'=16,'space'=32] {'cuts'}, dimensions={0} | all-to-all | bytes 262144 | tf_op jit(solution)/shard_map/all_to_all | solution.py:408
  165.3 1.1 shard_map.52
Async XLA Ops:
  4.2 23.4 %copy-start = (f32[3,4,64,512]{3,2,1,0:T(8,128)S(1)}, f32[3,4,64,512]{3,2,1,0:T(8,128)}, u32[]{:S(2)}) copy-start(f32[3,4,64,512]{3,2,1,0:T(8,128)} %velocity.5) | copy-start | bytes 4718596
  4.2 23.4 %copy-start.1 = (f32[1,4,64,512]{3,2,1,0:T(8,128)S(1)}, f32[1,4,64,512]{3,2,1,0:T(8,128)}, u32[]{:S(2)}) copy-start(f32[1,4,64,512]{3,2,1,0:T(8,128)} %starts.3) | copy-start | bytes 1572868
  4.2 23.4 %copy-start.2 = (f32[4,64,512]{2,1,0:T(8,128)S(1)}, f32[4,64,512]{2,1,0:T(8,128)}, u32[]{:S(2)}) copy-start(f32[4,64,512]{2,1,0:T(8,128)} %diffusivity.5) | copy-start | bytes 1572868
  4.2 29.1 %collective-permute-start.1 = (f32[3,3,64,512]{3,2,1,0:T(8,128)}, f32[3,3,64,512]{3,2,1,0:T(8,128)S(1)}, u32[]{:S(2)}, u32[]{:S(2)}) collective-permute-start(f32[3,3,64,512]{3,2,1,0:T(8,128)} %get-tuple-element.22), channel_id=1, source_target_pairs={{0,1},{1,0},{2,3},{3,2},{4,5},{5,4},{6,7},{7,6},{8,9},{9,8},{10,11... | collective-permute-start | bytes 3538952 | tf_op jit(solution)/shard_map/ppermute | solution.py:306
  9.8 38.8 %collective-permute-start.3 = (f32[3,3,64,512]{3,2,1,0:T(8,128)}, f32[3,3,64,512]{3,2,1,0:T(8,128)S(1)}, u32[]{:S(2)}, u32[]{:S(2)}) collective-permute-start(f32[3,3,64,512]{3,2,1,0:T(8,128)} %get-tuple-element.25), channel_id=1, source_target_pairs={{0,287},{1,258},{2,257},{3,260},{4,259},{5,262},{6,261},{7,264},{8... | collective-permute-start | bytes 3538952 | tf_op jit(solution)/shard_map/ppermute | solution.py:324
  13.3 18.0 %collective-permute-start = (f32[7,64,512]{2,1,0:T(8,128)}, f32[7,64,512]{2,1,0:T(8,128)S(1)}, u32[]{:S(2)}, u32[]{:S(2)}) collective-permute-start(f32[7,64,512]{2,1,0:T(8,128)} %get-tuple-element.20), channel_id=1, source_target_pairs={{0,1},{1,0},{2,3},{3,2},{4,5},{5,4},{6,7},{7,6},{8,9},{9,8},{10,11... | collective-permute-start | bytes 2752520 | tf_op jit(solution)/shard_map/ppermute | solution.py:306
  17.1 31.6 %collective-permute-start.2 = (f32[7,64,512]{2,1,0:T(8,128)}, f32[7,64,512]{2,1,0:T(8,128)S(1)}, u32[]{:S(2)}, u32[]{:S(2)}) collective-permute-start(f32[7,64,512]{2,1,0:T(8,128)} %get-tuple-element.24), channel_id=1, source_target_pairs={{0,31},{1,2},{2,1},{3,4},{4,3},{5,6},{6,5},{7,8},{8,7},{9,10},{10,... | collective-permute-start | bytes 2752520 | tf_op jit(solution)/shard_map/ppermute | solution.py:315
  28.9 20.4 %collective-permute-start.6 = (f32[1,4,2,8,128]{4,3,2,1,0:T(8,128)S(1)}, f32[1,4,2,8,128]{4,3,2,1,0:T(8,128)S(1)}, u32[]{:S(2)}, u32[]{:S(2)}) collective-permute-start(f32[1,4,2,8,128]{4,3,2,1,0:T(8,128)S(1)} %bitcast.8), channel_id=1, source_target_pairs={{0,24},{1,25},{2,26},{3,27},{4,28},{5,29},{6,30},{7,31},{8,16},{9,... | collective-permute-start | bytes 98312 | tf_op jit(solution)/shard_map/ppermute | solution.py:334
  31.3 17.9 %collective-permute-start.5 = (f32[1,4,2,8,128]{4,3,2,1,0:T(8,128)S(1)}, f32[1,4,2,8,128]{4,3,2,1,0:T(8,128)S(1)}, u32[]{:S(2)}, u32[]{:S(2)}) collective-permute-start(f32[1,4,2,8,128]{4,3,2,1,0:T(8,128)S(1)} %bitcast.9), channel_id=1, source_target_pairs={{0,16},{1,17},{2,18},{3,19},{4,20},{5,21},{6,22},{7,23},{8,24},{9,... | collective-permute-start | bytes 98312 | tf_op jit(solution)/shard_map/ppermute | solution.py:334
  33.3 16.0 %collective-permute-start.4 = (f32[1,4,2,8,128]{4,3,2,1,0:T(8,128)S(1)}, f32[1,4,2,8,128]{4,3,2,1,0:T(8,128)S(1)}, u32[]{:S(2)}, u32[]{:S(2)}) collective-permute-start(f32[1,4,2,8,128]{4,3,2,1,0:T(8,128)S(1)} %bitcast.10), channel_id=1, source_target_pairs={{0,8},{1,9},{2,10},{3,11},{4,12},{5,13},{6,14},{7,15},{8,0},{9,1},... | collective-permute-start | bytes 98312 | tf_op jit(solution)/shard_map/ppermute | solution.py:334
  41.1 0.7 copy-start.3
  52.7 13.6 %collective-permute-start.7 = (f32[4,8,8,512]{3,2,1,0:T(8,128)S(1)}, f32[4,8,8,512]{3,2,1,0:T(8,128)S(1)}, u32[]{:S(2)}, u32[]{:S(2)}) collective-permute-start(f32[4,8,8,512]{3,2,1,0:T(8,128)S(1)} %get-tuple-element.27.state), channel_id=1, source_target_pairs={{0,1},{1,0},{2,3},{3,2},{4,5},{5,4},{6,7},{7,6},{8,9},{9,8},{10,11... | collective-permute-start | bytes 1572872 | tf_op jit(solution)/shard_map/ppermute | solution.py:306
  54.7 16.1 %collective-permute-start.8 = (f32[4,8,8,512]{3,2,1,0:T(8,128)S(1)}, f32[4,8,8,512]{3,2,1,0:T(8,128)S(1)}, u32[]{:S(2)}, u32[]{:S(2)}) collective-permute-start(f32[4,8,8,512]{3,2,1,0:T(8,128)S(1)} %get-tuple-element.27.state), channel_id=1, source_target_pairs={{0,31},{1,2},{2,1},{3,4},{4,3},{5,6},{6,5},{7,8},{8,7},{9,10},{10,... | collective-permute-start | bytes 1572872 | tf_op jit(solution)/shard_map/ppermute | solution.py:315
  58.3 10.6 %collective-permute-start.9 = (f32[4,4,2,8,128]{4,3,2,1,0:T(8,128)S(1)}, f32[4,4,2,8,128]{4,3,2,1,0:T(8,128)S(1)}, u32[]{:S(2)}, u32[]{:S(2)}) collective-permute-start(f32[4,4,2,8,128]{4,3,2,1,0:T(8,128)S(1)} %get-tuple-element.28.refs_0_), channel_id=1, source_target_pairs={{0,4},{1,5},{2,6},{3,7},{4,0},{5,1},{6,2},{7,3},{8,12},{9,13},{10,... | collective-permute-start | bytes 393224 | tf_op jit(solution)/shard_map/ppermute | solution.py:334
  61.3 7.6 %collective-permute-start.10 = (f32[2,8,128]{2,1,0:T(8,128)S(1)}, f32[2,8,128]{2,1,0:T(8,128)S(1)}, u32[]{:S(2)}, u32[]{:S(2)}) collective-permute-start(f32[2,8,128]{2,1,0:T(8,128)S(1)} %get-tuple-element.23.earlier.refs_4_.refs_2_), channel_id=1, source_target_pairs={{32,0},{64,32},{96,64},{128,96},{160,128},{192,160},{224,192},{256... | collective-permute-start | bytes 24584 | tf_op jit(solution)/shard_map/ppermute | solution.py:366
  74.1 10.7 %collective-permute-start.11 = (f32[4,8,8,512]{3,2,1,0:T(8,128)S(1)}, f32[4,8,8,512]{3,2,1,0:T(8,128)S(1)}, u32[]{:S(2)}, u32[]{:S(2)}) collective-permute-start(f32[4,8,8,512]{3,2,1,0:T(8,128)S(1)} %get-tuple-element.29.state), channel_id=1, source_target_pairs={{0,1},{1,0},{2,3},{3,2},{4,5},{5,4},{6,7},{7,6},{8,9},{9,8},{10,11... | collective-permute-start | bytes 1572872 | tf_op jit(solution)/shard_map/ppermute | solution.py:306
  76.0 16.1 %collective-permute-start.12 = (f32[4,8,8,512]{3,2,1,0:T(8,128)S(1)}, f32[4,8,8,512]{3,2,1,0:T(8,128)S(1)}, u32[]{:S(2)}, u32[]{:S(2)}) collective-permute-start(f32[4,8,8,512]{3,2,1,0:T(8,128)S(1)} %get-tuple-element.29.state), channel_id=1, source_target_pairs={{0,31},{1,2},{2,1},{3,4},{4,3},{5,6},{6,5},{7,8},{8,7},{9,10},{10,... | collective-permute-start | bytes 1572872 | tf_op jit(solution)/shard_map/ppermute | solution.py:315
  79.6 11.2 %collective-permute-start.13 = (f32[8,4,2,8,128]{4,3,2,1,0:T(8,128)S(1)}, f32[8,4,2,8,128]{4,3,2,1,0:T(8,128)S(1)}, u32[]{:S(2)}, u32[]{:S(2)}) collective-permute-start(f32[8,4,2,8,128]{4,3,2,1,0:T(8,128)S(1)} %get-tuple-element.30.refs_0_), channel_id=1, source_target_pairs={{0,258},{1,259},{2,256},{3,257},{4,262},{5,263},{6,260},{7,261},{8... | collective-permute-start | bytes 786440 | tf_op jit(solution)/shard_map/ppermute | solution.py:333
  95.4 8.0 %collective-permute-start.14 = (f32[4,8,8,512]{3,2,1,0:T(8,128)S(1)}, f32[4,8,8,512]{3,2,1,0:T(8,128)S(1)}, u32[]{:S(2)}, u32[]{:S(2)}) collective-permute-start(f32[4,8,8,512]{3,2,1,0:T(8,128)S(1)} %get-tuple-element.31.state), channel_id=1, source_target_pairs={{0,1},{1,0},{2,3},{3,2},{4,5},{5,4},{6,7},{7,6},{8,9},{9,8},{10,11... | collective-permute-start | bytes 1572872 | tf_op jit(solution)/shard_map/ppermute | solution.py:306
  97.3 8.6 %collective-permute-start.16 = (f32[16,4,2,8,128]{4,3,2,1,0:T(8,128)S(1)}, f32[16,4,2,8,128]{4,3,2,1,0:T(8,128)S(1)}, u32[]{:S(2)}, u32[]{:S(2)}) collective-permute-start(f32[16,4,2,8,128]{4,3,2,1,0:T(8,128)S(1)} %get-tuple-element.32.some), channel_id=1, source_target_pairs={{0,1},{1,0},{2,3},{3,2},{4,5},{5,4},{6,7},{7,6},{8,9},{9,8},{10,11... | collective-permute-start | bytes 1572872 | tf_op jit(solution)/shard_map/ppermute | solution.py:334
  99.7 16.1 %collective-permute-start.15 = (f32[4,8,8,512]{3,2,1,0:T(8,128)S(1)}, f32[4,8,8,512]{3,2,1,0:T(8,128)S(1)}, u32[]{:S(2)}, u32[]{:S(2)}) collective-permute-start(f32[4,8,8,512]{3,2,1,0:T(8,128)S(1)} %get-tuple-element.31.state), channel_id=1, source_target_pairs={{0,31},{1,2},{2,1},{3,4},{4,3},{5,6},{6,5},{7,8},{8,7},{9,10},{10,... | collective-permute-start | bytes 1572872 | tf_op jit(solution)/shard_map/ppermute | solution.py:315

commit v7 on v6

--- a/solution.py
+++ b/solution.py
@@ -122,7 +122,7 @@
                 coarse_old[h] = mean
 
 
-def side_kernel(velocity, mixed, earlier, weights, buffer):
+def side_kernel(velocity, mixed, weights, buffer):
     def layer(x, carry):
         for f in range(3):
             spread(velocity[f, x], buffer.at[f])
@@ -136,56 +136,43 @@
     lax.fori_loop(0, REACH, layer, 0)
 
 
-def fine_layer(source, weights, target, x, wx, tx):
-    first, last = source[x, 0], source[x, 7]
-    behind, now = pltpu.roll(last, 1, 0), first
+def fine_layers(source, weights, target, x, wx, tx, depth):
+    firsts = [source[x + i, 0] for i in range(depth)]
+    lasts = [source[x + i, 7] for i in range(depth)]
+    behind = [pltpu.roll(last, 1, 0) for last in lasts]
+    now = firsts
     for j in range(8):
-        ahead = pltpu.roll(first, 7, 0) if j == 7 else last if j == 6 else source[x, j + 1]
-        target[tx, j] = (
-            (weights[wx, 0, j] * now + weights[wx, 1, j] * source[x - 1, j])
-            + (weights[wx, 2, j] * source[x + 1, j] + weights[wx, 3, j] * behind)
-            + (weights[wx, 4, j] * ahead + weights[wx, 5, j] * pltpu.roll(now, 1, 1))
-            + weights[wx, 6, j] * pltpu.roll(now, 511, 1)
-        )
+        below, above = source[x - 1, j], source[x + depth, j]
+        column = [below, *now, above]
+        ahead = []
+        for i in range(depth):
+            if j == 7:
+                ahead.append(pltpu.roll(firsts[i], 7, 0))
+            else:
+                ahead.append(lasts[i] if j == 6 else source[x + i, j + 1])
+        for i in range(depth):
+            target[tx + i, j] = (
+                (weights[wx + i, 0, j] * now[i] + weights[wx + i, 1, j] * column[i])
+                + (weights[wx + i, 2, j] * column[i + 2] + weights[wx + i, 3, j] * behind[i])
+                + (weights[wx + i, 4, j] * ahead[i] + weights[wx + i, 5, j] * pltpu.roll(now[i], 1, 1))
+                + weights[wx + i, 6, j] * pltpu.roll(now[i], 511, 1)
+            )
         behind, now = now, ahead
 
 
-def enter(one, blocks, raw, buffer):
-    def layer(x, carry):
-        for i, (ref, begin) in enumerate(blocks):
-            if raw:
-                spread(ref[x], buffer.at[i])
-            for j in range(8):
-                one[begin + x, j] = spread_tile(buffer.at[i], j) if raw else ref[x, j]
+def sweep(source, goal, begin, count, weights, first, shift=0):
+    def pair(i, carry):
+        fine_layers(source, weights, goal, begin + 2 * i, first + 2 * i, begin + 2 * i - shift, 2)
         return carry
 
-    lax.fori_loop(0, LAYERS, layer, 0)
-
-
-def sweep(source, goal, begin, count, weights, first, shift=0):
-    def body(i, carry):
-        fine_layer(source, weights, goal, begin + i, first + i, begin + i - shift)
-        return carry
-
-    lax.fori_loop(0, count, body, 0)
-
-
-def inner_kernel(raw, place, state, inner, own, own_inner, passed, one, two, buffer):
-    core = place[2]
-    enter(one, ((state, LAYERS), (inner, 2 * LAYERS * (1 - core))), raw, buffer)
-    source, target = one, two
-    for step in range(1, LAYERS):
-        count = LAYERS - step
-        sweep(source, target, LAYERS + (1 - core) * step, count, own, (1 - core) * step)
-        above, below = 2 * LAYERS, step
-        sweep(source, target, above - core * (above - below), count, own_inner, core * (step - 1))
-        for i in range(2):
-            on_first, on_second = LAYERS + step + i, 2 * LAYERS - 1 - step - i
-            passed[step - 1, i] = target[on_first - core * (on_first - on_second)]
-        source, target = target, source
-
-
-def outer_kernel(raw, final, place, state, passed, outer, own, own_outer, *refs):
+    if count > 1:
+        lax.fori_loop(0, count // 2, pair, 0)
+    if count % 2:
+        last = count - 1
+        fine_layers(source, weights, goal, begin + last, first + last, begin + last - shift, 1)
+
+
+def round_kernel(raw, final, place, state, outer, inner, own, own_outer, own_inner, *refs):
     if final:
         later, after, out, residual, one, two, buffer = refs
     else:
@@ -195,21 +182,27 @@
             joined[begin : begin + part.shape[0]] = part[...]
             begin += part.shape[0]
     core = place[2]
-    enter(one, ((state, LAYERS), (outer, 2 * LAYERS * core)), raw, buffer)
+
+    def enter(x, carry):
+        blocks = ((state, LAYERS), (outer, 2 * LAYERS * core), (inner, 2 * LAYERS * (1 - core)))
+        for i, (ref, begin) in enumerate(blocks):
+            if raw:
+                spread(ref[x], buffer.at[i])
+            for j in range(8):
+                one[begin + x, j] = spread_tile(buffer.at[i], j) if raw else ref[x, j]
+        return carry
+
+    lax.fori_loop(0, LAYERS, enter, 0)
     source, target = one, two
     for step in range(1, LAYERS + 1):
         ends = step == LAYERS
         goal = out if ends else target
-        shift = LAYERS if ends else 0
-        count = LAYERS - step
-        if count:
+        depth = LAYERS - step
+        sweep(source, goal, LAYERS, LAYERS, own, 0, LAYERS if ends else 0)
+        if depth > 0:
             below, above = step, 2 * LAYERS
-            sweep(source, goal, below + core * (above - below), count, own_outer, (1 - core) * (step - 1))
-        sweep(source, goal, LAYERS + core * count, step, own, core * count, shift)
-        if not ends:
-            for i in range(2):
-                on_first, on_second = LAYERS + step + i, 2 * LAYERS - 1 - step - i
-                target[on_first - core * (on_first - on_second)] = passed[step - 1, i]
+            sweep(source, goal, below + core * (above - below), depth, own_outer, (1 - core) * (step - 1))
+            sweep(source, goal, above - core * (above - below), depth, own_inner, core * (step - 1))
         source, target = target, source
     if final:
         sums = half_sums(lambda j: (out[0, j] + out[1, j]) + (out[2, j] + out[3, j]))
@@ -348,7 +341,6 @@
             [(3, REACH, 64, 512), (LAYERS + REACH, 64, 512)],
             [SMEM, ANY, ANY, ANY],
             [pltpu.SemaphoreType.DMA((3,))],
-            limit=60,
         )(place, velocity, diffusivity, starts)
 
     fields_outer, mixed_outer = cut(True)
@@ -365,23 +357,18 @@
     )(velocity, diffusivity, starts[0])
     coarse_later = lax.ppermute(coarse_old, "cuts", [((n + 1) % slices, n) for n in range(slices)])
     gathered = coarse_fields[None]
-    weigh_side = call(side_kernel, [(REACH, 7, *TILE)], [VMEM, VMEM, ANY], [columns])
-    inner_weights = weigh_side(fields_inner, mixed_inner, coarse_old)[0]
+    outer_weights, inner_weights = [
+        call(side_kernel, [(REACH, 7, *TILE)], [VMEM, VMEM], [columns])(*halos)[0]
+        for halos in ((fields_outer, mixed_outer), (fields_inner, mixed_inner))
+    ]
     state, inner, outer = starts[0], mixed_inner, mixed_outer
     scratch = [pltpu.VMEM((3 * LAYERS, *TILE), F32)] * 2 + [columns]
     for index in range(ROUNDS):
         raw, final = index == 0, index == ROUNDS - 1
         if index > 0:
             inner, outer = swap_inner(state), swap_outer(state)
-        passed = call(
-            functools.partial(inner_kernel, raw),
-            [(LAYERS - 1, 2, *TILE)],
-            [SMEM] + [VMEM] * 4,
-            scratch,
-        )(place, state, inner, own_weights, inner_weights)[0]
-        if raw:
-            outer_weights = weigh_side(fields_outer, mixed_outer, passed)[0]
-        operands = [place, state, passed, outer, own_weights, outer_weights]
+        operands = [place, state, outer, inner, own_weights, outer_weights, inner_weights]
+        specs = [SMEM] + [VMEM] * 6
         if final:
             weights = call(
                 coarse_weight_kernel,
@@ -389,15 +376,15 @@
                 [SMEM, VMEM, VMEM],
             )(place, gathered, across(gathered, 1))[0]
             operands += [coarse_later, weights]
-            specs = [SMEM] + [VMEM] * 6 + [ANY]
+            specs += [VMEM, ANY]
             outs = [block, (count, *COARSE)]
         else:
             bits = ((8, 16, 24), (4,), (2,))[index]
             parts = [gathered] + [across(gathered, b) for b in bits]
             operands += parts + [coarse_later if index == 1 else coarse_old]
-            specs = [SMEM] + [VMEM] * (5 + len(parts)) + [ANY]
+            specs += [VMEM] * len(parts) + [ANY]
             outs = [block, (len(parts) * gathered.shape[0], 4, *COARSE)]
-        state, gathered = call(functools.partial(outer_kernel, raw, final), outs, specs, scratch)(*operands)
+        state, gathered = call(functools.partial(round_kernel, raw, final), outs, specs, scratch)(*operands)
     residuals = lax.all_to_all(gathered, "space", 0, 0)
     shares = call(
         chain_kernel,

time: 167 us -> 167 us (level)
  waiting for transfers between devices: 19.8 us -> 39.8 us
  Pallas kernels: 48.5 us -> 35.6 us
  starting transfers between devices: 64.2 us -> 56.6 us
  local copies, waits for them, and re-layouts: 0.11 us -> 3.5 us
  blocking collectives: 32.6 us -> 30.7 us
    ppermute x4, waiting for transfers between devices: 16.4 us -> 26.1 us  [swap_outer(): lax.ppermute(block, 'space', [(p, outer_partner(p, count)) for p in range...]
    pallas_call x10 -> x6, Pallas kernels: 25 us -> 17.4 us  [the longest x4 16.3 us: shards(): call(functools.partial(round_kernel, raw, final), outs, specs, scratch)]
    pallas_call x2, Pallas kernels: 7.05 us -> 1.76 us  [cut(): call(functools.partial(cut_kernel, outer=outer), [(3, REACH, 64, 512), (L...]
    ppermute x5, waiting for transfers between devices: 0.01 us -> 4.83 us  [across(): return lax.ppermute(block, 'space', [(p, p ^ bits) for p in range(count)])]
    ppermute x5, starting transfers between devices: 17.6 us -> 13.5 us  [across(): return lax.ppermute(block, 'space', [(p, p ^ bits) for p in range(count)])]
    ppermute x1, waiting for transfers between devices: 3.44 us -> 7.46 us  [across(): return lax.ppermute(block, ('cuts', 'space'), route)]
    ppermute x4, starting transfers between devices: 21.4 us -> 17.6 us  [swap_outer(): lax.ppermute(block, 'space', [(p, outer_partner(p, count)) for p in range...]
    unnamed x8, local copies, waits for them, and re-layouts: 0.11 us -> 3.5 us
  transfers between devices with their start and end apart: 17 -> 17, of which waited for: 5 -> 7; matrix products, arithmetic and copies ran while one was open for 0% -> 0% of each run, Pallas kernels for 10% -> 2%
where the time goes in v7:
time: 167 us
  starting transfers between devices  56.6 us (34%)
  waiting for transfers between devices  39.8 us (24%)
  Pallas kernels  35.6 us (21%)
  blocking collectives  30.7 us (18%)
  local copies, waits for them, and re-layouts  3.5 us (2%)
    ppermute x4, waiting for transfers between devices, swap_outer(): lax.ppermute(block, 'space', [(p, outer_partner(p, count)) for p in range...  26.1 us
    ppermute x4, starting transfers between devices, swap_outer(): lax.ppermute(block, 'space', [(p, outer_partner(p, count)) for p in range...  17.6 us
    all_to_all x1, blocking collectives, shards(): residuals = lax.all_to_all(gathered, 'space', 0, 0)  17.6 us
    pallas_call x4, Pallas kernels, shards(): call(functools.partial(round_kernel, raw, final), outs, specs, scratch)  16.3 us
    ppermute x5, starting transfers between devices, across(): return lax.ppermute(block, 'space', [(p, p ^ bits) for p in range(count)])  13.5 us
    ppermute x5, starting transfers between devices, swap_inner(): return lax.ppermute(block, 'space', [(p, p ^ 1) for p in range(count)])  13.3 us
    pallas_call x1, Pallas kernels, shards(): call(chain_kernel, [(slices, *COARSE)], [SMEM, VMEM, VMEM], [pltpu.VMEM((...  13.3 us
    all_to_all x1, blocking collectives, shards(): shares = lax.all_to_all(shares, 'cuts', 0, 0)  13.1 us
  transfers between devices with their start and end apart: 17, of which 7 were waited for; matrix products, arithmetic and copies ran while one was open for 0% of the time, Pallas kernels for 2%

profile of v7, /device:TPU:2, one launch (start us, length us, event | category | flops | bytes accessed | tf_op | source)
XLA Modules:
  0.0 166.5 jit_solution(4699499019992498207)
XLA Ops:
  0.0 0.1 pad_add_fusion.place
  0.1 0.0 copy-start
  0.1 1.4 copy-done
  1.5 0.0 copy-start.2
  1.5 1.0 copy-done.2
  2.5 0.0 copy-start.3
  2.5 1.0 copy-done.3
  3.6 0.9 shard_map.37
  4.5 0.0 copy-start.1
  4.5 3.0 %collective-permute-start.2 = (f32[3,3,64,512]{3,2,1,0:T(8,128)S(1)}, f32[3,3,64,512]{3,2,1,0:T(8,128)S(1)}, u32[]{:S(2)}, u32[]{:S(2)}) collective-permute-start(f32[3,3,64,512]{3,2,1,0:T(8,128)S(1)} %get-tuple-element.23), channel_id=1, source_target_pairs={{0,287},{1,258},{2,257},{3,260},{4,259},{5,262},{6,261},{7,264},{8... | collective-permute-start | bytes 3538952 | tf_op jit(solution)/shard_map/ppermute | solution.py:317
  7.4 0.9 shard_map.38
  8.3 4.4 %collective-permute-start.3 = (f32[3,3,64,512]{3,2,1,0:T(8,128)S(1)}, f32[3,3,64,512]{3,2,1,0:T(8,128)S(1)}, u32[]{:S(2)}, u32[]{:S(2)}) collective-permute-start(f32[3,3,64,512]{3,2,1,0:T(8,128)S(1)} %get-tuple-element.24), channel_id=1, source_target_pairs={{0,1},{1,0},{2,3},{3,2},{4,5},{5,4},{6,7},{7,6},{8,9},{9,8},{10,11... | collective-permute-start | bytes 3538952 | tf_op jit(solution)/shard_map/ppermute | solution.py:299
  12.7 9.8 %collective-permute-start = (f32[7,64,512]{2,1,0:T(8,128)S(1)}, f32[7,64,512]{2,1,0:T(8,128)S(1)}, u32[]{:S(2)}, u32[]{:S(2)}) collective-permute-start(f32[7,64,512]{2,1,0:T(8,128)S(1)} %get-tuple-element.20), channel_id=1, source_target_pairs={{0,31},{1,2},{2,1},{3,4},{4,3},{5,6},{6,5},{7,8},{8,7},{9,10},{10,... | collective-permute-start | bytes 2752520 | tf_op jit(solution)/shard_map/ppermute | solution.py:308
  22.6 1.9 %collective-permute-start.1 = (f32[7,64,512]{2,1,0:T(8,128)S(1)}, f32[7,64,512]{2,1,0:T(8,128)S(1)}, u32[]{:S(2)}, u32[]{:S(2)}) collective-permute-start(f32[7,64,512]{2,1,0:T(8,128)S(1)} %get-tuple-element.21), channel_id=1, source_target_pairs={{0,1},{1,0},{2,3},{3,2},{4,5},{5,4},{6,7},{7,6},{8,9},{9,8},{10,11... | collective-permute-start | bytes 2752520 | tf_op jit(solution)/shard_map/ppermute | solution.py:299
  24.5 0.0 copy-done.1
  24.5 1.3 shard_map.39
  25.8 1.9 %collective-permute-start.4 = (f32[1,4,2,8,128]{4,3,2,1,0:T(8,128)S(1)}, f32[1,4,2,8,128]{4,3,2,1,0:T(8,128)S(1)}, u32[]{:S(2)}, u32[]{:S(2)}) collective-permute-start(f32[1,4,2,8,128]{4,3,2,1,0:T(8,128)S(1)} %bitcast.7), channel_id=1, source_target_pairs={{0,8},{1,9},{2,10},{3,11},{4,12},{5,13},{6,14},{7,15},{8,0},{9,1},... | collective-permute-start | bytes 98312 | tf_op jit(solution)/shard_map/ppermute | solution.py:327
  27.7 15.7 %collective-permute-done.mixed.outer = f32[7,64,512]{2,1,0:T(8,128)S(1)} collective-permute-done((f32[7,64,512]{2,1,0:T(8,128)S(1)}, f32[7,64,512]{2,1,0:T(8,128)S(1)}, u32[]{:S(2)}, u32[]{:S(2)}) %collective-permute-start) | collective-permute-done | bytes 917536 | tf_op jit(solution)/shard_map/ppermute | solution.py:308
  43.5 3.8 %collective-permute-start.5 = (f32[1,4,2,8,128]{4,3,2,1,0:T(8,128)S(1)}, f32[1,4,2,8,128]{4,3,2,1,0:T(8,128)S(1)}, u32[]{:S(2)}, u32[]{:S(2)}) collective-permute-start(f32[1,4,2,8,128]{4,3,2,1,0:T(8,128)S(1)} %bitcast.8), channel_id=1, source_target_pairs={{0,16},{1,17},{2,18},{3,19},{4,20},{5,21},{6,22},{7,23},{8,24},{9,... | collective-permute-start | bytes 98312 | tf_op jit(solution)/shard_map/ppermute | solution.py:327
  47.3 0.0 collective-permute-done.2.velocity
  47.3 1.9 %collective-permute-start.6 = (f32[1,4,2,8,128]{4,3,2,1,0:T(8,128)S(1)}, f32[1,4,2,8,128]{4,3,2,1,0:T(8,128)S(1)}, u32[]{:S(2)}, u32[]{:S(2)}) collective-permute-start(f32[1,4,2,8,128]{4,3,2,1,0:T(8,128)S(1)} %bitcast.9), channel_id=1, source_target_pairs={{0,24},{1,25},{2,26},{3,27},{4,28},{5,29},{6,30},{7,31},{8,16},{9,... | collective-permute-start | bytes 98312 | tf_op jit(solution)/shard_map/ppermute | solution.py:327
  49.3 0.6 shard_map.40.own_outer
  49.8 0.0 collective-permute-done.1.mixed.inner
  49.8 0.0 collective-permute-done.3.velocity
  49.8 0.6 shard_map.41.own_inner
  50.4 0.0 collective-permute-done.4.refs_1_
  50.4 2.7 %collective-permute-done.5.refs_2_ = f32[1,4,2,8,128]{4,3,2,1,0:T(8,128)S(1)} collective-permute-done((f32[1,4,2,8,128]{4,3,2,1,0:T(8,128)S(1)}, f32[1,4,2,8,128]{4,3,2,1,0:T(8,128)S(1)}, u32[]{:S(2)}, u32[]{:S(2)}) %collective-permute-start.5) | collective-permute-done | bytes 32800 | tf_op jit(solution)/shard_map/ppermute | solution.py:327
  53.2 2.1 %collective-permute-done.6.refs_3_ = f32[1,4,2,8,128]{4,3,2,1,0:T(8,128)S(1)} collective-permute-done((f32[1,4,2,8,128]{4,3,2,1,0:T(8,128)S(1)}, f32[1,4,2,8,128]{4,3,2,1,0:T(8,128)S(1)}, u32[]{:S(2)}, u32[]{:S(2)}) %collective-permute-start.6) | collective-permute-done | bytes 32800 | tf_op jit(solution)/shard_map/ppermute | solution.py:327
  55.3 4.3 %shard_map.42 = (f32[4,8,8,512]{3,2,1,0:T(8,128)S(1)}, f32[4,4,2,8,128]{4,3,2,1,0:T(8,128)S(1)}) custom-call(s32[3]{0:T(128)S(1)} %pad_add_fusion.place, f32[4,64,512]{2,1,0:T(8,128)S(1)} %bitcast.6, f32[7,64,512]{2,1,0:T(8,128)S(1)} %collective-permute-done.mixed.outer, f32[7,64,512]{2,1,0:T(8,128)S(1)} %collective-permute-done.1.mixed.inner, ...), custom_call_target="tpu_custom_call" | custom-call | tf_op jit(solution)/shard_map/pallas_call | solution.py:387
  59.5 1.9 %collective-permute-start.7 = (f32[4,8,8,512]{3,2,1,0:T(8,128)S(1)}, f32[4,8,8,512]{3,2,1,0:T(8,128)S(1)}, u32[]{:S(2)}, u32[]{:S(2)}) collective-permute-start(f32[4,8,8,512]{3,2,1,0:T(8,128)S(1)} %get-tuple-element.27.state), channel_id=1, source_target_pairs={{0,31},{1,2},{2,1},{3,4},{4,3},{5,6},{6,5},{7,8},{8,7},{9,10},{10,... | collective-permute-start | bytes 1572872 | tf_op jit(solution)/shard_map/ppermute | solution.py:308
  61.5 1.9 %collective-permute-start.8 = (f32[4,8,8,512]{3,2,1,0:T(8,128)S(1)}, f32[4,8,8,512]{3,2,1,0:T(8,128)S(1)}, u32[]{:S(2)}, u32[]{:S(2)}) collective-permute-start(f32[4,8,8,512]{3,2,1,0:T(8,128)S(1)} %get-tuple-element.27.state), channel_id=1, source_target_pairs={{0,1},{1,0},{2,3},{3,2},{4,5},{5,4},{6,7},{7,6},{8,9},{9,8},{10,11... | collective-permute-start | bytes 1572872 | tf_op jit(solution)/shard_map/ppermute | solution.py:299
  63.4 3.9 %collective-permute-start.9 = (f32[4,4,2,8,128]{4,3,2,1,0:T(8,128)S(1)}, f32[4,4,2,8,128]{4,3,2,1,0:T(8,128)S(1)}, u32[]{:S(2)}, u32[]{:S(2)}) collective-permute-start(f32[4,4,2,8,128]{4,3,2,1,0:T(8,128)S(1)} %get-tuple-element.28.refs_0_), channel_id=1, source_target_pairs={{0,4},{1,5},{2,6},{3,7},{4,0},{5,1},{6,2},{7,3},{8,12},{9,13},{10,... | collective-permute-start | bytes 393224 | tf_op jit(solution)/shard_map/ppermute | solution.py:327
  67.2 6.6 %collective-permute-start.10 = (f32[2,8,128]{2,1,0:T(8,128)S(1)}, f32[2,8,128]{2,1,0:T(8,128)S(1)}, u32[]{:S(2)}, u32[]{:S(2)}) collective-permute-start(f32[2,8,128]{2,1,0:T(8,128)S(1)} %get-tuple-element.26.refs_4_.refs_2_), channel_id=1, source_target_pairs={{32,0},{64,32},{96,64},{128,96},{160,128},{192,160},{224,192},{256... | collective-permute-start | bytes 24584 | tf_op jit(solution)/shard_map/ppermute | solution.py:358
  73.8 1.3 collective-permute-done.10.refs_2_.refs_0_
  75.2 0.0 collective-permute-done.9.refs_1_
  75.2 0.0 collective-permute-done.7.outer
  75.2 0.0 collective-permute-done.8.inner
  75.2 4.0 %shard_map.43 = (f32[4,8,8,512]{3,2,1,0:T(8,128)S(1)}, f32[8,4,2,8,128]{4,3,2,1,0:T(8,128)S(1)}) custom-call(s32[3]{0:T(128)S(1)} %pad_add_fusion.place, f32[4,8,8,512]{3,2,1,0:T(8,128)S(1)} %get-tuple-element.27.state, f32[4,8,8,512]{3,2,1,0:T(8,128)S(1)} %collective-permute-done.7.outer, f32[4,8,8,512]{3,2,1,0:T(8,128)S(1)} %collective-permute-done.8.inner, ...), custom_call_target="tpu_custom_call" | custom-call | tf_op jit(solution)/shard_map/pallas_call | solution.py:387
  79.2 2.4 %collective-permute-start.11 = (f32[4,8,8,512]{3,2,1,0:T(8,128)S(1)}, f32[4,8,8,512]{3,2,1,0:T(8,128)S(1)}, u32[]{:S(2)}, u32[]{:S(2)}) collective-permute-start(f32[4,8,8,512]{3,2,1,0:T(8,128)S(1)} %get-tuple-element.29.state), channel_id=1, source_target_pairs={{0,31},{1,2},{2,1},{3,4},{4,3},{5,6},{6,5},{7,8},{8,7},{9,10},{10,... | collective-permute-start | bytes 1572872 | tf_op jit(solution)/shard_map/ppermute | solution.py:308
  81.5 3.1 %collective-permute-start.12 = (f32[4,8,8,512]{3,2,1,0:T(8,128)S(1)}, f32[4,8,8,512]{3,2,1,0:T(8,128)S(1)}, u32[]{:S(2)}, u32[]{:S(2)}) collective-permute-start(f32[4,8,8,512]{3,2,1,0:T(8,128)S(1)} %get-tuple-element.29.state), channel_id=1, source_target_pairs={{0,1},{1,0},{2,3},{3,2},{4,5},{5,4},{6,7},{7,6},{8,9},{9,8},{10,11... | collective-permute-start | bytes 1572872 | tf_op jit(solution)/shard_map/ppermute | solution.py:299
  84.7 2.7 %collective-permute-start.13 = (f32[8,4,2,8,128]{4,3,2,1,0:T(8,128)S(1)}, f32[8,4,2,8,128]{4,3,2,1,0:T(8,128)S(1)}, u32[]{:S(2)}, u32[]{:S(2)}) collective-permute-start(f32[8,4,2,8,128]{4,3,2,1,0:T(8,128)S(1)} %get-tuple-element.30.refs_0_), channel_id=1, source_target_pairs={{0,258},{1,259},{2,256},{3,257},{4,262},{5,263},{6,260},{7,261},{8... | collective-permute-start | bytes 786440 | tf_op jit(solution)/shard_map/ppermute | solution.py:326
  87.3 7.5 %collective-permute-done.13.refs_1_ = f32[8,4,2,8,128]{4,3,2,1,0:T(8,128)S(1)} collective-permute-done((f32[8,4,2,8,128]{4,3,2,1,0:T(8,128)S(1)}, f32[8,4,2,8,128]{4,3,2,1,0:T(8,128)S(1)}, u32[]{:S(2)}, u32[]{:S(2)}) %collective-permute-start.13) | collective-permute-done | bytes 262176 | tf_op jit(solution)/shard_map/ppermute | solution.py:326
  94.8 0.5 collective-permute-done.11.outer
  95.3 0.0 collective-permute-done.12.inner
  95.3 4.0 %shard_map.44 = (f32[4,8,8,512]{3,2,1,0:T(8,128)S(1)}, f32[16,4,2,8,128]{4,3,2,1,0:T(8,128)S(1)}) custom-call(s32[3]{0:T(128)S(1)} %pad_add_fusion.place, f32[4,8,8,512]{3,2,1,0:T(8,128)S(1)} %get-tuple-element.29.state, f32[4,8,8,512]{3,2,1,0:T(8,128)S(1)} %collective-permute-done.11.outer, f32[4,8,8,512]{3,2,1,0:T(8,128)S(1)} %collective-permute-done.12.inner, ...), custom_call_target="tpu_custom_call" | custom-call | tf_op jit(solution)/shard_map/pallas_call | solution.py:387
  99.3 1.9 %collective-permute-start.16 = (f32[16,4,2,8,128]{4,3,2,1,0:T(8,128)S(1)}, f32[16,4,2,8,128]{4,3,2,1,0:T(8,128)S(1)}, u32[]{:S(2)}, u32[]{:S(2)}) collective-permute-start(f32[16,4,2,8,128]{4,3,2,1,0:T(8,128)S(1)} %get-tuple-element.32.some), channel_id=1, source_target_pairs={{0,1},{1,0},{2,3},{3,2},{4,5},{5,4},{6,7},{7,6},{8,9},{9,8},{10,11... | collective-permute-start | bytes 1572872 | tf_op jit(solution)/shard_map/ppermute | solution.py:327
  101.2 3.5 %collective-permute-start.14 = (f32[4,8,8,512]{3,2,1,0:T(8,128)S(1)}, f32[4,8,8,512]{3,2,1,0:T(8,128)S(1)}, u32[]{:S(2)}, u32[]{:S(2)}) collective-permute-start(f32[4,8,8,512]{3,2,1,0:T(8,128)S(1)} %get-tuple-element.31.state), channel_id=1, source_target_pairs={{0,31},{1,2},{2,1},{3,4},{4,3},{5,6},{6,5},{7,8},{8,7},{9,10},{10,... | collective-permute-start | bytes 1572872 | tf_op jit(solution)/shard_map/ppermute | solution.py:308
  104.6 2.0 %collective-permute-start.15 = (f32[4,8,8,512]{3,2,1,0:T(8,128)S(1)}, f32[4,8,8,512]{3,2,1,0:T(8,128)S(1)}, u32[]{:S(2)}, u32[]{:S(2)}) collective-permute-start(f32[4,8,8,512]{3,2,1,0:T(8,128)S(1)} %get-tuple-element.31.state), channel_id=1, source_target_pairs={{0,1},{1,0},{2,3},{3,2},{4,5},{5,4},{6,7},{7,6},{8,9},{9,8},{10,11... | collective-permute-start | bytes 1572872 | tf_op jit(solution)/shard_map/ppermute | solution.py:299
  106.6 0.0 collective-permute-done.16.others
  106.6 0.7 shard_map.45.refs_1_.weights
  107.4 9.9 %collective-permute-done.14.outer = f32[4,8,8,512]{3,2,1,0:T(8,128)S(1)} collective-permute-done((f32[4,8,8,512]{3,2,1,0:T(8,128)S(1)}, f32[4,8,8,512]{3,2,1,0:T(8,128)S(1)}, u32[]{:S(2)}, u32[]{:S(2)}) %collective-permute-start.14) | collective-permute-done | bytes 524320 | tf_op jit(solution)/shard_map/ppermute | solution.py:308
  117.3 0.0 collective-permute-done.15.inner
  117.3 4.1 %shard_map.46 = (f32[4,8,8,512]{3,2,1,0:T(8,128)S(1)}, f32[32,2,8,128]{3,2,1,0:T(8,128)S(1)}) custom-call(s32[3]{0:T(128)S(1)} %pad_add_fusion.place, f32[4,8,8,512]{3,2,1,0:T(8,128)S(1)} %get-tuple-element.31.state, f32[4,8,8,512]{3,2,1,0:T(8,128)S(1)} %collective-permute-done.14.outer, f32[4,8,8,512]{3,2,1,0:T(8,128)S(1)} %collective-permute-done.15.inner, ...), custom_call_target="tpu_custom_call" | custom-call | tf_op jit(solution)/shard_map/pallas_call | solution.py:387
  121.4 17.6 %all_to_all.10.residuals = f32[32,2,8,128]{3,2,1,0:T(8,128)S(1)} all-to-all(f32[32,2,8,128]{3,2,1,0:T(8,128)S(1)} %get-tuple-element.33), channel_id=1, replica_groups=mesh['cuts'=16,'space'=32] {'space'}, dimensions={0} | all-to-all | bytes 524288 | tf_op jit(solution)/shard_map/all_to_all | solution.py:388
  139.0 13.3 %shard_map.47 = f32[16,2,8,128]{3,2,1,0:T(8,128)S(1)} custom-call(s32[3]{0:T(128)S(1)} %pad_add_fusion.place, f32[32,2,8,128]{3,2,1,0:T(8,128)S(1)} %all_to_all.10.residuals, f32[32,7,2,8,128]{4,3,2,1,0:T(8,128)S(1)} %shard_map.45.refs_1_.weights), custom_call_target="tpu_custom_call" | custom-call | tf_op jit(solution)/shard_map/pallas_call | solution.py:389
  152.3 13.1 %all_to_all.11.shares = f32[16,2,8,128]{3,2,1,0:T(8,128)S(1)} all-to-all(f32[16,2,8,128]{3,2,1,0:T(8,128)S(1)} %shard_map.47), channel_id=1, replica_groups=mesh['cuts'=16,'space'=32] {'cuts'}, dimensions={0} | all-to-all | bytes 262144 | tf_op jit(solution)/shard_map/all_to_all | solution.py:395
  165.4 1.1 shard_map.48
Async XLA Ops:
  0.1 1.4 copy-start
  1.5 1.0 copy-start.2
  2.5 1.0 copy-start.3
  4.5 20.0 %copy-start.1 = (f32[3,4,64,512]{3,2,1,0:T(8,128)S(1)}, f32[3,4,64,512]{3,2,1,0:T(8,128)}, u32[]{:S(2)}) copy-start(f32[3,4,64,512]{3,2,1,0:T(8,128)} %velocity.5) | copy-start | bytes 4718596
  4.5 42.8 %collective-permute-start.2 = (f32[3,3,64,512]{3,2,1,0:T(8,128)S(1)}, f32[3,3,64,512]{3,2,1,0:T(8,128)S(1)}, u32[]{:S(2)}, u32[]{:S(2)}) collective-permute-start(f32[3,3,64,512]{3,2,1,0:T(8,128)S(1)} %get-tuple-element.23), channel_id=1, source_target_pairs={{0,287},{1,258},{2,257},{3,260},{4,259},{5,262},{6,261},{7,264},{8... | collective-permute-start | bytes 3538952 | tf_op jit(solution)/shard_map/ppermute | solution.py:317
  8.3 41.5 %collective-permute-start.3 = (f32[3,3,64,512]{3,2,1,0:T(8,128)S(1)}, f32[3,3,64,512]{3,2,1,0:T(8,128)S(1)}, u32[]{:S(2)}, u32[]{:S(2)}) collective-permute-start(f32[3,3,64,512]{3,2,1,0:T(8,128)S(1)} %get-tuple-element.24), channel_id=1, source_target_pairs={{0,1},{1,0},{2,3},{3,2},{4,5},{5,4},{6,7},{7,6},{8,9},{9,8},{10,11... | collective-permute-start | bytes 3538952 | tf_op jit(solution)/shard_map/ppermute | solution.py:299
  12.7 30.7 %collective-permute-start = (f32[7,64,512]{2,1,0:T(8,128)S(1)}, f32[7,64,512]{2,1,0:T(8,128)S(1)}, u32[]{:S(2)}, u32[]{:S(2)}) collective-permute-start(f32[7,64,512]{2,1,0:T(8,128)S(1)} %get-tuple-element.20), channel_id=1, source_target_pairs={{0,31},{1,2},{2,1},{3,4},{4,3},{5,6},{6,5},{7,8},{8,7},{9,10},{10,... | collective-permute-start | bytes 2752520 | tf_op jit(solution)/shard_map/ppermute | solution.py:308
  22.6 27.3 %collective-permute-start.1 = (f32[7,64,512]{2,1,0:T(8,128)S(1)}, f32[7,64,512]{2,1,0:T(8,128)S(1)}, u32[]{:S(2)}, u32[]{:S(2)}) collective-permute-start(f32[7,64,512]{2,1,0:T(8,128)S(1)} %get-tuple-element.21), channel_id=1, source_target_pairs={{0,1},{1,0},{2,3},{3,2},{4,5},{5,4},{6,7},{7,6},{8,9},{9,8},{10,11... | collective-permute-start | bytes 2752520 | tf_op jit(solution)/shard_map/ppermute | solution.py:299
  25.8 24.6 %collective-permute-start.4 = (f32[1,4,2,8,128]{4,3,2,1,0:T(8,128)S(1)}, f32[1,4,2,8,128]{4,3,2,1,0:T(8,128)S(1)}, u32[]{:S(2)}, u32[]{:S(2)}) collective-permute-start(f32[1,4,2,8,128]{4,3,2,1,0:T(8,128)S(1)} %bitcast.7), channel_id=1, source_target_pairs={{0,8},{1,9},{2,10},{3,11},{4,12},{5,13},{6,14},{7,15},{8,0},{9,1},... | collective-permute-start | bytes 98312 | tf_op jit(solution)/shard_map/ppermute | solution.py:327
  43.5 9.7 %collective-permute-start.5 = (f32[1,4,2,8,128]{4,3,2,1,0:T(8,128)S(1)}, f32[1,4,2,8,128]{4,3,2,1,0:T(8,128)S(1)}, u32[]{:S(2)}, u32[]{:S(2)}) collective-permute-start(f32[1,4,2,8,128]{4,3,2,1,0:T(8,128)S(1)} %bitcast.8), channel_id=1, source_target_pairs={{0,16},{1,17},{2,18},{3,19},{4,20},{5,21},{6,22},{7,23},{8,24},{9,... | collective-permute-start | bytes 98312 | tf_op jit(solution)/shard_map/ppermute | solution.py:327
  47.3 8.0 %collective-permute-start.6 = (f32[1,4,2,8,128]{4,3,2,1,0:T(8,128)S(1)}, f32[1,4,2,8,128]{4,3,2,1,0:T(8,128)S(1)}, u32[]{:S(2)}, u32[]{:S(2)}) collective-permute-start(f32[1,4,2,8,128]{4,3,2,1,0:T(8,128)S(1)} %bitcast.9), channel_id=1, source_target_pairs={{0,24},{1,25},{2,26},{3,27},{4,28},{5,29},{6,30},{7,31},{8,16},{9,... | collective-permute-start | bytes 98312 | tf_op jit(solution)/shard_map/ppermute | solution.py:327
  59.5 15.7 %collective-permute-start.7 = (f32[4,8,8,512]{3,2,1,0:T(8,128)S(1)}, f32[4,8,8,512]{3,2,1,0:T(8,128)S(1)}, u32[]{:S(2)}, u32[]{:S(2)}) collective-permute-start(f32[4,8,8,512]{3,2,1,0:T(8,128)S(1)} %get-tuple-element.27.state), channel_id=1, source_target_pairs={{0,31},{1,2},{2,1},{3,4},{4,3},{5,6},{6,5},{7,8},{8,7},{9,10},{10,... | collective-permute-start | bytes 1572872 | tf_op jit(solution)/shard_map/ppermute | solution.py:308
  61.5 13.7 %collective-permute-start.8 = (f32[4,8,8,512]{3,2,1,0:T(8,128)S(1)}, f32[4,8,8,512]{3,2,1,0:T(8,128)S(1)}, u32[]{:S(2)}, u32[]{:S(2)}) collective-permute-start(f32[4,8,8,512]{3,2,1,0:T(8,128)S(1)} %get-tuple-element.27.state), channel_id=1, source_target_pairs={{0,1},{1,0},{2,3},{3,2},{4,5},{5,4},{6,7},{7,6},{8,9},{9,8},{10,11... | collective-permute-start | bytes 1572872 | tf_op jit(solution)/shard_map/ppermute | solution.py:299
  63.4 11.8 %collective-permute-start.9 = (f32[4,4,2,8,128]{4,3,2,1,0:T(8,128)S(1)}, f32[4,4,2,8,128]{4,3,2,1,0:T(8,128)S(1)}, u32[]{:S(2)}, u32[]{:S(2)}) collective-permute-start(f32[4,4,2,8,128]{4,3,2,1,0:T(8,128)S(1)} %get-tuple-element.28.refs_0_), channel_id=1, source_target_pairs={{0,4},{1,5},{2,6},{3,7},{4,0},{5,1},{6,2},{7,3},{8,12},{9,13},{10,... | collective-permute-start | bytes 393224 | tf_op jit(solution)/shard_map/ppermute | solution.py:327
  67.2 7.9 %collective-permute-start.10 = (f32[2,8,128]{2,1,0:T(8,128)S(1)}, f32[2,8,128]{2,1,0:T(8,128)S(1)}, u32[]{:S(2)}, u32[]{:S(2)}) collective-permute-start(f32[2,8,128]{2,1,0:T(8,128)S(1)} %get-tuple-element.26.refs_4_.refs_2_), channel_id=1, source_target_pairs={{32,0},{64,32},{96,64},{128,96},{160,128},{192,160},{224,192},{256... | collective-permute-start | bytes 24584 | tf_op jit(solution)/shard_map/ppermute | solution.py:358
  79.2 16.1 %collective-permute-start.11 = (f32[4,8,8,512]{3,2,1,0:T(8,128)S(1)}, f32[4,8,8,512]{3,2,1,0:T(8,128)S(1)}, u32[]{:S(2)}, u32[]{:S(2)}) collective-permute-start(f32[4,8,8,512]{3,2,1,0:T(8,128)S(1)} %get-tuple-element.29.state), channel_id=1, source_target_pairs={{0,31},{1,2},{2,1},{3,4},{4,3},{5,6},{6,5},{7,8},{8,7},{9,10},{10,... | collective-permute-start | bytes 1572872 | tf_op jit(solution)/shard_map/ppermute | solution.py:308
  81.5 13.7 %collective-permute-start.12 = (f32[4,8,8,512]{3,2,1,0:T(8,128)S(1)}, f32[4,8,8,512]{3,2,1,0:T(8,128)S(1)}, u32[]{:S(2)}, u32[]{:S(2)}) collective-permute-start(f32[4,8,8,512]{3,2,1,0:T(8,128)S(1)} %get-tuple-element.29.state), channel_id=1, source_target_pairs={{0,1},{1,0},{2,3},{3,2},{4,5},{5,4},{6,7},{7,6},{8,9},{9,8},{10,11... | collective-permute-start | bytes 1572872 | tf_op jit(solution)/shard_map/ppermute | solution.py:299
  84.7 10.1 %collective-permute-start.13 = (f32[8,4,2,8,128]{4,3,2,1,0:T(8,128)S(1)}, f32[8,4,2,8,128]{4,3,2,1,0:T(8,128)S(1)}, u32[]{:S(2)}, u32[]{:S(2)}) collective-permute-start(f32[8,4,2,8,128]{4,3,2,1,0:T(8,128)S(1)} %get-tuple-element.30.refs_0_), channel_id=1, source_target_pairs={{0,258},{1,259},{2,256},{3,257},{4,262},{5,263},{6,260},{7,261},{8... | collective-permute-start | bytes 786440 | tf_op jit(solution)/shard_map/ppermute | solution.py:326
  99.3 7.4 %collective-permute-start.16 = (f32[16,4,2,8,128]{4,3,2,1,0:T(8,128)S(1)}, f32[16,4,2,8,128]{4,3,2,1,0:T(8,128)S(1)}, u32[]{:S(2)}, u32[]{:S(2)}) collective-permute-start(f32[16,4,2,8,128]{4,3,2,1,0:T(8,128)S(1)} %get-tuple-element.32.some), channel_id=1, source_target_pairs={{0,1},{1,0},{2,3},{3,2},{4,5},{5,4},{6,7},{7,6},{8,9},{9,8},{10,11... | collective-permute-start | bytes 1572872 | tf_op jit(solution)/shard_map/ppermute | solution.py:327
  101.2 16.1 %collective-permute-start.14 = (f32[4,8,8,512]{3,2,1,0:T(8,128)S(1)}, f32[4,8,8,512]{3,2,1,0:T(8,128)S(1)}, u32[]{:S(2)}, u32[]{:S(2)}) collective-permute-start(f32[4,8,8,512]{3,2,1,0:T(8,128)S(1)} %get-tuple-element.31.state), channel_id=1, source_target_pairs={{0,31},{1,2},{2,1},{3,4},{4,3},{5,6},{6,5},{7,8},{8,7},{9,10},{10,... | collective-permute-start | bytes 1572872 | tf_op jit(solution)/shard_map/ppermute | solution.py:308
  104.6 12.7 %collective-permute-start.15 = (f32[4,8,8,512]{3,2,1,0:T(8,128)S(1)}, f32[4,8,8,512]{3,2,1,0:T(8,128)S(1)}, u32[]{:S(2)}, u32[]{:S(2)}) collective-permute-start(f32[4,8,8,512]{3,2,1,0:T(8,128)S(1)} %get-tuple-element.31.state), channel_id=1, source_target_pairs={{0,1},{1,0},{2,3},{3,2},{4,5},{5,4},{6,7},{7,6},{8,9},{9,8},{10,11... | collective-permute-start | bytes 1572872 | tf_op jit(solution)/shard_map/ppermute | solution.py:299

commit v8 on v7

--- a/solution.py
+++ b/solution.py
@@ -82,13 +82,22 @@
     return weights
 
 
-def cut_kernel(place, velocity, diffusivity, starts, fields, mixed, ready, *, outer):
-    begin = place[2] if outer else 1 - place[2]
-    copies = [
-        pltpu.make_async_copy(velocity.at[:, pl.ds(begin, REACH)], fields, ready.at[0]),
-        pltpu.make_async_copy(diffusivity.at[pl.ds(begin, REACH)], mixed.at[pl.ds(LAYERS, REACH)], ready.at[1]),
-        pltpu.make_async_copy(starts.at[0], mixed.at[pl.ds(0, LAYERS)], ready.at[2]),
+STATE_AT = 3 * REACH
+INNER = STATE_AT + LAYERS + REACH
+
+
+def cut_kernel(place, velocity, diffusivity, starts, fields, mixed, inner, ready):
+    core = place[2]
+    pairs = [
+        (diffusivity.at[pl.ds(core, REACH)], mixed.at[pl.ds(LAYERS, REACH)]),
+        (starts.at[0], mixed.at[pl.ds(0, LAYERS)]),
+        (diffusivity.at[pl.ds(1 - core, REACH)], inner.at[pl.ds(STATE_AT + LAYERS, REACH)]),
+        (starts.at[0], inner.at[pl.ds(STATE_AT, LAYERS)]),
     ]
+    for f in range(3):
+        pairs.append((velocity.at[f, pl.ds(core, REACH)], fields.at[pl.ds(f * REACH, REACH)]))
+        pairs.append((velocity.at[f, pl.ds(1 - core, REACH)], inner.at[pl.ds(f * REACH, REACH)]))
+    copies = [pltpu.make_async_copy(*pair, ready.at[i]) for i, pair in enumerate(pairs)]
     for copy in copies:
         copy.start()
     for copy in copies:
@@ -122,11 +131,13 @@
                 coarse_old[h] = mean
 
 
-def side_kernel(velocity, mixed, weights, buffer):
+def side_kernel(at, *refs):
+    *fields, earlier, weights, buffer = refs
+
     def layer(x, carry):
         for f in range(3):
-            spread(velocity[f, x], buffer.at[f])
-        spread(mixed[LAYERS + x], buffer.at[3])
+            spread(fields[0][f * REACH + x], buffer.at[f])
+        spread(fields[-1][at + x], buffer.at[3])
         for j in range(8):
             parts = [spread_tile(buffer.at[f], j) for f in range(4)]
             for i, weight in enumerate(weigh(parts[:3], parts[3], STEP, 1.0)):
@@ -141,6 +152,7 @@
     lasts = [source[x + i, 7] for i in range(depth)]
     behind = [pltpu.roll(last, 1, 0) for last in lasts]
     now = firsts
+    done = []
     for j in range(8):
         below, above = source[x - 1, j], source[x + depth, j]
         column = [below, *now, above]
@@ -151,13 +163,18 @@
             else:
                 ahead.append(lasts[i] if j == 6 else source[x + i, j + 1])
         for i in range(depth):
-            target[tx + i, j] = (
+            value = (
                 (weights[wx + i, 0, j] * now[i] + weights[wx + i, 1, j] * column[i])
                 + (weights[wx + i, 2, j] * column[i + 2] + weights[wx + i, 3, j] * behind[i])
                 + (weights[wx + i, 4, j] * ahead[i] + weights[wx + i, 5, j] * pltpu.roll(now[i], 1, 1))
                 + weights[wx + i, 6, j] * pltpu.roll(now[i], 511, 1)
             )
+            done.append((tx + i, j, value))
         behind, now = now, ahead
+        if j % 2:
+            for at, tile, value in done:
+                target[at, tile] = value
+            done = []
 
 
 def sweep(source, goal, begin, count, weights, first, shift=0):
@@ -176,7 +193,7 @@
     if final:
         later, after, out, residual, one, two, buffer = refs
     else:
-        *parts, early, out, joined, one, two, buffer = refs
+        *parts, out, joined, one, two, buffer = refs
         begin = 0
         for part in parts:
             joined[begin : begin + part.shape[0]] = part[...]
@@ -187,7 +204,7 @@
         blocks = ((state, LAYERS), (outer, 2 * LAYERS * core), (inner, 2 * LAYERS * (1 - core)))
         for i, (ref, begin) in enumerate(blocks):
             if raw:
-                spread(ref[x], buffer.at[i])
+                spread(ref[(STATE_AT if ref is inner else 0) + x], buffer.at[i])
             for j in range(8):
                 one[begin + x, j] = spread_tile(buffer.at[i], j) if raw else ref[x, j]
         return carry
@@ -235,7 +252,7 @@
 
 
 def mask_of(i):
-    return 8 * (i & 3) | (i & 4) | ((i >> 2) & 2) | (i >> 4)
+    return 8 * (i & 3) | ((i >> 1) & 2) | ((i >> 1) & 4) | (i >> 4)
 
 
 def coarse_weight_kernel(place, some, others, weights):
@@ -249,9 +266,10 @@
                 weights[x, k, h] = weight
 
 
-def chain_kernel(place, residuals, weights, shares, one, two):
+def chain_kernel(place, residuals, given, shares, weights, one, two):
     count = weights.shape[0]
     slices = shares.shape[0]
+    weights[...] = given[...]
     slice_index = place[0]
     layer_index = place[1]
     shares[...] = jnp.zeros(shares.shape, F32)
@@ -335,20 +353,15 @@
     place = jnp.stack([lax.axis_index("cuts"), row, row & 1]).astype(jnp.int32)
     columns = pltpu.VMEM((5, 4, 64, 128), F32)
 
-    def cut(outer):
-        return call(
-            functools.partial(cut_kernel, outer=outer),
-            [(3, REACH, 64, 512), (LAYERS + REACH, 64, 512)],
-            [SMEM, ANY, ANY, ANY],
-            [pltpu.SemaphoreType.DMA((3,))],
-        )(place, velocity, diffusivity, starts)
-
-    fields_outer, mixed_outer = cut(True)
-    fields_inner, mixed_inner = cut(False)
-    mixed_inner = swap_inner(mixed_inner)
+    fields_outer, mixed_outer, all_inner = call(
+        cut_kernel,
+        [(3 * REACH, 64, 512), (LAYERS + REACH, 64, 512), (INNER, 64, 512)],
+        [SMEM, ANY, ANY, ANY],
+        [pltpu.SemaphoreType.DMA((10,))],
+    )(place, velocity, diffusivity, starts)
+    fields_outer = swap_outer_fields(fields_outer)
     mixed_outer = swap_outer(mixed_outer)
-    fields_inner = swap_inner(fields_inner)
-    fields_outer = swap_outer_fields(fields_outer)
+    all_inner = swap_inner(all_inner)
     own_weights, coarse_fields, coarse_old = call(
         own_kernel,
         [(LAYERS, 7, *TILE), (4, *COARSE), COARSE],
@@ -357,11 +370,14 @@
     )(velocity, diffusivity, starts[0])
     coarse_later = lax.ppermute(coarse_old, "cuts", [((n + 1) % slices, n) for n in range(slices)])
     gathered = coarse_fields[None]
-    outer_weights, inner_weights = [
-        call(side_kernel, [(REACH, 7, *TILE)], [VMEM, VMEM], [columns])(*halos)[0]
-        for halos in ((fields_outer, mixed_outer), (fields_inner, mixed_inner))
-    ]
-    state, inner, outer = starts[0], mixed_inner, mixed_outer
+    side = [(REACH, 7, *TILE)]
+    inner_weights = call(functools.partial(side_kernel, STATE_AT + LAYERS), side, [VMEM, ANY], [columns])(
+        all_inner, coarse_old
+    )[0]
+    outer_weights = call(functools.partial(side_kernel, LAYERS), side, [VMEM, VMEM, ANY], [columns])(
+        fields_outer, mixed_outer, inner_weights
+    )[0]
+    state, inner, outer = starts[0], all_inner, mixed_outer
     scratch = [pltpu.VMEM((3 * LAYERS, *TILE), F32)] * 2 + [columns]
     for index in range(ROUNDS):
         raw, final = index == 0, index == ROUNDS - 1
@@ -379,10 +395,9 @@
             specs += [VMEM, ANY]
             outs = [block, (count, *COARSE)]
         else:
-            bits = ((8, 16, 24), (4,), (2,))[index]
-            parts = [gathered] + [across(gathered, b) for b in bits]
-            operands += parts + [coarse_later if index == 1 else coarse_old]
-            specs += [VMEM] * len(parts) + [ANY]
+            parts = [gathered] + [across(gathered, b) for b in ((8, 16, 24), (2,), (4,))[index]]
+            operands += parts
+            specs += [VMEM] * len(parts)
             outs = [block, (len(parts) * gathered.shape[0], 4, *COARSE)]
         state, gathered = call(functools.partial(round_kernel, raw, final), outs, specs, scratch)(*operands)
     residuals = lax.all_to_all(gathered, "space", 0, 0)
@@ -390,7 +405,7 @@
         chain_kernel,
         [(slices, *COARSE)],
         [SMEM, VMEM, VMEM],
-        [pltpu.VMEM((count, *COARSE), F32)] * 2,
+        [pltpu.VMEM((count, 7, *COARSE), F32)] + [pltpu.VMEM((count, *COARSE), F32)] * 2,
     )(place, residuals, weights)[0]
     shares = lax.all_to_all(shares, "cuts", 0, 0)
     return call(finish_kernel, [(1, LAYERS, 64, 512)], [VMEM, VMEM], [columns])(shares, state)[0]

time: 167 us -> 159 us (0.952)
  waiting for transfers between devices: 39.8 us -> 23.4 us
  starting transfers between devices: 56.6 us -> 66.9 us
  Pallas kernels: 35.6 us -> 33.1 us
    ppermute x4, waiting for transfers between devices: 26.1 us -> 6.68 us  [swap_outer(): lax.ppermute(block, 'space', [(p, outer_partner(p, count)) for p in range...]
    ppermute x4, starting transfers between devices: 17.6 us -> 24.6 us  [swap_outer(): lax.ppermute(block, 'space', [(p, outer_partner(p, count)) for p in range...]
    ppermute x5, starting transfers between devices: 13.5 us -> 18 us  [across(): return lax.ppermute(block, 'space', [(p, p ^ bits) for p in range(count)])]
    ppermute x1, waiting for transfers between devices: 0.01 us -> 4.26 us  [swap_outer_fields(): return lax.ppermute(block, ('cuts', 'space'), route)]
    ppermute x1, waiting for transfers between devices: 7.46 us -> 4.14 us  [across(): return lax.ppermute(block, ('cuts', 'space'), route)]
    ppermute x5, waiting for transfers between devices: 4.83 us -> 7.72 us  [across(): return lax.ppermute(block, 'space', [(p, p ^ bits) for p in range(count)])]
    pallas_call x1, Pallas kernels: 13.3 us -> 10.7 us  [shards(): call(chain_kernel, [(slices, *COARSE)], [SMEM, VMEM, VMEM], [pltpu.VMEM((...]
    ppermute x5 -> x4, starting transfers between devices: 13.3 us -> 10.8 us  [swap_inner(): return lax.ppermute(block, 'space', [(p, p ^ 1) for p in range(count)])]
  transfers between devices with their start and end apart: 17 -> 16, of which waited for: 7 -> 7; matrix products, arithmetic and copies ran while one was open for 0% -> 0% of each run, Pallas kernels for 2% -> 2%
where the time goes in v8:
time: 159 us; the launch traced here: 158 us
  starting transfers between devices  66.9 us (42%)
  Pallas kernels  33.1 us (21%)
  blocking collectives  31 us (19%)
  waiting for transfers between devices  23.4 us (15%)
  local copies, waits for them, and re-layouts  3.49 us (2%)
    ppermute x4, starting transfers between devices, swap_outer(): lax.ppermute(block, 'space', [(p, outer_partner(p, count)) for p in range...  24.6 us
    ppermute x5, starting transfers between devices, across(): return lax.ppermute(block, 'space', [(p, p ^ bits) for p in range(count)])  18 us
    all_to_all x1, blocking collectives, shards(): residuals = lax.all_to_all(gathered, 'space', 0, 0)  16.6 us
    pallas_call x4, Pallas kernels, shards(): call(functools.partial(round_kernel, raw, final), outs, specs, scratch)  16 us
    all_to_all x1, blocking collectives, shards(): shares = lax.all_to_all(shares, 'cuts', 0, 0)  14.4 us
    ppermute x4, starting transfers between devices, swap_inner(): return lax.ppermute(block, 'space', [(p, p ^ 1) for p in range(count)])  10.8 us
    pallas_call x1, Pallas kernels, shards(): call(chain_kernel, [(slices, *COARSE)], [SMEM, VMEM, VMEM], [pltpu.VMEM((...  10.7 us
    ppermute x5, waiting for transfers between devices, across(): return lax.ppermute(block, 'space', [(p, p ^ bits) for p in range(count)])  7.72 us
  transfers between devices with their start and end apart: 16, of which 7 were waited for; matrix products, arithmetic and copies ran while one was open for 0% of the time, Pallas kernels for 2%

profile of v8, /device:TPU:2, one launch (start us, length us, event | category | flops | bytes accessed | tf_op | source)
XLA Modules:
  0.0 158.2 jit_solution(11856749652603868350)
XLA Ops:
  0.0 0.1 pad_add_fusion.place
  0.1 0.0 copy-start
  0.1 1.4 copy-done
  1.5 0.0 copy-start.2
  1.5 1.0 copy-done.2
  2.5 0.0 copy-start.3
  2.5 1.0 copy-done.3
  3.6 0.0 copy-start.1
  3.6 2.2 %shard_map.37 = (f32[9,64,512]{2,1,0:T(8,128)S(1)}, f32[7,64,512]{2,1,0:T(8,128)S(1)}, f32[16,64,512]{2,1,0:T(8,128)S(1)}) custom-call(s32[3]{0:T(128)S(1)} %pad_add_fusion.place, f32[3,4,64,512]{3,2,1,0:T(8,128)S(1)} %copy-done, f32[4,64,512]{2,1,0:T(8,128)S(1)} %copy-done.3, f32[1,4,64,512]{3,2,1,0:T(8,128)S(1)} %copy-done.2), custom_call_target="tpu_custom_call" | custom-call | tf_op jit(solution)/shard_map/pallas_call | solution.py:356
  5.8 1.9 %collective-permute-start.1 = (f32[16,64,512]{2,1,0:T(8,128)S(1)}, f32[16,64,512]{2,1,0:T(8,128)S(1)}, u32[]{:S(2)}, u32[]{:S(2)}) collective-permute-start(f32[16,64,512]{2,1,0:T(8,128)S(1)} %get-tuple-element.20), channel_id=1, source_target_pairs={{0,1},{1,0},{2,3},{3,2},{4,5},{5,4},{6,7},{7,6},{8,9},{9,8},{10,11... | collective-permute-start | bytes 6291464 | tf_op jit(solution)/shard_map/ppermute | solution.py:317
  7.7 3.5 %collective-permute-start.2 = (f32[9,64,512]{2,1,0:T(8,128)S(1)}, f32[9,64,512]{2,1,0:T(8,128)S(1)}, u32[]{:S(2)}, u32[]{:S(2)}) collective-permute-start(f32[9,64,512]{2,1,0:T(8,128)S(1)} %get-tuple-element.22), channel_id=1, source_target_pairs={{0,287},{1,258},{2,257},{3,260},{4,259},{5,262},{6,261},{7,264},{8... | collective-permute-start | bytes 3538952 | tf_op jit(solution)/shard_map/ppermute | solution.py:335
  11.2 6.3 %collective-permute-start = (f32[7,64,512]{2,1,0:T(8,128)S(1)}, f32[7,64,512]{2,1,0:T(8,128)S(1)}, u32[]{:S(2)}, u32[]{:S(2)}) collective-permute-start(f32[7,64,512]{2,1,0:T(8,128)S(1)} %get-tuple-element.19), channel_id=1, source_target_pairs={{0,31},{1,2},{2,1},{3,4},{4,3},{5,6},{6,5},{7,8},{8,7},{9,10},{10,... | collective-permute-start | bytes 2752520 | tf_op jit(solution)/shard_map/ppermute | solution.py:326
  17.6 0.0 copy-done.1
  17.6 1.3 shard_map.38
  18.9 3.1 %collective-permute-start.3 = (f32[1,4,2,8,128]{4,3,2,1,0:T(8,128)S(1)}, f32[1,4,2,8,128]{4,3,2,1,0:T(8,128)S(1)}, u32[]{:S(2)}, u32[]{:S(2)}) collective-permute-start(f32[1,4,2,8,128]{4,3,2,1,0:T(8,128)S(1)} %bitcast.7), channel_id=1, source_target_pairs={{0,8},{1,9},{2,10},{3,11},{4,12},{5,13},{6,14},{7,15},{8,0},{9,1},... | collective-permute-start | bytes 98312 | tf_op jit(solution)/shard_map/ppermute | solution.py:345
  22.0 9.1 %collective-permute-start.4 = (f32[1,4,2,8,128]{4,3,2,1,0:T(8,128)S(1)}, f32[1,4,2,8,128]{4,3,2,1,0:T(8,128)S(1)}, u32[]{:S(2)}, u32[]{:S(2)}) collective-permute-start(f32[1,4,2,8,128]{4,3,2,1,0:T(8,128)S(1)} %bitcast.8), channel_id=1, source_target_pairs={{0,16},{1,17},{2,18},{3,19},{4,20},{5,21},{6,22},{7,23},{8,24},{9,... | collective-permute-start | bytes 98312 | tf_op jit(solution)/shard_map/ppermute | solution.py:345
  31.1 0.0 collective-permute-done.1.refs_0_.inner
  31.1 1.9 %collective-permute-start.5 = (f32[1,4,2,8,128]{4,3,2,1,0:T(8,128)S(1)}, f32[1,4,2,8,128]{4,3,2,1,0:T(8,128)S(1)}, u32[]{:S(2)}, u32[]{:S(2)}) collective-permute-start(f32[1,4,2,8,128]{4,3,2,1,0:T(8,128)S(1)} %bitcast.9), channel_id=1, source_target_pairs={{0,24},{1,25},{2,26},{3,27},{4,28},{5,29},{6,30},{7,31},{8,16},{9,... | collective-permute-start | bytes 98312 | tf_op jit(solution)/shard_map/ppermute | solution.py:345
  33.0 0.6 shard_map.39.refs_2_.own_inner
  33.6 0.0 collective-permute-done.refs_1_.outer
  33.6 4.3 %collective-permute-done.2.refs_0_ = f32[9,64,512]{2,1,0:T(8,128)S(1)} collective-permute-done((f32[9,64,512]{2,1,0:T(8,128)S(1)}, f32[9,64,512]{2,1,0:T(8,128)S(1)}, u32[]{:S(2)}, u32[]{:S(2)}) %collective-permute-start.2) | collective-permute-done | bytes 1179680 | tf_op jit(solution)/shard_map/ppermute | solution.py:335
  37.9 0.6 shard_map.40.own_outer
  38.5 0.0 collective-permute-done.3.refs_1_
  38.5 0.0 collective-permute-done.4.refs_2_
  38.5 1.0 collective-permute-done.5.refs_3_
  39.4 4.2 %shard_map.41 = (f32[4,8,8,512]{3,2,1,0:T(8,128)S(1)}, f32[4,4,2,8,128]{4,3,2,1,0:T(8,128)S(1)}) custom-call(s32[3]{0:T(128)S(1)} %pad_add_fusion.place, f32[4,64,512]{2,1,0:T(8,128)S(1)} %bitcast.6, f32[7,64,512]{2,1,0:T(8,128)S(1)} %collective-permute-done.refs_1_.outer, f32[16,64,512]{2,1,0:T(8,128)S(1)} %collective-permute-done.1.refs_0_.inner, ...), custom_call_target="tpu_custom_call" | custom-call | tf_op jit(solution)/shard_map/pallas_call | solution.py:402
  43.6 8.2 %collective-permute-start.6 = (f32[4,8,8,512]{3,2,1,0:T(8,128)S(1)}, f32[4,8,8,512]{3,2,1,0:T(8,128)S(1)}, u32[]{:S(2)}, u32[]{:S(2)}) collective-permute-start(f32[4,8,8,512]{3,2,1,0:T(8,128)S(1)} %get-tuple-element.25.state), channel_id=1, source_target_pairs={{0,31},{1,2},{2,1},{3,4},{4,3},{5,6},{6,5},{7,8},{8,7},{9,10},{10,... | collective-permute-start | bytes 1572872 | tf_op jit(solution)/shard_map/ppermute | solution.py:326
  51.8 5.0 %collective-permute-start.7 = (f32[4,8,8,512]{3,2,1,0:T(8,128)S(1)}, f32[4,8,8,512]{3,2,1,0:T(8,128)S(1)}, u32[]{:S(2)}, u32[]{:S(2)}) collective-permute-start(f32[4,8,8,512]{3,2,1,0:T(8,128)S(1)} %get-tuple-element.25.state), channel_id=1, source_target_pairs={{0,1},{1,0},{2,3},{3,2},{4,5},{5,4},{6,7},{7,6},{8,9},{9,8},{10,11... | collective-permute-start | bytes 1572872 | tf_op jit(solution)/shard_map/ppermute | solution.py:317
  56.9 4.0 %collective-permute-start.8 = (f32[4,4,2,8,128]{4,3,2,1,0:T(8,128)S(1)}, f32[4,4,2,8,128]{4,3,2,1,0:T(8,128)S(1)}, u32[]{:S(2)}, u32[]{:S(2)}) collective-permute-start(f32[4,4,2,8,128]{4,3,2,1,0:T(8,128)S(1)} %get-tuple-element.26.refs_0_), channel_id=1, source_target_pairs={{0,258},{1,259},{2,256},{3,257},{4,262},{5,263},{6,260},{7,261},{8... | collective-permute-start | bytes 393224 | tf_op jit(solution)/shard_map/ppermute | solution.py:344
  60.9 4.1 %collective-permute-done.8.refs_1_ = f32[4,4,2,8,128]{4,3,2,1,0:T(8,128)S(1)} collective-permute-done((f32[4,4,2,8,128]{4,3,2,1,0:T(8,128)S(1)}, f32[4,4,2,8,128]{4,3,2,1,0:T(8,128)S(1)}, u32[]{:S(2)}, u32[]{:S(2)}) %collective-permute-start.8) | collective-permute-done | bytes 131104 | tf_op jit(solution)/shard_map/ppermute | solution.py:344
  65.0 0.0 collective-permute-done.6.outer
  65.0 0.0 collective-permute-done.7.inner
  65.0 3.9 %shard_map.42 = (f32[4,8,8,512]{3,2,1,0:T(8,128)S(1)}, f32[8,4,2,8,128]{4,3,2,1,0:T(8,128)S(1)}) custom-call(s32[3]{0:T(128)S(1)} %pad_add_fusion.place, f32[4,8,8,512]{3,2,1,0:T(8,128)S(1)} %get-tuple-element.25.state, f32[4,8,8,512]{3,2,1,0:T(8,128)S(1)} %collective-permute-done.6.outer, f32[4,8,8,512]{3,2,1,0:T(8,128)S(1)} %collective-permute-done.7.inner, ...), custom_call_target="tpu_custom_call" | custom-call | tf_op jit(solution)/shard_map/pallas_call | solution.py:402
  68.9 1.9 %collective-permute-start.10 = (f32[4,8,8,512]{3,2,1,0:T(8,128)S(1)}, f32[4,8,8,512]{3,2,1,0:T(8,128)S(1)}, u32[]{:S(2)}, u32[]{:S(2)}) collective-permute-start(f32[4,8,8,512]{3,2,1,0:T(8,128)S(1)} %get-tuple-element.27.state), channel_id=1, source_target_pairs={{0,1},{1,0},{2,3},{3,2},{4,5},{5,4},{6,7},{7,6},{8,9},{9,8},{10,11... | collective-permute-start | bytes 1572872 | tf_op jit(solution)/shard_map/ppermute | solution.py:317
  70.8 6.2 %collective-permute-start.9 = (f32[4,8,8,512]{3,2,1,0:T(8,128)S(1)}, f32[4,8,8,512]{3,2,1,0:T(8,128)S(1)}, u32[]{:S(2)}, u32[]{:S(2)}) collective-permute-start(f32[4,8,8,512]{3,2,1,0:T(8,128)S(1)} %get-tuple-element.27.state), channel_id=1, source_target_pairs={{0,31},{1,2},{2,1},{3,4},{4,3},{5,6},{6,5},{7,8},{8,7},{9,10},{10,... | collective-permute-start | bytes 1572872 | tf_op jit(solution)/shard_map/ppermute | solution.py:326
  77.0 1.9 %collective-permute-start.11 = (f32[8,4,2,8,128]{4,3,2,1,0:T(8,128)S(1)}, f32[8,4,2,8,128]{4,3,2,1,0:T(8,128)S(1)}, u32[]{:S(2)}, u32[]{:S(2)}) collective-permute-start(f32[8,4,2,8,128]{4,3,2,1,0:T(8,128)S(1)} %get-tuple-element.28.refs_0_), channel_id=1, source_target_pairs={{0,4},{1,5},{2,6},{3,7},{4,0},{5,1},{6,2},{7,3},{8,12},{9,13},{10,... | collective-permute-start | bytes 786440 | tf_op jit(solution)/shard_map/ppermute | solution.py:345
  79.0 6.7 %collective-permute-done.11.refs_1_ = f32[8,4,2,8,128]{4,3,2,1,0:T(8,128)S(1)} collective-permute-done((f32[8,4,2,8,128]{4,3,2,1,0:T(8,128)S(1)}, f32[8,4,2,8,128]{4,3,2,1,0:T(8,128)S(1)}, u32[]{:S(2)}, u32[]{:S(2)}) %collective-permute-start.11) | collective-permute-done | bytes 262176 | tf_op jit(solution)/shard_map/ppermute | solution.py:345
  85.7 0.0 collective-permute-done.10.inner
  85.7 3.6 %collective-permute-done.9.outer = f32[4,8,8,512]{3,2,1,0:T(8,128)S(1)} collective-permute-done((f32[4,8,8,512]{3,2,1,0:T(8,128)S(1)}, f32[4,8,8,512]{3,2,1,0:T(8,128)S(1)}, u32[]{:S(2)}, u32[]{:S(2)}) %collective-permute-start.9) | collective-permute-done | bytes 524320 | tf_op jit(solution)/shard_map/ppermute | solution.py:326
  89.3 3.9 %shard_map.43 = (f32[4,8,8,512]{3,2,1,0:T(8,128)S(1)}, f32[16,4,2,8,128]{4,3,2,1,0:T(8,128)S(1)}) custom-call(s32[3]{0:T(128)S(1)} %pad_add_fusion.place, f32[4,8,8,512]{3,2,1,0:T(8,128)S(1)} %get-tuple-element.27.state, f32[4,8,8,512]{3,2,1,0:T(8,128)S(1)} %collective-permute-done.9.outer, f32[4,8,8,512]{3,2,1,0:T(8,128)S(1)} %collective-permute-done.10.inner, ...), custom_call_target="tpu_custom_call" | custom-call | tf_op jit(solution)/shard_map/pallas_call | solution.py:402
  93.2 1.9 %collective-permute-start.15 = (f32[16,4,2,8,128]{4,3,2,1,0:T(8,128)S(1)}, f32[16,4,2,8,128]{4,3,2,1,0:T(8,128)S(1)}, u32[]{:S(2)}, u32[]{:S(2)}) collective-permute-start(f32[16,4,2,8,128]{4,3,2,1,0:T(8,128)S(1)} %get-tuple-element.30.some), channel_id=1, source_target_pairs={{0,1},{1,0},{2,3},{3,2},{4,5},{5,4},{6,7},{7,6},{8,9},{9,8},{10,11... | collective-permute-start | bytes 1572872 | tf_op jit(solution)/shard_map/ppermute | solution.py:345
  95.1 3.8 %collective-permute-start.12 = (f32[4,8,8,512]{3,2,1,0:T(8,128)S(1)}, f32[4,8,8,512]{3,2,1,0:T(8,128)S(1)}, u32[]{:S(2)}, u32[]{:S(2)}) collective-permute-start(f32[4,8,8,512]{3,2,1,0:T(8,128)S(1)} %get-tuple-element.29.state), channel_id=1, source_target_pairs={{0,31},{1,2},{2,1},{3,4},{4,3},{5,6},{6,5},{7,8},{8,7},{9,10},{10,... | collective-permute-start | bytes 1572872 | tf_op jit(solution)/shard_map/ppermute | solution.py:326
  99.0 1.9 %collective-permute-start.13 = (f32[4,8,8,512]{3,2,1,0:T(8,128)S(1)}, f32[4,8,8,512]{3,2,1,0:T(8,128)S(1)}, u32[]{:S(2)}, u32[]{:S(2)}) collective-permute-start(f32[4,8,8,512]{3,2,1,0:T(8,128)S(1)} %get-tuple-element.29.state), channel_id=1, source_target_pairs={{0,1},{1,0},{2,3},{3,2},{4,5},{5,4},{6,7},{7,6},{8,9},{9,8},{10,11... | collective-permute-start | bytes 1572872 | tf_op jit(solution)/shard_map/ppermute | solution.py:317
  100.9 6.1 %collective-permute-start.14 = (f32[2,8,128]{2,1,0:T(8,128)S(1)}, f32[2,8,128]{2,1,0:T(8,128)S(1)}, u32[]{:S(2)}, u32[]{:S(2)}) collective-permute-start(f32[2,8,128]{2,1,0:T(8,128)S(1)} %get-tuple-element.23.refs_1_), channel_id=1, source_target_pairs={{32,0},{64,32},{96,64},{128,96},{160,128},{192,160},{224,192},{256... | collective-permute-start | bytes 24584 | tf_op jit(solution)/shard_map/ppermute | solution.py:371
  107.0 0.0 collective-permute-done.15.others
  107.0 0.7 shard_map.44.refs_1_.given
  107.8 0.6 collective-permute-done.14.refs_0_
  108.4 3.1 %collective-permute-done.12.outer = f32[4,8,8,512]{3,2,1,0:T(8,128)S(1)} collective-permute-done((f32[4,8,8,512]{3,2,1,0:T(8,128)S(1)}, f32[4,8,8,512]{3,2,1,0:T(8,128)S(1)}, u32[]{:S(2)}, u32[]{:S(2)}) %collective-permute-start.12) | collective-permute-done | bytes 524320 | tf_op jit(solution)/shard_map/ppermute | solution.py:326
  111.4 0.0 collective-permute-done.13.inner
  111.4 4.0 %shard_map.45 = (f32[4,8,8,512]{3,2,1,0:T(8,128)S(1)}, f32[32,2,8,128]{3,2,1,0:T(8,128)S(1)}) custom-call(s32[3]{0:T(128)S(1)} %pad_add_fusion.place, f32[4,8,8,512]{3,2,1,0:T(8,128)S(1)} %get-tuple-element.29.state, f32[4,8,8,512]{3,2,1,0:T(8,128)S(1)} %collective-permute-done.12.outer, f32[4,8,8,512]{3,2,1,0:T(8,128)S(1)} %collective-permute-done.13.inner, ...), custom_call_target="tpu_custom_call" | custom-call | tf_op jit(solution)/shard_map/pallas_call | solution.py:402
  115.5 16.6 %all_to_all.10.residuals = f32[32,2,8,128]{3,2,1,0:T(8,128)S(1)} all-to-all(f32[32,2,8,128]{3,2,1,0:T(8,128)S(1)} %get-tuple-element.31), channel_id=1, replica_groups=mesh['cuts'=16,'space'=32] {'space'}, dimensions={0} | all-to-all | bytes 524288 | tf_op jit(solution)/shard_map/all_to_all | solution.py:403
  132.0 10.7 %shard_map.46 = f32[16,2,8,128]{3,2,1,0:T(8,128)S(1)} custom-call(s32[3]{0:T(128)S(1)} %pad_add_fusion.place, f32[32,2,8,128]{3,2,1,0:T(8,128)S(1)} %all_to_all.10.residuals, f32[32,7,2,8,128]{4,3,2,1,0:T(8,128)S(1)} %shard_map.44.refs_1_.given), custom_call_target="tpu_custom_call" | custom-call | tf_op jit(solution)/shard_map/pallas_call | solution.py:404
  142.7 14.4 %all_to_all.11.shares = f32[16,2,8,128]{3,2,1,0:T(8,128)S(1)} all-to-all(f32[16,2,8,128]{3,2,1,0:T(8,128)S(1)} %shard_map.46), channel_id=1, replica_groups=mesh['cuts'=16,'space'=32] {'cuts'}, dimensions={0} | all-to-all | bytes 262144 | tf_op jit(solution)/shard_map/all_to_all | solution.py:410
  157.1 1.1 shard_map.47
Async XLA Ops:
  0.1 1.4 copy-start
  1.5 1.0 copy-start.2
  2.5 1.0 copy-start.3
  3.6 14.0 %copy-start.1 = (f32[3,4,64,512]{3,2,1,0:T(8,128)S(1)}, f32[3,4,64,512]{3,2,1,0:T(8,128)}, u32[]{:S(2)}) copy-start(f32[3,4,64,512]{3,2,1,0:T(8,128)} %velocity.3) | copy-start | bytes 4718596
  5.8 25.3 %collective-permute-start.1 = (f32[16,64,512]{2,1,0:T(8,128)S(1)}, f32[16,64,512]{2,1,0:T(8,128)S(1)}, u32[]{:S(2)}, u32[]{:S(2)}) collective-permute-start(f32[16,64,512]{2,1,0:T(8,128)S(1)} %get-tuple-element.20), channel_id=1, source_target_pairs={{0,1},{1,0},{2,3},{3,2},{4,5},{5,4},{6,7},{7,6},{8,9},{9,8},{10,11... | collective-permute-start | bytes 6291464 | tf_op jit(solution)/shard_map/ppermute | solution.py:317
  7.7 30.2 %collective-permute-start.2 = (f32[9,64,512]{2,1,0:T(8,128)S(1)}, f32[9,64,512]{2,1,0:T(8,128)S(1)}, u32[]{:S(2)}, u32[]{:S(2)}) collective-permute-start(f32[9,64,512]{2,1,0:T(8,128)S(1)} %get-tuple-element.22), channel_id=1, source_target_pairs={{0,287},{1,258},{2,257},{3,260},{4,259},{5,262},{6,261},{7,264},{8... | collective-permute-start | bytes 3538952 | tf_op jit(solution)/shard_map/ppermute | solution.py:335
  11.2 22.4 %collective-permute-start = (f32[7,64,512]{2,1,0:T(8,128)S(1)}, f32[7,64,512]{2,1,0:T(8,128)S(1)}, u32[]{:S(2)}, u32[]{:S(2)}) collective-permute-start(f32[7,64,512]{2,1,0:T(8,128)S(1)} %get-tuple-element.19), channel_id=1, source_target_pairs={{0,31},{1,2},{2,1},{3,4},{4,3},{5,6},{6,5},{7,8},{8,7},{9,10},{10,... | collective-permute-start | bytes 2752520 | tf_op jit(solution)/shard_map/ppermute | solution.py:326
  18.9 19.6 %collective-permute-start.3 = (f32[1,4,2,8,128]{4,3,2,1,0:T(8,128)S(1)}, f32[1,4,2,8,128]{4,3,2,1,0:T(8,128)S(1)}, u32[]{:S(2)}, u32[]{:S(2)}) collective-permute-start(f32[1,4,2,8,128]{4,3,2,1,0:T(8,128)S(1)} %bitcast.7), channel_id=1, source_target_pairs={{0,8},{1,9},{2,10},{3,11},{4,12},{5,13},{6,14},{7,15},{8,0},{9,1},... | collective-permute-start | bytes 98312 | tf_op jit(solution)/shard_map/ppermute | solution.py:345
  22.0 16.5 %collective-permute-start.4 = (f32[1,4,2,8,128]{4,3,2,1,0:T(8,128)S(1)}, f32[1,4,2,8,128]{4,3,2,1,0:T(8,128)S(1)}, u32[]{:S(2)}, u32[]{:S(2)}) collective-permute-start(f32[1,4,2,8,128]{4,3,2,1,0:T(8,128)S(1)} %bitcast.8), channel_id=1, source_target_pairs={{0,16},{1,17},{2,18},{3,19},{4,20},{5,21},{6,22},{7,23},{8,24},{9,... | collective-permute-start | bytes 98312 | tf_op jit(solution)/shard_map/ppermute | solution.py:345
  31.1 8.3 %collective-permute-start.5 = (f32[1,4,2,8,128]{4,3,2,1,0:T(8,128)S(1)}, f32[1,4,2,8,128]{4,3,2,1,0:T(8,128)S(1)}, u32[]{:S(2)}, u32[]{:S(2)}) collective-permute-start(f32[1,4,2,8,128]{4,3,2,1,0:T(8,128)S(1)} %bitcast.9), channel_id=1, source_target_pairs={{0,24},{1,25},{2,26},{3,27},{4,28},{5,29},{6,30},{7,31},{8,16},{9,... | collective-permute-start | bytes 98312 | tf_op jit(solution)/shard_map/ppermute | solution.py:345
  43.6 21.4 %collective-permute-start.6 = (f32[4,8,8,512]{3,2,1,0:T(8,128)S(1)}, f32[4,8,8,512]{3,2,1,0:T(8,128)S(1)}, u32[]{:S(2)}, u32[]{:S(2)}) collective-permute-start(f32[4,8,8,512]{3,2,1,0:T(8,128)S(1)} %get-tuple-element.25.state), channel_id=1, source_target_pairs={{0,31},{1,2},{2,1},{3,4},{4,3},{5,6},{6,5},{7,8},{8,7},{9,10},{10,... | collective-permute-start | bytes 1572872 | tf_op jit(solution)/shard_map/ppermute | solution.py:326
  51.8 13.2 %collective-permute-start.7 = (f32[4,8,8,512]{3,2,1,0:T(8,128)S(1)}, f32[4,8,8,512]{3,2,1,0:T(8,128)S(1)}, u32[]{:S(2)}, u32[]{:S(2)}) collective-permute-start(f32[4,8,8,512]{3,2,1,0:T(8,128)S(1)} %get-tuple-element.25.state), channel_id=1, source_target_pairs={{0,1},{1,0},{2,3},{3,2},{4,5},{5,4},{6,7},{7,6},{8,9},{9,8},{10,11... | collective-permute-start | bytes 1572872 | tf_op jit(solution)/shard_map/ppermute | solution.py:317
  56.9 8.1 %collective-permute-start.8 = (f32[4,4,2,8,128]{4,3,2,1,0:T(8,128)S(1)}, f32[4,4,2,8,128]{4,3,2,1,0:T(8,128)S(1)}, u32[]{:S(2)}, u32[]{:S(2)}) collective-permute-start(f32[4,4,2,8,128]{4,3,2,1,0:T(8,128)S(1)} %get-tuple-element.26.refs_0_), channel_id=1, source_target_pairs={{0,258},{1,259},{2,256},{3,257},{4,262},{5,263},{6,260},{7,261},{8... | collective-permute-start | bytes 393224 | tf_op jit(solution)/shard_map/ppermute | solution.py:344
  68.9 16.8 %collective-permute-start.10 = (f32[4,8,8,512]{3,2,1,0:T(8,128)S(1)}, f32[4,8,8,512]{3,2,1,0:T(8,128)S(1)}, u32[]{:S(2)}, u32[]{:S(2)}) collective-permute-start(f32[4,8,8,512]{3,2,1,0:T(8,128)S(1)} %get-tuple-element.27.state), channel_id=1, source_target_pairs={{0,1},{1,0},{2,3},{3,2},{4,5},{5,4},{6,7},{7,6},{8,9},{9,8},{10,11... | collective-permute-start | bytes 1572872 | tf_op jit(solution)/shard_map/ppermute | solution.py:317
  70.8 18.5 %collective-permute-start.9 = (f32[4,8,8,512]{3,2,1,0:T(8,128)S(1)}, f32[4,8,8,512]{3,2,1,0:T(8,128)S(1)}, u32[]{:S(2)}, u32[]{:S(2)}) collective-permute-start(f32[4,8,8,512]{3,2,1,0:T(8,128)S(1)} %get-tuple-element.27.state), channel_id=1, source_target_pairs={{0,31},{1,2},{2,1},{3,4},{4,3},{5,6},{6,5},{7,8},{8,7},{9,10},{10,... | collective-permute-start | bytes 1572872 | tf_op jit(solution)/shard_map/ppermute | solution.py:326
  77.0 8.7 %collective-permute-start.11 = (f32[8,4,2,8,128]{4,3,2,1,0:T(8,128)S(1)}, f32[8,4,2,8,128]{4,3,2,1,0:T(8,128)S(1)}, u32[]{:S(2)}, u32[]{:S(2)}) collective-permute-start(f32[8,4,2,8,128]{4,3,2,1,0:T(8,128)S(1)} %get-tuple-element.28.refs_0_), channel_id=1, source_target_pairs={{0,4},{1,5},{2,6},{3,7},{4,0},{5,1},{6,2},{7,3},{8,12},{9,13},{10,... | collective-permute-start | bytes 786440 | tf_op jit(solution)/shard_map/ppermute | solution.py:345
  93.2 13.8 %collective-permute-start.15 = (f32[16,4,2,8,128]{4,3,2,1,0:T(8,128)S(1)}, f32[16,4,2,8,128]{4,3,2,1,0:T(8,128)S(1)}, u32[]{:S(2)}, u32[]{:S(2)}) collective-permute-start(f32[16,4,2,8,128]{4,3,2,1,0:T(8,128)S(1)} %get-tuple-element.30.some), channel_id=1, source_target_pairs={{0,1},{1,0},{2,3},{3,2},{4,5},{5,4},{6,7},{7,6},{8,9},{9,8},{10,11... | collective-permute-start | bytes 1572872 | tf_op jit(solution)/shard_map/ppermute | solution.py:345
  95.1 16.3 %collective-permute-start.12 = (f32[4,8,8,512]{3,2,1,0:T(8,128)S(1)}, f32[4,8,8,512]{3,2,1,0:T(8,128)S(1)}, u32[]{:S(2)}, u32[]{:S(2)}) collective-permute-start(f32[4,8,8,512]{3,2,1,0:T(8,128)S(1)} %get-tuple-element.29.state), channel_id=1, source_target_pairs={{0,31},{1,2},{2,1},{3,4},{4,3},{5,6},{6,5},{7,8},{8,7},{9,10},{10,... | collective-permute-start | bytes 1572872 | tf_op jit(solution)/shard_map/ppermute | solution.py:326
  99.0 12.5 %collective-permute-start.13 = (f32[4,8,8,512]{3,2,1,0:T(8,128)S(1)}, f32[4,8,8,512]{3,2,1,0:T(8,128)S(1)}, u32[]{:S(2)}, u32[]{:S(2)}) collective-permute-start(f32[4,8,8,512]{3,2,1,0:T(8,128)S(1)} %get-tuple-element.29.state), channel_id=1, source_target_pairs={{0,1},{1,0},{2,3},{3,2},{4,5},{5,4},{6,7},{7,6},{8,9},{9,8},{10,11... | collective-permute-start | bytes 1572872 | tf_op jit(solution)/shard_map/ppermute | solution.py:317
  100.9 7.5 %collective-permute-start.14 = (f32[2,8,128]{2,1,0:T(8,128)S(1)}, f32[2,8,128]{2,1,0:T(8,128)S(1)}, u32[]{:S(2)}, u32[]{:S(2)}) collective-permute-start(f32[2,8,128]{2,1,0:T(8,128)S(1)} %get-tuple-element.23.refs_1_), channel_id=1, source_target_pairs={{32,0},{64,32},{96,64},{128,96},{160,128},{192,160},{224,192},{256... | collective-permute-start | bytes 24584 | tf_op jit(solution)/shard_map/ppermute | solution.py:371

commit v9 on v8

--- a/solution.py
+++ b/solution.py
@@ -19,15 +19,17 @@
 ANY = pl.BlockSpec(memory_space=pl.ANY)
 F32 = jnp.float32
 MIB = 1024 * 1024
-
-
-def call(body, outs, ins, scratch=(), limit=24, out=VMEM):
+SMALL = pl.CostEstimate(flops=1, bytes_accessed=1, transcendentals=0)
+
+
+def call(body, outs, ins, scratch=(), limit=24, cost=None):
     return pl.pallas_call(
         body,
         out_shape=[jax.ShapeDtypeStruct(s, F32) for s in outs],
         in_specs=ins,
-        out_specs=[out] * len(outs),
+        out_specs=[VMEM] * len(outs),
         scratch_shapes=list(scratch),
+        cost_estimate=cost,
         compiler_params=pltpu.CompilerParams(vmem_limit_bytes=limit * MIB),
     )
 
@@ -82,11 +84,23 @@
     return weights
 
 
+def run(pairs, ready):
+    copies = [pltpu.make_async_copy(*pair, ready.at[i]) for i, pair in enumerate(pairs)]
+    for copy in copies:
+        copy.start()
+    for copy in copies:
+        copy.wait()
+
+
+def cut_fields_kernel(place, velocity, fields, ready):
+    run([(velocity.at[f, pl.ds(place[2], REACH)], fields.at[pl.ds(f * REACH, REACH)]) for f in range(3)], ready)
+
+
 STATE_AT = 3 * REACH
 INNER = STATE_AT + LAYERS + REACH
 
 
-def cut_kernel(place, velocity, diffusivity, starts, fields, mixed, inner, ready):
+def cut_kernel(place, velocity, diffusivity, starts, earlier, mixed, inner, ready):
     core = place[2]
     pairs = [
         (diffusivity.at[pl.ds(core, REACH)], mixed.at[pl.ds(LAYERS, REACH)]),
@@ -95,13 +109,8 @@
         (starts.at[0], inner.at[pl.ds(STATE_AT, LAYERS)]),
     ]
     for f in range(3):
-        pairs.append((velocity.at[f, pl.ds(core, REACH)], fields.at[pl.ds(f * REACH, REACH)]))
         pairs.append((velocity.at[f, pl.ds(1 - core, REACH)], inner.at[pl.ds(f * REACH, REACH)]))
-    copies = [pltpu.make_async_copy(*pair, ready.at[i]) for i, pair in enumerate(pairs)]
-    for copy in copies:
-        copy.start()
-    for copy in copies:
-        copy.wait()
+    run(pairs, ready)
 
 
 def own_kernel(velocity, diffusivity, starts, weights, coarse_fields, coarse_old, buffer):
@@ -189,24 +198,24 @@
         fine_layers(source, weights, goal, begin + last, first + last, begin + last - shift, 1)
 
 
-def round_kernel(raw, final, place, state, outer, inner, own, own_outer, own_inner, *refs):
-    if final:
-        later, after, out, residual, one, two, buffer = refs
-    else:
-        *parts, out, joined, one, two, buffer = refs
-        begin = 0
-        for part in parts:
-            joined[begin : begin + part.shape[0]] = part[...]
-            begin += part.shape[0]
+def join(parts, joined):
+    begin = 0
+    for part in parts:
+        joined[begin : begin + part.shape[0]] = part[...]
+        begin += part.shape[0]
+
+
+def first_kernel(place, state, outer, inner, own, own_outer, own_inner, *refs):
+    *parts, out, near, far, joined, one, two, buffer = refs
+    join(parts, joined)
     core = place[2]
 
     def enter(x, carry):
         blocks = ((state, LAYERS), (outer, 2 * LAYERS * core), (inner, 2 * LAYERS * (1 - core)))
         for i, (ref, begin) in enumerate(blocks):
-            if raw:
-                spread(ref[(STATE_AT if ref is inner else 0) + x], buffer.at[i])
+            spread(ref[(STATE_AT if ref is inner else 0) + x], buffer.at[i])
             for j in range(8):
-                one[begin + x, j] = spread_tile(buffer.at[i], j) if raw else ref[x, j]
+                one[begin + x, j] = spread_tile(buffer.at[i], j)
         return carry
 
     lax.fori_loop(0, LAYERS, enter, 0)
@@ -221,6 +230,66 @@
             sweep(source, goal, below + core * (above - below), depth, own_outer, (1 - core) * (step - 1))
             sweep(source, goal, above - core * (above - below), depth, own_inner, core * (step - 1))
         source, target = target, source
+    for i in range(2):
+        near[i] = out[2 * core + i]
+        far[i] = out[2 - 2 * core + i]
+
+
+def passed_at(step, core):
+    return 2 + step + core * (6 - 2 * step)
+
+
+def near_kernel(place, state, inner, near, own, own_inner, own_outer, passed, rest, one, two):
+    core = place[2]
+
+    def enter(x, carry):
+        for j in range(8):
+            one[LAYERS + x, j] = state[x, j]
+            one[2 * LAYERS * (1 - core) + x, j] = inner[x, j]
+        return carry
+
+    lax.fori_loop(0, LAYERS, enter, 0)
+    for i in range(2):
+        one[2 + 6 * core + i] = near[i]
+    sweep(one, two, 3 + 5 * core, 1, own_outer, 2 - 2 * core)
+    sweep(one, two, 4, 4, own, 0)
+    sweep(one, two, 8 - 7 * core, 3, own_inner, 0)
+    for i in range(2):
+        passed[0, i] = two[passed_at(1, core) + i]
+    sweep(two, one, 4, 4, own, 0)
+    sweep(two, one, 8 - 6 * core, 2, own_inner, core)
+    for i in range(2):
+        passed[1, i] = one[passed_at(2, core) + i]
+    sweep(one, two, 5 - core, 3, own, 1 - core)
+    sweep(one, two, 8 - 5 * core, 1, own_inner, 2 * core)
+    for i in range(2):
+        passed[2, i] = two[passed_at(3, core) + i]
+    sweep(two, rest, 6 - 2 * core, 2, own, 2 - 2 * core, 6 - 2 * core)
+
+
+def far_kernel(final, place, near, far, own, own_outer, passed, rest, *refs):
+    if final:
+        later, after, out, residual, one, two = refs
+    else:
+        *parts, out, next_near, joined, one, two = refs
+        join(parts, joined)
+    core = place[2]
+    for i in range(2):
+        one[10 * core + i] = far[i]
+        one[2 + 6 * core + i] = near[i]
+    sweep(one, two, 1 + 8 * core, 2, own_outer, core)
+    for i in range(2):
+        two[passed_at(1, core) + i] = passed[0, i]
+    sweep(two, one, 2 + 6 * core, 2, own_outer, 1 - core)
+    for i in range(2):
+        one[passed_at(2, core) + i] = passed[1, i]
+    sweep(one, two, 3 + 5 * core, 1, own_outer, 2 - 2 * core)
+    sweep(one, two, 4 + 3 * core, 1, own, 3 * core)
+    for i in range(2):
+        two[passed_at(3, core) + i] = passed[2, i]
+    sweep(two, out, 4 + 2 * core, 2, own, 2 * core, LAYERS)
+    for i in range(2):
+        out[2 - 2 * core + i] = rest[i]
     if final:
         sums = half_sums(lambda j: (out[0, j] + out[1, j]) + (out[2, j] + out[3, j]))
         means = exact_dot(jnp.concatenate(sums, axis=0), fours((512, 128), 0)) * (1.0 / 64)
@@ -228,6 +297,9 @@
             left = means[8 * h : 8 * h + 8] - later[h]
             for copy in range(residual.shape[0]):
                 residual[copy, h] = left
+    else:
+        for i in range(2):
+            next_near[i] = out[2 * core + i]
 
 
 def coarse_step(read, weights, write, count):
@@ -353,12 +425,20 @@
     place = jnp.stack([lax.axis_index("cuts"), row, row & 1]).astype(jnp.int32)
     columns = pltpu.VMEM((5, 4, 64, 128), F32)
 
-    fields_outer, mixed_outer, all_inner = call(
+    fields_outer = call(
+        cut_fields_kernel,
+        [(3 * REACH, 64, 512)],
+        [SMEM, ANY],
+        [pltpu.SemaphoreType.DMA((3,))],
+        cost=SMALL,
+    )(place, velocity)[0]
+    mixed_outer, all_inner = call(
         cut_kernel,
-        [(3 * REACH, 64, 512), (LAYERS + REACH, 64, 512), (INNER, 64, 512)],
-        [SMEM, ANY, ANY, ANY],
-        [pltpu.SemaphoreType.DMA((10,))],
-    )(place, velocity, diffusivity, starts)
+        [(LAYERS + REACH, 64, 512), (INNER, 64, 512)],
+        [SMEM, ANY, ANY, ANY, ANY],
+        [pltpu.SemaphoreType.DMA((7,))],
+        cost=SMALL,
+    )(place, velocity, diffusivity, starts, fields_outer)
     fields_outer = swap_outer_fields(fields_outer)
     mixed_outer = swap_outer(mixed_outer)
     all_inner = swap_inner(all_inner)
@@ -367,23 +447,36 @@
         [(LAYERS, 7, *TILE), (4, *COARSE), COARSE],
         [VMEM] * 3,
         [columns],
+        cost=SMALL,
     )(velocity, diffusivity, starts[0])
     coarse_later = lax.ppermute(coarse_old, "cuts", [((n + 1) % slices, n) for n in range(slices)])
     gathered = coarse_fields[None]
     side = [(REACH, 7, *TILE)]
-    inner_weights = call(functools.partial(side_kernel, STATE_AT + LAYERS), side, [VMEM, ANY], [columns])(
+    inner_weights = call(functools.partial(side_kernel, STATE_AT + LAYERS), side, [VMEM, ANY], [columns], cost=SMALL)(
         all_inner, coarse_old
     )[0]
-    outer_weights = call(functools.partial(side_kernel, LAYERS), side, [VMEM, VMEM, ANY], [columns])(
+    outer_weights = call(functools.partial(side_kernel, LAYERS), side, [VMEM, VMEM, ANY], [columns], cost=SMALL)(
         fields_outer, mixed_outer, inner_weights
     )[0]
-    state, inner, outer = starts[0], all_inner, mixed_outer
-    scratch = [pltpu.VMEM((3 * LAYERS, *TILE), F32)] * 2 + [columns]
-    for index in range(ROUNDS):
-        raw, final = index == 0, index == ROUNDS - 1
-        if index > 0:
-            inner, outer = swap_inner(state), swap_outer(state)
-        operands = [place, state, outer, inner, own_weights, outer_weights, inner_weights]
+    pair = (2, *TILE)
+    scratch = [pltpu.VMEM((3 * LAYERS, *TILE), F32)] * 2
+    parts = [gathered] + [across(gathered, bits) for bits in (8, 16, 24)]
+    state, near, far, gathered = call(
+        first_kernel,
+        [block, pair, pair, (4, 4, *COARSE)],
+        [SMEM] + [VMEM] * (6 + len(parts)),
+        scratch + [columns],
+    )(place, starts[0], mixed_outer, all_inner, own_weights, outer_weights, inner_weights, *parts)
+    for index in range(1, ROUNDS):
+        final = index == ROUNDS - 1
+        near, inner, far = swap_outer(near), swap_inner(state), swap_outer(far)
+        passed, rest = call(
+            near_kernel,
+            [(LAYERS - 1, *pair), pair],
+            [SMEM] + [VMEM] * 6,
+            scratch,
+        )(place, state, inner, near, own_weights, inner_weights, outer_weights)
+        operands = [place, near, far, own_weights, outer_weights, passed, rest]
         specs = [SMEM] + [VMEM] * 6
         if final:
             weights = call(
@@ -395,11 +488,12 @@
             specs += [VMEM, ANY]
             outs = [block, (count, *COARSE)]
         else:
-            parts = [gathered] + [across(gathered, b) for b in ((8, 16, 24), (2,), (4,))[index]]
+            parts = [gathered, across(gathered, (2, 4)[index - 1])]
             operands += parts
             specs += [VMEM] * len(parts)
-            outs = [block, (len(parts) * gathered.shape[0], 4, *COARSE)]
-        state, gathered = call(functools.partial(round_kernel, raw, final), outs, specs, scratch)(*operands)
+            outs = [block, pair, (2 * gathered.shape[0], 4, *COARSE)]
+        state, *near, gathered = call(functools.partial(far_kernel, final), outs, specs, scratch)(*operands)
+        near, far = near[0] if near else None, rest
     residuals = lax.all_to_all(gathered, "space", 0, 0)
     shares = call(
         chain_kernel,

time: 159 us -> 158 us (level)
  waiting for transfers between devices: 23.4 us -> 11.2 us
  starting transfers between devices: 66.9 us -> 75.5 us
  Pallas kernels: 33.1 us -> 36.3 us
  local copies, waits for them, and re-layouts: 3.49 us -> 1.46 us
  blocking collectives: 31 us -> 32.9 us
    ppermute x5, waiting for transfers between devices: 7.72 us -> 0.97 us  [across(): return lax.ppermute(block, 'space', [(p, p ^ bits) for p in range(count)])]
    ppermute x5, starting transfers between devices: 18 us -> 23.3 us  [across(): return lax.ppermute(block, 'space', [(p, p ^ bits) for p in range(count)])]
    ppermute x4, starting transfers between devices: 10.8 us -> 15.7 us  [swap_inner(): return lax.ppermute(block, 'space', [(p, p ^ 1) for p in range(count)])]
    ppermute x1, waiting for transfers between devices: 4.14 us -> 0.24 us  [across(): return lax.ppermute(block, ('cuts', 'space'), route)]
    pallas_call x5 -> x9, Pallas kernels: 18.2 us -> 21.4 us  [the longest x3 9.17 us: shards(): call(near_kernel, [(LAYERS - 1, *pair), pair], [SMEM] + [VMEM] * 6, scratch)]
    unnamed x8, local copies, waits for them, and re-layouts: 3.49 us -> 1.46 us
    all_to_all x1, blocking collectives: 16.6 us -> 18.4 us  [shards(): residuals = lax.all_to_all(gathered, 'space', 0, 0)]
    ppermute x4 -> x7, starting transfers between devices: 24.6 us -> 23 us  [swap_outer(): lax.ppermute(block, 'space', [(p, outer_partner(p, count)) for p in range...]
  transfers between devices with their start and end apart: 16 -> 19, of which waited for: 7 -> 8; matrix products, arithmetic and copies ran while one was open for 0% -> 0% of each run, Pallas kernels for 2% -> 8%
where the time goes in v9:
time: 158 us
  starting transfers between devices  75.5 us (48%)
  Pallas kernels  36.3 us (23%)
  blocking collectives  32.9 us (21%)
  waiting for transfers between devices  11.2 us (7%)
    ppermute x5, starting transfers between devices, across(): return lax.ppermute(block, 'space', [(p, p ^ bits) for p in range(count)])  23.3 us
    ppermute x7, starting transfers between devices, swap_outer(): lax.ppermute(block, 'space', [(p, outer_partner(p, count)) for p in range...  23 us
    all_to_all x1, blocking collectives, shards(): residuals = lax.all_to_all(gathered, 'space', 0, 0)  18.4 us
    ppermute x4, starting transfers between devices, swap_inner(): return lax.ppermute(block, 'space', [(p, p ^ 1) for p in range(count)])  15.7 us
    all_to_all x1, blocking collectives, shards(): shares = lax.all_to_all(shares, 'cuts', 0, 0)  14.4 us
    pallas_call x1, Pallas kernels, shards(): call(chain_kernel, [(slices, *COARSE)], [SMEM, VMEM, VMEM], [pltpu.VMEM((...  10.7 us
    pallas_call x3, Pallas kernels, shards(): call(near_kernel, [(LAYERS - 1, *pair), pair], [SMEM] + [VMEM] * 6, scratch)  9.17 us
    ppermute x7, waiting for transfers between devices, swap_outer(): lax.ppermute(block, 'space', [(p, outer_partner(p, count)) for p in range...  5.72 us
  transfers between devices with their start and end apart: 19, of which 8 were waited for; matrix products, arithmetic and copies ran while one was open for 0% of the time, Pallas kernels for 8%

profile of v9, /device:TPU:2, one launch (start us, length us, event | category | flops | bytes accessed | tf_op | source)
XLA Modules:
  0.0 157.7 jit_solution(2191853149071087025)
XLA Ops:
  0.0 0.1 pad_add_fusion.place
  0.1 0.0 copy-start
  0.1 1.4 copy-done
  1.5 0.0 copy-start.2
  1.5 0.0 copy-start.3
  1.5 1.1 shard_map.37.earlier
  2.6 0.0 copy-done.2
  2.6 0.0 copy-done.3
  2.7 0.0 copy-start.1
  2.7 1.6 %shard_map.38 = (f32[7,64,512]{2,1,0:T(8,128)S(1)}, f32[16,64,512]{2,1,0:T(8,128)S(1)}) custom-call(s32[3]{0:T(128)S(1)} %pad_add_fusion.place, f32[3,4,64,512]{3,2,1,0:T(8,128)S(1)} %copy-done, f32[4,64,512]{2,1,0:T(8,128)S(1)} %copy-done.3, f32[1,4,64,512]{3,2,1,0:T(8,128)S(1)} %copy-done.2, f32[9,64,512]{2,1,0:T(8,128)S(1)} %shard_map.37.earlier), custom_call_target="tpu_custom_call" | custom-call | flops 1 | bytes 1 | tf_op jit(solution)/shard_map/pallas_call | solution.py:435
  4.3 1.9 %collective-permute-start.1 = (f32[16,64,512]{2,1,0:T(8,128)S(1)}, f32[16,64,512]{2,1,0:T(8,128)S(1)}, u32[]{:S(2)}, u32[]{:S(2)}) collective-permute-start(f32[16,64,512]{2,1,0:T(8,128)S(1)} %get-tuple-element.29), channel_id=1, source_target_pairs={{0,1},{1,0},{2,3},{3,2},{4,5},{5,4},{6,7},{7,6},{8,9},{9,8},{10,11... | collective-permute-start | bytes 6291464 | tf_op jit(solution)/shard_map/ppermute | solution.py:389
  6.2 3.5 %collective-permute-start.2 = (f32[9,64,512]{2,1,0:T(8,128)S(1)}, f32[9,64,512]{2,1,0:T(8,128)S(1)}, u32[]{:S(2)}, u32[]{:S(2)}) collective-permute-start(f32[9,64,512]{2,1,0:T(8,128)S(1)} %shard_map.37.earlier), channel_id=1, source_target_pairs={{0,287},{1,258},{2,257},{3,260},{4,259},{5,262},{6,261},{7,264},{8... | collective-permute-start | bytes 3538952 | tf_op jit(solution)/shard_map/ppermute | solution.py:407
  9.8 6.3 %collective-permute-start = (f32[7,64,512]{2,1,0:T(8,128)S(1)}, f32[7,64,512]{2,1,0:T(8,128)S(1)}, u32[]{:S(2)}, u32[]{:S(2)}) collective-permute-start(f32[7,64,512]{2,1,0:T(8,128)S(1)} %get-tuple-element.28), channel_id=1, source_target_pairs={{0,31},{1,2},{2,1},{3,4},{4,3},{5,6},{6,5},{7,8},{8,7},{9,10},{10,... | collective-permute-start | bytes 2752520 | tf_op jit(solution)/shard_map/ppermute | solution.py:398
  16.1 0.0 copy-done.1
  16.1 1.3 shard_map.39
  17.4 7.9 %collective-permute-start.5 = (f32[1,4,2,8,128]{4,3,2,1,0:T(8,128)S(1)}, f32[1,4,2,8,128]{4,3,2,1,0:T(8,128)S(1)}, u32[]{:S(2)}, u32[]{:S(2)}) collective-permute-start(f32[1,4,2,8,128]{4,3,2,1,0:T(8,128)S(1)} %bitcast.7), channel_id=1, source_target_pairs={{0,24},{1,25},{2,26},{3,27},{4,28},{5,29},{6,30},{7,31},{8,16},{9,... | collective-permute-start | bytes 98312 | tf_op jit(solution)/shard_map/ppermute | solution.py:417
  25.3 1.9 %collective-permute-start.4 = (f32[1,4,2,8,128]{4,3,2,1,0:T(8,128)S(1)}, f32[1,4,2,8,128]{4,3,2,1,0:T(8,128)S(1)}, u32[]{:S(2)}, u32[]{:S(2)}) collective-permute-start(f32[1,4,2,8,128]{4,3,2,1,0:T(8,128)S(1)} %bitcast.8), channel_id=1, source_target_pairs={{0,16},{1,17},{2,18},{3,19},{4,20},{5,21},{6,22},{7,23},{8,24},{9,... | collective-permute-start | bytes 98312 | tf_op jit(solution)/shard_map/ppermute | solution.py:417
  27.3 0.0 collective-permute-done.1.refs_0_.inner
  27.3 4.3 %collective-permute-start.3 = (f32[1,4,2,8,128]{4,3,2,1,0:T(8,128)S(1)}, f32[1,4,2,8,128]{4,3,2,1,0:T(8,128)S(1)}, u32[]{:S(2)}, u32[]{:S(2)}) collective-permute-start(f32[1,4,2,8,128]{4,3,2,1,0:T(8,128)S(1)} %bitcast.9), channel_id=1, source_target_pairs={{0,8},{1,9},{2,10},{3,11},{4,12},{5,13},{6,14},{7,15},{8,0},{9,1},... | collective-permute-start | bytes 98312 | tf_op jit(solution)/shard_map/ppermute | solution.py:417
  31.6 0.6 shard_map.40.refs_2_.own_inner
  32.1 0.0 collective-permute-done.refs_1_.outer
  32.1 4.3 %collective-permute-done.2.refs_0_ = f32[9,64,512]{2,1,0:T(8,128)S(1)} collective-permute-done((f32[9,64,512]{2,1,0:T(8,128)S(1)}, f32[9,64,512]{2,1,0:T(8,128)S(1)}, u32[]{:S(2)}, u32[]{:S(2)}) %collective-permute-start.2) | collective-permute-done | bytes 1179680 | tf_op jit(solution)/shard_map/ppermute | solution.py:407
  36.4 0.6 shard_map.41.own_outer
  37.0 0.0 collective-permute-done.5.refs_3_
  37.0 0.0 collective-permute-done.4.refs_2_
  37.0 0.0 collective-permute-done.3.refs_1_
  37.0 4.2 %shard_map.42 = (f32[4,8,8,512]{3,2,1,0:T(8,128)S(1)}, f32[2,8,8,512]{3,2,1,0:T(8,128)S(1)}, f32[2,8,8,512]{3,2,1,0:T(8,128)S(1)}, f32[4,4,2,8,128]{4,3,2,1,0:T(8,128)S(1)}) custom-call(s32[3]{0:T(128)S(1)} %pad_add_fusion.place, f32[4,64,512]{2,1,0:T(8,128)S(1)} %bitcast.6, f32[7,64,512]{2,1,0:T(8,128)S(1)} %collective-permute-done.refs_1_.outer, ...), custom_call_target="tpu_custom_call" | custom-call | tf_op jit(solution)/shard_map/pallas_call | solution.py:464
  41.2 10.0 %collective-permute-start.8 = (f32[4,8,8,512]{3,2,1,0:T(8,128)S(1)}, f32[4,8,8,512]{3,2,1,0:T(8,128)S(1)}, u32[]{:S(2)}, u32[]{:S(2)}) collective-permute-start(f32[4,8,8,512]{3,2,1,0:T(8,128)S(1)} %get-tuple-element.35.state), channel_id=1, source_target_pairs={{0,1},{1,0},{2,3},{3,2},{4,5},{5,4},{6,7},{7,6},{8,9},{9,8},{10,11... | collective-permute-start | bytes 1572872 | tf_op jit(solution)/shard_map/ppermute | solution.py:389
  51.2 3.6 %collective-permute-start.6 = (f32[2,8,8,512]{3,2,1,0:T(8,128)S(1)}, f32[2,8,8,512]{3,2,1,0:T(8,128)S(1)}, u32[]{:S(2)}, u32[]{:S(2)}) collective-permute-start(f32[2,8,8,512]{3,2,1,0:T(8,128)S(1)} %get-tuple-element.33), channel_id=1, source_target_pairs={{0,31},{1,2},{2,1},{3,4},{4,3},{5,6},{6,5},{7,8},{8,7},{9,10},{10,... | collective-permute-start | bytes 786440 | tf_op jit(solution)/shard_map/ppermute | solution.py:398
  54.8 1.9 %collective-permute-start.7 = (f32[2,8,8,512]{3,2,1,0:T(8,128)S(1)}, f32[2,8,8,512]{3,2,1,0:T(8,128)S(1)}, u32[]{:S(2)}, u32[]{:S(2)}) collective-permute-start(f32[2,8,8,512]{3,2,1,0:T(8,128)S(1)} %get-tuple-element.34), channel_id=1, source_target_pairs={{0,31},{1,2},{2,1},{3,4},{4,3},{5,6},{6,5},{7,8},{8,7},{9,10},{10,... | collective-permute-start | bytes 786440 | tf_op jit(solution)/shard_map/ppermute | solution.py:398
  56.8 4.6 %collective-permute-start.9 = (f32[4,4,2,8,128]{4,3,2,1,0:T(8,128)S(1)}, f32[4,4,2,8,128]{4,3,2,1,0:T(8,128)S(1)}, u32[]{:S(2)}, u32[]{:S(2)}) collective-permute-start(f32[4,4,2,8,128]{4,3,2,1,0:T(8,128)S(1)} %get-tuple-element.38.refs_0_), channel_id=1, source_target_pairs={{0,258},{1,259},{2,256},{3,257},{4,262},{5,263},{6,260},{7,261},{8... | collective-permute-start | bytes 393224 | tf_op jit(solution)/shard_map/ppermute | solution.py:416
  61.4 0.3 collective-permute-done.6.near
  61.7 0.0 collective-permute-done.8.inner
  61.7 3.1 %shard_map.43 = (f32[3,2,8,8,512]{4,3,2,1,0:T(8,128)S(1)}, f32[2,8,8,512]{3,2,1,0:T(8,128)S(1)}) custom-call(s32[3]{0:T(128)S(1)} %pad_add_fusion.place, f32[4,8,8,512]{3,2,1,0:T(8,128)S(1)} %get-tuple-element.35.state, f32[4,8,8,512]{3,2,1,0:T(8,128)S(1)} %collective-permute-done.8.inner, f32[2,8,8,512]{3,2,1,0:T(8,128)S(1)} %collective-permute-done.6.near, ...), custom_call_target="tpu_custom_call" | custom-call | tf_op jit(solution)/shard_map/pallas_call | solution.py:473
  64.8 0.2 collective-permute-done.9.refs_1_
  65.0 2.3 %collective-permute-done.7.far = f32[2,8,8,512]{3,2,1,0:T(8,128)S(1)} collective-permute-done((f32[2,8,8,512]{3,2,1,0:T(8,128)S(1)}, f32[2,8,8,512]{3,2,1,0:T(8,128)S(1)}, u32[]{:S(2)}, u32[]{:S(2)}) %collective-permute-start.7) | collective-permute-done | bytes 262176 | tf_op jit(solution)/shard_map/ppermute | solution.py:398
  67.3 1.7 %shard_map.44 = (f32[4,8,8,512]{3,2,1,0:T(8,128)S(1)}, f32[2,8,8,512]{3,2,1,0:T(8,128)S(1)}, f32[8,4,2,8,128]{4,3,2,1,0:T(8,128)S(1)}) custom-call(s32[3]{0:T(128)S(1)} %pad_add_fusion.place, f32[2,8,8,512]{3,2,1,0:T(8,128)S(1)} %collective-permute-done.6.near, f32[2,8,8,512]{3,2,1,0:T(8,128)S(1)} %collective-permute-done.7.far, ...), custom_call_target="tpu_custom_call" | custom-call | tf_op jit(solution)/shard_map/pallas_call | solution.py:495
  69.0 1.9 %collective-permute-start.12 = (f32[4,8,8,512]{3,2,1,0:T(8,128)S(1)}, f32[4,8,8,512]{3,2,1,0:T(8,128)S(1)}, u32[]{:S(2)}, u32[]{:S(2)}) collective-permute-start(f32[4,8,8,512]{3,2,1,0:T(8,128)S(1)} %get-tuple-element.40.state), channel_id=1, source_target_pairs={{0,1},{1,0},{2,3},{3,2},{4,5},{5,4},{6,7},{7,6},{8,9},{9,8},{10,11... | collective-permute-start | bytes 1572872 | tf_op jit(solution)/shard_map/ppermute | solution.py:389
  70.9 3.6 %collective-permute-start.10 = (f32[2,8,8,512]{3,2,1,0:T(8,128)S(1)}, f32[2,8,8,512]{3,2,1,0:T(8,128)S(1)}, u32[]{:S(2)}, u32[]{:S(2)}) collective-permute-start(f32[2,8,8,512]{3,2,1,0:T(8,128)S(1)} %get-tuple-element.39), channel_id=1, source_target_pairs={{0,31},{1,2},{2,1},{3,4},{4,3},{5,6},{6,5},{7,8},{8,7},{9,10},{10,... | collective-permute-start | bytes 786440 | tf_op jit(solution)/shard_map/ppermute | solution.py:398
  74.6 4.0 %collective-permute-start.13 = (f32[8,4,2,8,128]{4,3,2,1,0:T(8,128)S(1)}, f32[8,4,2,8,128]{4,3,2,1,0:T(8,128)S(1)}, u32[]{:S(2)}, u32[]{:S(2)}) collective-permute-start(f32[8,4,2,8,128]{4,3,2,1,0:T(8,128)S(1)} %get-tuple-element.43.refs_0_), channel_id=1, source_target_pairs={{0,4},{1,5},{2,6},{3,7},{4,0},{5,1},{6,2},{7,3},{8,12},{9,13},{10,... | collective-permute-start | bytes 786440 | tf_op jit(solution)/shard_map/ppermute | solution.py:417
  78.5 1.9 %collective-permute-start.11 = (f32[2,8,8,512]{3,2,1,0:T(8,128)S(1)}, f32[2,8,8,512]{3,2,1,0:T(8,128)S(1)}, u32[]{:S(2)}, u32[]{:S(2)}) collective-permute-start(f32[2,8,8,512]{3,2,1,0:T(8,128)S(1)} %get-tuple-element.37.rest), channel_id=1, source_target_pairs={{0,31},{1,2},{2,1},{3,4},{4,3},{5,6},{6,5},{7,8},{8,7},{9,10},{10,... | collective-permute-start | bytes 786440 | tf_op jit(solution)/shard_map/ppermute | solution.py:398
  80.5 0.8 collective-permute-done.10.near
  81.3 0.0 collective-permute-done.12.inner
  81.3 3.1 %shard_map.45 = (f32[3,2,8,8,512]{4,3,2,1,0:T(8,128)S(1)}, f32[2,8,8,512]{3,2,1,0:T(8,128)S(1)}) custom-call(s32[3]{0:T(128)S(1)} %pad_add_fusion.place, f32[4,8,8,512]{3,2,1,0:T(8,128)S(1)} %get-tuple-element.40.state, f32[4,8,8,512]{3,2,1,0:T(8,128)S(1)} %collective-permute-done.12.inner, f32[2,8,8,512]{3,2,1,0:T(8,128)S(1)} %collective-permute-done.10.near, ...), custom_call_target="tpu_custom_call" | custom-call | tf_op jit(solution)/shard_map/pallas_call | solution.py:473
  84.3 1.0 collective-permute-done.13.refs_1_
  85.3 0.9 collective-permute-done.11.far
  86.2 1.7 %shard_map.46 = (f32[4,8,8,512]{3,2,1,0:T(8,128)S(1)}, f32[2,8,8,512]{3,2,1,0:T(8,128)S(1)}, f32[16,4,2,8,128]{4,3,2,1,0:T(8,128)S(1)}) custom-call(s32[3]{0:T(128)S(1)} %pad_add_fusion.place, f32[2,8,8,512]{3,2,1,0:T(8,128)S(1)} %collective-permute-done.10.near, f32[2,8,8,512]{3,2,1,0:T(8,128)S(1)} %collective-permute-done.11.far, ...), custom_call_target="tpu_custom_call" | custom-call | tf_op jit(solution)/shard_map/pallas_call | solution.py:495
  87.9 5.2 %collective-permute-start.18 = (f32[16,4,2,8,128]{4,3,2,1,0:T(8,128)S(1)}, f32[16,4,2,8,128]{4,3,2,1,0:T(8,128)S(1)}, u32[]{:S(2)}, u32[]{:S(2)}) collective-permute-start(f32[16,4,2,8,128]{4,3,2,1,0:T(8,128)S(1)} %get-tuple-element.48.some), channel_id=1, source_target_pairs={{0,1},{1,0},{2,3},{3,2},{4,5},{5,4},{6,7},{7,6},{8,9},{9,8},{10,11... | collective-permute-start | bytes 1572872 | tf_op jit(solution)/shard_map/ppermute | solution.py:417
  93.2 1.9 %collective-permute-start.16 = (f32[4,8,8,512]{3,2,1,0:T(8,128)S(1)}, f32[4,8,8,512]{3,2,1,0:T(8,128)S(1)}, u32[]{:S(2)}, u32[]{:S(2)}) collective-permute-start(f32[4,8,8,512]{3,2,1,0:T(8,128)S(1)} %get-tuple-element.45.state), channel_id=1, source_target_pairs={{0,1},{1,0},{2,3},{3,2},{4,5},{5,4},{6,7},{7,6},{8,9},{9,8},{10,11... | collective-permute-start | bytes 1572872 | tf_op jit(solution)/shard_map/ppermute | solution.py:389
  95.1 3.4 %collective-permute-start.14 = (f32[2,8,8,512]{3,2,1,0:T(8,128)S(1)}, f32[2,8,8,512]{3,2,1,0:T(8,128)S(1)}, u32[]{:S(2)}, u32[]{:S(2)}) collective-permute-start(f32[2,8,8,512]{3,2,1,0:T(8,128)S(1)} %get-tuple-element.44), channel_id=1, source_target_pairs={{0,31},{1,2},{2,1},{3,4},{4,3},{5,6},{6,5},{7,8},{8,7},{9,10},{10,... | collective-permute-start | bytes 786440 | tf_op jit(solution)/shard_map/ppermute | solution.py:398
  98.5 2.1 %collective-permute-start.15 = (f32[2,8,8,512]{3,2,1,0:T(8,128)S(1)}, f32[2,8,8,512]{3,2,1,0:T(8,128)S(1)}, u32[]{:S(2)}, u32[]{:S(2)}) collective-permute-start(f32[2,8,8,512]{3,2,1,0:T(8,128)S(1)} %get-tuple-element.42.rest), channel_id=1, source_target_pairs={{0,31},{1,2},{2,1},{3,4},{4,3},{5,6},{6,5},{7,8},{8,7},{9,10},{10,... | collective-permute-start | bytes 786440 | tf_op jit(solution)/shard_map/ppermute | solution.py:398
  100.7 5.3 %collective-permute-start.17 = (f32[2,8,128]{2,1,0:T(8,128)S(1)}, f32[2,8,128]{2,1,0:T(8,128)S(1)}, u32[]{:S(2)}, u32[]{:S(2)}) collective-permute-start(f32[2,8,128]{2,1,0:T(8,128)S(1)} %get-tuple-element.31.refs_1_), channel_id=1, source_target_pairs={{32,0},{64,32},{96,64},{128,96},{160,128},{192,160},{224,192},{256... | collective-permute-start | bytes 24584 | tf_op jit(solution)/shard_map/ppermute | solution.py:452
  106.0 0.0 collective-permute-done.18.others
  106.0 0.7 shard_map.48.refs_1_.given
  106.7 0.0 collective-permute-done.14.near
  106.8 0.0 collective-permute-done.16.inner
  106.8 3.1 %shard_map.47 = (f32[3,2,8,8,512]{4,3,2,1,0:T(8,128)S(1)}, f32[2,8,8,512]{3,2,1,0:T(8,128)S(1)}) custom-call(s32[3]{0:T(128)S(1)} %pad_add_fusion.place, f32[4,8,8,512]{3,2,1,0:T(8,128)S(1)} %get-tuple-element.45.state, f32[4,8,8,512]{3,2,1,0:T(8,128)S(1)} %collective-permute-done.16.inner, f32[2,8,8,512]{3,2,1,0:T(8,128)S(1)} %collective-permute-done.14.near, ...), custom_call_target="tpu_custom_call" | custom-call | tf_op jit(solution)/shard_map/pallas_call | solution.py:473
  109.8 0.0 collective-permute-done.17.refs_0_
  109.8 1.4 collective-permute-done.15.far
  111.2 1.9 %shard_map.49 = (f32[4,8,8,512]{3,2,1,0:T(8,128)S(1)}, f32[32,2,8,128]{3,2,1,0:T(8,128)S(1)}) custom-call(s32[3]{0:T(128)S(1)} %pad_add_fusion.place, f32[2,8,8,512]{3,2,1,0:T(8,128)S(1)} %collective-permute-done.14.near, f32[2,8,8,512]{3,2,1,0:T(8,128)S(1)} %collective-permute-done.15.far, f32[4,7,8,8,512]{4,3,2,1,0:T(8,128)S(1)} %get-tuple-element.30.own, ...), custom_call_target="tpu_custom_call" | custom-call | tf_op jit(solution)/shard_map/pallas_call | solution.py:495
  113.1 18.4 %all_to_all.10.residuals = f32[32,2,8,128]{3,2,1,0:T(8,128)S(1)} all-to-all(f32[32,2,8,128]{3,2,1,0:T(8,128)S(1)} %get-tuple-element.49), channel_id=1, replica_groups=mesh['cuts'=16,'space'=32] {'space'}, dimensions={0} | all-to-all | bytes 524288 | tf_op jit(solution)/shard_map/all_to_all | solution.py:497
  131.5 10.7 %shard_map.50 = f32[16,2,8,128]{3,2,1,0:T(8,128)S(1)} custom-call(s32[3]{0:T(128)S(1)} %pad_add_fusion.place, f32[32,2,8,128]{3,2,1,0:T(8,128)S(1)} %all_to_all.10.residuals, f32[32,7,2,8,128]{4,3,2,1,0:T(8,128)S(1)} %shard_map.48.refs_1_.given), custom_call_target="tpu_custom_call" | custom-call | tf_op jit(solution)/shard_map/pallas_call | solution.py:498
  142.2 14.4 %all_to_all.11.shares = f32[16,2,8,128]{3,2,1,0:T(8,128)S(1)} all-to-all(f32[16,2,8,128]{3,2,1,0:T(8,128)S(1)} %shard_map.50), channel_id=1, replica_groups=mesh['cuts'=16,'space'=32] {'cuts'}, dimensions={0} | all-to-all | bytes 262144 | tf_op jit(solution)/shard_map/all_to_all | solution.py:504
  156.6 1.1 shard_map.51
Async XLA Ops:
  0.1 1.4 copy-start
  1.5 1.1 copy-start.2
  1.5 1.2 copy-start.3
  2.7 13.4 %copy-start.1 = (f32[3,4,64,512]{3,2,1,0:T(8,128)S(1)}, f32[3,4,64,512]{3,2,1,0:T(8,128)}, u32[]{:S(2)}) copy-start(f32[3,4,64,512]{3,2,1,0:T(8,128)} %velocity.5) | copy-start | bytes 4718596
  4.3 23.0 %collective-permute-start.1 = (f32[16,64,512]{2,1,0:T(8,128)S(1)}, f32[16,64,512]{2,1,0:T(8,128)S(1)}, u32[]{:S(2)}, u32[]{:S(2)}) collective-permute-start(f32[16,64,512]{2,1,0:T(8,128)S(1)} %get-tuple-element.29), channel_id=1, source_target_pairs={{0,1},{1,0},{2,3},{3,2},{4,5},{5,4},{6,7},{7,6},{8,9},{9,8},{10,11... | collective-permute-start | bytes 6291464 | tf_op jit(solution)/shard_map/ppermute | solution.py:389
  6.2 30.2 %collective-permute-start.2 = (f32[9,64,512]{2,1,0:T(8,128)S(1)}, f32[9,64,512]{2,1,0:T(8,128)S(1)}, u32[]{:S(2)}, u32[]{:S(2)}) collective-permute-start(f32[9,64,512]{2,1,0:T(8,128)S(1)} %shard_map.37.earlier), channel_id=1, source_target_pairs={{0,287},{1,258},{2,257},{3,260},{4,259},{5,262},{6,261},{7,264},{8... | collective-permute-start | bytes 3538952 | tf_op jit(solution)/shard_map/ppermute | solution.py:407
  9.8 22.4 %collective-permute-start = (f32[7,64,512]{2,1,0:T(8,128)S(1)}, f32[7,64,512]{2,1,0:T(8,128)S(1)}, u32[]{:S(2)}, u32[]{:S(2)}) collective-permute-start(f32[7,64,512]{2,1,0:T(8,128)S(1)} %get-tuple-element.28), channel_id=1, source_target_pairs={{0,31},{1,2},{2,1},{3,4},{4,3},{5,6},{6,5},{7,8},{8,7},{9,10},{10,... | collective-permute-start | bytes 2752520 | tf_op jit(solution)/shard_map/ppermute | solution.py:398
  17.4 19.6 %collective-permute-start.5 = (f32[1,4,2,8,128]{4,3,2,1,0:T(8,128)S(1)}, f32[1,4,2,8,128]{4,3,2,1,0:T(8,128)S(1)}, u32[]{:S(2)}, u32[]{:S(2)}) collective-permute-start(f32[1,4,2,8,128]{4,3,2,1,0:T(8,128)S(1)} %bitcast.7), channel_id=1, source_target_pairs={{0,24},{1,25},{2,26},{3,27},{4,28},{5,29},{6,30},{7,31},{8,16},{9,... | collective-permute-start | bytes 98312 | tf_op jit(solution)/shard_map/ppermute | solution.py:417
  25.3 11.6 %collective-permute-start.4 = (f32[1,4,2,8,128]{4,3,2,1,0:T(8,128)S(1)}, f32[1,4,2,8,128]{4,3,2,1,0:T(8,128)S(1)}, u32[]{:S(2)}, u32[]{:S(2)}) collective-permute-start(f32[1,4,2,8,128]{4,3,2,1,0:T(8,128)S(1)} %bitcast.8), channel_id=1, source_target_pairs={{0,16},{1,17},{2,18},{3,19},{4,20},{5,21},{6,22},{7,23},{8,24},{9,... | collective-permute-start | bytes 98312 | tf_op jit(solution)/shard_map/ppermute | solution.py:417
  27.3 9.7 %collective-permute-start.3 = (f32[1,4,2,8,128]{4,3,2,1,0:T(8,128)S(1)}, f32[1,4,2,8,128]{4,3,2,1,0:T(8,128)S(1)}, u32[]{:S(2)}, u32[]{:S(2)}) collective-permute-start(f32[1,4,2,8,128]{4,3,2,1,0:T(8,128)S(1)} %bitcast.9), channel_id=1, source_target_pairs={{0,8},{1,9},{2,10},{3,11},{4,12},{5,13},{6,14},{7,15},{8,0},{9,1},... | collective-permute-start | bytes 98312 | tf_op jit(solution)/shard_map/ppermute | solution.py:417
  41.2 20.5 %collective-permute-start.8 = (f32[4,8,8,512]{3,2,1,0:T(8,128)S(1)}, f32[4,8,8,512]{3,2,1,0:T(8,128)S(1)}, u32[]{:S(2)}, u32[]{:S(2)}) collective-permute-start(f32[4,8,8,512]{3,2,1,0:T(8,128)S(1)} %get-tuple-element.35.state), channel_id=1, source_target_pairs={{0,1},{1,0},{2,3},{3,2},{4,5},{5,4},{6,7},{7,6},{8,9},{9,8},{10,11... | collective-permute-start | bytes 1572872 | tf_op jit(solution)/shard_map/ppermute | solution.py:389
  51.2 10.5 %collective-permute-start.6 = (f32[2,8,8,512]{3,2,1,0:T(8,128)S(1)}, f32[2,8,8,512]{3,2,1,0:T(8,128)S(1)}, u32[]{:S(2)}, u32[]{:S(2)}) collective-permute-start(f32[2,8,8,512]{3,2,1,0:T(8,128)S(1)} %get-tuple-element.33), channel_id=1, source_target_pairs={{0,31},{1,2},{2,1},{3,4},{4,3},{5,6},{6,5},{7,8},{8,7},{9,10},{10,... | collective-permute-start | bytes 786440 | tf_op jit(solution)/shard_map/ppermute | solution.py:398
  54.8 12.5 %collective-permute-start.7 = (f32[2,8,8,512]{3,2,1,0:T(8,128)S(1)}, f32[2,8,8,512]{3,2,1,0:T(8,128)S(1)}, u32[]{:S(2)}, u32[]{:S(2)}) collective-permute-start(f32[2,8,8,512]{3,2,1,0:T(8,128)S(1)} %get-tuple-element.34), channel_id=1, source_target_pairs={{0,31},{1,2},{2,1},{3,4},{4,3},{5,6},{6,5},{7,8},{8,7},{9,10},{10,... | collective-permute-start | bytes 786440 | tf_op jit(solution)/shard_map/ppermute | solution.py:398
  56.8 8.2 %collective-permute-start.9 = (f32[4,4,2,8,128]{4,3,2,1,0:T(8,128)S(1)}, f32[4,4,2,8,128]{4,3,2,1,0:T(8,128)S(1)}, u32[]{:S(2)}, u32[]{:S(2)}) collective-permute-start(f32[4,4,2,8,128]{4,3,2,1,0:T(8,128)S(1)} %get-tuple-element.38.refs_0_), channel_id=1, source_target_pairs={{0,258},{1,259},{2,256},{3,257},{4,262},{5,263},{6,260},{7,261},{8... | collective-permute-start | bytes 393224 | tf_op jit(solution)/shard_map/ppermute | solution.py:416
  69.0 12.3 %collective-permute-start.12 = (f32[4,8,8,512]{3,2,1,0:T(8,128)S(1)}, f32[4,8,8,512]{3,2,1,0:T(8,128)S(1)}, u32[]{:S(2)}, u32[]{:S(2)}) collective-permute-start(f32[4,8,8,512]{3,2,1,0:T(8,128)S(1)} %get-tuple-element.40.state), channel_id=1, source_target_pairs={{0,1},{1,0},{2,3},{3,2},{4,5},{5,4},{6,7},{7,6},{8,9},{9,8},{10,11... | collective-permute-start | bytes 1572872 | tf_op jit(solution)/shard_map/ppermute | solution.py:389
  70.9 10.3 %collective-permute-start.10 = (f32[2,8,8,512]{3,2,1,0:T(8,128)S(1)}, f32[2,8,8,512]{3,2,1,0:T(8,128)S(1)}, u32[]{:S(2)}, u32[]{:S(2)}) collective-permute-start(f32[2,8,8,512]{3,2,1,0:T(8,128)S(1)} %get-tuple-element.39), channel_id=1, source_target_pairs={{0,31},{1,2},{2,1},{3,4},{4,3},{5,6},{6,5},{7,8},{8,7},{9,10},{10,... | collective-permute-start | bytes 786440 | tf_op jit(solution)/shard_map/ppermute | solution.py:398
  74.6 10.7 %collective-permute-start.13 = (f32[8,4,2,8,128]{4,3,2,1,0:T(8,128)S(1)}, f32[8,4,2,8,128]{4,3,2,1,0:T(8,128)S(1)}, u32[]{:S(2)}, u32[]{:S(2)}) collective-permute-start(f32[8,4,2,8,128]{4,3,2,1,0:T(8,128)S(1)} %get-tuple-element.43.refs_0_), channel_id=1, source_target_pairs={{0,4},{1,5},{2,6},{3,7},{4,0},{5,1},{6,2},{7,3},{8,12},{9,13},{10,... | collective-permute-start | bytes 786440 | tf_op jit(solution)/shard_map/ppermute | solution.py:417
  78.5 7.7 %collective-permute-start.11 = (f32[2,8,8,512]{3,2,1,0:T(8,128)S(1)}, f32[2,8,8,512]{3,2,1,0:T(8,128)S(1)}, u32[]{:S(2)}, u32[]{:S(2)}) collective-permute-start(f32[2,8,8,512]{3,2,1,0:T(8,128)S(1)} %get-tuple-element.37.rest), channel_id=1, source_target_pairs={{0,31},{1,2},{2,1},{3,4},{4,3},{5,6},{6,5},{7,8},{8,7},{9,10},{10,... | collective-permute-start | bytes 786440 | tf_op jit(solution)/shard_map/ppermute | solution.py:398
  87.9 18.1 %collective-permute-start.18 = (f32[16,4,2,8,128]{4,3,2,1,0:T(8,128)S(1)}, f32[16,4,2,8,128]{4,3,2,1,0:T(8,128)S(1)}, u32[]{:S(2)}, u32[]{:S(2)}) collective-permute-start(f32[16,4,2,8,128]{4,3,2,1,0:T(8,128)S(1)} %get-tuple-element.48.some), channel_id=1, source_target_pairs={{0,1},{1,0},{2,3},{3,2},{4,5},{5,4},{6,7},{7,6},{8,9},{9,8},{10,11... | collective-permute-start | bytes 1572872 | tf_op jit(solution)/shard_map/ppermute | solution.py:417
  93.2 13.6 %collective-permute-start.16 = (f32[4,8,8,512]{3,2,1,0:T(8,128)S(1)}, f32[4,8,8,512]{3,2,1,0:T(8,128)S(1)}, u32[]{:S(2)}, u32[]{:S(2)}) collective-permute-start(f32[4,8,8,512]{3,2,1,0:T(8,128)S(1)} %get-tuple-element.45.state), channel_id=1, source_target_pairs={{0,1},{1,0},{2,3},{3,2},{4,5},{5,4},{6,7},{7,6},{8,9},{9,8},{10,11... | collective-permute-start | bytes 1572872 | tf_op jit(solution)/shard_map/ppermute | solution.py:389
  95.1 11.7 %collective-permute-start.14 = (f32[2,8,8,512]{3,2,1,0:T(8,128)S(1)}, f32[2,8,8,512]{3,2,1,0:T(8,128)S(1)}, u32[]{:S(2)}, u32[]{:S(2)}) collective-permute-start(f32[2,8,8,512]{3,2,1,0:T(8,128)S(1)} %get-tuple-element.44), channel_id=1, source_target_pairs={{0,31},{1,2},{2,1},{3,4},{4,3},{5,6},{6,5},{7,8},{8,7},{9,10},{10,... | collective-permute-start | bytes 786440 | tf_op jit(solution)/shard_map/ppermute | solution.py:398
  98.5 12.7 %collective-permute-start.15 = (f32[2,8,8,512]{3,2,1,0:T(8,128)S(1)}, f32[2,8,8,512]{3,2,1,0:T(8,128)S(1)}, u32[]{:S(2)}, u32[]{:S(2)}) collective-permute-start(f32[2,8,8,512]{3,2,1,0:T(8,128)S(1)} %get-tuple-element.42.rest), channel_id=1, source_target_pairs={{0,31},{1,2},{2,1},{3,4},{4,3},{5,6},{6,5},{7,8},{8,7},{9,10},{10,... | collective-permute-start | bytes 786440 | tf_op jit(solution)/shard_map/ppermute | solution.py:398
  100.7 9.2 %collective-permute-start.17 = (f32[2,8,128]{2,1,0:T(8,128)S(1)}, f32[2,8,128]{2,1,0:T(8,128)S(1)}, u32[]{:S(2)}, u32[]{:S(2)}) collective-permute-start(f32[2,8,128]{2,1,0:T(8,128)S(1)} %get-tuple-element.31.refs_1_), channel_id=1, source_target_pairs={{32,0},{64,32},{96,64},{128,96},{160,128},{192,160},{224,192},{256... | collective-permute-start | bytes 24584 | tf_op jit(solution)/shard_map/ppermute | solution.py:452

commit v10 on v9

--- a/solution.py
+++ b/solution.py
@@ -9,6 +9,7 @@
 
 RATIO = 4
 LAYERS = 4
+COARSE_STEPS = 4
 REACH = 3
 ROUNDS = 4
 TILE = (8, 8, 512)
@@ -271,7 +272,7 @@
     if final:
         later, after, out, residual, one, two = refs
     else:
-        *parts, out, next_near, joined, one, two = refs
+        *parts, early, out, next_near, joined, one, two = refs
         join(parts, joined)
     core = place[2]
     for i in range(2):
@@ -302,11 +303,10 @@
             next_near[i] = out[2 * core + i]
 
 
-def coarse_step(read, weights, write, count):
-    first = read(0)
-    behind, now = read(count - 1), first
-    for x in range(count):
-        ahead = read(x + 1) if x + 1 < count else first
+def coarse_step(read, weights, write, begin, end, count):
+    behind, now = read((begin - 1) % count), read(begin)
+    for x in range(begin, end):
+        ahead = read((x + 1) % count)
         for h in range(2):
             behind_y = now[0] if h else pltpu.roll(now[1], 1, 0)
             ahead_y = pltpu.roll(now[0], 7, 0) if h else now[1]
@@ -341,11 +341,14 @@
 def chain_kernel(place, residuals, given, shares, weights, one, two):
     count = weights.shape[0]
     slices = shares.shape[0]
-    weights[...] = given[...]
     slice_index = place[0]
     layer_index = place[1]
+    middle = count // 2
     shares[...] = jnp.zeros(shares.shape, F32)
-    one[...] = residuals[...]
+    for x in range(count):
+        at = (x - layer_index + middle) & (count - 1)
+        weights[at] = given[x]
+        one[at] = residuals[x]
 
     def reader(ref):
         return lambda x: [ref[x, h] for h in range(2)]
@@ -356,14 +359,28 @@
 
         return write
 
+    def propagate(ranges):
+        for (source, target), (begin, end) in zip(((one, two), (two, one)) * 2, ranges, strict=True):
+            coarse_step(reader(source), weights, writer(target), begin, end, count)
+
+    def share(n):
+        for h in range(2):
+            shares[n, h] = one[middle, h]
+
     def link(n, carry):
-        for source, target in ((one, two), (two, one)) * 2:
-            coarse_step(reader(source), weights, writer(target), count)
-        for h in range(2):
-            shares[n, h] = one[layer_index, h]
+        propagate([(0, count)] * 4)
+        share(n)
         return carry
 
-    lax.fori_loop(slice_index + 1, slices, link, 0)
+    narrow = 4
+    lax.fori_loop(slice_index + 1, slices - narrow, link, 0)
+    for left in range(narrow - 1, -1, -1):
+
+        @pl.when(slices - 1 - slice_index > left)
+        def _(left=left):
+            reach = [COARSE_STEPS * left + COARSE_STEPS - 1 - step for step in range(COARSE_STEPS)]
+            propagate([(middle - r, middle + r + 1) for r in reach])
+            share(slices - 1 - left)
 
 
 def finish_kernel(shares, state, out, buffer):
@@ -489,8 +506,8 @@
             outs = [block, (count, *COARSE)]
         else:
             parts = [gathered, across(gathered, (2, 4)[index - 1])]
-            operands += parts
-            specs += [VMEM] * len(parts)
+            operands += parts + [coarse_later if index == 2 else coarse_old]
+            specs += [VMEM] * len(parts) + [ANY]
             outs = [block, pair, (2 * gathered.shape[0], 4, *COARSE)]
         state, *near, gathered = call(functools.partial(far_kernel, final), outs, specs, scratch)(*operands)
         near, far = near[0] if near else None, rest

time: 158 us -> 157 us (level)
  waiting for transfers between devices: 11.2 us -> 15.2 us
  starting transfers between devices: 75.5 us -> 72.2 us
    ppermute x7, waiting for transfers between devices: 5.72 us -> 9.93 us  [swap_outer(): lax.ppermute(block, 'space', [(p, outer_partner(p, count)) for p in range...]
    ppermute x5, starting transfers between devices: 23.3 us -> 20.2 us  [across(): return lax.ppermute(block, 'space', [(p, p ^ bits) for p in range(count)])]
  transfers between devices with their start and end apart: 19 -> 19, of which waited for: 8 -> 5; matrix products, arithmetic and copies ran while one was open for 0% -> 0% of each run, Pallas kernels for 8% -> 8%
where the time goes in v10:
time: 157 us
  starting transfers between devices  72.2 us (46%)
  Pallas kernels  34.8 us (22%)
  blocking collectives  32.7 us (21%)
  waiting for transfers between devices  15.2 us (10%)
    ppermute x7, starting transfers between devices, swap_outer(): lax.ppermute(block, 'space', [(p, outer_partner(p, count)) for p in range...  24.3 us
    ppermute x5, starting transfers between devices, across(): return lax.ppermute(block, 'space', [(p, p ^ bits) for p in range(count)])  20.2 us
    all_to_all x1, blocking collectives, shards(): residuals = lax.all_to_all(gathered, 'space', 0, 0)  19.7 us
    ppermute x4, starting transfers between devices, swap_inner(): return lax.ppermute(block, 'space', [(p, p ^ 1) for p in range(count)])  15 us
    all_to_all x1, blocking collectives, shards(): shares = lax.all_to_all(shares, 'cuts', 0, 0)  13 us
    ppermute x7, waiting for transfers between devices, swap_outer(): lax.ppermute(block, 'space', [(p, outer_partner(p, count)) for p in range...  9.93 us
    pallas_call x3, Pallas kernels, shards(): call(near_kernel, [(LAYERS - 1, *pair), pair], [SMEM] + [VMEM] * 6, scratch)  9.17 us
    pallas_call x1, Pallas kernels, shards(): call(chain_kernel, [(slices, *COARSE)], [SMEM, VMEM, VMEM], [pltpu.VMEM((...  9.15 us
  transfers between devices with their start and end apart: 19, of which 5 were waited for; matrix products, arithmetic and copies ran while one was open for 0% of the time, Pallas kernels for 8%

profile of v10, /device:TPU:2, one launch (start us, length us, event | category | flops | bytes accessed | tf_op | source)
XLA Modules:
  0.0 156.7 jit_solution(5843757700916654869)
XLA Ops:
  0.0 0.1 pad_add_fusion.place
  0.1 0.0 copy-start
  0.1 1.4 copy-done
  1.5 0.0 copy-start.2
  1.5 0.0 copy-start.3
  1.5 1.1 shard_map.37.earlier
  2.6 0.0 copy-done.2
  2.6 0.0 copy-done.3
  2.7 0.0 copy-start.1
  2.7 1.6 %shard_map.38 = (f32[7,64,512]{2,1,0:T(8,128)S(1)}, f32[16,64,512]{2,1,0:T(8,128)S(1)}) custom-call(s32[3]{0:T(128)S(1)} %pad_add_fusion.place, f32[3,4,64,512]{3,2,1,0:T(8,128)S(1)} %copy-done, f32[4,64,512]{2,1,0:T(8,128)S(1)} %copy-done.3, f32[1,4,64,512]{3,2,1,0:T(8,128)S(1)} %copy-done.2, f32[9,64,512]{2,1,0:T(8,128)S(1)} %shard_map.37.earlier), custom_call_target="tpu_custom_call" | custom-call | flops 1 | bytes 1 | tf_op jit(solution)/shard_map/pallas_call | solution.py:452
  4.3 1.9 %collective-permute-start.1 = (f32[16,64,512]{2,1,0:T(8,128)S(1)}, f32[16,64,512]{2,1,0:T(8,128)S(1)}, u32[]{:S(2)}, u32[]{:S(2)}) collective-permute-start(f32[16,64,512]{2,1,0:T(8,128)S(1)} %get-tuple-element.29), channel_id=1, source_target_pairs={{0,1},{1,0},{2,3},{3,2},{4,5},{5,4},{6,7},{7,6},{8,9},{9,8},{10,11... | collective-permute-start | bytes 6291464 | tf_op jit(solution)/shard_map/ppermute | solution.py:406
  6.2 3.5 %collective-permute-start.2 = (f32[9,64,512]{2,1,0:T(8,128)S(1)}, f32[9,64,512]{2,1,0:T(8,128)S(1)}, u32[]{:S(2)}, u32[]{:S(2)}) collective-permute-start(f32[9,64,512]{2,1,0:T(8,128)S(1)} %shard_map.37.earlier), channel_id=1, source_target_pairs={{0,287},{1,258},{2,257},{3,260},{4,259},{5,262},{6,261},{7,264},{8... | collective-permute-start | bytes 3538952 | tf_op jit(solution)/shard_map/ppermute | solution.py:424
  9.8 6.3 %collective-permute-start = (f32[7,64,512]{2,1,0:T(8,128)S(1)}, f32[7,64,512]{2,1,0:T(8,128)S(1)}, u32[]{:S(2)}, u32[]{:S(2)}) collective-permute-start(f32[7,64,512]{2,1,0:T(8,128)S(1)} %get-tuple-element.28), channel_id=1, source_target_pairs={{0,31},{1,2},{2,1},{3,4},{4,3},{5,6},{6,5},{7,8},{8,7},{9,10},{10,... | collective-permute-start | bytes 2752520 | tf_op jit(solution)/shard_map/ppermute | solution.py:415
  16.1 0.0 copy-done.1
  16.1 1.3 shard_map.39
  17.4 3.1 %collective-permute-start.3 = (f32[1,4,2,8,128]{4,3,2,1,0:T(8,128)S(1)}, f32[1,4,2,8,128]{4,3,2,1,0:T(8,128)S(1)}, u32[]{:S(2)}, u32[]{:S(2)}) collective-permute-start(f32[1,4,2,8,128]{4,3,2,1,0:T(8,128)S(1)} %bitcast.7), channel_id=1, source_target_pairs={{0,8},{1,9},{2,10},{3,11},{4,12},{5,13},{6,14},{7,15},{8,0},{9,1},... | collective-permute-start | bytes 98312 | tf_op jit(solution)/shard_map/ppermute | solution.py:434
  20.5 9.1 %collective-permute-start.4 = (f32[1,4,2,8,128]{4,3,2,1,0:T(8,128)S(1)}, f32[1,4,2,8,128]{4,3,2,1,0:T(8,128)S(1)}, u32[]{:S(2)}, u32[]{:S(2)}) collective-permute-start(f32[1,4,2,8,128]{4,3,2,1,0:T(8,128)S(1)} %bitcast.8), channel_id=1, source_target_pairs={{0,16},{1,17},{2,18},{3,19},{4,20},{5,21},{6,22},{7,23},{8,24},{9,... | collective-permute-start | bytes 98312 | tf_op jit(solution)/shard_map/ppermute | solution.py:434
  29.6 0.0 collective-permute-done.1.refs_0_.inner
  29.6 1.9 %collective-permute-start.5 = (f32[1,4,2,8,128]{4,3,2,1,0:T(8,128)S(1)}, f32[1,4,2,8,128]{4,3,2,1,0:T(8,128)S(1)}, u32[]{:S(2)}, u32[]{:S(2)}) collective-permute-start(f32[1,4,2,8,128]{4,3,2,1,0:T(8,128)S(1)} %bitcast.9), channel_id=1, source_target_pairs={{0,24},{1,25},{2,26},{3,27},{4,28},{5,29},{6,30},{7,31},{8,16},{9,... | collective-permute-start | bytes 98312 | tf_op jit(solution)/shard_map/ppermute | solution.py:434
  31.6 0.6 shard_map.40.refs_2_.own_inner
  32.1 0.0 collective-permute-done.refs_1_.outer
  32.1 4.3 %collective-permute-done.2.refs_0_ = f32[9,64,512]{2,1,0:T(8,128)S(1)} collective-permute-done((f32[9,64,512]{2,1,0:T(8,128)S(1)}, f32[9,64,512]{2,1,0:T(8,128)S(1)}, u32[]{:S(2)}, u32[]{:S(2)}) %collective-permute-start.2) | collective-permute-done | bytes 1179680 | tf_op jit(solution)/shard_map/ppermute | solution.py:424
  36.4 0.6 shard_map.41.own_outer
  37.0 0.0 collective-permute-done.3.refs_1_
  37.0 0.0 collective-permute-done.4.refs_2_
  37.0 1.0 collective-permute-done.5.refs_3_
  38.0 4.2 %shard_map.42 = (f32[4,8,8,512]{3,2,1,0:T(8,128)S(1)}, f32[2,8,8,512]{3,2,1,0:T(8,128)S(1)}, f32[2,8,8,512]{3,2,1,0:T(8,128)S(1)}, f32[4,4,2,8,128]{4,3,2,1,0:T(8,128)S(1)}) custom-call(s32[3]{0:T(128)S(1)} %pad_add_fusion.place, f32[4,64,512]{2,1,0:T(8,128)S(1)} %bitcast.6, f32[7,64,512]{2,1,0:T(8,128)S(1)} %collective-permute-done.refs_1_.outer, ...), custom_call_target="tpu_custom_call" | custom-call | tf_op jit(solution)/shard_map/pallas_call | solution.py:481
  42.2 9.3 %collective-permute-start.8 = (f32[4,8,8,512]{3,2,1,0:T(8,128)S(1)}, f32[4,8,8,512]{3,2,1,0:T(8,128)S(1)}, u32[]{:S(2)}, u32[]{:S(2)}) collective-permute-start(f32[4,8,8,512]{3,2,1,0:T(8,128)S(1)} %get-tuple-element.35.state), channel_id=1, source_target_pairs={{0,1},{1,0},{2,3},{3,2},{4,5},{5,4},{6,7},{7,6},{8,9},{9,8},{10,11... | collective-permute-start | bytes 1572872 | tf_op jit(solution)/shard_map/ppermute | solution.py:406
  51.5 3.4 %collective-permute-start.6 = (f32[2,8,8,512]{3,2,1,0:T(8,128)S(1)}, f32[2,8,8,512]{3,2,1,0:T(8,128)S(1)}, u32[]{:S(2)}, u32[]{:S(2)}) collective-permute-start(f32[2,8,8,512]{3,2,1,0:T(8,128)S(1)} %get-tuple-element.33), channel_id=1, source_target_pairs={{0,31},{1,2},{2,1},{3,4},{4,3},{5,6},{6,5},{7,8},{8,7},{9,10},{10,... | collective-permute-start | bytes 786440 | tf_op jit(solution)/shard_map/ppermute | solution.py:415
  54.8 2.2 %collective-permute-start.7 = (f32[2,8,8,512]{3,2,1,0:T(8,128)S(1)}, f32[2,8,8,512]{3,2,1,0:T(8,128)S(1)}, u32[]{:S(2)}, u32[]{:S(2)}) collective-permute-start(f32[2,8,8,512]{3,2,1,0:T(8,128)S(1)} %get-tuple-element.34), channel_id=1, source_target_pairs={{0,31},{1,2},{2,1},{3,4},{4,3},{5,6},{6,5},{7,8},{8,7},{9,10},{10,... | collective-permute-start | bytes 786440 | tf_op jit(solution)/shard_map/ppermute | solution.py:415
  57.1 4.3 %collective-permute-start.9 = (f32[4,4,2,8,128]{4,3,2,1,0:T(8,128)S(1)}, f32[4,4,2,8,128]{4,3,2,1,0:T(8,128)S(1)}, u32[]{:S(2)}, u32[]{:S(2)}) collective-permute-start(f32[4,4,2,8,128]{4,3,2,1,0:T(8,128)S(1)} %get-tuple-element.38.refs_0_), channel_id=1, source_target_pairs={{0,258},{1,259},{2,256},{3,257},{4,262},{5,263},{6,260},{7,261},{8... | collective-permute-start | bytes 393224 | tf_op jit(solution)/shard_map/ppermute | solution.py:433
  61.4 3.4 %collective-permute-done.6.near = f32[2,8,8,512]{3,2,1,0:T(8,128)S(1)} collective-permute-done((f32[2,8,8,512]{3,2,1,0:T(8,128)S(1)}, f32[2,8,8,512]{3,2,1,0:T(8,128)S(1)}, u32[]{:S(2)}, u32[]{:S(2)}) %collective-permute-start.6) | collective-permute-done | bytes 262176 | tf_op jit(solution)/shard_map/ppermute | solution.py:415
  64.8 0.0 collective-permute-done.8.inner
  64.8 3.1 %shard_map.43 = (f32[3,2,8,8,512]{4,3,2,1,0:T(8,128)S(1)}, f32[2,8,8,512]{3,2,1,0:T(8,128)S(1)}) custom-call(s32[3]{0:T(128)S(1)} %pad_add_fusion.place, f32[4,8,8,512]{3,2,1,0:T(8,128)S(1)} %get-tuple-element.35.state, f32[4,8,8,512]{3,2,1,0:T(8,128)S(1)} %collective-permute-done.8.inner, f32[2,8,8,512]{3,2,1,0:T(8,128)S(1)} %collective-permute-done.6.near, ...), custom_call_target="tpu_custom_call" | custom-call | tf_op jit(solution)/shard_map/pallas_call | solution.py:490
  67.8 0.0 collective-permute-done.9.refs_1_
  67.9 0.0 collective-permute-done.7.far
  67.9 1.7 %shard_map.44 = (f32[4,8,8,512]{3,2,1,0:T(8,128)S(1)}, f32[2,8,8,512]{3,2,1,0:T(8,128)S(1)}, f32[8,4,2,8,128]{4,3,2,1,0:T(8,128)S(1)}) custom-call(s32[3]{0:T(128)S(1)} %pad_add_fusion.place, f32[2,8,8,512]{3,2,1,0:T(8,128)S(1)} %collective-permute-done.6.near, f32[2,8,8,512]{3,2,1,0:T(8,128)S(1)} %collective-permute-done.7.far, ...), custom_call_target="tpu_custom_call" | custom-call | tf_op jit(solution)/shard_map/pallas_call | solution.py:512
  69.5 1.9 %collective-permute-start.12 = (f32[4,8,8,512]{3,2,1,0:T(8,128)S(1)}, f32[4,8,8,512]{3,2,1,0:T(8,128)S(1)}, u32[]{:S(2)}, u32[]{:S(2)}) collective-permute-start(f32[4,8,8,512]{3,2,1,0:T(8,128)S(1)} %get-tuple-element.40.state), channel_id=1, source_target_pairs={{0,1},{1,0},{2,3},{3,2},{4,5},{5,4},{6,7},{7,6},{8,9},{9,8},{10,11... | collective-permute-start | bytes 1572872 | tf_op jit(solution)/shard_map/ppermute | solution.py:406
  71.5 3.1 %collective-permute-start.10 = (f32[2,8,8,512]{3,2,1,0:T(8,128)S(1)}, f32[2,8,8,512]{3,2,1,0:T(8,128)S(1)}, u32[]{:S(2)}, u32[]{:S(2)}) collective-permute-start(f32[2,8,8,512]{3,2,1,0:T(8,128)S(1)} %get-tuple-element.39), channel_id=1, source_target_pairs={{0,31},{1,2},{2,1},{3,4},{4,3},{5,6},{6,5},{7,8},{8,7},{9,10},{10,... | collective-permute-start | bytes 786440 | tf_op jit(solution)/shard_map/ppermute | solution.py:415
  74.6 2.5 %collective-permute-start.11 = (f32[2,8,8,512]{3,2,1,0:T(8,128)S(1)}, f32[2,8,8,512]{3,2,1,0:T(8,128)S(1)}, u32[]{:S(2)}, u32[]{:S(2)}) collective-permute-start(f32[2,8,8,512]{3,2,1,0:T(8,128)S(1)} %get-tuple-element.37.rest), channel_id=1, source_target_pairs={{0,31},{1,2},{2,1},{3,4},{4,3},{5,6},{6,5},{7,8},{8,7},{9,10},{10,... | collective-permute-start | bytes 786440 | tf_op jit(solution)/shard_map/ppermute | solution.py:415
  77.0 3.1 %collective-permute-start.13 = (f32[8,4,2,8,128]{4,3,2,1,0:T(8,128)S(1)}, f32[8,4,2,8,128]{4,3,2,1,0:T(8,128)S(1)}, u32[]{:S(2)}, u32[]{:S(2)}) collective-permute-start(f32[8,4,2,8,128]{4,3,2,1,0:T(8,128)S(1)} %get-tuple-element.43.refs_0_), channel_id=1, source_target_pairs={{0,4},{1,5},{2,6},{3,7},{4,0},{5,1},{6,2},{7,3},{8,12},{9,13},{10,... | collective-permute-start | bytes 786440 | tf_op jit(solution)/shard_map/ppermute | solution.py:434
  80.1 4.8 %collective-permute-start.14 = (f32[2,8,128]{2,1,0:T(8,128)S(1)}, f32[2,8,128]{2,1,0:T(8,128)S(1)}, u32[]{:S(2)}, u32[]{:S(2)}) collective-permute-start(f32[2,8,128]{2,1,0:T(8,128)S(1)} %get-tuple-element.31.refs_1_.refs_2_), channel_id=1, source_target_pairs={{32,0},{64,32},{96,64},{128,96},{160,128},{192,160},{224,192},{256... | collective-permute-start | bytes 24584 | tf_op jit(solution)/shard_map/ppermute | solution.py:469
  84.9 0.0 collective-permute-done.10.near
  84.9 0.0 collective-permute-done.12.inner
  84.9 3.1 %shard_map.45 = (f32[3,2,8,8,512]{4,3,2,1,0:T(8,128)S(1)}, f32[2,8,8,512]{3,2,1,0:T(8,128)S(1)}) custom-call(s32[3]{0:T(128)S(1)} %pad_add_fusion.place, f32[4,8,8,512]{3,2,1,0:T(8,128)S(1)} %get-tuple-element.40.state, f32[4,8,8,512]{3,2,1,0:T(8,128)S(1)} %collective-permute-done.12.inner, f32[2,8,8,512]{3,2,1,0:T(8,128)S(1)} %collective-permute-done.10.near, ...), custom_call_target="tpu_custom_call" | custom-call | tf_op jit(solution)/shard_map/pallas_call | solution.py:490
  88.0 0.0 collective-permute-done.14.refs_2_.refs_0_
  88.0 0.0 collective-permute-done.11.far
  88.0 0.0 collective-permute-done.13.refs_1_
  88.0 1.7 %shard_map.46 = (f32[4,8,8,512]{3,2,1,0:T(8,128)S(1)}, f32[2,8,8,512]{3,2,1,0:T(8,128)S(1)}, f32[16,4,2,8,128]{4,3,2,1,0:T(8,128)S(1)}) custom-call(s32[3]{0:T(128)S(1)} %pad_add_fusion.place, f32[2,8,8,512]{3,2,1,0:T(8,128)S(1)} %collective-permute-done.10.near, f32[2,8,8,512]{3,2,1,0:T(8,128)S(1)} %collective-permute-done.11.far, ...), custom_call_target="tpu_custom_call" | custom-call | tf_op jit(solution)/shard_map/pallas_call | solution.py:512
  89.7 3.0 %collective-permute-start.18 = (f32[16,4,2,8,128]{4,3,2,1,0:T(8,128)S(1)}, f32[16,4,2,8,128]{4,3,2,1,0:T(8,128)S(1)}, u32[]{:S(2)}, u32[]{:S(2)}) collective-permute-start(f32[16,4,2,8,128]{4,3,2,1,0:T(8,128)S(1)} %get-tuple-element.48.some), channel_id=1, source_target_pairs={{0,1},{1,0},{2,3},{3,2},{4,5},{5,4},{6,7},{7,6},{8,9},{9,8},{10,11... | collective-permute-start | bytes 1572872 | tf_op jit(solution)/shard_map/ppermute | solution.py:434
  92.8 1.9 %collective-permute-start.17 = (f32[4,8,8,512]{3,2,1,0:T(8,128)S(1)}, f32[4,8,8,512]{3,2,1,0:T(8,128)S(1)}, u32[]{:S(2)}, u32[]{:S(2)}) collective-permute-start(f32[4,8,8,512]{3,2,1,0:T(8,128)S(1)} %get-tuple-element.45.state), channel_id=1, source_target_pairs={{0,1},{1,0},{2,3},{3,2},{4,5},{5,4},{6,7},{7,6},{8,9},{9,8},{10,11... | collective-permute-start | bytes 1572872 | tf_op jit(solution)/shard_map/ppermute | solution.py:406
  94.7 4.7 %collective-permute-start.15 = (f32[2,8,8,512]{3,2,1,0:T(8,128)S(1)}, f32[2,8,8,512]{3,2,1,0:T(8,128)S(1)}, u32[]{:S(2)}, u32[]{:S(2)}) collective-permute-start(f32[2,8,8,512]{3,2,1,0:T(8,128)S(1)} %get-tuple-element.44), channel_id=1, source_target_pairs={{0,31},{1,2},{2,1},{3,4},{4,3},{5,6},{6,5},{7,8},{8,7},{9,10},{10,... | collective-permute-start | bytes 786440 | tf_op jit(solution)/shard_map/ppermute | solution.py:415
  99.4 2.1 %collective-permute-start.16 = (f32[2,8,8,512]{3,2,1,0:T(8,128)S(1)}, f32[2,8,8,512]{3,2,1,0:T(8,128)S(1)}, u32[]{:S(2)}, u32[]{:S(2)}) collective-permute-start(f32[2,8,8,512]{3,2,1,0:T(8,128)S(1)} %get-tuple-element.42.rest), channel_id=1, source_target_pairs={{0,31},{1,2},{2,1},{3,4},{4,3},{5,6},{6,5},{7,8},{8,7},{9,10},{10,... | collective-permute-start | bytes 786440 | tf_op jit(solution)/shard_map/ppermute | solution.py:415
  101.5 0.0 collective-permute-done.18.others
  101.5 0.7 shard_map.48.refs_1_.given
  102.3 4.0 %collective-permute-done.15.near = f32[2,8,8,512]{3,2,1,0:T(8,128)S(1)} collective-permute-done((f32[2,8,8,512]{3,2,1,0:T(8,128)S(1)}, f32[2,8,8,512]{3,2,1,0:T(8,128)S(1)}, u32[]{:S(2)}, u32[]{:S(2)}) %collective-permute-start.15) | collective-permute-done | bytes 262176 | tf_op jit(solution)/shard_map/ppermute | solution.py:415
  106.3 0.0 collective-permute-done.17.inner
  106.3 3.1 %shard_map.47 = (f32[3,2,8,8,512]{4,3,2,1,0:T(8,128)S(1)}, f32[2,8,8,512]{3,2,1,0:T(8,128)S(1)}) custom-call(s32[3]{0:T(128)S(1)} %pad_add_fusion.place, f32[4,8,8,512]{3,2,1,0:T(8,128)S(1)} %get-tuple-element.45.state, f32[4,8,8,512]{3,2,1,0:T(8,128)S(1)} %collective-permute-done.17.inner, f32[2,8,8,512]{3,2,1,0:T(8,128)S(1)} %collective-permute-done.15.near, ...), custom_call_target="tpu_custom_call" | custom-call | tf_op jit(solution)/shard_map/pallas_call | solution.py:490
  109.3 2.5 %collective-permute-done.16.far = f32[2,8,8,512]{3,2,1,0:T(8,128)S(1)} collective-permute-done((f32[2,8,8,512]{3,2,1,0:T(8,128)S(1)}, f32[2,8,8,512]{3,2,1,0:T(8,128)S(1)}, u32[]{:S(2)}, u32[]{:S(2)}) %collective-permute-start.16) | collective-permute-done | bytes 262176 | tf_op jit(solution)/shard_map/ppermute | solution.py:415
  111.9 1.9 %shard_map.49 = (f32[4,8,8,512]{3,2,1,0:T(8,128)S(1)}, f32[32,2,8,128]{3,2,1,0:T(8,128)S(1)}) custom-call(s32[3]{0:T(128)S(1)} %pad_add_fusion.place, f32[2,8,8,512]{3,2,1,0:T(8,128)S(1)} %collective-permute-done.15.near, f32[2,8,8,512]{3,2,1,0:T(8,128)S(1)} %collective-permute-done.16.far, f32[4,7,8,8,512]{4,3,2,1,0:T(8,128)S(1)} %get-tuple-element.30.own, ...), custom_call_target="tpu_custom_call" | custom-call | tf_op jit(solution)/shard_map/pallas_call | solution.py:512
  113.8 19.7 %all_to_all.10.residuals = f32[32,2,8,128]{3,2,1,0:T(8,128)S(1)} all-to-all(f32[32,2,8,128]{3,2,1,0:T(8,128)S(1)} %get-tuple-element.49), channel_id=1, replica_groups=mesh['cuts'=16,'space'=32] {'space'}, dimensions={0} | all-to-all | bytes 524288 | tf_op jit(solution)/shard_map/all_to_all | solution.py:514
  133.5 9.2 %shard_map.50 = f32[16,2,8,128]{3,2,1,0:T(8,128)S(1)} custom-call(s32[3]{0:T(128)S(1)} %pad_add_fusion.place, f32[32,2,8,128]{3,2,1,0:T(8,128)S(1)} %all_to_all.10.residuals, f32[32,7,2,8,128]{4,3,2,1,0:T(8,128)S(1)} %shard_map.48.refs_1_.given), custom_call_target="tpu_custom_call" | custom-call | tf_op jit(solution)/shard_map/pallas_call | solution.py:515
  142.7 13.0 %all_to_all.11.shares = f32[16,2,8,128]{3,2,1,0:T(8,128)S(1)} all-to-all(f32[16,2,8,128]{3,2,1,0:T(8,128)S(1)} %shard_map.50), channel_id=1, replica_groups=mesh['cuts'=16,'space'=32] {'cuts'}, dimensions={0} | all-to-all | bytes 262144 | tf_op jit(solution)/shard_map/all_to_all | solution.py:521
  155.7 1.1 shard_map.51
Async XLA Ops:
  0.1 1.4 copy-start
  1.5 1.1 copy-start.2
  1.5 1.2 copy-start.3
  2.7 13.4 %copy-start.1 = (f32[3,4,64,512]{3,2,1,0:T(8,128)S(1)}, f32[3,4,64,512]{3,2,1,0:T(8,128)}, u32[]{:S(2)}) copy-start(f32[3,4,64,512]{3,2,1,0:T(8,128)} %velocity.5) | copy-start | bytes 4718596
  4.3 25.3 %collective-permute-start.1 = (f32[16,64,512]{2,1,0:T(8,128)S(1)}, f32[16,64,512]{2,1,0:T(8,128)S(1)}, u32[]{:S(2)}, u32[]{:S(2)}) collective-permute-start(f32[16,64,512]{2,1,0:T(8,128)S(1)} %get-tuple-element.29), channel_id=1, source_target_pairs={{0,1},{1,0},{2,3},{3,2},{4,5},{5,4},{6,7},{7,6},{8,9},{9,8},{10,11... | collective-permute-start | bytes 6291464 | tf_op jit(solution)/shard_map/ppermute | solution.py:406
  6.2 30.2 %collective-permute-start.2 = (f32[9,64,512]{2,1,0:T(8,128)S(1)}, f32[9,64,512]{2,1,0:T(8,128)S(1)}, u32[]{:S(2)}, u32[]{:S(2)}) collective-permute-start(f32[9,64,512]{2,1,0:T(8,128)S(1)} %shard_map.37.earlier), channel_id=1, source_target_pairs={{0,287},{1,258},{2,257},{3,260},{4,259},{5,262},{6,261},{7,264},{8... | collective-permute-start | bytes 3538952 | tf_op jit(solution)/shard_map/ppermute | solution.py:424
  9.8 22.4 %collective-permute-start = (f32[7,64,512]{2,1,0:T(8,128)S(1)}, f32[7,64,512]{2,1,0:T(8,128)S(1)}, u32[]{:S(2)}, u32[]{:S(2)}) collective-permute-start(f32[7,64,512]{2,1,0:T(8,128)S(1)} %get-tuple-element.28), channel_id=1, source_target_pairs={{0,31},{1,2},{2,1},{3,4},{4,3},{5,6},{6,5},{7,8},{8,7},{9,10},{10,... | collective-permute-start | bytes 2752520 | tf_op jit(solution)/shard_map/ppermute | solution.py:415
  17.4 19.6 %collective-permute-start.3 = (f32[1,4,2,8,128]{4,3,2,1,0:T(8,128)S(1)}, f32[1,4,2,8,128]{4,3,2,1,0:T(8,128)S(1)}, u32[]{:S(2)}, u32[]{:S(2)}) collective-permute-start(f32[1,4,2,8,128]{4,3,2,1,0:T(8,128)S(1)} %bitcast.7), channel_id=1, source_target_pairs={{0,8},{1,9},{2,10},{3,11},{4,12},{5,13},{6,14},{7,15},{8,0},{9,1},... | collective-permute-start | bytes 98312 | tf_op jit(solution)/shard_map/ppermute | solution.py:434
  20.5 16.5 %collective-permute-start.4 = (f32[1,4,2,8,128]{4,3,2,1,0:T(8,128)S(1)}, f32[1,4,2,8,128]{4,3,2,1,0:T(8,128)S(1)}, u32[]{:S(2)}, u32[]{:S(2)}) collective-permute-start(f32[1,4,2,8,128]{4,3,2,1,0:T(8,128)S(1)} %bitcast.8), channel_id=1, source_target_pairs={{0,16},{1,17},{2,18},{3,19},{4,20},{5,21},{6,22},{7,23},{8,24},{9,... | collective-permute-start | bytes 98312 | tf_op jit(solution)/shard_map/ppermute | solution.py:434
  29.6 8.3 %collective-permute-start.5 = (f32[1,4,2,8,128]{4,3,2,1,0:T(8,128)S(1)}, f32[1,4,2,8,128]{4,3,2,1,0:T(8,128)S(1)}, u32[]{:S(2)}, u32[]{:S(2)}) collective-permute-start(f32[1,4,2,8,128]{4,3,2,1,0:T(8,128)S(1)} %bitcast.9), channel_id=1, source_target_pairs={{0,24},{1,25},{2,26},{3,27},{4,28},{5,29},{6,30},{7,31},{8,16},{9,... | collective-permute-start | bytes 98312 | tf_op jit(solution)/shard_map/ppermute | solution.py:434
  42.2 22.6 %collective-permute-start.8 = (f32[4,8,8,512]{3,2,1,0:T(8,128)S(1)}, f32[4,8,8,512]{3,2,1,0:T(8,128)S(1)}, u32[]{:S(2)}, u32[]{:S(2)}) collective-permute-start(f32[4,8,8,512]{3,2,1,0:T(8,128)S(1)} %get-tuple-element.35.state), channel_id=1, source_target_pairs={{0,1},{1,0},{2,3},{3,2},{4,5},{5,4},{6,7},{7,6},{8,9},{9,8},{10,11... | collective-permute-start | bytes 1572872 | tf_op jit(solution)/shard_map/ppermute | solution.py:406
  51.5 13.3 %collective-permute-start.6 = (f32[2,8,8,512]{3,2,1,0:T(8,128)S(1)}, f32[2,8,8,512]{3,2,1,0:T(8,128)S(1)}, u32[]{:S(2)}, u32[]{:S(2)}) collective-permute-start(f32[2,8,8,512]{3,2,1,0:T(8,128)S(1)} %get-tuple-element.33), channel_id=1, source_target_pairs={{0,31},{1,2},{2,1},{3,4},{4,3},{5,6},{6,5},{7,8},{8,7},{9,10},{10,... | collective-permute-start | bytes 786440 | tf_op jit(solution)/shard_map/ppermute | solution.py:415
  54.8 13.0 %collective-permute-start.7 = (f32[2,8,8,512]{3,2,1,0:T(8,128)S(1)}, f32[2,8,8,512]{3,2,1,0:T(8,128)S(1)}, u32[]{:S(2)}, u32[]{:S(2)}) collective-permute-start(f32[2,8,8,512]{3,2,1,0:T(8,128)S(1)} %get-tuple-element.34), channel_id=1, source_target_pairs={{0,31},{1,2},{2,1},{3,4},{4,3},{5,6},{6,5},{7,8},{8,7},{9,10},{10,... | collective-permute-start | bytes 786440 | tf_op jit(solution)/shard_map/ppermute | solution.py:415
  57.1 10.8 %collective-permute-start.9 = (f32[4,4,2,8,128]{4,3,2,1,0:T(8,128)S(1)}, f32[4,4,2,8,128]{4,3,2,1,0:T(8,128)S(1)}, u32[]{:S(2)}, u32[]{:S(2)}) collective-permute-start(f32[4,4,2,8,128]{4,3,2,1,0:T(8,128)S(1)} %get-tuple-element.38.refs_0_), channel_id=1, source_target_pairs={{0,258},{1,259},{2,256},{3,257},{4,262},{5,263},{6,260},{7,261},{8... | collective-permute-start | bytes 393224 | tf_op jit(solution)/shard_map/ppermute | solution.py:433
  69.5 15.4 %collective-permute-start.12 = (f32[4,8,8,512]{3,2,1,0:T(8,128)S(1)}, f32[4,8,8,512]{3,2,1,0:T(8,128)S(1)}, u32[]{:S(2)}, u32[]{:S(2)}) collective-permute-start(f32[4,8,8,512]{3,2,1,0:T(8,128)S(1)} %get-tuple-element.40.state), channel_id=1, source_target_pairs={{0,1},{1,0},{2,3},{3,2},{4,5},{5,4},{6,7},{7,6},{8,9},{9,8},{10,11... | collective-permute-start | bytes 1572872 | tf_op jit(solution)/shard_map/ppermute | solution.py:406
  71.5 13.4 %collective-permute-start.10 = (f32[2,8,8,512]{3,2,1,0:T(8,128)S(1)}, f32[2,8,8,512]{3,2,1,0:T(8,128)S(1)}, u32[]{:S(2)}, u32[]{:S(2)}) collective-permute-start(f32[2,8,8,512]{3,2,1,0:T(8,128)S(1)} %get-tuple-element.39), channel_id=1, source_target_pairs={{0,31},{1,2},{2,1},{3,4},{4,3},{5,6},{6,5},{7,8},{8,7},{9,10},{10,... | collective-permute-start | bytes 786440 | tf_op jit(solution)/shard_map/ppermute | solution.py:415
  74.6 13.5 %collective-permute-start.11 = (f32[2,8,8,512]{3,2,1,0:T(8,128)S(1)}, f32[2,8,8,512]{3,2,1,0:T(8,128)S(1)}, u32[]{:S(2)}, u32[]{:S(2)}) collective-permute-start(f32[2,8,8,512]{3,2,1,0:T(8,128)S(1)} %get-tuple-element.37.rest), channel_id=1, source_target_pairs={{0,31},{1,2},{2,1},{3,4},{4,3},{5,6},{6,5},{7,8},{8,7},{9,10},{10,... | collective-permute-start | bytes 786440 | tf_op jit(solution)/shard_map/ppermute | solution.py:415
  77.0 11.0 %collective-permute-start.13 = (f32[8,4,2,8,128]{4,3,2,1,0:T(8,128)S(1)}, f32[8,4,2,8,128]{4,3,2,1,0:T(8,128)S(1)}, u32[]{:S(2)}, u32[]{:S(2)}) collective-permute-start(f32[8,4,2,8,128]{4,3,2,1,0:T(8,128)S(1)} %get-tuple-element.43.refs_0_), channel_id=1, source_target_pairs={{0,4},{1,5},{2,6},{3,7},{4,0},{5,1},{6,2},{7,3},{8,12},{9,13},{10,... | collective-permute-start | bytes 786440 | tf_op jit(solution)/shard_map/ppermute | solution.py:434
  80.1 7.9 %collective-permute-start.14 = (f32[2,8,128]{2,1,0:T(8,128)S(1)}, f32[2,8,128]{2,1,0:T(8,128)S(1)}, u32[]{:S(2)}, u32[]{:S(2)}) collective-permute-start(f32[2,8,128]{2,1,0:T(8,128)S(1)} %get-tuple-element.31.refs_1_.refs_2_), channel_id=1, source_target_pairs={{32,0},{64,32},{96,64},{128,96},{160,128},{192,160},{224,192},{256... | collective-permute-start | bytes 24584 | tf_op jit(solution)/shard_map/ppermute | solution.py:469
  89.7 11.8 %collective-permute-start.18 = (f32[16,4,2,8,128]{4,3,2,1,0:T(8,128)S(1)}, f32[16,4,2,8,128]{4,3,2,1,0:T(8,128)S(1)}, u32[]{:S(2)}, u32[]{:S(2)}) collective-permute-start(f32[16,4,2,8,128]{4,3,2,1,0:T(8,128)S(1)} %get-tuple-element.48.some), channel_id=1, source_target_pairs={{0,1},{1,0},{2,3},{3,2},{4,5},{5,4},{6,7},{7,6},{8,9},{9,8},{10,11... | collective-permute-start | bytes 1572872 | tf_op jit(solution)/shard_map/ppermute | solution.py:434
  92.8 13.5 %collective-permute-start.17 = (f32[4,8,8,512]{3,2,1,0:T(8,128)S(1)}, f32[4,8,8,512]{3,2,1,0:T(8,128)S(1)}, u32[]{:S(2)}, u32[]{:S(2)}) collective-permute-start(f32[4,8,8,512]{3,2,1,0:T(8,128)S(1)} %get-tuple-element.45.state), channel_id=1, source_target_pairs={{0,1},{1,0},{2,3},{3,2},{4,5},{5,4},{6,7},{7,6},{8,9},{9,8},{10,11... | collective-permute-start | bytes 1572872 | tf_op jit(solution)/shard_map/ppermute | solution.py:406
  94.7 11.6 %collective-permute-start.15 = (f32[2,8,8,512]{3,2,1,0:T(8,128)S(1)}, f32[2,8,8,512]{3,2,1,0:T(8,128)S(1)}, u32[]{:S(2)}, u32[]{:S(2)}) collective-permute-start(f32[2,8,8,512]{3,2,1,0:T(8,128)S(1)} %get-tuple-element.44), channel_id=1, source_target_pairs={{0,31},{1,2},{2,1},{3,4},{4,3},{5,6},{6,5},{7,8},{8,7},{9,10},{10,... | collective-permute-start | bytes 786440 | tf_op jit(solution)/shard_map/ppermute | solution.py:415
  99.4 12.5 %collective-permute-start.16 = (f32[2,8,8,512]{3,2,1,0:T(8,128)S(1)}, f32[2,8,8,512]{3,2,1,0:T(8,128)S(1)}, u32[]{:S(2)}, u32[]{:S(2)}) collective-permute-start(f32[2,8,8,512]{3,2,1,0:T(8,128)S(1)} %get-tuple-element.42.rest), channel_id=1, source_target_pairs={{0,31},{1,2},{2,1},{3,4},{4,3},{5,6},{6,5},{7,8},{8,7},{9,10},{10,... | collective-permute-start | bytes 786440 | tf_op jit(solution)/shard_map/ppermute | solution.py:415

commit v11 on v10

--- a/solution.py
+++ b/solution.py
@@ -206,30 +206,59 @@
         begin += part.shape[0]
 
 
-def first_kernel(place, state, outer, inner, own, own_outer, own_inner, *refs):
+def first_inner_kernel(place, state, inner, own, own_inner, passed, one, two, buffer):
+    core = place[2]
+
+    def enter(x, carry):
+        blocks = ((state, x, LAYERS), (inner, STATE_AT + x, 2 * LAYERS * (1 - core)))
+        for i, (ref, at, begin) in enumerate(blocks):
+            spread(ref[at], buffer.at[i])
+            for j in range(8):
+                one[begin + x, j] = spread_tile(buffer.at[i], j)
+        return carry
+
+    lax.fori_loop(0, LAYERS, enter, 0)
+    source, target = one, two
+    for step in range(1, LAYERS):
+        count = LAYERS - step
+        sweep(source, target, LAYERS + (1 - core) * step, count, own, (1 - core) * step)
+        above, below = 2 * LAYERS, step
+        sweep(source, target, above - core * (above - below), count, own_inner, core * (step - 1))
+        for i in range(2):
+            on_first, on_second = LAYERS + step + i, 2 * LAYERS - 1 - step - i
+            passed[step - 1, i] = target[on_first - core * (on_first - on_second)]
+        source, target = target, source
+
+
+def first_outer_kernel(place, state, outer, own, own_outer, passed, *refs):
     *parts, out, near, far, joined, one, two, buffer = refs
     join(parts, joined)
     core = place[2]
 
     def enter(x, carry):
-        blocks = ((state, LAYERS), (outer, 2 * LAYERS * core), (inner, 2 * LAYERS * (1 - core)))
-        for i, (ref, begin) in enumerate(blocks):
-            spread(ref[(STATE_AT if ref is inner else 0) + x], buffer.at[i])
-            for j in range(8):
-                one[begin + x, j] = spread_tile(buffer.at[i], j)
+        spread(outer[x], buffer.at[0])
+        for j in range(8):
+            one[2 * LAYERS * core + x, j] = spread_tile(buffer.at[0], j)
         return carry
 
     lax.fori_loop(0, LAYERS, enter, 0)
+    for i in range(2):
+        spread(state[2 * core + i], buffer.at[1 + i])
+        for j in range(8):
+            one[LAYERS + 2 * core + i, j] = spread_tile(buffer.at[1 + i], j)
     source, target = one, two
     for step in range(1, LAYERS + 1):
         ends = step == LAYERS
         goal = out if ends else target
-        depth = LAYERS - step
-        sweep(source, goal, LAYERS, LAYERS, own, 0, LAYERS if ends else 0)
-        if depth > 0:
+        count = LAYERS - step
+        if count:
             below, above = step, 2 * LAYERS
-            sweep(source, goal, below + core * (above - below), depth, own_outer, (1 - core) * (step - 1))
-            sweep(source, goal, above - core * (above - below), depth, own_inner, core * (step - 1))
+            sweep(source, goal, below + core * (above - below), count, own_outer, (1 - core) * (step - 1))
+        sweep(source, goal, LAYERS + core * count, step, own, core * count, LAYERS if ends else 0)
+        if not ends:
+            for i in range(2):
+                on_first, on_second = LAYERS + step + i, 2 * LAYERS - 1 - step - i
+                target[on_first - core * (on_first - on_second)] = passed[step - 1, i]
         source, target = target, source
     for i in range(2):
         near[i] = out[2 * core + i]
@@ -472,18 +501,24 @@
     inner_weights = call(functools.partial(side_kernel, STATE_AT + LAYERS), side, [VMEM, ANY], [columns], cost=SMALL)(
         all_inner, coarse_old
     )[0]
-    outer_weights = call(functools.partial(side_kernel, LAYERS), side, [VMEM, VMEM, ANY], [columns], cost=SMALL)(
-        fields_outer, mixed_outer, inner_weights
-    )[0]
     pair = (2, *TILE)
     scratch = [pltpu.VMEM((3 * LAYERS, *TILE), F32)] * 2
     parts = [gathered] + [across(gathered, bits) for bits in (8, 16, 24)]
+    passed = call(
+        first_inner_kernel,
+        [(LAYERS - 1, *pair)],
+        [SMEM] + [VMEM] * 4,
+        scratch + [columns],
+    )(place, starts[0], all_inner, own_weights, inner_weights)[0]
+    outer_weights = call(functools.partial(side_kernel, LAYERS), side, [VMEM, VMEM, ANY], [columns], cost=SMALL)(
+        fields_outer, mixed_outer, passed
+    )[0]
     state, near, far, gathered = call(
-        first_kernel,
+        first_outer_kernel,
         [block, pair, pair, (4, 4, *COARSE)],
-        [SMEM] + [VMEM] * (6 + len(parts)),
+        [SMEM] + [VMEM] * (5 + len(parts)),
         scratch + [columns],
-    )(place, starts[0], mixed_outer, all_inner, own_weights, outer_weights, inner_weights, *parts)
+    )(place, starts[0], mixed_outer, own_weights, outer_weights, passed, *parts)
     for index in range(1, ROUNDS):
         final = index == ROUNDS - 1
         near, inner, far = swap_outer(near), swap_inner(state), swap_outer(far)

time: 157 us -> 156 us (level)
  starting transfers between devices: 72.2 us -> 75.9 us
  waiting for transfers between devices: 15.2 us -> 11.8 us
  blocking collectives: 32.7 us -> 29.8 us
    ppermute x5, starting transfers between devices: 20.2 us -> 24.2 us  [across(): return lax.ppermute(block, 'space', [(p, p ^ bits) for p in range(count)])]
    all_to_all x1, blocking collectives: 19.7 us -> 17.1 us  [shards(): residuals = lax.all_to_all(gathered, 'space', 0, 0)]
    ppermute x1, waiting for transfers between devices: 4.26 us -> 2.1 us  [swap_outer_fields(): return lax.ppermute(block, ('cuts', 'space'), route)]
    pallas_call x1 -> x2, Pallas kernels: 4.22 us -> 4.77 us  [the longest x1 2.62 us: shards(): call(first_outer_kernel, [block, pair, pair, (4, 4, *COARSE)], [SMEM] + [...]
  transfers between devices with their start and end apart: 19 -> 19, of which waited for: 5 -> 5; matrix products, arithmetic and copies ran while one was open for 0% -> 0% of each run, Pallas kernels for 8% -> 9%
where the time goes in v11:
time: 156 us; the launch traced here: 155 us
  starting transfers between devices  75.9 us (49%)
  Pallas kernels  35.3 us (23%)
  blocking collectives  29.8 us (19%)
  waiting for transfers between devices  11.8 us (8%)
    ppermute x5, starting transfers between devices, across(): return lax.ppermute(block, 'space', [(p, p ^ bits) for p in range(count)])  24.2 us
    ppermute x7, starting transfers between devices, swap_outer(): lax.ppermute(block, 'space', [(p, outer_partner(p, count)) for p in range...  23.2 us
    all_to_all x1, blocking collectives, shards(): residuals = lax.all_to_all(gathered, 'space', 0, 0)  17.1 us
    ppermute x4, starting transfers between devices, swap_inner(): return lax.ppermute(block, 'space', [(p, p ^ 1) for p in range(count)])  15.7 us
    all_to_all x1, blocking collectives, shards(): shares = lax.all_to_all(shares, 'cuts', 0, 0)  12.8 us
    ppermute x7, waiting for transfers between devices, swap_outer(): lax.ppermute(block, 'space', [(p, outer_partner(p, count)) for p in range...  9.42 us
    pallas_call x3, Pallas kernels, shards(): call(near_kernel, [(LAYERS - 1, *pair), pair], [SMEM] + [VMEM] * 6, scratch)  9.17 us
    pallas_call x1, Pallas kernels, shards(): call(chain_kernel, [(slices, *COARSE)], [SMEM, VMEM, VMEM], [pltpu.VMEM((...  9.15 us
  transfers between devices with their start and end apart: 19, of which 5 were waited for; matrix products, arithmetic and copies ran while one was open for 0% of the time, Pallas kernels for 9%

profile of v11, /device:TPU:2, one launch (start us, length us, event | category | flops | bytes accessed | tf_op | source)
XLA Modules:
  0.0 154.8 jit_solution(9184148356723588767)
XLA Ops:
  0.0 0.1 pad_add_fusion.place
  0.1 0.0 copy-start
  0.1 1.4 copy-done
  1.5 0.0 copy-start.2
  1.5 0.0 copy-start.3
  1.5 1.1 shard_map.37.earlier
  2.6 0.0 copy-done.2
  2.6 0.0 copy-done.3
  2.7 1.6 %shard_map.38 = (f32[7,64,512]{2,1,0:T(8,128)S(1)}, f32[16,64,512]{2,1,0:T(8,128)S(1)}) custom-call(s32[3]{0:T(128)S(1)} %pad_add_fusion.place, f32[3,4,64,512]{3,2,1,0:T(8,128)S(1)} %copy-done, f32[4,64,512]{2,1,0:T(8,128)S(1)} %copy-done.3, f32[1,4,64,512]{3,2,1,0:T(8,128)S(1)} %copy-done.2, f32[9,64,512]{2,1,0:T(8,128)S(1)} %shard_map.37.earlier), custom_call_target="tpu_custom_call" | custom-call | flops 1 | bytes 1 | tf_op jit(solution)/shard_map/pallas_call | solution.py:481
  4.3 1.9 %collective-permute-start.2 = (f32[16,64,512]{2,1,0:T(8,128)S(1)}, f32[16,64,512]{2,1,0:T(8,128)S(1)}, u32[]{:S(2)}, u32[]{:S(2)}) collective-permute-start(f32[16,64,512]{2,1,0:T(8,128)S(1)} %get-tuple-element.30), channel_id=1, source_target_pairs={{0,1},{1,0},{2,3},{3,2},{4,5},{5,4},{6,7},{7,6},{8,9},{9,8},{10,11... | collective-permute-start | bytes 6291464 | tf_op jit(solution)/shard_map/ppermute | solution.py:435
  6.2 3.5 %collective-permute-start.1 = (f32[9,64,512]{2,1,0:T(8,128)S(1)}, f32[9,64,512]{2,1,0:T(8,128)S(1)}, u32[]{:S(2)}, u32[]{:S(2)}) collective-permute-start(f32[9,64,512]{2,1,0:T(8,128)S(1)} %shard_map.37.earlier), channel_id=1, source_target_pairs={{0,287},{1,258},{2,257},{3,260},{4,259},{5,262},{6,261},{7,264},{8... | collective-permute-start | bytes 3538952 | tf_op jit(solution)/shard_map/ppermute | solution.py:453
  9.8 6.3 %collective-permute-start = (f32[7,64,512]{2,1,0:T(8,128)S(1)}, f32[7,64,512]{2,1,0:T(8,128)S(1)}, u32[]{:S(2)}, u32[]{:S(2)}) collective-permute-start(f32[7,64,512]{2,1,0:T(8,128)S(1)} %get-tuple-element.28), channel_id=1, source_target_pairs={{0,31},{1,2},{2,1},{3,4},{4,3},{5,6},{6,5},{7,8},{8,7},{9,10},{10,... | collective-permute-start | bytes 2752520 | tf_op jit(solution)/shard_map/ppermute | solution.py:444
  16.1 0.0 copy-done.1
  16.1 1.3 shard_map.39
  17.4 7.9 %collective-permute-start.5 = (f32[1,4,2,8,128]{4,3,2,1,0:T(8,128)S(1)}, f32[1,4,2,8,128]{4,3,2,1,0:T(8,128)S(1)}, u32[]{:S(2)}, u32[]{:S(2)}) collective-permute-start(f32[1,4,2,8,128]{4,3,2,1,0:T(8,128)S(1)} %bitcast.8), channel_id=1, source_target_pairs={{0,24},{1,25},{2,26},{3,27},{4,28},{5,29},{6,30},{7,31},{8,16},{9,... | collective-permute-start | bytes 98312 | tf_op jit(solution)/shard_map/ppermute | solution.py:463
  25.4 1.9 %collective-permute-start.4 = (f32[1,4,2,8,128]{4,3,2,1,0:T(8,128)S(1)}, f32[1,4,2,8,128]{4,3,2,1,0:T(8,128)S(1)}, u32[]{:S(2)}, u32[]{:S(2)}) collective-permute-start(f32[1,4,2,8,128]{4,3,2,1,0:T(8,128)S(1)} %bitcast.9), channel_id=1, source_target_pairs={{0,16},{1,17},{2,18},{3,19},{4,20},{5,21},{6,22},{7,23},{8,24},{9,... | collective-permute-start | bytes 98312 | tf_op jit(solution)/shard_map/ppermute | solution.py:463
  27.3 0.0 collective-permute-done.2.refs_0_.inner
  27.3 4.3 %collective-permute-start.3 = (f32[1,4,2,8,128]{4,3,2,1,0:T(8,128)S(1)}, f32[1,4,2,8,128]{4,3,2,1,0:T(8,128)S(1)}, u32[]{:S(2)}, u32[]{:S(2)}) collective-permute-start(f32[1,4,2,8,128]{4,3,2,1,0:T(8,128)S(1)} %bitcast.10), channel_id=1, source_target_pairs={{0,8},{1,9},{2,10},{3,11},{4,12},{5,13},{6,14},{7,15},{8,0},{9,1},... | collective-permute-start | bytes 98312 | tf_op jit(solution)/shard_map/ppermute | solution.py:463
  31.6 0.6 shard_map.40.own_inner
  32.1 2.2 %shard_map.41.refs_2_.passed = f32[3,2,8,8,512]{4,3,2,1,0:T(8,128)S(1)} custom-call(s32[3]{0:T(128)S(1)} %pad_add_fusion.place, f32[4,64,512]{2,1,0:T(8,128)S(1)} %bitcast.6, f32[16,64,512]{2,1,0:T(8,128)S(1)} %collective-permute-done.2.refs_0_.inner, f32[4,7,8,8,512]{4,3,2,1,0:T(8,128)S(1)} %get-tuple-element.29.own, ...), custom_call_target="tpu_custom_call" | custom-call | tf_op jit(solution)/shard_map/pallas_call | solution.py:507
  34.3 0.0 collective-permute-done.refs_1_.outer
  34.3 2.1 %collective-permute-done.1.refs_0_ = f32[9,64,512]{2,1,0:T(8,128)S(1)} collective-permute-done((f32[9,64,512]{2,1,0:T(8,128)S(1)}, f32[9,64,512]{2,1,0:T(8,128)S(1)}, u32[]{:S(2)}, u32[]{:S(2)}) %collective-permute-start.1) | collective-permute-done | bytes 1179680 | tf_op jit(solution)/shard_map/ppermute | solution.py:453
  36.4 0.6 shard_map.42.own_outer
  37.0 0.0 collective-permute-done.5.refs_3_
  37.0 0.0 collective-permute-done.4.refs_2_
  37.0 0.0 collective-permute-done.3.refs_1_
  37.0 2.6 %shard_map.43 = (f32[4,8,8,512]{3,2,1,0:T(8,128)S(1)}, f32[2,8,8,512]{3,2,1,0:T(8,128)S(1)}, f32[2,8,8,512]{3,2,1,0:T(8,128)S(1)}, f32[4,4,2,8,128]{4,3,2,1,0:T(8,128)S(1)}) custom-call(s32[3]{0:T(128)S(1)} %pad_add_fusion.place, f32[4,64,512]{2,1,0:T(8,128)S(1)} %bitcast.7, f32[7,64,512]{2,1,0:T(8,128)S(1)} %collective-permute-done.refs_1_.outer, ...), custom_call_target="tpu_custom_call" | custom-call | tf_op jit(solution)/shard_map/pallas_call | solution.py:516
  39.6 10.0 %collective-permute-start.8 = (f32[4,8,8,512]{3,2,1,0:T(8,128)S(1)}, f32[4,8,8,512]{3,2,1,0:T(8,128)S(1)}, u32[]{:S(2)}, u32[]{:S(2)}) collective-permute-start(f32[4,8,8,512]{3,2,1,0:T(8,128)S(1)} %get-tuple-element.35.state), channel_id=1, source_target_pairs={{0,1},{1,0},{2,3},{3,2},{4,5},{5,4},{6,7},{7,6},{8,9},{9,8},{10,11... | collective-permute-start | bytes 1572872 | tf_op jit(solution)/shard_map/ppermute | solution.py:435
  49.6 3.6 %collective-permute-start.6 = (f32[2,8,8,512]{3,2,1,0:T(8,128)S(1)}, f32[2,8,8,512]{3,2,1,0:T(8,128)S(1)}, u32[]{:S(2)}, u32[]{:S(2)}) collective-permute-start(f32[2,8,8,512]{3,2,1,0:T(8,128)S(1)} %get-tuple-element.33), channel_id=1, source_target_pairs={{0,31},{1,2},{2,1},{3,4},{4,3},{5,6},{6,5},{7,8},{8,7},{9,10},{10,... | collective-permute-start | bytes 786440 | tf_op jit(solution)/shard_map/ppermute | solution.py:444
  53.2 1.9 %collective-permute-start.7 = (f32[2,8,8,512]{3,2,1,0:T(8,128)S(1)}, f32[2,8,8,512]{3,2,1,0:T(8,128)S(1)}, u32[]{:S(2)}, u32[]{:S(2)}) collective-permute-start(f32[2,8,8,512]{3,2,1,0:T(8,128)S(1)} %get-tuple-element.34), channel_id=1, source_target_pairs={{0,31},{1,2},{2,1},{3,4},{4,3},{5,6},{6,5},{7,8},{8,7},{9,10},{10,... | collective-permute-start | bytes 786440 | tf_op jit(solution)/shard_map/ppermute | solution.py:444
  55.2 4.6 %collective-permute-start.9 = (f32[4,4,2,8,128]{4,3,2,1,0:T(8,128)S(1)}, f32[4,4,2,8,128]{4,3,2,1,0:T(8,128)S(1)}, u32[]{:S(2)}, u32[]{:S(2)}) collective-permute-start(f32[4,4,2,8,128]{4,3,2,1,0:T(8,128)S(1)} %get-tuple-element.38.refs_0_), channel_id=1, source_target_pairs={{0,258},{1,259},{2,256},{3,257},{4,262},{5,263},{6,260},{7,261},{8... | collective-permute-start | bytes 393224 | tf_op jit(solution)/shard_map/ppermute | solution.py:462
  59.8 0.3 collective-permute-done.6.near
  60.1 0.0 collective-permute-done.8.inner
  60.1 3.1 %shard_map.44 = (f32[3,2,8,8,512]{4,3,2,1,0:T(8,128)S(1)}, f32[2,8,8,512]{3,2,1,0:T(8,128)S(1)}) custom-call(s32[3]{0:T(128)S(1)} %pad_add_fusion.place, f32[4,8,8,512]{3,2,1,0:T(8,128)S(1)} %get-tuple-element.35.state, f32[4,8,8,512]{3,2,1,0:T(8,128)S(1)} %collective-permute-done.8.inner, f32[2,8,8,512]{3,2,1,0:T(8,128)S(1)} %collective-permute-done.6.near, ...), custom_call_target="tpu_custom_call" | custom-call | tf_op jit(solution)/shard_map/pallas_call | solution.py:525
  63.2 0.2 collective-permute-done.9.refs_1_
  63.4 2.3 %collective-permute-done.7.far = f32[2,8,8,512]{3,2,1,0:T(8,128)S(1)} collective-permute-done((f32[2,8,8,512]{3,2,1,0:T(8,128)S(1)}, f32[2,8,8,512]{3,2,1,0:T(8,128)S(1)}, u32[]{:S(2)}, u32[]{:S(2)}) %collective-permute-start.7) | collective-permute-done | bytes 262176 | tf_op jit(solution)/shard_map/ppermute | solution.py:444
  65.7 1.7 %shard_map.45 = (f32[4,8,8,512]{3,2,1,0:T(8,128)S(1)}, f32[2,8,8,512]{3,2,1,0:T(8,128)S(1)}, f32[8,4,2,8,128]{4,3,2,1,0:T(8,128)S(1)}) custom-call(s32[3]{0:T(128)S(1)} %pad_add_fusion.place, f32[2,8,8,512]{3,2,1,0:T(8,128)S(1)} %collective-permute-done.6.near, f32[2,8,8,512]{3,2,1,0:T(8,128)S(1)} %collective-permute-done.7.far, ...), custom_call_target="tpu_custom_call" | custom-call | tf_op jit(solution)/shard_map/pallas_call | solution.py:547
  67.4 1.9 %collective-permute-start.12 = (f32[4,8,8,512]{3,2,1,0:T(8,128)S(1)}, f32[4,8,8,512]{3,2,1,0:T(8,128)S(1)}, u32[]{:S(2)}, u32[]{:S(2)}) collective-permute-start(f32[4,8,8,512]{3,2,1,0:T(8,128)S(1)} %get-tuple-element.40.state), channel_id=1, source_target_pairs={{0,1},{1,0},{2,3},{3,2},{4,5},{5,4},{6,7},{7,6},{8,9},{9,8},{10,11... | collective-permute-start | bytes 1572872 | tf_op jit(solution)/shard_map/ppermute | solution.py:435
  69.3 3.6 %collective-permute-start.10 = (f32[2,8,8,512]{3,2,1,0:T(8,128)S(1)}, f32[2,8,8,512]{3,2,1,0:T(8,128)S(1)}, u32[]{:S(2)}, u32[]{:S(2)}) collective-permute-start(f32[2,8,8,512]{3,2,1,0:T(8,128)S(1)} %get-tuple-element.39), channel_id=1, source_target_pairs={{0,31},{1,2},{2,1},{3,4},{4,3},{5,6},{6,5},{7,8},{8,7},{9,10},{10,... | collective-permute-start | bytes 786440 | tf_op jit(solution)/shard_map/ppermute | solution.py:444
  73.0 4.0 %collective-permute-start.13 = (f32[8,4,2,8,128]{4,3,2,1,0:T(8,128)S(1)}, f32[8,4,2,8,128]{4,3,2,1,0:T(8,128)S(1)}, u32[]{:S(2)}, u32[]{:S(2)}) collective-permute-start(f32[8,4,2,8,128]{4,3,2,1,0:T(8,128)S(1)} %get-tuple-element.43.refs_0_), channel_id=1, source_target_pairs={{0,4},{1,5},{2,6},{3,7},{4,0},{5,1},{6,2},{7,3},{8,12},{9,13},{10,... | collective-permute-start | bytes 786440 | tf_op jit(solution)/shard_map/ppermute | solution.py:463
  77.0 1.9 %collective-permute-start.11 = (f32[2,8,8,512]{3,2,1,0:T(8,128)S(1)}, f32[2,8,8,512]{3,2,1,0:T(8,128)S(1)}, u32[]{:S(2)}, u32[]{:S(2)}) collective-permute-start(f32[2,8,8,512]{3,2,1,0:T(8,128)S(1)} %get-tuple-element.37.rest), channel_id=1, source_target_pairs={{0,31},{1,2},{2,1},{3,4},{4,3},{5,6},{6,5},{7,8},{8,7},{9,10},{10,... | collective-permute-start | bytes 786440 | tf_op jit(solution)/shard_map/ppermute | solution.py:444
  78.9 4.7 %collective-permute-start.14 = (f32[2,8,128]{2,1,0:T(8,128)S(1)}, f32[2,8,128]{2,1,0:T(8,128)S(1)}, u32[]{:S(2)}, u32[]{:S(2)}) collective-permute-start(f32[2,8,128]{2,1,0:T(8,128)S(1)} %get-tuple-element.31.refs_1_.refs_2_), channel_id=1, source_target_pairs={{32,0},{64,32},{96,64},{128,96},{160,128},{192,160},{224,192},{256... | collective-permute-start | bytes 24584 | tf_op jit(solution)/shard_map/ppermute | solution.py:498
  83.6 0.0 collective-permute-done.10.near
  83.6 0.0 collective-permute-done.12.inner
  83.6 3.1 %shard_map.46 = (f32[3,2,8,8,512]{4,3,2,1,0:T(8,128)S(1)}, f32[2,8,8,512]{3,2,1,0:T(8,128)S(1)}) custom-call(s32[3]{0:T(128)S(1)} %pad_add_fusion.place, f32[4,8,8,512]{3,2,1,0:T(8,128)S(1)} %get-tuple-element.40.state, f32[4,8,8,512]{3,2,1,0:T(8,128)S(1)} %collective-permute-done.12.inner, f32[2,8,8,512]{3,2,1,0:T(8,128)S(1)} %collective-permute-done.10.near, ...), custom_call_target="tpu_custom_call" | custom-call | tf_op jit(solution)/shard_map/pallas_call | solution.py:525
  86.7 0.0 collective-permute-done.14.refs_2_.refs_0_
  86.7 0.0 collective-permute-done.13.refs_1_
  86.7 0.0 collective-permute-done.11.far
  86.7 1.7 %shard_map.47 = (f32[4,8,8,512]{3,2,1,0:T(8,128)S(1)}, f32[2,8,8,512]{3,2,1,0:T(8,128)S(1)}, f32[16,4,2,8,128]{4,3,2,1,0:T(8,128)S(1)}) custom-call(s32[3]{0:T(128)S(1)} %pad_add_fusion.place, f32[2,8,8,512]{3,2,1,0:T(8,128)S(1)} %collective-permute-done.10.near, f32[2,8,8,512]{3,2,1,0:T(8,128)S(1)} %collective-permute-done.11.far, ...), custom_call_target="tpu_custom_call" | custom-call | tf_op jit(solution)/shard_map/pallas_call | solution.py:547
  88.4 6.1 %collective-permute-start.18 = (f32[16,4,2,8,128]{4,3,2,1,0:T(8,128)S(1)}, f32[16,4,2,8,128]{4,3,2,1,0:T(8,128)S(1)}, u32[]{:S(2)}, u32[]{:S(2)}) collective-permute-start(f32[16,4,2,8,128]{4,3,2,1,0:T(8,128)S(1)} %get-tuple-element.48.some), channel_id=1, source_target_pairs={{0,1},{1,0},{2,3},{3,2},{4,5},{5,4},{6,7},{7,6},{8,9},{9,8},{10,11... | collective-permute-start | bytes 1572872 | tf_op jit(solution)/shard_map/ppermute | solution.py:463
  94.5 1.9 %collective-permute-start.17 = (f32[4,8,8,512]{3,2,1,0:T(8,128)S(1)}, f32[4,8,8,512]{3,2,1,0:T(8,128)S(1)}, u32[]{:S(2)}, u32[]{:S(2)}) collective-permute-start(f32[4,8,8,512]{3,2,1,0:T(8,128)S(1)} %get-tuple-element.45.state), channel_id=1, source_target_pairs={{0,1},{1,0},{2,3},{3,2},{4,5},{5,4},{6,7},{7,6},{8,9},{9,8},{10,11... | collective-permute-start | bytes 1572872 | tf_op jit(solution)/shard_map/ppermute | solution.py:435
  96.4 2.6 %collective-permute-start.15 = (f32[2,8,8,512]{3,2,1,0:T(8,128)S(1)}, f32[2,8,8,512]{3,2,1,0:T(8,128)S(1)}, u32[]{:S(2)}, u32[]{:S(2)}) collective-permute-start(f32[2,8,8,512]{3,2,1,0:T(8,128)S(1)} %get-tuple-element.44), channel_id=1, source_target_pairs={{0,31},{1,2},{2,1},{3,4},{4,3},{5,6},{6,5},{7,8},{8,7},{9,10},{10,... | collective-permute-start | bytes 786440 | tf_op jit(solution)/shard_map/ppermute | solution.py:444
  99.1 3.1 %collective-permute-start.16 = (f32[2,8,8,512]{3,2,1,0:T(8,128)S(1)}, f32[2,8,8,512]{3,2,1,0:T(8,128)S(1)}, u32[]{:S(2)}, u32[]{:S(2)}) collective-permute-start(f32[2,8,8,512]{3,2,1,0:T(8,128)S(1)} %get-tuple-element.42.rest), channel_id=1, source_target_pairs={{0,31},{1,2},{2,1},{3,4},{4,3},{5,6},{6,5},{7,8},{8,7},{9,10},{10,... | collective-permute-start | bytes 786440 | tf_op jit(solution)/shard_map/ppermute | solution.py:444
  102.2 0.0 collective-permute-done.18.others
  102.2 0.7 shard_map.49.refs_1_.given
  103.0 6.8 %collective-permute-done.15.near = f32[2,8,8,512]{3,2,1,0:T(8,128)S(1)} collective-permute-done((f32[2,8,8,512]{3,2,1,0:T(8,128)S(1)}, f32[2,8,8,512]{3,2,1,0:T(8,128)S(1)}, u32[]{:S(2)}, u32[]{:S(2)}) %collective-permute-start.15) | collective-permute-done | bytes 262176 | tf_op jit(solution)/shard_map/ppermute | solution.py:444
  109.8 0.0 collective-permute-done.17.inner
  109.8 3.1 %shard_map.48 = (f32[3,2,8,8,512]{4,3,2,1,0:T(8,128)S(1)}, f32[2,8,8,512]{3,2,1,0:T(8,128)S(1)}) custom-call(s32[3]{0:T(128)S(1)} %pad_add_fusion.place, f32[4,8,8,512]{3,2,1,0:T(8,128)S(1)} %get-tuple-element.45.state, f32[4,8,8,512]{3,2,1,0:T(8,128)S(1)} %collective-permute-done.17.inner, f32[2,8,8,512]{3,2,1,0:T(8,128)S(1)} %collective-permute-done.15.near, ...), custom_call_target="tpu_custom_call" | custom-call | tf_op jit(solution)/shard_map/pallas_call | solution.py:525
  112.8 0.0 collective-permute-done.16.far
  112.8 1.9 %shard_map.50 = (f32[4,8,8,512]{3,2,1,0:T(8,128)S(1)}, f32[32,2,8,128]{3,2,1,0:T(8,128)S(1)}) custom-call(s32[3]{0:T(128)S(1)} %pad_add_fusion.place, f32[2,8,8,512]{3,2,1,0:T(8,128)S(1)} %collective-permute-done.15.near, f32[2,8,8,512]{3,2,1,0:T(8,128)S(1)} %collective-permute-done.16.far, f32[4,7,8,8,512]{4,3,2,1,0:T(8,128)S(1)} %get-tuple-element.29.own, ...), custom_call_target="tpu_custom_call" | custom-call | tf_op jit(solution)/shard_map/pallas_call | solution.py:547
  114.7 17.1 %all_to_all.10.residuals = f32[32,2,8,128]{3,2,1,0:T(8,128)S(1)} all-to-all(f32[32,2,8,128]{3,2,1,0:T(8,128)S(1)} %get-tuple-element.49), channel_id=1, replica_groups=mesh['cuts'=16,'space'=32] {'space'}, dimensions={0} | all-to-all | bytes 524288 | tf_op jit(solution)/shard_map/all_to_all | solution.py:549
  131.8 9.2 %shard_map.51 = f32[16,2,8,128]{3,2,1,0:T(8,128)S(1)} custom-call(s32[3]{0:T(128)S(1)} %pad_add_fusion.place, f32[32,2,8,128]{3,2,1,0:T(8,128)S(1)} %all_to_all.10.residuals, f32[32,7,2,8,128]{4,3,2,1,0:T(8,128)S(1)} %shard_map.49.refs_1_.given), custom_call_target="tpu_custom_call" | custom-call | tf_op jit(solution)/shard_map/pallas_call | solution.py:550
  140.9 12.8 %all_to_all.11.shares = f32[16,2,8,128]{3,2,1,0:T(8,128)S(1)} all-to-all(f32[16,2,8,128]{3,2,1,0:T(8,128)S(1)} %shard_map.51), channel_id=1, replica_groups=mesh['cuts'=16,'space'=32] {'cuts'}, dimensions={0} | all-to-all | bytes 262144 | tf_op jit(solution)/shard_map/all_to_all | solution.py:556
  153.7 1.1 shard_map.52
  (1 shorter events, 0.0 us)
Async XLA Ops:
  0.1 1.4 copy-start
  1.5 1.1 copy-start.2
  1.5 1.2 copy-start.3
  2.7 13.4 %copy-start.1 = (f32[3,4,64,512]{3,2,1,0:T(8,128)S(1)}, f32[3,4,64,512]{3,2,1,0:T(8,128)}, u32[]{:S(2)}) copy-start(f32[3,4,64,512]{3,2,1,0:T(8,128)} %velocity.5) | copy-start | bytes 4718596
  4.3 23.0 %collective-permute-start.2 = (f32[16,64,512]{2,1,0:T(8,128)S(1)}, f32[16,64,512]{2,1,0:T(8,128)S(1)}, u32[]{:S(2)}, u32[]{:S(2)}) collective-permute-start(f32[16,64,512]{2,1,0:T(8,128)S(1)} %get-tuple-element.30), channel_id=1, source_target_pairs={{0,1},{1,0},{2,3},{3,2},{4,5},{5,4},{6,7},{7,6},{8,9},{9,8},{10,11... | collective-permute-start | bytes 6291464 | tf_op jit(solution)/shard_map/ppermute | solution.py:435
  6.2 30.2 %collective-permute-start.1 = (f32[9,64,512]{2,1,0:T(8,128)S(1)}, f32[9,64,512]{2,1,0:T(8,128)S(1)}, u32[]{:S(2)}, u32[]{:S(2)}) collective-permute-start(f32[9,64,512]{2,1,0:T(8,128)S(1)} %shard_map.37.earlier), channel_id=1, source_target_pairs={{0,287},{1,258},{2,257},{3,260},{4,259},{5,262},{6,261},{7,264},{8... | collective-permute-start | bytes 3538952 | tf_op jit(solution)/shard_map/ppermute | solution.py:453
  9.8 24.5 %collective-permute-start = (f32[7,64,512]{2,1,0:T(8,128)S(1)}, f32[7,64,512]{2,1,0:T(8,128)S(1)}, u32[]{:S(2)}, u32[]{:S(2)}) collective-permute-start(f32[7,64,512]{2,1,0:T(8,128)S(1)} %get-tuple-element.28), channel_id=1, source_target_pairs={{0,31},{1,2},{2,1},{3,4},{4,3},{5,6},{6,5},{7,8},{8,7},{9,10},{10,... | collective-permute-start | bytes 2752520 | tf_op jit(solution)/shard_map/ppermute | solution.py:444
  17.4 19.6 %collective-permute-start.5 = (f32[1,4,2,8,128]{4,3,2,1,0:T(8,128)S(1)}, f32[1,4,2,8,128]{4,3,2,1,0:T(8,128)S(1)}, u32[]{:S(2)}, u32[]{:S(2)}) collective-permute-start(f32[1,4,2,8,128]{4,3,2,1,0:T(8,128)S(1)} %bitcast.8), channel_id=1, source_target_pairs={{0,24},{1,25},{2,26},{3,27},{4,28},{5,29},{6,30},{7,31},{8,16},{9,... | collective-permute-start | bytes 98312 | tf_op jit(solution)/shard_map/ppermute | solution.py:463
  25.4 11.6 %collective-permute-start.4 = (f32[1,4,2,8,128]{4,3,2,1,0:T(8,128)S(1)}, f32[1,4,2,8,128]{4,3,2,1,0:T(8,128)S(1)}, u32[]{:S(2)}, u32[]{:S(2)}) collective-permute-start(f32[1,4,2,8,128]{4,3,2,1,0:T(8,128)S(1)} %bitcast.9), channel_id=1, source_target_pairs={{0,16},{1,17},{2,18},{3,19},{4,20},{5,21},{6,22},{7,23},{8,24},{9,... | collective-permute-start | bytes 98312 | tf_op jit(solution)/shard_map/ppermute | solution.py:463
  27.3 9.7 %collective-permute-start.3 = (f32[1,4,2,8,128]{4,3,2,1,0:T(8,128)S(1)}, f32[1,4,2,8,128]{4,3,2,1,0:T(8,128)S(1)}, u32[]{:S(2)}, u32[]{:S(2)}) collective-permute-start(f32[1,4,2,8,128]{4,3,2,1,0:T(8,128)S(1)} %bitcast.10), channel_id=1, source_target_pairs={{0,8},{1,9},{2,10},{3,11},{4,12},{5,13},{6,14},{7,15},{8,0},{9,1},... | collective-permute-start | bytes 98312 | tf_op jit(solution)/shard_map/ppermute | solution.py:463
  39.6 20.5 %collective-permute-start.8 = (f32[4,8,8,512]{3,2,1,0:T(8,128)S(1)}, f32[4,8,8,512]{3,2,1,0:T(8,128)S(1)}, u32[]{:S(2)}, u32[]{:S(2)}) collective-permute-start(f32[4,8,8,512]{3,2,1,0:T(8,128)S(1)} %get-tuple-element.35.state), channel_id=1, source_target_pairs={{0,1},{1,0},{2,3},{3,2},{4,5},{5,4},{6,7},{7,6},{8,9},{9,8},{10,11... | collective-permute-start | bytes 1572872 | tf_op jit(solution)/shard_map/ppermute | solution.py:435
  49.6 10.5 %collective-permute-start.6 = (f32[2,8,8,512]{3,2,1,0:T(8,128)S(1)}, f32[2,8,8,512]{3,2,1,0:T(8,128)S(1)}, u32[]{:S(2)}, u32[]{:S(2)}) collective-permute-start(f32[2,8,8,512]{3,2,1,0:T(8,128)S(1)} %get-tuple-element.33), channel_id=1, source_target_pairs={{0,31},{1,2},{2,1},{3,4},{4,3},{5,6},{6,5},{7,8},{8,7},{9,10},{10,... | collective-permute-start | bytes 786440 | tf_op jit(solution)/shard_map/ppermute | solution.py:444
  53.2 12.5 %collective-permute-start.7 = (f32[2,8,8,512]{3,2,1,0:T(8,128)S(1)}, f32[2,8,8,512]{3,2,1,0:T(8,128)S(1)}, u32[]{:S(2)}, u32[]{:S(2)}) collective-permute-start(f32[2,8,8,512]{3,2,1,0:T(8,128)S(1)} %get-tuple-element.34), channel_id=1, source_target_pairs={{0,31},{1,2},{2,1},{3,4},{4,3},{5,6},{6,5},{7,8},{8,7},{9,10},{10,... | collective-permute-start | bytes 786440 | tf_op jit(solution)/shard_map/ppermute | solution.py:444
  55.2 8.2 %collective-permute-start.9 = (f32[4,4,2,8,128]{4,3,2,1,0:T(8,128)S(1)}, f32[4,4,2,8,128]{4,3,2,1,0:T(8,128)S(1)}, u32[]{:S(2)}, u32[]{:S(2)}) collective-permute-start(f32[4,4,2,8,128]{4,3,2,1,0:T(8,128)S(1)} %get-tuple-element.38.refs_0_), channel_id=1, source_target_pairs={{0,258},{1,259},{2,256},{3,257},{4,262},{5,263},{6,260},{7,261},{8... | collective-permute-start | bytes 393224 | tf_op jit(solution)/shard_map/ppermute | solution.py:462
  67.4 16.2 %collective-permute-start.12 = (f32[4,8,8,512]{3,2,1,0:T(8,128)S(1)}, f32[4,8,8,512]{3,2,1,0:T(8,128)S(1)}, u32[]{:S(2)}, u32[]{:S(2)}) collective-permute-start(f32[4,8,8,512]{3,2,1,0:T(8,128)S(1)} %get-tuple-element.40.state), channel_id=1, source_target_pairs={{0,1},{1,0},{2,3},{3,2},{4,5},{5,4},{6,7},{7,6},{8,9},{9,8},{10,11... | collective-permute-start | bytes 1572872 | tf_op jit(solution)/shard_map/ppermute | solution.py:435
  69.3 14.3 %collective-permute-start.10 = (f32[2,8,8,512]{3,2,1,0:T(8,128)S(1)}, f32[2,8,8,512]{3,2,1,0:T(8,128)S(1)}, u32[]{:S(2)}, u32[]{:S(2)}) collective-permute-start(f32[2,8,8,512]{3,2,1,0:T(8,128)S(1)} %get-tuple-element.39), channel_id=1, source_target_pairs={{0,31},{1,2},{2,1},{3,4},{4,3},{5,6},{6,5},{7,8},{8,7},{9,10},{10,... | collective-permute-start | bytes 786440 | tf_op jit(solution)/shard_map/ppermute | solution.py:444
  73.0 13.7 %collective-permute-start.13 = (f32[8,4,2,8,128]{4,3,2,1,0:T(8,128)S(1)}, f32[8,4,2,8,128]{4,3,2,1,0:T(8,128)S(1)}, u32[]{:S(2)}, u32[]{:S(2)}) collective-permute-start(f32[8,4,2,8,128]{4,3,2,1,0:T(8,128)S(1)} %get-tuple-element.43.refs_0_), channel_id=1, source_target_pairs={{0,4},{1,5},{2,6},{3,7},{4,0},{5,1},{6,2},{7,3},{8,12},{9,13},{10,... | collective-permute-start | bytes 786440 | tf_op jit(solution)/shard_map/ppermute | solution.py:463
  77.0 9.8 %collective-permute-start.11 = (f32[2,8,8,512]{3,2,1,0:T(8,128)S(1)}, f32[2,8,8,512]{3,2,1,0:T(8,128)S(1)}, u32[]{:S(2)}, u32[]{:S(2)}) collective-permute-start(f32[2,8,8,512]{3,2,1,0:T(8,128)S(1)} %get-tuple-element.37.rest), channel_id=1, source_target_pairs={{0,31},{1,2},{2,1},{3,4},{4,3},{5,6},{6,5},{7,8},{8,7},{9,10},{10,... | collective-permute-start | bytes 786440 | tf_op jit(solution)/shard_map/ppermute | solution.py:444
  78.9 7.8 %collective-permute-start.14 = (f32[2,8,128]{2,1,0:T(8,128)S(1)}, f32[2,8,128]{2,1,0:T(8,128)S(1)}, u32[]{:S(2)}, u32[]{:S(2)}) collective-permute-start(f32[2,8,128]{2,1,0:T(8,128)S(1)} %get-tuple-element.31.refs_1_.refs_2_), channel_id=1, source_target_pairs={{32,0},{64,32},{96,64},{128,96},{160,128},{192,160},{224,192},{256... | collective-permute-start | bytes 24584 | tf_op jit(solution)/shard_map/ppermute | solution.py:498
  88.4 13.8 %collective-permute-start.18 = (f32[16,4,2,8,128]{4,3,2,1,0:T(8,128)S(1)}, f32[16,4,2,8,128]{4,3,2,1,0:T(8,128)S(1)}, u32[]{:S(2)}, u32[]{:S(2)}) collective-permute-start(f32[16,4,2,8,128]{4,3,2,1,0:T(8,128)S(1)} %get-tuple-element.48.some), channel_id=1, source_target_pairs={{0,1},{1,0},{2,3},{3,2},{4,5},{5,4},{6,7},{7,6},{8,9},{9,8},{10,11... | collective-permute-start | bytes 1572872 | tf_op jit(solution)/shard_map/ppermute | solution.py:463
  94.5 15.2 %collective-permute-start.17 = (f32[4,8,8,512]{3,2,1,0:T(8,128)S(1)}, f32[4,8,8,512]{3,2,1,0:T(8,128)S(1)}, u32[]{:S(2)}, u32[]{:S(2)}) collective-permute-start(f32[4,8,8,512]{3,2,1,0:T(8,128)S(1)} %get-tuple-element.45.state), channel_id=1, source_target_pairs={{0,1},{1,0},{2,3},{3,2},{4,5},{5,4},{6,7},{7,6},{8,9},{9,8},{10,11... | collective-permute-start | bytes 1572872 | tf_op jit(solution)/shard_map/ppermute | solution.py:435
  96.4 13.3 %collective-permute-start.15 = (f32[2,8,8,512]{3,2,1,0:T(8,128)S(1)}, f32[2,8,8,512]{3,2,1,0:T(8,128)S(1)}, u32[]{:S(2)}, u32[]{:S(2)}) collective-permute-start(f32[2,8,8,512]{3,2,1,0:T(8,128)S(1)} %get-tuple-element.44), channel_id=1, source_target_pairs={{0,31},{1,2},{2,1},{3,4},{4,3},{5,6},{6,5},{7,8},{8,7},{9,10},{10,... | collective-permute-start | bytes 786440 | tf_op jit(solution)/shard_map/ppermute | solution.py:444
  99.1 13.7 %collective-permute-start.16 = (f32[2,8,8,512]{3,2,1,0:T(8,128)S(1)}, f32[2,8,8,512]{3,2,1,0:T(8,128)S(1)}, u32[]{:S(2)}, u32[]{:S(2)}) collective-permute-start(f32[2,8,8,512]{3,2,1,0:T(8,128)S(1)} %get-tuple-element.42.rest), channel_id=1, source_target_pairs={{0,31},{1,2},{2,1},{3,4},{4,3},{5,6},{6,5},{7,8},{8,7},{9,10},{10,... | collective-permute-start | bytes 786440 | tf_op jit(solution)/shard_map/ppermute | solution.py:444

commit v12 on v11

--- a/solution.py
+++ b/solution.py
@@ -541,7 +541,7 @@
             outs = [block, (count, *COARSE)]
         else:
             parts = [gathered, across(gathered, (2, 4)[index - 1])]
-            operands += parts + [coarse_later if index == 2 else coarse_old]
+            operands += parts + [coarse_later if index == 1 else coarse_old]
             specs += [VMEM] * len(parts) + [ANY]
             outs = [block, pair, (2 * gathered.shape[0], 4, *COARSE)]
         state, *near, gathered = call(functools.partial(far_kernel, final), outs, specs, scratch)(*operands)

time: 156 us -> 157 us (level)
    ppermute x1, starting transfers between devices: 4.71 us -> 8.08 us  [shards(): lax.ppermute(coarse_old, 'cuts', [((n + 1) % slices, n) for n in range(sl...]
    ppermute x5, starting transfers between devices: 24.2 us -> 22.1 us  [across(): return lax.ppermute(block, 'space', [(p, p ^ bits) for p in range(count)])]
  transfers between devices with their start and end apart: 19 -> 19, of which waited for: 5 -> 3; matrix products, arithmetic and copies ran while one was open for 0% -> 0% of each run, Pallas kernels for 9% -> 9%
where the time goes in v12:
time: 157 us
  starting transfers between devices  77.1 us (49%)
  Pallas kernels  35.3 us (22%)
  blocking collectives  30.5 us (19%)
  waiting for transfers between devices  11.8 us (8%)
    ppermute x7, starting transfers between devices, swap_outer(): lax.ppermute(block, 'space', [(p, outer_partner(p, count)) for p in range...  23.1 us
    ppermute x5, starting transfers between devices, across(): return lax.ppermute(block, 'space', [(p, p ^ bits) for p in range(count)])  22.1 us
    all_to_all x1, blocking collectives, shards(): residuals = lax.all_to_all(gathered, 'space', 0, 0)  17.7 us
    ppermute x4, starting transfers between devices, swap_inner(): return lax.ppermute(block, 'space', [(p, p ^ 1) for p in range(count)])  15.7 us
    all_to_all x1, blocking collectives, shards(): shares = lax.all_to_all(shares, 'cuts', 0, 0)  12.7 us
    ppermute x7, waiting for transfers between devices, swap_outer(): lax.ppermute(block, 'space', [(p, outer_partner(p, count)) for p in range...  9.71 us
    pallas_call x3, Pallas kernels, shards(): call(near_kernel, [(LAYERS - 1, *pair), pair], [SMEM] + [VMEM] * 6, scratch)  9.17 us
    pallas_call x1, Pallas kernels, shards(): call(chain_kernel, [(slices, *COARSE)], [SMEM, VMEM, VMEM], [pltpu.VMEM((...  9.15 us
  transfers between devices with their start and end apart: 19, of which 3 were waited for; matrix products, arithmetic and copies ran while one was open for 0% of the time, Pallas kernels for 9%

profile of v12, /device:TPU:2, one launch (start us, length us, event | category | flops | bytes accessed | tf_op | source)
XLA Modules:
  0.0 156.7 jit_solution(4498539151326185638)
XLA Ops:
  0.0 0.1 pad_add_fusion.place
  0.1 0.0 copy-start
  0.1 1.4 copy-done
  1.5 0.0 copy-start.2
  1.5 0.0 copy-start.3
  1.5 1.1 shard_map.37.earlier
  2.6 0.0 copy-done.2
  2.6 0.0 copy-done.3
  2.7 1.6 %shard_map.38 = (f32[7,64,512]{2,1,0:T(8,128)S(1)}, f32[16,64,512]{2,1,0:T(8,128)S(1)}) custom-call(s32[3]{0:T(128)S(1)} %pad_add_fusion.place, f32[3,4,64,512]{3,2,1,0:T(8,128)S(1)} %copy-done, f32[4,64,512]{2,1,0:T(8,128)S(1)} %copy-done.3, f32[1,4,64,512]{3,2,1,0:T(8,128)S(1)} %copy-done.2, f32[9,64,512]{2,1,0:T(8,128)S(1)} %shard_map.37.earlier), custom_call_target="tpu_custom_call" | custom-call | flops 1 | bytes 1 | tf_op jit(solution)/shard_map/pallas_call | solution.py:481
  4.3 1.9 %collective-permute-start.2 = (f32[16,64,512]{2,1,0:T(8,128)S(1)}, f32[16,64,512]{2,1,0:T(8,128)S(1)}, u32[]{:S(2)}, u32[]{:S(2)}) collective-permute-start(f32[16,64,512]{2,1,0:T(8,128)S(1)} %get-tuple-element.30), channel_id=1, source_target_pairs={{0,1},{1,0},{2,3},{3,2},{4,5},{5,4},{6,7},{7,6},{8,9},{9,8},{10,11... | collective-permute-start | bytes 6291464 | tf_op jit(solution)/shard_map/ppermute | solution.py:435
  6.2 3.5 %collective-permute-start.1 = (f32[9,64,512]{2,1,0:T(8,128)S(1)}, f32[9,64,512]{2,1,0:T(8,128)S(1)}, u32[]{:S(2)}, u32[]{:S(2)}) collective-permute-start(f32[9,64,512]{2,1,0:T(8,128)S(1)} %shard_map.37.earlier), channel_id=1, source_target_pairs={{0,287},{1,258},{2,257},{3,260},{4,259},{5,262},{6,261},{7,264},{8... | collective-permute-start | bytes 3538952 | tf_op jit(solution)/shard_map/ppermute | solution.py:453
  9.8 6.3 %collective-permute-start = (f32[7,64,512]{2,1,0:T(8,128)S(1)}, f32[7,64,512]{2,1,0:T(8,128)S(1)}, u32[]{:S(2)}, u32[]{:S(2)}) collective-permute-start(f32[7,64,512]{2,1,0:T(8,128)S(1)} %get-tuple-element.28), channel_id=1, source_target_pairs={{0,31},{1,2},{2,1},{3,4},{4,3},{5,6},{6,5},{7,8},{8,7},{9,10},{10,... | collective-permute-start | bytes 2752520 | tf_op jit(solution)/shard_map/ppermute | solution.py:444
  16.1 0.0 copy-done.1
  16.1 1.3 shard_map.39
  17.4 7.9 %collective-permute-start.5 = (f32[1,4,2,8,128]{4,3,2,1,0:T(8,128)S(1)}, f32[1,4,2,8,128]{4,3,2,1,0:T(8,128)S(1)}, u32[]{:S(2)}, u32[]{:S(2)}) collective-permute-start(f32[1,4,2,8,128]{4,3,2,1,0:T(8,128)S(1)} %bitcast.8), channel_id=1, source_target_pairs={{0,24},{1,25},{2,26},{3,27},{4,28},{5,29},{6,30},{7,31},{8,16},{9,... | collective-permute-start | bytes 98312 | tf_op jit(solution)/shard_map/ppermute | solution.py:463
  25.4 1.9 %collective-permute-start.4 = (f32[1,4,2,8,128]{4,3,2,1,0:T(8,128)S(1)}, f32[1,4,2,8,128]{4,3,2,1,0:T(8,128)S(1)}, u32[]{:S(2)}, u32[]{:S(2)}) collective-permute-start(f32[1,4,2,8,128]{4,3,2,1,0:T(8,128)S(1)} %bitcast.9), channel_id=1, source_target_pairs={{0,16},{1,17},{2,18},{3,19},{4,20},{5,21},{6,22},{7,23},{8,24},{9,... | collective-permute-start | bytes 98312 | tf_op jit(solution)/shard_map/ppermute | solution.py:463
  27.3 0.0 collective-permute-done.2.refs_0_.inner
  27.3 4.3 %collective-permute-start.3 = (f32[1,4,2,8,128]{4,3,2,1,0:T(8,128)S(1)}, f32[1,4,2,8,128]{4,3,2,1,0:T(8,128)S(1)}, u32[]{:S(2)}, u32[]{:S(2)}) collective-permute-start(f32[1,4,2,8,128]{4,3,2,1,0:T(8,128)S(1)} %bitcast.10), channel_id=1, source_target_pairs={{0,8},{1,9},{2,10},{3,11},{4,12},{5,13},{6,14},{7,15},{8,0},{9,1},... | collective-permute-start | bytes 98312 | tf_op jit(solution)/shard_map/ppermute | solution.py:463
  31.6 0.6 shard_map.40.own_inner
  32.1 2.2 %shard_map.41.refs_2_.passed = f32[3,2,8,8,512]{4,3,2,1,0:T(8,128)S(1)} custom-call(s32[3]{0:T(128)S(1)} %pad_add_fusion.place, f32[4,64,512]{2,1,0:T(8,128)S(1)} %bitcast.6, f32[16,64,512]{2,1,0:T(8,128)S(1)} %collective-permute-done.2.refs_0_.inner, f32[4,7,8,8,512]{4,3,2,1,0:T(8,128)S(1)} %get-tuple-element.29.own, ...), custom_call_target="tpu_custom_call" | custom-call | tf_op jit(solution)/shard_map/pallas_call | solution.py:507
  34.3 0.0 collective-permute-done.refs_1_.outer
  34.3 2.1 %collective-permute-done.1.refs_0_ = f32[9,64,512]{2,1,0:T(8,128)S(1)} collective-permute-done((f32[9,64,512]{2,1,0:T(8,128)S(1)}, f32[9,64,512]{2,1,0:T(8,128)S(1)}, u32[]{:S(2)}, u32[]{:S(2)}) %collective-permute-start.1) | collective-permute-done | bytes 1179680 | tf_op jit(solution)/shard_map/ppermute | solution.py:453
  36.4 0.6 shard_map.42.own_outer
  37.0 0.0 collective-permute-done.5.refs_3_
  37.0 0.0 collective-permute-done.4.refs_2_
  37.0 0.0 collective-permute-done.3.refs_1_
  37.0 2.6 %shard_map.43 = (f32[4,8,8,512]{3,2,1,0:T(8,128)S(1)}, f32[2,8,8,512]{3,2,1,0:T(8,128)S(1)}, f32[2,8,8,512]{3,2,1,0:T(8,128)S(1)}, f32[4,4,2,8,128]{4,3,2,1,0:T(8,128)S(1)}) custom-call(s32[3]{0:T(128)S(1)} %pad_add_fusion.place, f32[4,64,512]{2,1,0:T(8,128)S(1)} %bitcast.7, f32[7,64,512]{2,1,0:T(8,128)S(1)} %collective-permute-done.refs_1_.outer, ...), custom_call_target="tpu_custom_call" | custom-call | tf_op jit(solution)/shard_map/pallas_call | solution.py:516
  39.6 10.0 %collective-permute-start.8 = (f32[4,8,8,512]{3,2,1,0:T(8,128)S(1)}, f32[4,8,8,512]{3,2,1,0:T(8,128)S(1)}, u32[]{:S(2)}, u32[]{:S(2)}) collective-permute-start(f32[4,8,8,512]{3,2,1,0:T(8,128)S(1)} %get-tuple-element.35.state), channel_id=1, source_target_pairs={{0,1},{1,0},{2,3},{3,2},{4,5},{5,4},{6,7},{7,6},{8,9},{9,8},{10,11... | collective-permute-start | bytes 1572872 | tf_op jit(solution)/shard_map/ppermute | solution.py:435
  49.6 3.6 %collective-permute-start.6 = (f32[2,8,8,512]{3,2,1,0:T(8,128)S(1)}, f32[2,8,8,512]{3,2,1,0:T(8,128)S(1)}, u32[]{:S(2)}, u32[]{:S(2)}) collective-permute-start(f32[2,8,8,512]{3,2,1,0:T(8,128)S(1)} %get-tuple-element.33), channel_id=1, source_target_pairs={{0,31},{1,2},{2,1},{3,4},{4,3},{5,6},{6,5},{7,8},{8,7},{9,10},{10,... | collective-permute-start | bytes 786440 | tf_op jit(solution)/shard_map/ppermute | solution.py:444
  53.2 1.9 %collective-permute-start.7 = (f32[2,8,8,512]{3,2,1,0:T(8,128)S(1)}, f32[2,8,8,512]{3,2,1,0:T(8,128)S(1)}, u32[]{:S(2)}, u32[]{:S(2)}) collective-permute-start(f32[2,8,8,512]{3,2,1,0:T(8,128)S(1)} %get-tuple-element.34), channel_id=1, source_target_pairs={{0,31},{1,2},{2,1},{3,4},{4,3},{5,6},{6,5},{7,8},{8,7},{9,10},{10,... | collective-permute-start | bytes 786440 | tf_op jit(solution)/shard_map/ppermute | solution.py:444
  55.2 4.6 %collective-permute-start.9 = (f32[4,4,2,8,128]{4,3,2,1,0:T(8,128)S(1)}, f32[4,4,2,8,128]{4,3,2,1,0:T(8,128)S(1)}, u32[]{:S(2)}, u32[]{:S(2)}) collective-permute-start(f32[4,4,2,8,128]{4,3,2,1,0:T(8,128)S(1)} %get-tuple-element.38.refs_0_), channel_id=1, source_target_pairs={{0,258},{1,259},{2,256},{3,257},{4,262},{5,263},{6,260},{7,261},{8... | collective-permute-start | bytes 393224 | tf_op jit(solution)/shard_map/ppermute | solution.py:462
  59.8 8.1 %collective-permute-start.10 = (f32[2,8,128]{2,1,0:T(8,128)S(1)}, f32[2,8,128]{2,1,0:T(8,128)S(1)}, u32[]{:S(2)}, u32[]{:S(2)}) collective-permute-start(f32[2,8,128]{2,1,0:T(8,128)S(1)} %get-tuple-element.31.refs_1_.refs_2_), channel_id=1, source_target_pairs={{32,0},{64,32},{96,64},{128,96},{160,128},{192,160},{224,192},{256... | collective-permute-start | bytes 24584 | tf_op jit(solution)/shard_map/ppermute | solution.py:498
  67.9 0.0 collective-permute-done.6.near
  67.9 0.0 collective-permute-done.8.inner
  67.9 3.1 %shard_map.44 = (f32[3,2,8,8,512]{4,3,2,1,0:T(8,128)S(1)}, f32[2,8,8,512]{3,2,1,0:T(8,128)S(1)}) custom-call(s32[3]{0:T(128)S(1)} %pad_add_fusion.place, f32[4,8,8,512]{3,2,1,0:T(8,128)S(1)} %get-tuple-element.35.state, f32[4,8,8,512]{3,2,1,0:T(8,128)S(1)} %collective-permute-done.8.inner, f32[2,8,8,512]{3,2,1,0:T(8,128)S(1)} %collective-permute-done.6.near, ...), custom_call_target="tpu_custom_call" | custom-call | tf_op jit(solution)/shard_map/pallas_call | solution.py:525
  71.0 0.0 collective-permute-done.10.refs_2_.refs_0_
  71.0 0.0 collective-permute-done.9.refs_1_
  71.0 0.0 collective-permute-done.7.far
  71.0 1.7 %shard_map.45 = (f32[4,8,8,512]{3,2,1,0:T(8,128)S(1)}, f32[2,8,8,512]{3,2,1,0:T(8,128)S(1)}, f32[8,4,2,8,128]{4,3,2,1,0:T(8,128)S(1)}) custom-call(s32[3]{0:T(128)S(1)} %pad_add_fusion.place, f32[2,8,8,512]{3,2,1,0:T(8,128)S(1)} %collective-permute-done.6.near, f32[2,8,8,512]{3,2,1,0:T(8,128)S(1)} %collective-permute-done.7.far, ...), custom_call_target="tpu_custom_call" | custom-call | tf_op jit(solution)/shard_map/pallas_call | solution.py:547
  72.7 1.9 %collective-permute-start.13 = (f32[4,8,8,512]{3,2,1,0:T(8,128)S(1)}, f32[4,8,8,512]{3,2,1,0:T(8,128)S(1)}, u32[]{:S(2)}, u32[]{:S(2)}) collective-permute-start(f32[4,8,8,512]{3,2,1,0:T(8,128)S(1)} %get-tuple-element.40.state), channel_id=1, source_target_pairs={{0,1},{1,0},{2,3},{3,2},{4,5},{5,4},{6,7},{7,6},{8,9},{9,8},{10,11... | collective-permute-start | bytes 1572872 | tf_op jit(solution)/shard_map/ppermute | solution.py:435
  74.6 1.9 %collective-permute-start.11 = (f32[2,8,8,512]{3,2,1,0:T(8,128)S(1)}, f32[2,8,8,512]{3,2,1,0:T(8,128)S(1)}, u32[]{:S(2)}, u32[]{:S(2)}) collective-permute-start(f32[2,8,8,512]{3,2,1,0:T(8,128)S(1)} %get-tuple-element.39), channel_id=1, source_target_pairs={{0,31},{1,2},{2,1},{3,4},{4,3},{5,6},{6,5},{7,8},{8,7},{9,10},{10,... | collective-permute-start | bytes 786440 | tf_op jit(solution)/shard_map/ppermute | solution.py:444
  76.5 2.0 %collective-permute-start.14 = (f32[8,4,2,8,128]{4,3,2,1,0:T(8,128)S(1)}, f32[8,4,2,8,128]{4,3,2,1,0:T(8,128)S(1)}, u32[]{:S(2)}, u32[]{:S(2)}) collective-permute-start(f32[8,4,2,8,128]{4,3,2,1,0:T(8,128)S(1)} %get-tuple-element.43.refs_0_), channel_id=1, source_target_pairs={{0,4},{1,5},{2,6},{3,7},{4,0},{5,1},{6,2},{7,3},{8,12},{9,13},{10,... | collective-permute-start | bytes 786440 | tf_op jit(solution)/shard_map/ppermute | solution.py:463
  78.6 3.5 %collective-permute-start.12 = (f32[2,8,8,512]{3,2,1,0:T(8,128)S(1)}, f32[2,8,8,512]{3,2,1,0:T(8,128)S(1)}, u32[]{:S(2)}, u32[]{:S(2)}) collective-permute-start(f32[2,8,8,512]{3,2,1,0:T(8,128)S(1)} %get-tuple-element.37.rest), channel_id=1, source_target_pairs={{0,31},{1,2},{2,1},{3,4},{4,3},{5,6},{6,5},{7,8},{8,7},{9,10},{10,... | collective-permute-start | bytes 786440 | tf_op jit(solution)/shard_map/ppermute | solution.py:444
  82.1 2.9 %collective-permute-done.11.near = f32[2,8,8,512]{3,2,1,0:T(8,128)S(1)} collective-permute-done((f32[2,8,8,512]{3,2,1,0:T(8,128)S(1)}, f32[2,8,8,512]{3,2,1,0:T(8,128)S(1)}, u32[]{:S(2)}, u32[]{:S(2)}) %collective-permute-start.11) | collective-permute-done | bytes 262176 | tf_op jit(solution)/shard_map/ppermute | solution.py:444
  85.0 0.0 collective-permute-done.13.inner
  85.0 3.1 %shard_map.46 = (f32[3,2,8,8,512]{4,3,2,1,0:T(8,128)S(1)}, f32[2,8,8,512]{3,2,1,0:T(8,128)S(1)}) custom-call(s32[3]{0:T(128)S(1)} %pad_add_fusion.place, f32[4,8,8,512]{3,2,1,0:T(8,128)S(1)} %get-tuple-element.40.state, f32[4,8,8,512]{3,2,1,0:T(8,128)S(1)} %collective-permute-done.13.inner, f32[2,8,8,512]{3,2,1,0:T(8,128)S(1)} %collective-permute-done.11.near, ...), custom_call_target="tpu_custom_call" | custom-call | tf_op jit(solution)/shard_map/pallas_call | solution.py:525
  88.1 0.0 collective-permute-done.14.refs_1_
  88.1 0.0 collective-permute-done.12.far
  88.1 1.7 %shard_map.47 = (f32[4,8,8,512]{3,2,1,0:T(8,128)S(1)}, f32[2,8,8,512]{3,2,1,0:T(8,128)S(1)}, f32[16,4,2,8,128]{4,3,2,1,0:T(8,128)S(1)}) custom-call(s32[3]{0:T(128)S(1)} %pad_add_fusion.place, f32[2,8,8,512]{3,2,1,0:T(8,128)S(1)} %collective-permute-done.11.near, f32[2,8,8,512]{3,2,1,0:T(8,128)S(1)} %collective-permute-done.12.far, ...), custom_call_target="tpu_custom_call" | custom-call | tf_op jit(solution)/shard_map/pallas_call | solution.py:547
  89.8 6.0 %collective-permute-start.18 = (f32[16,4,2,8,128]{4,3,2,1,0:T(8,128)S(1)}, f32[16,4,2,8,128]{4,3,2,1,0:T(8,128)S(1)}, u32[]{:S(2)}, u32[]{:S(2)}) collective-permute-start(f32[16,4,2,8,128]{4,3,2,1,0:T(8,128)S(1)} %get-tuple-element.48.some), channel_id=1, source_target_pairs={{0,1},{1,0},{2,3},{3,2},{4,5},{5,4},{6,7},{7,6},{8,9},{9,8},{10,11... | collective-permute-start | bytes 1572872 | tf_op jit(solution)/shard_map/ppermute | solution.py:463
  95.8 1.9 %collective-permute-start.17 = (f32[4,8,8,512]{3,2,1,0:T(8,128)S(1)}, f32[4,8,8,512]{3,2,1,0:T(8,128)S(1)}, u32[]{:S(2)}, u32[]{:S(2)}) collective-permute-start(f32[4,8,8,512]{3,2,1,0:T(8,128)S(1)} %get-tuple-element.45.state), channel_id=1, source_target_pairs={{0,1},{1,0},{2,3},{3,2},{4,5},{5,4},{6,7},{7,6},{8,9},{9,8},{10,11... | collective-permute-start | bytes 1572872 | tf_op jit(solution)/shard_map/ppermute | solution.py:435
  97.7 1.9 %collective-permute-start.15 = (f32[2,8,8,512]{3,2,1,0:T(8,128)S(1)}, f32[2,8,8,512]{3,2,1,0:T(8,128)S(1)}, u32[]{:S(2)}, u32[]{:S(2)}) collective-permute-start(f32[2,8,8,512]{3,2,1,0:T(8,128)S(1)} %get-tuple-element.44), channel_id=1, source_target_pairs={{0,31},{1,2},{2,1},{3,4},{4,3},{5,6},{6,5},{7,8},{8,7},{9,10},{10,... | collective-permute-start | bytes 786440 | tf_op jit(solution)/shard_map/ppermute | solution.py:444
  99.6 3.8 %collective-permute-start.16 = (f32[2,8,8,512]{3,2,1,0:T(8,128)S(1)}, f32[2,8,8,512]{3,2,1,0:T(8,128)S(1)}, u32[]{:S(2)}, u32[]{:S(2)}) collective-permute-start(f32[2,8,8,512]{3,2,1,0:T(8,128)S(1)} %get-tuple-element.42.rest), channel_id=1, source_target_pairs={{0,31},{1,2},{2,1},{3,4},{4,3},{5,6},{6,5},{7,8},{8,7},{9,10},{10,... | collective-permute-start | bytes 786440 | tf_op jit(solution)/shard_map/ppermute | solution.py:444
  103.5 0.0 collective-permute-done.18.others
  103.5 0.7 shard_map.49.refs_1_.given
  104.2 6.8 %collective-permute-done.15.near = f32[2,8,8,512]{3,2,1,0:T(8,128)S(1)} collective-permute-done((f32[2,8,8,512]{3,2,1,0:T(8,128)S(1)}, f32[2,8,8,512]{3,2,1,0:T(8,128)S(1)}, u32[]{:S(2)}, u32[]{:S(2)}) %collective-permute-start.15) | collective-permute-done | bytes 262176 | tf_op jit(solution)/shard_map/ppermute | solution.py:444
  111.0 0.0 collective-permute-done.17.inner
  111.0 3.1 %shard_map.48 = (f32[3,2,8,8,512]{4,3,2,1,0:T(8,128)S(1)}, f32[2,8,8,512]{3,2,1,0:T(8,128)S(1)}) custom-call(s32[3]{0:T(128)S(1)} %pad_add_fusion.place, f32[4,8,8,512]{3,2,1,0:T(8,128)S(1)} %get-tuple-element.45.state, f32[4,8,8,512]{3,2,1,0:T(8,128)S(1)} %collective-permute-done.17.inner, f32[2,8,8,512]{3,2,1,0:T(8,128)S(1)} %collective-permute-done.15.near, ...), custom_call_target="tpu_custom_call" | custom-call | tf_op jit(solution)/shard_map/pallas_call | solution.py:525
  114.1 0.0 collective-permute-done.16.far
  114.1 1.9 %shard_map.50 = (f32[4,8,8,512]{3,2,1,0:T(8,128)S(1)}, f32[32,2,8,128]{3,2,1,0:T(8,128)S(1)}) custom-call(s32[3]{0:T(128)S(1)} %pad_add_fusion.place, f32[2,8,8,512]{3,2,1,0:T(8,128)S(1)} %collective-permute-done.15.near, f32[2,8,8,512]{3,2,1,0:T(8,128)S(1)} %collective-permute-done.16.far, f32[4,7,8,8,512]{4,3,2,1,0:T(8,128)S(1)} %get-tuple-element.29.own, ...), custom_call_target="tpu_custom_call" | custom-call | tf_op jit(solution)/shard_map/pallas_call | solution.py:547
  116.0 17.7 %all_to_all.10.residuals = f32[32,2,8,128]{3,2,1,0:T(8,128)S(1)} all-to-all(f32[32,2,8,128]{3,2,1,0:T(8,128)S(1)} %get-tuple-element.49), channel_id=1, replica_groups=mesh['cuts'=16,'space'=32] {'space'}, dimensions={0} | all-to-all | bytes 524288 | tf_op jit(solution)/shard_map/all_to_all | solution.py:549
  133.7 9.2 %shard_map.51 = f32[16,2,8,128]{3,2,1,0:T(8,128)S(1)} custom-call(s32[3]{0:T(128)S(1)} %pad_add_fusion.place, f32[32,2,8,128]{3,2,1,0:T(8,128)S(1)} %all_to_all.10.residuals, f32[32,7,2,8,128]{4,3,2,1,0:T(8,128)S(1)} %shard_map.49.refs_1_.given), custom_call_target="tpu_custom_call" | custom-call | tf_op jit(solution)/shard_map/pallas_call | solution.py:550
  142.9 12.7 %all_to_all.11.shares = f32[16,2,8,128]{3,2,1,0:T(8,128)S(1)} all-to-all(f32[16,2,8,128]{3,2,1,0:T(8,128)S(1)} %shard_map.51), channel_id=1, replica_groups=mesh['cuts'=16,'space'=32] {'cuts'}, dimensions={0} | all-to-all | bytes 262144 | tf_op jit(solution)/shard_map/all_to_all | solution.py:556
  155.6 1.1 shard_map.52
  (1 shorter events, 0.0 us)
Async XLA Ops:
  0.1 1.4 copy-start
  1.5 1.1 copy-start.2
  1.5 1.2 copy-start.3
  2.7 13.4 %copy-start.1 = (f32[3,4,64,512]{3,2,1,0:T(8,128)S(1)}, f32[3,4,64,512]{3,2,1,0:T(8,128)}, u32[]{:S(2)}) copy-start(f32[3,4,64,512]{3,2,1,0:T(8,128)} %velocity.5) | copy-start | bytes 4718596
  4.3 23.0 %collective-permute-start.2 = (f32[16,64,512]{2,1,0:T(8,128)S(1)}, f32[16,64,512]{2,1,0:T(8,128)S(1)}, u32[]{:S(2)}, u32[]{:S(2)}) collective-permute-start(f32[16,64,512]{2,1,0:T(8,128)S(1)} %get-tuple-element.30), channel_id=1, source_target_pairs={{0,1},{1,0},{2,3},{3,2},{4,5},{5,4},{6,7},{7,6},{8,9},{9,8},{10,11... | collective-permute-start | bytes 6291464 | tf_op jit(solution)/shard_map/ppermute | solution.py:435
  6.2 30.2 %collective-permute-start.1 = (f32[9,64,512]{2,1,0:T(8,128)S(1)}, f32[9,64,512]{2,1,0:T(8,128)S(1)}, u32[]{:S(2)}, u32[]{:S(2)}) collective-permute-start(f32[9,64,512]{2,1,0:T(8,128)S(1)} %shard_map.37.earlier), channel_id=1, source_target_pairs={{0,287},{1,258},{2,257},{3,260},{4,259},{5,262},{6,261},{7,264},{8... | collective-permute-start | bytes 3538952 | tf_op jit(solution)/shard_map/ppermute | solution.py:453
  9.8 24.5 %collective-permute-start = (f32[7,64,512]{2,1,0:T(8,128)S(1)}, f32[7,64,512]{2,1,0:T(8,128)S(1)}, u32[]{:S(2)}, u32[]{:S(2)}) collective-permute-start(f32[7,64,512]{2,1,0:T(8,128)S(1)} %get-tuple-element.28), channel_id=1, source_target_pairs={{0,31},{1,2},{2,1},{3,4},{4,3},{5,6},{6,5},{7,8},{8,7},{9,10},{10,... | collective-permute-start | bytes 2752520 | tf_op jit(solution)/shard_map/ppermute | solution.py:444
  17.4 19.6 %collective-permute-start.5 = (f32[1,4,2,8,128]{4,3,2,1,0:T(8,128)S(1)}, f32[1,4,2,8,128]{4,3,2,1,0:T(8,128)S(1)}, u32[]{:S(2)}, u32[]{:S(2)}) collective-permute-start(f32[1,4,2,8,128]{4,3,2,1,0:T(8,128)S(1)} %bitcast.8), channel_id=1, source_target_pairs={{0,24},{1,25},{2,26},{3,27},{4,28},{5,29},{6,30},{7,31},{8,16},{9,... | collective-permute-start | bytes 98312 | tf_op jit(solution)/shard_map/ppermute | solution.py:463
  25.4 11.6 %collective-permute-start.4 = (f32[1,4,2,8,128]{4,3,2,1,0:T(8,128)S(1)}, f32[1,4,2,8,128]{4,3,2,1,0:T(8,128)S(1)}, u32[]{:S(2)}, u32[]{:S(2)}) collective-permute-start(f32[1,4,2,8,128]{4,3,2,1,0:T(8,128)S(1)} %bitcast.9), channel_id=1, source_target_pairs={{0,16},{1,17},{2,18},{3,19},{4,20},{5,21},{6,22},{7,23},{8,24},{9,... | collective-permute-start | bytes 98312 | tf_op jit(solution)/shard_map/ppermute | solution.py:463
  27.3 9.7 %collective-permute-start.3 = (f32[1,4,2,8,128]{4,3,2,1,0:T(8,128)S(1)}, f32[1,4,2,8,128]{4,3,2,1,0:T(8,128)S(1)}, u32[]{:S(2)}, u32[]{:S(2)}) collective-permute-start(f32[1,4,2,8,128]{4,3,2,1,0:T(8,128)S(1)} %bitcast.10), channel_id=1, source_target_pairs={{0,8},{1,9},{2,10},{3,11},{4,12},{5,13},{6,14},{7,15},{8,0},{9,1},... | collective-permute-start | bytes 98312 | tf_op jit(solution)/shard_map/ppermute | solution.py:463
  39.6 28.3 %collective-permute-start.8 = (f32[4,8,8,512]{3,2,1,0:T(8,128)S(1)}, f32[4,8,8,512]{3,2,1,0:T(8,128)S(1)}, u32[]{:S(2)}, u32[]{:S(2)}) collective-permute-start(f32[4,8,8,512]{3,2,1,0:T(8,128)S(1)} %get-tuple-element.35.state), channel_id=1, source_target_pairs={{0,1},{1,0},{2,3},{3,2},{4,5},{5,4},{6,7},{7,6},{8,9},{9,8},{10,11... | collective-permute-start | bytes 1572872 | tf_op jit(solution)/shard_map/ppermute | solution.py:435
  49.6 18.3 %collective-permute-start.6 = (f32[2,8,8,512]{3,2,1,0:T(8,128)S(1)}, f32[2,8,8,512]{3,2,1,0:T(8,128)S(1)}, u32[]{:S(2)}, u32[]{:S(2)}) collective-permute-start(f32[2,8,8,512]{3,2,1,0:T(8,128)S(1)} %get-tuple-element.33), channel_id=1, source_target_pairs={{0,31},{1,2},{2,1},{3,4},{4,3},{5,6},{6,5},{7,8},{8,7},{9,10},{10,... | collective-permute-start | bytes 786440 | tf_op jit(solution)/shard_map/ppermute | solution.py:444
  53.2 17.8 %collective-permute-start.7 = (f32[2,8,8,512]{3,2,1,0:T(8,128)S(1)}, f32[2,8,8,512]{3,2,1,0:T(8,128)S(1)}, u32[]{:S(2)}, u32[]{:S(2)}) collective-permute-start(f32[2,8,8,512]{3,2,1,0:T(8,128)S(1)} %get-tuple-element.34), channel_id=1, source_target_pairs={{0,31},{1,2},{2,1},{3,4},{4,3},{5,6},{6,5},{7,8},{8,7},{9,10},{10,... | collective-permute-start | bytes 786440 | tf_op jit(solution)/shard_map/ppermute | solution.py:444
  55.2 15.8 %collective-permute-start.9 = (f32[4,4,2,8,128]{4,3,2,1,0:T(8,128)S(1)}, f32[4,4,2,8,128]{4,3,2,1,0:T(8,128)S(1)}, u32[]{:S(2)}, u32[]{:S(2)}) collective-permute-start(f32[4,4,2,8,128]{4,3,2,1,0:T(8,128)S(1)} %get-tuple-element.38.refs_0_), channel_id=1, source_target_pairs={{0,258},{1,259},{2,256},{3,257},{4,262},{5,263},{6,260},{7,261},{8... | collective-permute-start | bytes 393224 | tf_op jit(solution)/shard_map/ppermute | solution.py:462
  59.8 11.2 %collective-permute-start.10 = (f32[2,8,128]{2,1,0:T(8,128)S(1)}, f32[2,8,128]{2,1,0:T(8,128)S(1)}, u32[]{:S(2)}, u32[]{:S(2)}) collective-permute-start(f32[2,8,128]{2,1,0:T(8,128)S(1)} %get-tuple-element.31.refs_1_.refs_2_), channel_id=1, source_target_pairs={{32,0},{64,32},{96,64},{128,96},{160,128},{192,160},{224,192},{256... | collective-permute-start | bytes 24584 | tf_op jit(solution)/shard_map/ppermute | solution.py:498
  72.7 12.3 %collective-permute-start.13 = (f32[4,8,8,512]{3,2,1,0:T(8,128)S(1)}, f32[4,8,8,512]{3,2,1,0:T(8,128)S(1)}, u32[]{:S(2)}, u32[]{:S(2)}) collective-permute-start(f32[4,8,8,512]{3,2,1,0:T(8,128)S(1)} %get-tuple-element.40.state), channel_id=1, source_target_pairs={{0,1},{1,0},{2,3},{3,2},{4,5},{5,4},{6,7},{7,6},{8,9},{9,8},{10,11... | collective-permute-start | bytes 1572872 | tf_op jit(solution)/shard_map/ppermute | solution.py:435
  74.6 10.4 %collective-permute-start.11 = (f32[2,8,8,512]{3,2,1,0:T(8,128)S(1)}, f32[2,8,8,512]{3,2,1,0:T(8,128)S(1)}, u32[]{:S(2)}, u32[]{:S(2)}) collective-permute-start(f32[2,8,8,512]{3,2,1,0:T(8,128)S(1)} %get-tuple-element.39), channel_id=1, source_target_pairs={{0,31},{1,2},{2,1},{3,4},{4,3},{5,6},{6,5},{7,8},{8,7},{9,10},{10,... | collective-permute-start | bytes 786440 | tf_op jit(solution)/shard_map/ppermute | solution.py:444
  76.5 11.6 %collective-permute-start.14 = (f32[8,4,2,8,128]{4,3,2,1,0:T(8,128)S(1)}, f32[8,4,2,8,128]{4,3,2,1,0:T(8,128)S(1)}, u32[]{:S(2)}, u32[]{:S(2)}) collective-permute-start(f32[8,4,2,8,128]{4,3,2,1,0:T(8,128)S(1)} %get-tuple-element.43.refs_0_), channel_id=1, source_target_pairs={{0,4},{1,5},{2,6},{3,7},{4,0},{5,1},{6,2},{7,3},{8,12},{9,13},{10,... | collective-permute-start | bytes 786440 | tf_op jit(solution)/shard_map/ppermute | solution.py:463
  78.6 9.5 %collective-permute-start.12 = (f32[2,8,8,512]{3,2,1,0:T(8,128)S(1)}, f32[2,8,8,512]{3,2,1,0:T(8,128)S(1)}, u32[]{:S(2)}, u32[]{:S(2)}) collective-permute-start(f32[2,8,8,512]{3,2,1,0:T(8,128)S(1)} %get-tuple-element.37.rest), channel_id=1, source_target_pairs={{0,31},{1,2},{2,1},{3,4},{4,3},{5,6},{6,5},{7,8},{8,7},{9,10},{10,... | collective-permute-start | bytes 786440 | tf_op jit(solution)/shard_map/ppermute | solution.py:444
  89.8 13.7 %collective-permute-start.18 = (f32[16,4,2,8,128]{4,3,2,1,0:T(8,128)S(1)}, f32[16,4,2,8,128]{4,3,2,1,0:T(8,128)S(1)}, u32[]{:S(2)}, u32[]{:S(2)}) collective-permute-start(f32[16,4,2,8,128]{4,3,2,1,0:T(8,128)S(1)} %get-tuple-element.48.some), channel_id=1, source_target_pairs={{0,1},{1,0},{2,3},{3,2},{4,5},{5,4},{6,7},{7,6},{8,9},{9,8},{10,11... | collective-permute-start | bytes 1572872 | tf_op jit(solution)/shard_map/ppermute | solution.py:463
  95.8 15.2 %collective-permute-start.17 = (f32[4,8,8,512]{3,2,1,0:T(8,128)S(1)}, f32[4,8,8,512]{3,2,1,0:T(8,128)S(1)}, u32[]{:S(2)}, u32[]{:S(2)}) collective-permute-start(f32[4,8,8,512]{3,2,1,0:T(8,128)S(1)} %get-tuple-element.45.state), channel_id=1, source_target_pairs={{0,1},{1,0},{2,3},{3,2},{4,5},{5,4},{6,7},{7,6},{8,9},{9,8},{10,11... | collective-permute-start | bytes 1572872 | tf_op jit(solution)/shard_map/ppermute | solution.py:435
  97.7 13.3 %collective-permute-start.15 = (f32[2,8,8,512]{3,2,1,0:T(8,128)S(1)}, f32[2,8,8,512]{3,2,1,0:T(8,128)S(1)}, u32[]{:S(2)}, u32[]{:S(2)}) collective-permute-start(f32[2,8,8,512]{3,2,1,0:T(8,128)S(1)} %get-tuple-element.44), channel_id=1, source_target_pairs={{0,31},{1,2},{2,1},{3,4},{4,3},{5,6},{6,5},{7,8},{8,7},{9,10},{10,... | collective-permute-start | bytes 786440 | tf_op jit(solution)/shard_map/ppermute | solution.py:444
  99.6 14.5 %collective-permute-start.16 = (f32[2,8,8,512]{3,2,1,0:T(8,128)S(1)}, f32[2,8,8,512]{3,2,1,0:T(8,128)S(1)}, u32[]{:S(2)}, u32[]{:S(2)}) collective-permute-start(f32[2,8,8,512]{3,2,1,0:T(8,128)S(1)} %get-tuple-element.42.rest), channel_id=1, source_target_pairs={{0,31},{1,2},{2,1},{3,4},{4,3},{5,6},{6,5},{7,8},{8,7},{9,10},{10,... | collective-permute-start | bytes 786440 | tf_op jit(solution)/shard_map/ppermute | solution.py:444
